TPU v7x, 32 devices: a whole 2x2x4 slice. The times are simulated.
32 devices in a mesh: member: 4 (over z), lon: 8 (over y, x, core).
Axes of the slice: x: 2, y: 2, z: 4, core: 2. Of those that a mesh axis runs over, the one named last changes fastest.
Arguments:
- latent: bfloat16 [8, 4, 360, 641], P('member', None, 'lon'), may hold values from -6 to 6
- member_seeds: int32 [8], P('member'), may hold values from 0 to 63
- member_table: bfloat16 [64, 641], replicated, may hold values from -6 to 6
- row_bands: int32 [4], replicated, may hold values from 0 to 15
- disco_basis: bfloat16 [16, 4, 7, 7], replicated, may hold values from -0.8984375 to 0.8984375
- w_disco: bfloat16 [2564, 641], replicated, may hold values from -0.125 to 0.125
- w_expand: bfloat16 [641, 1282], replicated, may hold values from -0.25 to 0.25
- w_reduce: bfloat16 [1282, 641], replicated, may hold values from -0.15625 to 0.15625
- w_decode: bfloat16 [641, 288], replicated, may hold values from -0.25 to 0.25
- target: bfloat16 [4, 360, 288], P(None, 'lon'), may hold values from -12 to 12
Outputs:
- latent_grad: bfloat16 [8, 4, 360, 641], P('member', None, 'lon')
- grad_disco: bfloat16 [2564, 641], replicated
- grad_expand: bfloat16 [641, 1282], replicated
- grad_reduce: bfloat16 [1282, 641], replicated
- grad_decode: bfloat16 [641, 288], replicated
All inputs are finite; a program needn't handle non-finite values.
Results may differ from a plain program's by a relative error of at most 0.025.
Values may be sent and summed in bfloat16 or wider, within the bound.
No kernel may reach another device: no remote copies, remote signals or barrier semaphores. Data moves between devices by JAX's collectives and lax.ppermute only.
A program may use at most 128 MiB of HBM per device.

v0:
```python
import math

import jax
import jax.numpy as jnp
from jax import lax
from jax.sharding import PartitionSpec as P

stencil_reach = 3
smooth = 0.5


def extended_2(x, sides, width):
    for axis, dim in sides:
        size, length = (lax.axis_size(axis), x.shape[dim])
        up = [(i, (i + 1) % size) for i in range(size)]
        down = [(j, i) for i, j in up]
        last = lax.slice_in_dim(x, length - width, length, axis=dim)
        first = lax.slice_in_dim(x, 0, width, axis=dim)
        before = lax.ppermute(last, axis, up)
        after = lax.ppermute(first, axis, down)
        x = jnp.concatenate([before, x, after], axis=dim)
    return x


def smooth_slope(difference):
    return difference / jnp.sqrt(difference * difference + smooth * smooth)


def gelu_value(value):
    return jax.nn.gelu(value, approximate=True)


def pick_rows(index, table):
    table_rows = table.shape[0]
    onehot = (index[:, None] == jnp.arange(table_rows, dtype=jnp.int32)[None, :]).astype(
        table.dtype
    )
    return jnp.dot(onehot, table.reshape(table_rows, -1), preferred_element_type=jnp.float32)


def selector(first_len, second_len, offset, sign):
    first = jnp.arange(first_len, dtype=jnp.int32)[:, None, None]
    second = jnp.arange(second_len, dtype=jnp.int32)[None, :, None]
    taps = jnp.arange(7, dtype=jnp.int32)[None, None, :]
    return (sign * (first - second) + offset == taps).astype(jnp.float32)


def spread_local(widened, stencil, lon_count):
    row_count = widened.shape[1]
    in_len = widened.shape[2]
    row_pick = selector(row_count, row_count, 3, 1)
    col_pick = selector(in_len, lon_count, 0, 1)
    table = jnp.einsum(
        "sra,wlb,rkab->swrkl", row_pick, col_pick, stencil.astype(jnp.float32)
    ).astype(jnp.bfloat16)
    summed = jnp.einsum("mswc,swrkl->mrlkc", widened, table, preferred_element_type=jnp.float32)
    out_shape = summed.shape
    return summed.astype(jnp.bfloat16).reshape(
        out_shape[0], out_shape[1], out_shape[2], out_shape[3] * out_shape[4]
    )


def collect_local(extended, stencil, out_len):
    ext_shape = extended.shape
    row_count = ext_shape[1]
    in_len = ext_shape[2]
    basis_count = stencil.shape[1]
    split = extended.reshape(
        ext_shape[0], row_count, in_len, basis_count, ext_shape[3] // basis_count
    )
    row_pick = selector(row_count, row_count, 3, -1)
    col_pick = selector(in_len, out_len, 6, -1)
    table = jnp.einsum(
        "rsa,wlb,rkab->rwksl", row_pick, col_pick, stencil.astype(jnp.float32)
    ).astype(jnp.bfloat16)
    return jnp.einsum("mrwkc,rwksl->mslc", split, table, preferred_element_type=jnp.float32)


def crps_slopes(owned, everyone, observed):
    member_total = everyone.shape[0]
    owned_wide = owned.astype(jnp.float32)
    every_wide = everyone.astype(jnp.float32)
    paired = jnp.sum(smooth_slope(owned_wide[:, None] - every_wide[None]), axis=1)
    direct = smooth_slope(owned_wide - observed.astype(jnp.float32)[None])
    return (direct - paired / (member_total - 1)).astype(jnp.bfloat16)


def per_device(
    latent,
    member_seeds,
    member_table,
    row_bands,
    disco_basis,
    w_disco,
    w_expand,
    w_reduce,
    w_decode,
    target,
):
    members_here, row_count, lon_count, chan_count = latent.shape
    basis_count = disco_basis.shape[1]
    stencil = (
        pick_rows(row_bands, disco_basis).astype(jnp.bfloat16).reshape(row_count, basis_count, 7, 7)
    )
    offsets = pick_rows(member_seeds, member_table)
    seeded = (latent.astype(jnp.float32) + offsets[:, None, None, :]).astype(jnp.bfloat16)
    widened = extended_2(seeded, (("lon", 2),), stencil_reach)
    spread = spread_local(widened, stencil, lon_count)
    flat_rows = members_here * row_count * lon_count
    spread_rows = spread.reshape(flat_rows, -1)
    seeded_rows = seeded.reshape(flat_rows, chan_count)
    conv_out = jnp.dot(spread_rows, w_disco, preferred_element_type=jnp.float32)
    hidden_in = (seeded_rows.astype(jnp.float32) + conv_out).astype(jnp.bfloat16)
    pre_act = jnp.dot(hidden_in, w_expand, preferred_element_type=jnp.float32)
    gelu_out = gelu_value(pre_act).astype(jnp.bfloat16)
    mixed = (
        hidden_in.astype(jnp.float32)
        + jnp.dot(gelu_out, w_reduce, preferred_element_type=jnp.float32)
    ).astype(jnp.bfloat16)
    fields = jnp.dot(mixed, w_decode, preferred_element_type=jnp.float32).astype(jnp.bfloat16)
    fields = fields.reshape(members_here, row_count, lon_count, -1)
    everyone = lax.all_gather(fields, "member", axis=0, tiled=True)
    field_grad = crps_slopes(fields, everyone, target)
    grad_rows = field_grad.reshape(flat_rows, -1)
    mixed_grad = jnp.einsum(
        "po,co->pc", grad_rows, w_decode, preferred_element_type=jnp.float32
    ).astype(jnp.bfloat16)
    gelu_grad = jnp.einsum("pc,hc->ph", mixed_grad, w_reduce, preferred_element_type=jnp.float32)
    unused, pullback = jax.vjp(gelu_value, pre_act)
    pre_grad = pullback(gelu_grad)[0].astype(jnp.bfloat16)
    back_expand = jnp.einsum("ph,ch->pc", pre_grad, w_expand, preferred_element_type=jnp.float32)
    hidden_grad = (mixed_grad.astype(jnp.float32) + back_expand).astype(jnp.bfloat16)
    spread_grad = jnp.einsum(
        "pc,kc->pk", hidden_grad, w_disco, preferred_element_type=jnp.float32
    ).astype(jnp.bfloat16)
    spread_grad = spread_grad.reshape(members_here, row_count, lon_count, -1)
    extended = extended_2(spread_grad, (("lon", 2),), stencil_reach)
    carried = collect_local(extended, stencil, lon_count)
    latent_grad = (
        hidden_grad.astype(jnp.float32).reshape(members_here, row_count, lon_count, chan_count)
        + carried
    ).astype(jnp.bfloat16)
    grad_disco = jnp.einsum(
        "pk,pc->kc", spread_rows, hidden_grad, preferred_element_type=jnp.float32
    )
    grad_expand = jnp.einsum("pc,ph->ch", hidden_in, pre_grad, preferred_element_type=jnp.float32)
    grad_reduce = jnp.einsum("ph,pc->hc", gelu_out, mixed_grad, preferred_element_type=jnp.float32)
    grad_decode = jnp.einsum("pc,po->co", mixed, grad_rows, preferred_element_type=jnp.float32)
    factor = 1.0 / math.sqrt(
        members_here * lax.axis_size("member") * row_count * lon_count * lax.axis_size("lon")
    )
    summed = lax.psum((grad_disco, grad_expand, grad_reduce, grad_decode), ("member", "lon"))
    finals = [(piece * factor).astype(jnp.bfloat16) for piece in summed]
    return (latent_grad, finals[0], finals[1], finals[2], finals[3])


def solution(mesh):
    placed = (
        P("member", None, "lon", None),
        P("member"),
        P(),
        P(),
        P(),
        P(),
        P(),
        P(),
        P(),
        P(None, "lon", None),
    )
    return jax.shard_map(
        per_device,
        mesh=mesh,
        in_specs=placed,
        out_specs=(P("member", None, "lon", None), P(), P(), P(), P()),
        check_vma=False,
    )
```

profile of v0, /device:TPU:0, one launch (start us, length us, event | category | flops | bytes accessed | tf_op | source)
XLA Modules:
  0.0 385.0 jit_solution(16366432439883252629)
XLA Ops:
  7.2 1.3 fusion.47
  8.5 2.2 add_convert_fusion
  10.7 0.9 copy-done.9
  11.6 0.7 fusion.57
  12.2 0.5 collective-permute-start
  12.7 2.9 collective-permute-start.1
  15.6 0.6 iota_subtract_fusion
  16.2 0.7 reshape.109
  16.9 1.0 convolution_convert_fusion.5
  17.8 0.1 reshape.110
  18.1 2.1 fusion.22
  20.2 2.4 reshape.115
  22.6 2.5 copy.86
  25.1 0.9 copy.87
  26.1 0.9 sub.105
  26.9 1.9 sub.106
  28.8 2.0 copy.88
  30.9 2.2 fusion.8
  33.1 3.1 copy.85
  36.2 4.7 %reshape_reshape.3 = bf16[360,2564]{1,0:T(8,128)(2,1)} reshape(bf16[2,4,45,4,641]{4,3,2,1,0:T(4,128)(2,1)} %copy.85) | data formatting | bytes 3692160 | tf_op jit(solution)/shard_map/reshape;reshape | solution.py:110
  40.9 4.0 %fusion.21 = bf16[360,641]{0,1:T(8,128)(2,1)S(1)} fusion(f32[360,641]{0,1:T(8,128)} %copy.86, bf16[360,2564]{1,0:T(8,128)(2,1)} %reshape_reshape.3, bf16[2564,641]{0,1:T(8,128)(2,1)S(1)} %copy-done), kind=kOutput, calls=%fused_computation.37 | convolution fusion | flops 1183798784 | bytes 6517688 | tf_op jit(solution)/shard_map/dot_general | solution.py:112
  45.0 1.2 fusion.58
  46.2 0.4 copy-done.13
  46.6 1.3 fusion.19
  48.0 0.8 copy-done.5
  48.8 1.1 convolution_convert_fusion.4
  49.9 1.8 copy.89
  51.7 1.8 reshape.111
  53.5 1.1 copy.90
  54.6 1.0 convert_element_type.123
  55.6 24.4 %all_gather.3 = bf16[8,4,45,288]{3,1,2,0:T(4,128)(2,1)S(1)} all-gather(bf16[2,4,45,288]{3,1,2,0:T(4,128)(2,1)S(1)} %copy.90), channel_id=1, replica_groups=mesh['member'=4,'lon'=8] {'member'}, dimensions={0}, use_global_device_ids=true | all-gather | bytes 1036800 | tf_op jit(solution)/shard_map/all_gather | solution.py:122
  80.1 1.9 fusion.2
  82.0 0.9 broadcast_multiply_fusion
  82.9 1.9 div.18
  84.8 2.0 copy.92
  86.8 1.5 subtract_convert_fusion
  88.3 1.6 convolution_convert_fusion.3
  89.9 3.9 %fusion.15 = bf16[360,1282]{0,1:T(8,128)(2,1)S(1)} fusion(f32[360,1282]{0,1:T(8,128)} %copy-done.18, bf16[360,641]{0,1:T(8,128)(2,1)S(1)} %convolution_convert_fusion.3, bf16[1282,641]{0,1:T(8,128)(2,1)S(1)} %copy-done.14), kind=kOutput, calls=%fused_computation.25 | convolution fusion | flops 600898688 | bytes 4874164 | tf_op jit(solution)/shard_map/pc,hc->ph/dot_general | solution.py:128
  93.8 3.2 fusion.55
  97.0 1.2 fusion.20
  98.3 3.0 fusion.60
  101.3 1.3 fusion.61
  102.6 5.0 %fusion.59 = f32[2564,641]{0,1:T(8,128)} fusion(bf16[360,2564]{1,0:T(8,128)(2,1)S(1)} %copy-done.1, bf16[360,641]{0,1:T(8,128)(2,1)S(1)} %fusion.20), kind=kOutput, calls=%fused_computation.87 | convolution fusion | flops 1183337216 | bytes 8881696 | tf_op jit(solution)/shard_map/pk,pc->kc/dot_general | solution.py:143
  107.7 4.4 %convolution_convert_fusion = bf16[360,2564]{1,0:T(8,128)(2,1)} fusion(bf16[360,641]{0,1:T(8,128)(2,1)} %copy-done.2, bf16[2564,641]{0,1:T(8,128)(2,1)S(1)} %copy-done), kind=kOutput, calls=%fused_computation.7 | convolution fusion | flops 1184260224 | bytes 5594648 | tf_op jit(solution)/shard_map/pc,kc->pk/dot_general | solution.py:133
  112.1 3.8 reshape.114
  115.9 1.9 fusion.56
  117.9 2.6 collective-permute-start.3
  120.5 1.4 fusion.23
  121.9 6.4 %concatenate.15 = bf16[2,4,45,4,641]{4,3,2,1,0:T(4,128)(2,1)} reshape(bf16[360,2564]{1,0:T(8,128)(2,1)} %convolution_convert_fusion) | data formatting | bytes 3692160 | tf_op jit(solution)/shard_map/concatenate | solution.py:21
  128.3 4.3 %reshape.130 = f32[2,4,45,641]{2,1,0,3:T(4,128)} reshape(bf16[360,641]{0,1:T(8,128)(2,1)} %copy-done.2) | data formatting | bytes 1384560 | tf_op jit(solution)/shard_map/reshape | solution.py:140
  132.6 3.4 copy.97
  136.0 3.9 %copy.100 = f32[2,4,45,641]{3,2,0,1:T(8,128)} copy(f32[2,4,45,641]{2,1,0,3:T(4,128)} %reshape.130) | data formatting | bytes 1846080 | tf_op jit(solution)/shard_map/reshape | solution.py:140
  139.9 1.8 reshape.131
  141.8 1.7 copy.96
  143.4 1.9 reshape.132
  145.3 1.0 copy.98
  146.3 3.8 fusion.18
  150.1 1.2 copy.101
  151.3 216.2 %all-reduce.3.cloned.1.call-done = (f32[2564,641]{0,1:T(8,128)}, f32[641,1282]{1,0:T(8,128)}, f32[1282,641]{0,1:T(8,128)}, f32[641,288]{0,1:T(8,128)}) async-done(((f32[2564,641]{0,1:T(8,128)}, f32[641,1282]{1,0:T(8,128)}, f32[1282,641]{0,1:T(8,128)}, f32[641,288]{0,1:T(8,128)}), (f32[2564,641]{0,1:T(8,128)}, f32[641,1282]{1,0:T(8,128)}, f32[1282,641]{0,1:T(8,128)}, ...) | async-done | bytes 13886640 | tf_op jit(solution)/shard_map/psum | solution.py:152
  367.5 5.5 %multiply_convert_fusion = bf16[2564,641]{0,1:T(8,128)(2,1)} fusion(f32[2564,641]{0,1:T(8,128)} %get-tuple-element.30), kind=kLoop, calls=%fused_computation | loop fusion | flops 3287048 | bytes 9861144 | tf_op jit(solution)/shard_map/convert_element_type | solution.py:153
  373.0 1.5 multiply_convert_fusion.1
  374.6 1.1 copy-done.3
  375.7 1.5 multiply_convert_fusion.2
  377.3 0.8 multiply_convert_fusion.4
  (49 shorter events, 0.4 us)
Async XLA Ops:
  7.2 33.7 %copy-start = (bf16[2564,641]{0,1:T(8,128)(2,1)S(1)}, bf16[2564,641]{0,1:T(8,128)(2,1)}, u32[]{:S(2)}) copy-start(bf16[2564,641]{0,1:T(8,128)(2,1)} %param.15) | copy-start | bytes 9861148
  7.2 9.7 %copy-start.17 = (s32[4]{0:T(128)S(1)}, s32[4]{0:T(128)}, u32[]{:S(2)}) copy-start(s32[4]{0:T(128)} %param.13) | copy-start | bytes 52
  7.2 360.3 %all-reduce.3.cloned.1.call-start = ((), (), s32[]{:S(2)}) async-start(), calls=%async_computation | async-start | bytes 30302208 | tf_op jit(solution)/shard_map/psum | solution.py:152
  7.2 9.0 %copy-start.12 = (bf16[16,4,7,7]{0,1,3,2:T(4,128)(2,1)S(1)}, bf16[16,4,7,7]{0,1,3,2:T(4,128)(2,1)}, u32[]{:S(2)}) copy-start(bf16[16,4,7,7]{0,1,3,2:T(4,128)(2,1)} %param.14) | copy-start | bytes 18820
  10.7 0.9 copy-start.9
  12.2 18.6 %collective-permute-start = (bf16[2,4,3,641]{3,2,1,0:T(4,128)(2,1)}, bf16[2,4,3,641]{3,2,1,0:T(4,128)(2,1)}, u32[]{:S(2)}, u32[]{:S(2)}) collective-permute-start(bf16[2,4,3,641]{3,2,1,0:T(4,128)(2,1)} %get-tuple-element.36), channel_id=1, source_target_pairs={{0,1},{1,2},{2,3},{3,4},{4,5},{5,6},{6,7},{7,0},{8,9},{9,10},{10,1... | collective-permute-start | bytes 92312 | tf_op jit(solution)/shard_map/ppermute | solution.py:19
  12.7 18.2 %collective-permute-start.1 = (bf16[2,4,3,641]{3,2,1,0:T(4,128)(2,1)}, bf16[2,4,3,641]{3,2,1,0:T(4,128)(2,1)}, u32[]{:S(2)}, u32[]{:S(2)}) collective-permute-start(bf16[2,4,3,641]{3,2,1,0:T(4,128)(2,1)} %get-tuple-element.37), channel_id=1, source_target_pairs={{1,0},{2,1},{3,2},{4,3},{5,4},{6,5},{7,6},{0,7},{9,8},{10,9},{11,1... | collective-permute-start | bytes 92312 | tf_op jit(solution)/shard_map/ppermute | solution.py:20
  40.9 4.0 %copy-start.15 = (bf16[641,1282]{1,0:T(8,128)(2,1)S(1)}, bf16[641,1282]{1,0:T(8,128)(2,1)}, u32[]{:S(2)}) copy-start(bf16[641,1282]{1,0:T(8,128)(2,1)} %param.16) | copy-start | bytes 4930576
  44.9 1.3 copy-start.10
  45.0 1.7 copy-start.13
  46.6 1.3 copy-start.18
  46.6 2.2 copy-start.7
  48.0 0.8 copy-start.5
  86.8 3.0 copy-start.14
  89.9 4.0 %copy-start.19 = (f32[360,1282]{0,1:T(8,128)S(1)}, f32[360,1282]{0,1:T(8,128)}, u32[]{:S(2)}) copy-start(f32[360,1282]{0,1:T(8,128)} %copy-done.18) | copy-start | bytes 5538244
  93.8 3.2 copy-start.16
  97.0 1.2 copy-start.11
  98.2 4.4 %copy-start.2 = (bf16[360,641]{0,1:T(8,128)(2,1)}, bf16[360,641]{0,1:T(8,128)(2,1)S(1)}, u32[]{:S(2)}) copy-start(bf16[360,641]{0,1:T(8,128)(2,1)S(1)} %fusion.20) | copy-start | bytes 1384564
  98.2 3.0 copy-start.6
  98.3 4.4 %copy-start.1 = (bf16[360,2564]{1,0:T(8,128)(2,1)S(1)}, bf16[360,2564]{1,0:T(8,128)(2,1)}, u32[]{:S(2)}) copy-start(bf16[360,2564]{1,0:T(8,128)(2,1)} %reshape_reshape.3) | copy-start | bytes 5538244
  117.8 22.1 %collective-permute-start.2 = (bf16[2,4,3,2564]{3,2,1,0:T(4,128)(2,1)}, bf16[2,4,3,2564]{3,2,1,0:T(4,128)(2,1)}, u32[]{:S(2)}, u32[]{:S(2)}) collective-permute-start(bf16[2,4,3,2564]{3,2,1,0:T(4,128)(2,1)} %get-tuple-element.34), channel_id=1, source_target_pairs={{0,1},{1,2},{2,3},{3,4},{4,5},{5,6},{6,7},{7,0},{8,9},{9,10},{10,1... | collective-permute-start | bytes 369224 | tf_op jit(solution)/shard_map/ppermute | solution.py:19
  117.9 25.6 %collective-permute-start.3 = (bf16[2,4,3,2564]{3,2,1,0:T(4,128)(2,1)}, bf16[2,4,3,2564]{3,2,1,0:T(4,128)(2,1)}, u32[]{:S(2)}, u32[]{:S(2)}) collective-permute-start(bf16[2,4,3,2564]{3,2,1,0:T(4,128)(2,1)} %get-tuple-element.35), channel_id=1, source_target_pairs={{1,0},{2,1},{3,2},{4,3},{5,4},{6,5},{7,6},{0,7},{9,8},{10,9},{11,1... | collective-permute-start | bytes 369224 | tf_op jit(solution)/shard_map/ppermute | solution.py:20
  367.5 5.5 %copy-start.4 = (f32[1282,641]{0,1:T(8,128)S(1)}, f32[1282,641]{0,1:T(8,128)}, u32[]{:S(2)}) copy-start(f32[1282,641]{0,1:T(8,128)} %get-tuple-element.32) | copy-start | bytes 9861148
  373.0 2.7 copy-start.3
  375.7 1.5 copy-start.8
Sparse Core Ops, SparseCore 0:
  107.8 259.7 all-reduce.2
where the time goes:
time: 386 us; the launch traced here: 385 us
  waiting for transfers between devices  216 us (56%)
  local copies, waits for them, and re-layouts  63.4 us (16%)
  matrix products  43 us (11%)
  blocking collectives  24.4 us (6%)
  other arithmetic  17.6 us (5%)
  between operations  14.3 us (4%)
  starting transfers between devices  6.02 us (2%)
    psum x1, waiting for transfers between devices, per_device(): lax.psum((grad_disco, grad_expand, grad_reduce, grad_decode), ('member',...  216 us
    all_gather x1, blocking collectives, per_device(): everyone = lax.all_gather(fields, 'member', axis=0, tiled=True)  24.4 us
    concatenate x6, local copies, waits for them, and re-layouts, extended_2(): x = jnp.concatenate([before, x, after], axis=dim)  16.2 us
    convert_element_type x4, other arithmetic, per_device(): finals = [(piece * factor).astype(jnp.bfloat16) for piece in summed]  9.41 us
    reshape x2, local copies, waits for them, and re-layouts, per_device(): hidden_grad.astype(jnp.float32)  8.21 us
  transfers between devices with their start and end apart: 5, of which 1 were waited for; matrix products, arithmetic and copies ran while one was open for 15% of the time, Pallas kernels for 0%

commit v1 on v0

v1 whole, which is shorter than its diff:
```python
import functools
import math

import jax
import jax.numpy as jnp
from jax import lax
from jax.experimental import pallas as pl
from jax.experimental.pallas import tpu as pltpu
from jax.sharding import PartitionSpec as P

reach = 3
taps = 2 * reach + 1
smooth = 0.5
LANES = 128
TILE = 16
VMEM_LIMIT = 56 * 2**20
F32 = jnp.float32
BF16 = jnp.bfloat16


def up(value, unit):
    return -(-value // unit) * unit


def dot(a, b, ca=1, cb=0):
    return lax.dot_general(a, b, (((ca,), (cb,)), ((), ())), preferred_element_type=F32)


def slope(d):
    return d * lax.rsqrt(d * d + smooth * smooth)


def vmem_call(body, outs, args, smem=0, scratch=(), name=None):
    specs = [pl.BlockSpec(memory_space=pltpu.SMEM)] * smem
    specs += [pl.BlockSpec(memory_space=pltpu.VMEM)] * (len(args) - smem)
    return pl.pallas_call(
        body,
        out_shape=[jax.ShapeDtypeStruct(shape, dtype) for shape, dtype in outs],
        in_specs=specs,
        out_specs=[pl.BlockSpec(memory_space=pltpu.VMEM)] * len(outs),
        scratch_shapes=list(scratch),
        compiler_params=pltpu.CompilerParams(vmem_limit_bytes=VMEM_LIMIT),
        name=name,
    )(*args)


def forward_body(
    dims, seeds, bands, basis, latent, left, right, table, w_disco, w_expand, w_reduce, w_decode,
    stencil_out, spread_out, hidden_out, gelu_out, slope_out, mixed_out, fields_out, wide,
):
    members, rows, lons, chans, lon_pad, slot, bases, piece, share = dims
    chan_pad = up(chans, LANES)
    points = rows * lon_pad
    per_tile = LANES // slot
    lane = lax.broadcasted_iota(jnp.int32, (lon_pad, LANES), 1)
    lon = lax.broadcasted_iota(jnp.int32, (lon_pad, LANES), 0)
    place = lane % slot
    own = place < lons
    before = (place >= lon_pad) & (place < lon_pad + reach)
    after = (place >= lon_pad + 8) & (place < lon_pad + 8 + reach)
    wide_lon = jnp.where(own, place + reach, jnp.where(before, place - lon_pad, place - lon_pad - 8 + lons + reach))
    tap = jnp.where((own | before | after) & (lon < lons), wide_lon - lon, -1)
    tap = jnp.where(lane < slot, tap, tap + 1000 * (lane // slot))
    masks = [[tap == 1000 * part + b for b in range(taps)] for part in range(per_tile)]
    for r in range(rows):
        band = bands[r]
        for k in range(bases):
            for t in range(rows // per_tile):
                block = jnp.zeros((lon_pad, LANES), F32)
                for part in range(per_tile):
                    a = t * per_tile + part - r + reach
                    if not 0 <= a < taps:
                        continue
                    base = ((band * bases + k) * taps + a) * taps
                    for b in range(taps):
                        block = jnp.where(masks[part][b], basis[base + b], block)
                stencil_out[k * points + r * lon_pad : k * points + (r + 1) * lon_pad, t * LANES : (t + 1) * LANES] = block.astype(BF16)
    seed_count = table.shape[0]
    mrow = lax.broadcasted_iota(jnp.int32, (TILE, seed_count), 0)
    mcol = lax.broadcasted_iota(jnp.int32, (TILE, seed_count), 1)
    onehot = jnp.zeros((TILE, seed_count), F32)
    for m in range(members):
        onehot = jnp.where((mrow == m) & (mcol == seeds[m]), 1.0, onehot)
    offsets = dot(onehot.astype(BF16), table[...])
    wide[...] = jnp.zeros_like(wide)
    for m in range(members):
        off = offsets[m : m + 1, :]
        for r in range(rows):
            for ref, start, count in ((latent, 0, lons), (left, lon_pad, reach), (right, lon_pad + 8, reach)):
                seeded = (ref[m, r].astype(F32) + off).astype(BF16).astype(F32)
                wide[m, r * slot + start : r * slot + start + count, :chans] = seeded
    for m in range(members):
        full = wide[m]
        carry = None
        for k in range(bases):
            moved = full if k == 0 else pltpu.roll(full, k, 1)
            out = dot(stencil_out[k * points : (k + 1) * points, :], moved.astype(BF16))
            width = chan_pad - LANES
            first = out[:, :LANES] if carry is None else out[:, :LANES] + carry
            rows_here = slice(m * points, (m + 1) * points)
            spread_out[rows_here, k * width : k * width + LANES] = first.astype(BF16)
            spread_out[rows_here, k * width + LANES : (k + 1) * width] = out[:, LANES:width].astype(BF16)
            carry = out[:, width:]
        spread_out[rows_here, bases * width : bases * width + LANES] = carry.astype(BF16)
    seeded_rows = jnp.concatenate(
        [wide[m, r * slot : r * slot + lon_pad, :chans] for m in range(members) for r in range(rows)], axis=0
    )
    conv = dot(spread_out[:, : bases * chans], w_disco[...])
    hidden = (seeded_rows + conv).astype(BF16)
    hidden_out[...] = hidden
    pre = dot(hidden, w_expand[...])
    rate = math.sqrt(2.0 / math.pi)
    square = pre * pre
    th = jnp.tanh(rate * (pre + 0.044715 * (square * pre)))
    half = 0.5 * (1.0 + th)
    act = (pre * half).astype(BF16)
    gelu_out[...] = act
    slope_out[...] = (half + 0.5 * pre * (1.0 - th * th) * (rate * (1.0 + 3 * 0.044715 * square))).astype(BF16)
    mixed = (hidden.astype(F32) + dot(act, w_reduce[...])).astype(BF16)
    mixed_out[...] = mixed
    fields = dot(mixed, w_decode[...])
    outs = fields.shape[1]
    turned = jnp.swapaxes(jnp.pad(fields, ((0, 0), (0, up(outs, LANES) - outs))), 0, 1)
    for q in range(share):
        low, high = q * piece, min((q + 1) * piece, up(outs, TILE))
        if high > low:
            fields_out[q, : high - low, :] = turned[low:high].astype(BF16)
        if high < (q + 1) * piece:
            start = max(high - low, 0)
            fields_out[q, start:, :] = jnp.zeros((piece - start, turned.shape[1]), BF16)


def crps_body(count, points, members, total, *refs):
    fields = [ref[...].astype(F32) for ref in refs[:count]]
    observed = refs[count][...].astype(F32)
    outs = refs[count + 1 :]
    turned = [[f] + [pltpu.roll(f, t * points, 1) for t in range(1, members)] for f in fields]
    for i in range(count):
        paired = jnp.zeros_like(observed)
        for j in range(count):
            for t in range(members):
                if i == j and t == 0:
                    continue
                paired = paired + slope(fields[i] - turned[j][t])
        outs[i][...] = (slope(fields[i] - observed) - paired * (1.0 / (total - 1))).astype(BF16)


def last_rows(values, col, height=TILE):
    tail = values[:, col:]
    extra = LANES - tail.shape[1]
    if extra:
        tail = jnp.concatenate([tail, jnp.zeros((tail.shape[0], extra), tail.dtype)], axis=1)
    return jnp.swapaxes(tail.astype(F32), 0, 1)[:height].astype(BF16)


def fold_rows(rows, width, first, into):
    n = rows.shape[1]
    count = -(-n // width)
    if count * width > n:
        rows = jnp.concatenate([rows, jnp.zeros((1, count * width - n), rows.dtype)], axis=1)
    at = lax.broadcasted_iota(jnp.int32, into.shape, 0)
    for t in range(count):
        into = jnp.where(at == first + t, rows[:, t * width : (t + 1) * width], into)
    return into, first + count


def backward_body(
    dims, scale, me, *refs,
):
    share, piece, outs, chans, hidden_units, width = dims
    grads = refs[:share]
    (w_decode, w_reduce, w_expand, slopes, hidden, gelu, mixed, packed, hidden_grad_out, turned_grad) = refs[share:]
    for d in range(share):
        turned_grad[pl.ds(pl.multiple_of(lax.rem(me[0] + d, share) * piece, TILE), piece), :] = grads[d][...]
    field_t = turned_grad[: up(outs, TILE)]
    field = jnp.swapaxes(field_t.astype(F32), 0, 1).astype(BF16)[:, :outs]
    mixed_grad = dot(field, w_decode[...], 1, 1).astype(BF16)
    gelu_grad = dot(mixed_grad, w_reduce[...], 1, 1)
    pre_grad = (gelu_grad * slopes[...].astype(F32)).astype(BF16)
    hidden_grad = (mixed_grad.astype(F32) + dot(pre_grad, w_expand[...], 1, 1)).astype(BF16)
    hidden_grad_out[...] = hidden_grad
    row = 0
    misc = jnp.zeros((TILE, width), F32)
    packed[row : row + hidden_units, :] = (dot(gelu[...], mixed_grad[:, :width], 0, 0) * scale).astype(BF16)
    tail = dot(last_rows(mixed_grad, width), gelu[...])
    misc, at = fold_rows(tail[0:1], width, 0, misc)
    row += up(hidden_units, TILE)
    for part in range(hidden_units // width):
        packed[row : row + chans, :] = (dot(hidden[...], pre_grad[:, part * width : (part + 1) * width], 0, 0) * scale).astype(BF16)
        row += up(chans, TILE)
    rest = hidden_units // width * width
    tail = dot(last_rows(pre_grad, rest), hidden[...])
    for i in range(hidden_units - rest):
        misc, at = fold_rows(tail[i : i + 1], width, at, misc)
    packed[row : row + outs, :] = (dot(field_t[:outs], mixed[:, :width]) * scale).astype(BF16)
    row += up(outs, TILE)
    tail = dot(last_rows(mixed[...], width), field)
    misc, at = fold_rows(tail[0:1], width, at, misc)
    packed[row : row + TILE, :] = (misc * scale).astype(BF16)
    if packed.shape[0] > row + TILE:
        packed[row + TILE :, :] = jnp.zeros((packed.shape[0] - row - TILE, width), BF16)


def disco_body(scale, width, tall, spread, hidden_grad, packed):
    grad = hidden_grad[...]
    value = dot(spread[...], grad[:, :width], 0, 0)
    packed[:tall, :] = (value[:tall] * scale).astype(BF16)
    tail = dot(last_rows(grad, width), spread[...])
    misc, at = fold_rows(tail[0:1, :tall], width, 0, jnp.zeros((TILE, width), F32))
    packed[tall : tall + TILE, :] = (misc * scale).astype(BF16)
    if packed.shape[0] > tall + TILE:
        packed[tall + TILE :, :] = jnp.zeros((packed.shape[0] - tall - TILE, width), BF16)


def collect_body(dims, hidden_grad, w_disco, stencil, out, left_out, right_out):
    members, rows, lons, chans, lon_pad, slot, bases = dims
    chan_pad = up(chans, LANES)
    points = rows * lon_pad
    width = chan_pad - LANES
    full = bases * width + LANES
    grad = dot(hidden_grad[...], w_disco[...], 1, 1).astype(BF16)
    grad = jnp.concatenate([grad, jnp.zeros((grad.shape[0], full - grad.shape[1]), BF16)], axis=1)
    for m in range(members):
        total = None
        for k in range(bases):
            part = dot(stencil[k * points : (k + 1) * points, :], grad[m * points : (m + 1) * points, k * width : k * width + chan_pad], 0, 0)
            part = part if k == 0 else pltpu.roll(part, chan_pad - k, 1)
            total = part if total is None else total + part
        for r in range(rows):
            at = r * slot
            own = hidden_grad[m * points + r * lon_pad : m * points + (r + 1) * lon_pad, :].astype(F32)
            out[m, r] = (own + total[at : at + lon_pad, :chans])[:lons]
            left_out[m, r] = total[at + lon_pad : at + lon_pad + 8, :chans][:reach]
            right_out[m, r] = total[at + lon_pad + 8 : at + lon_pad + 16, :chans][:reach]


def bits_of(axis):
    size, out, bit = lax.axis_size(axis), [], 1
    while bit < size:
        out.append((axis, bit))
        bit *= 2
    return out


def swap(x, pair):
    members, lons = lax.axis_size("member"), lax.axis_size("lon")
    perm = []
    for m in range(members):
        for n in range(lons):
            axis, bit = pair[n % 2]
            to = (m ^ bit) * lons + n if axis == "member" else m * lons + (n ^ bit)
            perm.append((m * lons + n, to))
    return lax.ppermute(x, ("member", "lon"), perm)


def my_bit(pair):
    bits = [lax.axis_index(axis) // bit % 2 for axis, bit in pair]
    return jnp.where(lax.axis_index("lon") % 2 == 0, bits[0], bits[1])


def add_rounded(a, b):
    return (a.astype(F32) + b.astype(F32)).astype(BF16)


def pick(state, start, count):
    kept, offset, got, got_offset = state
    mine = lax.dynamic_slice_in_dim(kept, offset + start, count, axis=0)
    return add_rounded(mine, lax.dynamic_slice_in_dim(got, got_offset + start, count, axis=0))


def streams():
    core, *lon = bits_of("lon")
    mem = bits_of("member")
    first = [(d, d) for d in lon + mem]
    second = [(d, d) for d in lon[1:] + mem[:1] + lon[:1] + mem[1:]]
    third = [(d, d) for d in mem[:1] + lon + mem[1:]]
    return (core, core), [first, second, third]


def row_unit():
    core, orders = streams()
    return 2 * 8 * 2 ** (len(orders[0]) - 1)


def all_sum(x, shares=(3, 3, 2)):
    core, orders = streams()
    count = x.shape[0] // 2
    bit = my_bit(core)
    got = swap(lax.dynamic_slice_in_dim(x, (1 - bit) * count, count, axis=0), core)
    unit = row_unit() // 2
    units = count // unit
    sizes = [units * s // sum(shares) * unit for s in shares[1:]]
    sizes = [count - sum(sizes)] + sizes
    steps = len(orders[0])
    lanes = range(len(orders))
    offsets = [sum(sizes[:i]) for i in lanes]
    states = [(x, bit * count + offsets[i], got, offsets[i]) for i in lanes]
    rows, trail = list(sizes), []
    for s in range(steps - 1):
        rows = [r // 2 for r in rows]
        sides = [my_bit(orders[i][s]) for i in lanes]
        gots = [swap(pick(states[i], (1 - sides[i]) * rows[i], rows[i]), orders[i][s]) for i in lanes]
        states = [(pick(states[i], sides[i] * rows[i], rows[i]), 0, gots[i], 0) for i in lanes]
        trail.append(sides)
    mine = [pick(states[i], 0, rows[i]) for i in lanes]
    outs = [add_rounded(mine[i], swap(mine[i], orders[i][-1])) for i in lanes]
    for s in range(steps - 2, -1, -1):
        gots = [swap(outs[i], orders[i][s]) for i in lanes]
        first = [trail[s][i] == 0 for i in lanes]
        outs = [
            jnp.concatenate([jnp.where(f, o, g), jnp.where(f, g, o)], axis=0)
            for f, o, g in zip(first, outs, gots)
        ]
    others = [swap(o, core) for o in outs]
    return jnp.concatenate([jnp.where(bit == side, o, q) for side in (0, 1) for o, q in zip(outs, others)], axis=0)


def shifted(x, axis, by):
    size = lax.axis_size(axis)
    return lax.ppermute(x, axis, [(i, (i + by) % size) for i in range(size)])


def spread_out(piece_of, axis):
    size = lax.axis_size(axis)
    return [piece_of(0)] + [shifted(piece_of(size - d), axis, -d) for d in range(1, size)]


def per_device(
    latent, member_seeds, member_table, row_bands, disco_basis, w_disco, w_expand, w_reduce, w_decode, target
):
    members, rows, lons, chans = latent.shape
    bases = disco_basis.shape[1]
    hidden_units = w_expand.shape[1]
    outs = w_decode.shape[1]
    share = lax.axis_size("member")
    total_members = members * share
    lon_pad = up(lons, TILE)
    slot = lon_pad + TILE
    points = rows * lon_pad
    flat = members * points
    width = chans // LANES * LANES
    full = bases * width + LANES
    piece = TILE * -(-up(outs, TILE) // (TILE * share))
    me = lax.axis_index("member")
    left = shifted(latent[:, :, lons - reach :], "lon", 1)
    right = shifted(latent[:, :, :reach], "lon", -1)
    dims = (members, rows, lons, chans, lon_pad, slot, bases, piece, share)
    stencil, spread, hidden, gelu, slopes, mixed, fields = vmem_call(
        functools.partial(forward_body, dims),
        [
            ((bases * points, rows * slot), BF16),
            ((flat, full), BF16),
            ((flat, chans), BF16),
            ((flat, hidden_units), BF16),
            ((flat, hidden_units), BF16),
            ((flat, chans), BF16),
            ((share, piece, flat), BF16),
        ],
        [
            member_seeds, row_bands, disco_basis.astype(F32).reshape(-1),
            latent, left, right, member_table, w_disco, w_expand, w_reduce, w_decode,
        ],
        smem=3,
        scratch=[pltpu.VMEM((members, rows * slot, up(chans, LANES)), F32)],
        name="forward",
    )
    observed = jnp.pad(target, ((0, 0), (0, lon_pad - lons), (0, share * piece - outs))).reshape(points, share * piece).T
    observed = jnp.concatenate([observed] * members, axis=1)
    observed = lax.dynamic_slice_in_dim(observed, me * piece, piece, axis=0)
    here = spread_out(lambda d: lax.dynamic_index_in_dim(fields, (me + d) % share, 0, keepdims=False), "member")
    grads = vmem_call(
        functools.partial(crps_body, share, points, members, total_members),
        [((piece, flat), BF16)] * share,
        here + [observed],
        name="crps",
    )
    back = spread_out(lambda d: grads[d], "member")
    scale = 1.0 / math.sqrt(total_members * rows * lons * lax.axis_size("lon"))
    unit = row_unit()
    height = up(hidden_units, TILE) + hidden_units // width * up(chans, TILE) + up(outs, TILE) + TILE
    packed, hidden_grad = vmem_call(
        functools.partial(backward_body, (share, piece, outs, chans, hidden_units, width), scale),
        [((up(height, unit), width), BF16), ((flat, chans), BF16)],
        [me.astype(jnp.int32).reshape(1)] + back + [w_decode, w_reduce, w_expand, slopes, hidden, gelu, mixed],
        smem=1,
        scratch=[pltpu.VMEM((share * piece, flat), BF16)],
        name="backward",
    )
    tall = up(bases * chans, TILE)
    (packed_disco,) = vmem_call(
        functools.partial(disco_body, scale, width, tall),
        [((up(tall + TILE, unit), width), BF16)],
        [spread, hidden_grad],
        name="disco",
    )
    summed = all_sum(packed)
    summed_disco = all_sum(packed_disco)
    dims = (members, rows, lons, chans, lon_pad, slot, bases)
    latent_grad, to_left, to_right = vmem_call(
        functools.partial(collect_body, dims),
        [(latent.shape, F32), ((members, rows, reach, chans), F32), ((members, rows, reach, chans), F32)],
        [hidden_grad, w_disco, stencil],
        name="collect",
    )
    from_right = shifted(to_left, "lon", -1)
    from_left = shifted(to_right, "lon", 1)
    edge = [(0, 0, 0)] * 2
    latent_grad = (
        latent_grad
        + lax.pad(from_right, jnp.float32(0), edge + [(lons - reach, 0, 0), (0, 0, 0)])
        + lax.pad(from_left, jnp.float32(0), edge + [(0, lons - reach, 0), (0, 0, 0)])
    ).astype(BF16)

    def column(block, first, count):
        wide = -(-count // width)
        return block[first : first + wide].reshape(-1)[:count]

    disco_col = column(summed_disco, tall, bases * chans)
    grad_disco = jnp.concatenate([summed_disco[: bases * chans], disco_col[:, None]], axis=1)
    row = 0
    misc = height - TILE
    grad_reduce = jnp.concatenate([summed[:hidden_units], column(summed, misc, hidden_units)[:, None]], axis=1)
    misc += -(-hidden_units // width)
    row += up(hidden_units, TILE)
    parts = []
    for part in range(hidden_units // width):
        parts.append(summed[row : row + chans])
        row += up(chans, TILE)
    for i in range(hidden_units - hidden_units // width * width):
        parts.append(column(summed, misc, chans)[:, None])
        misc += -(-chans // width)
    grad_expand = jnp.concatenate(parts, axis=1)
    grad_decode = jnp.concatenate([summed[row : row + outs].T, column(summed, misc, outs)[None]], axis=0)
    return latent_grad, grad_disco, grad_expand, grad_reduce, grad_decode


def solution(mesh):
    placed = (
        P("member", None, "lon", None),
        P("member"),
        P(),
        P(),
        P(),
        P(),
        P(),
        P(),
        P(),
        P(None, "lon", None),
    )
    return jax.shard_map(
        per_device,
        mesh=mesh,
        in_specs=placed,
        out_specs=(P("member", None, "lon", None), P(), P(), P(), P()),
        check_vma=False,
    )
```

time: 386 us -> 233 us (0.60)
  waiting for transfers between devices: 216 us -> 61.4 us
  starting transfers between devices: 6.02 us -> 58.3 us
  matrix products: 43 us -> 0 us
  Pallas kernels: 0 us -> 37 us
  blocking collectives: 24.4 us -> 0 us
  local copies, waits for them, and re-layouts: 63.4 us -> 44.3 us
  between operations: 14.3 us -> 1.4 us
  other arithmetic: 17.6 us -> 29.4 us
    psum x1 -> x0, waiting for transfers between devices: 216 us -> none  [per_device(): lax.psum((grad_disco, grad_expand, grad_reduce, grad_decode), ('member',...]
    ppermute x4 -> x60, waiting for transfers between devices: 0.01 us -> 61.4 us  [the longest x50 48 us: swap(): return lax.ppermute(x, ('member', 'lon'), perm)]
    ppermute x4 -> x60, starting transfers between devices: 5.98 us -> 58.3 us  [the longest x50 44.4 us: swap(): return lax.ppermute(x, ('member', 'lon'), perm)]
    dot_general x18 -> x0, matrix products: 43 us -> none  [the longest x1 4.98 us: per_device(): jnp.einsum('pk,pc->kc', spread_rows, hidden_grad, preferred_element_type=...]
    pallas_call x0 -> x5, Pallas kernels: none -> 37 us  [vmem_call(): pl.pallas_call(body, out_shape=[jax.ShapeDtypeStruct(shape, dtype) for sh...]
    all_gather x1 -> x0, blocking collectives: 24.4 us -> none  [per_device(): everyone = lax.all_gather(fields, 'member', axis=0, tiled=True)]
    unnamed x42 -> x60, local copies, waits for them, and re-layouts: 4.55 us -> 23.7 us
    reshape x7, local copies, waits for them, and re-layouts: 15.7 us -> 2.59 us  [the longest x2 1.12 us: per_device(): disco_basis.astype(F32).reshape(-1)]
  transfers between devices with their start and end apart: 5 -> 60, of which waited for: 1 -> 25; matrix products, arithmetic and copies ran while one was open for 15% -> 24% of each run, Pallas kernels for 0% -> 3%
where the time goes in v1:
time: 233 us; the launch traced here: 232 us
  waiting for transfers between devices  61.4 us (26%)
  starting transfers between devices  58.3 us (25%)
  local copies, waits for them, and re-layouts  44.3 us (19%)
  Pallas kernels  37 us (16%)
  other arithmetic  29.4 us (13%)
    ppermute x50, waiting for transfers between devices, swap(): return lax.ppermute(x, ('member', 'lon'), perm)  48 us
    ppermute x50, starting transfers between devices, swap(): return lax.ppermute(x, ('member', 'lon'), perm)  44.4 us
    pallas_call x5, Pallas kernels, vmem_call(): pl.pallas_call(body, out_shape=[jax.ShapeDtypeStruct(shape, dtype) for sh...  37 us
    unnamed x60, local copies, waits for them, and re-layouts  23.7 us
    ppermute x10, starting transfers between devices, shifted(): return lax.ppermute(x, axis, [(i, (i + by) % size) for i in range(size)])  13.9 us
    ppermute x10, waiting for transfers between devices, shifted(): return lax.ppermute(x, axis, [(i, (i + by) % size) for i in range(size)])  13.5 us
    convert_element_type x30, other arithmetic, add_rounded(): return (a.astype(F32) + b.astype(F32)).astype(BF16)  8.55 us
    concatenate x18, other arithmetic, all_sum(): jnp.concatenate([jnp.where(f, o, g), jnp.where(f, g, o)], axis=0)  5.35 us
  transfers between devices with their start and end apart: 60, of which 25 were waited for; matrix products, arithmetic and copies ran while one was open for 24% of the time, Pallas kernels for 3%

profile of v1, /device:TPU:0, one launch (start us, length us, event | category | flops | bytes accessed | tf_op | source)
XLA Modules:
  0.0 231.8 jit_solution(5004956168981121930)
XLA Ops:
  3.3 3.3 %collective-permute-start.1 = (bf16[2,4,3,641]{3,2,1,0:T(4,128)(2,1)}, bf16[2,4,3,641]{3,2,1,0:T(4,128)(2,1)S(1)}, u32[]{:S(2)}, u32[]{:S(2)}) collective-permute-start(bf16[2,4,3,641]{3,2,1,0:T(4,128)(2,1)} %get-tuple-element.81), channel_id=1, source_target_pairs={{0,7},{1,0},{2,1},{3,2},{4,3},{5,4},{6,5},{7,6},{8,15},{9,8},{10,9... | collective-permute-start | bytes 92312 | tf_op jit(solution)/shard_map/ppermute | solution.py:320
  10.5 3.8 %copy.34.w_reduce.refs_5_ = bf16[1282,641]{1,0:T(8,128)(2,1)} copy(bf16[1282,641]{0,1:T(8,128)(2,1)} %param.17) | data formatting | bytes 3287048 | tf_op args[7]
  14.4 4.0 %copy.33.w_disco = bf16[2564,641]{1,0:T(8,128)(2,1)} copy(bf16[2564,641]{0,1:T(8,128)(2,1)S(1)} %copy-done.10) | data formatting | bytes 6574096 | tf_op args[5]
  19.0 11.6 %forward.1 = (bf16[768,256]{1,0:T(8,128)(2,1)}, bf16[384,2688]{1,0:T(8,128)(2,1)}, bf16[384,641]{1,0:T(8,128)(2,1)}, bf16[384,1282]{1,0:T(8,128)(2,1)}, bf16[384...) custom-call(s32[2]{0:T(128)} %seeds.1, s32[4]{0:T(128)} %bands.1, f32[3136]{0:T(1024)} %reshape.45.basis, ...), custom_call_target="tpu_custom_call" | custom-call | tf_op jit(solution)/shard_map/forward/pallas_call | solution.py:36
  30.6 1.6 dynamic-slice_bitcast_fusion
  32.2 1.6 collective-permute-start.4
  33.8 2.6 %collective-permute-start.3 = (bf16[80,384]{1,0:T(8,128)(2,1)S(1)}, bf16[80,384]{1,0:T(8,128)(2,1)S(1)}, u32[]{:S(2)}, u32[]{:S(2)}) collective-permute-start(bf16[80,384]{1,0:T(8,128)(2,1)S(1)} %get-tuple-element.106), channel_id=1, source_target_pairs={{0,16},{8,24},{16,0},{24,8},{1,17},{9,25},{17,1},{25,9},{2,18},{10... | collective-permute-start | bytes 184328 | tf_op jit(solution)/shard_map/ppermute | solution.py:320
  36.4 1.3 collective-permute-start.2
  38.8 2.2 collective-permute-done.3.refs_2_
  41.6 2.6 %crps.1 = (bf16[80,384]{1,0:T(8,128)(2,1)}, bf16[80,384]{1,0:T(8,128)(2,1)}, bf16[80,384]{1,0:T(8,128)(2,1)}, bf16[80,384]{1,0:T(8,128)(2,1)}) custom-call(bf16[80,384]{1,0:T(8,128)(2,1)} %get-tuple-element.108.refs_0_, bf16[80,384]{1,0:T(8,128)(2,1)} %copy-done.23, bf16[80,384]{1,0:T(8,128)(2,1)} %copy-done.22, bf16[80,384]{1,0:T(8,128)(2,1)} %copy-done.21, ...), custom_call_target="tpu_custom_call" | custom-call | tf_op jit(solution)/shard_map/crps/pallas_call | solution.py:36
  44.2 2.7 %collective-permute-start.5 = (bf16[80,384]{1,0:T(8,128)(2,1)}, bf16[80,384]{1,0:T(8,128)(2,1)S(1)}, u32[]{:S(2)}, u32[]{:S(2)}) collective-permute-start(bf16[80,384]{1,0:T(8,128)(2,1)} %get-tuple-element.23), channel_id=1, source_target_pairs={{0,24},{8,0},{16,8},{24,16},{1,25},{9,1},{17,9},{25,17},{2,26},{10... | collective-permute-start | bytes 184328 | tf_op jit(solution)/shard_map/ppermute | solution.py:320
  47.5 1.6 collective-permute-done.5.refs_1_
  49.1 3.1 %collective-permute-done.6.refs_2_ = bf16[80,384]{1,0:T(8,128)(2,1)S(1)} collective-permute-done((bf16[80,384]{1,0:T(8,128)(2,1)}, bf16[80,384]{1,0:T(8,128)(2,1)S(1)}, u32[]{:S(2)}, u32[]{:S(2)}) %collective-permute-start.6) | collective-permute-done | bytes 61472 | tf_op jit(solution)/shard_map/ppermute | solution.py:320
  53.8 10.1 %backward.1 = (bf16[2944,640]{1,0:T(8,128)(2,1)}, bf16[384,641]{1,0:T(8,128)(2,1)}) custom-call(s32[1]{0:T(128)} %bitcast.me, bf16[80,384]{1,0:T(8,128)(2,1)} %get-tuple-element.22.refs_0_, bf16[80,384]{1,0:T(8,128)(2,1)} %copy-done.18, bf16[80,384]{1,0:T(8,128)(2,1)} %copy-done.19, bf16[80,384]{1,0:T(8,128)(2,1)} %copy-done.20, ...), custom_call_target="tpu_custom_call" | custom-call | tf_op jit(solution)/shard_map/backward/pallas_call | solution.py:36
  63.9 6.0 %disco.1 = bf16[2688,640]{1,0:T(8,128)(2,1)} custom-call(bf16[384,2688]{1,0:T(8,128)(2,1)} %get-tuple-element.35.spread, bf16[384,641]{1,0:T(8,128)(2,1)} %get-tuple-element.30.hidden_grad), custom_call_target="tpu_custom_call" | custom-call | tf_op jit(solution)/shard_map/disco/pallas_call | solution.py:36
  69.9 2.8 %constant_dynamic-slice_fusion.1 = bf16[1344,640]{1,0:T(8,128)(2,1)} fusion(bf16[2688,640]{1,0:T(8,128)(2,1)} %disco.1, s32[]{:T(128)S(6)} %select_n.690), kind=kLoop, calls=%fused_computation.132 | loop fusion | bytes 3440644 | tf_op jit(solution)/shard_map/dynamic_slice | solution.py:289
  72.7 1.5 constant_dynamic-slice_fusion
  74.7 6.7 %collect.1 = (f32[2,4,45,641]{3,2,1,0:T(8,128)}, f32[2,4,3,641]{3,2,1,0:T(4,128)}, f32[2,4,3,641]{3,2,1,0:T(4,128)}) custom-call(bf16[384,641]{1,0:T(8,128)(2,1)} %get-tuple-element.30.hidden_grad, bf16[2564,641]{1,0:T(8,128)(2,1)} %copy.33.w_disco, bf16[768,256]{1,0:T(8,128)(2,1)} %get-tuple-element.31.stencil), custom_call_target="tpu_custom_call" | custom-call | tf_op jit(solution)/shard_map/collect/pallas_call | solution.py:36
  81.4 1.8 collective-permute-start.8
  83.2 2.8 %collective-permute-done.8 = f32[2,4,3,641]{3,2,1,0:T(4,128)S(1)} collective-permute-done((f32[2,4,3,641]{3,2,1,0:T(4,128)}, f32[2,4,3,641]{3,2,1,0:T(4,128)S(1)}, u32[]{:S(2)}, u32[]{:S(2)}) %collective-permute-start.8) | collective-permute-done | bytes 61568 | tf_op jit(solution)/shard_map/ppermute | solution.py:320
  86.0 2.5 %collective-permute-done.9 = f32[2,4,3,641]{3,2,1,0:T(4,128)} collective-permute-done((f32[2,4,3,641]{3,2,1,0:T(4,128)}, f32[2,4,3,641]{3,2,1,0:T(4,128)}, u32[]{:S(2)}, u32[]{:S(2)}) %collective-permute-start.9) | collective-permute-done | bytes 61568 | tf_op jit(solution)/shard_map/ppermute | solution.py:320
  88.5 1.4 add_convert_fusion
  92.7 1.5 add_convert_fusion.8
  97.9 1.4 collective-permute-start.36
  101.5 2.1 collective-permute-start.28
  104.9 2.0 collective-permute-done.28
  106.9 1.7 collective-permute-start.44
  108.6 1.4 collective-permute-start.29
  110.1 2.7 %collective-permute-done.29 = bf16[40,640]{1,0:T(8,128)(2,1)S(1)} collective-permute-done((bf16[40,640]{1,0:T(8,128)(2,1)S(1)}, bf16[40,640]{1,0:T(8,128)(2,1)S(1)}, u32[]{:S(2)}, u32[]{:S(2)}) %collective-permute-start.29) | collective-permute-done | bytes 51232 | tf_op jit(solution)/shard_map/ppermute | solution.py:253
  112.8 1.6 collective-permute-start.20
  114.4 1.6 collective-permute-start.30
  117.5 2.5 %collective-permute-done.30 = bf16[40,640]{1,0:T(8,128)(2,1)S(1)} collective-permute-done((bf16[40,640]{1,0:T(8,128)(2,1)S(1)}, bf16[40,640]{1,0:T(8,128)(2,1)S(1)}, u32[]{:S(2)}, u32[]{:S(2)}) %collective-permute-start.30) | collective-permute-done | bytes 51232 | tf_op jit(solution)/shard_map/ppermute | solution.py:253
  121.4 3.6 %collective-permute-done.31 = bf16[40,640]{1,0:T(8,128)(2,1)S(1)} collective-permute-done((bf16[40,640]{1,0:T(8,128)(2,1)S(1)}, bf16[40,640]{1,0:T(8,128)(2,1)S(1)}, u32[]{:S(2)}, u32[]{:S(2)}) %collective-permute-start.31) | collective-permute-done | bytes 51232 | tf_op jit(solution)/shard_map/ppermute | solution.py:253
  124.9 1.7 collective-permute-start.21
  127.8 1.5 collective-permute-done.21
  129.3 2.0 collective-permute-done.38
  132.3 2.0 collective-permute-start.39
  134.6 3.2 %collective-permute-done.22 = bf16[56,640]{1,0:T(8,128)(2,1)S(1)} collective-permute-done((bf16[56,640]{1,0:T(8,128)(2,1)S(1)}, bf16[56,640]{1,0:T(8,128)(2,1)S(1)}, u32[]{:S(2)}, u32[]{:S(2)}) %collective-permute-start.22) | collective-permute-done | bytes 71712 | tf_op jit(solution)/shard_map/ppermute | solution.py:253
  138.4 1.7 collective-permute-start.23
  140.2 1.6 collective-permute-start.40
  141.9 2.5 %collective-permute-done.40 = bf16[40,640]{1,0:T(8,128)(2,1)S(1)} collective-permute-done((bf16[40,640]{1,0:T(8,128)(2,1)S(1)}, bf16[40,640]{1,0:T(8,128)(2,1)S(1)}, u32[]{:S(2)}, u32[]{:S(2)}) %collective-permute-start.40) | collective-permute-done | bytes 51232 | tf_op jit(solution)/shard_map/ppermute | solution.py:253
  144.4 1.5 collective-permute-start.45
  146.5 1.9 collective-permute-start.14
  148.4 2.2 collective-permute-done.41
  150.7 1.4 collective-permute-done.14
  152.1 1.6 collective-permute-start.42
  153.7 1.3 collective-permute-done.54
  155.2 2.2 collective-permute-start.55
  158.6 2.0 collective-permute-done.55
  160.6 3.2 %collective-permute-start.25 = (bf16[224,640]{1,0:T(8,128)(2,1)S(1)}, bf16[224,640]{1,0:T(8,128)(2,1)S(1)}, u32[]{:S(2)}, u32[]{:S(2)}) collective-permute-start(bf16[224,640]{1,0:T(8,128)(2,1)S(1)} %pad_maximum_fusion.16), channel_id=1, source_target_pairs={{0,4},{1,5},{2,6},{3,7},{4,0},{5,1},{6,2},{7,3},{8,12},{9,13},{10,... | collective-permute-start | bytes 860168 | tf_op jit(solution)/shard_map/ppermute | solution.py:253
  163.8 1.5 collective-permute-start.56
  165.5 2.8 %collective-permute-done.56 = bf16[64,640]{1,0:T(8,128)(2,1)S(1)} collective-permute-done((bf16[64,640]{1,0:T(8,128)(2,1)S(1)}, bf16[64,640]{1,0:T(8,128)(2,1)S(1)}, u32[]{:S(2)}, u32[]{:S(2)}) %collective-permute-start.56) | collective-permute-done | bytes 81952 | tf_op jit(solution)/shard_map/ppermute | solution.py:253
  169.7 4.5 %collective-permute-done.47 = bf16[80,640]{1,0:T(8,128)(2,1)S(1)} collective-permute-done((bf16[80,640]{1,0:T(8,128)(2,1)S(1)}, bf16[80,640]{1,0:T(8,128)(2,1)S(1)}, u32[]{:S(2)}, u32[]{:S(2)}) %collective-permute-start.47) | collective-permute-done | bytes 102432 | tf_op jit(solution)/shard_map/ppermute | solution.py:253
  177.9 1.6 collective-permute-done.48
  182.7 10.8 %collective-permute-done.49 = bf16[160,640]{1,0:T(8,128)(2,1)S(1)} collective-permute-done((bf16[160,640]{1,0:T(8,128)(2,1)S(1)}, bf16[160,640]{1,0:T(8,128)(2,1)S(1)}, u32[]{:S(2)}, u32[]{:S(2)}) %collective-permute-start.49) | collective-permute-done | bytes 204832 | tf_op jit(solution)/shard_map/ppermute | solution.py:253
  194.3 1.5 collective-permute-start.50
  199.9 1.5 broadcast_in_dim.18
  201.4 1.5 broadcast_in_dim.19
  202.9 1.7 broadcast_in_dim.20
  214.0 2.4 %pad_maximum_fusion = bf16[2564,641]{1,0:T(8,128)(2,1)} fusion(bf16[2564,1]{1,0:T(8,128)(2,1)S(1)} %broadcast_in_dim.17, bf16[2564,640]{1,0:T(8,128)(2,1)S(1)} %slice.73), kind=kLoop, calls=%fused_computation | loop fusion | flops 6574096 | bytes 6574096 | tf_op jit(solution)/shard_map/concatenate | solution.py:419
  216.4 6.2 %copy.47 = bf16[2564,641]{0,1:T(8,128)(2,1)} copy(bf16[2564,641]{1,0:T(8,128)(2,1)} %pad_maximum_fusion) | data formatting | bytes 6574096
  222.6 1.5 broadcast_select_fusion
  225.7 2.5 %copy.48 = bf16[1282,641]{0,1:T(8,128)(2,1)} copy(bf16[1282,641]{1,0:T(8,128)(2,1)S(1)} %fusion) | data formatting | bytes 3287048
  228.2 3.6 %concatenate.108 = bf16[641,1282]{1,0:T(8,128)(2,1)} concatenate(bf16[641,640]{1,0:T(8,128)(2,1)} %get-tuple-element.68, bf16[641,640]{1,0:T(8,128)(2,1)S(1)} %get-tuple-element.67, bf16[641,1]{1,0:T(8,128)(2,1)S(1)} %copy-done.14, bf16[641,1]{1,0:T(8,128)(2,1)S(1)} %copy-done.15), dimensions={1} | concatenate | bytes 3287048 | tf_op jit(solution)/shard_map/concatenate | solution.py:432
  (229 shorter events, 53.7 us)
Async XLA Ops:
  0.6 8.9 %copy-start.17 = (bf16[641,288]{0,1:T(8,128)(2,1)S(1)}, bf16[641,288]{0,1:T(8,128)(2,1)}, u32[]{:S(2)}) copy-start(bf16[641,288]{0,1:T(8,128)(2,1)} %param.18) | copy-start | bytes 1107652
  3.3 15.1 %collective-permute-start.1 = (bf16[2,4,3,641]{3,2,1,0:T(4,128)(2,1)}, bf16[2,4,3,641]{3,2,1,0:T(4,128)(2,1)S(1)}, u32[]{:S(2)}, u32[]{:S(2)}) collective-permute-start(bf16[2,4,3,641]{3,2,1,0:T(4,128)(2,1)} %get-tuple-element.81), channel_id=1, source_target_pairs={{0,7},{1,0},{2,1},{3,2},{4,3},{5,4},{6,5},{7,6},{8,15},{9,8},{10,9... | collective-permute-start | bytes 92312 | tf_op jit(solution)/shard_map/ppermute | solution.py:320
  6.7 11.8 %collective-permute-start = (bf16[2,4,3,641]{3,2,1,0:T(4,128)(2,1)}, bf16[2,4,3,641]{3,2,1,0:T(4,128)(2,1)}, u32[]{:S(2)}, u32[]{:S(2)}) collective-permute-start(bf16[2,4,3,641]{3,2,1,0:T(4,128)(2,1)} %get-tuple-element.82), channel_id=1, source_target_pairs={{0,1},{1,2},{2,3},{3,4},{4,5},{5,6},{6,7},{7,0},{8,9},{9,10},{10,1... | collective-permute-start | bytes 92312 | tf_op jit(solution)/shard_map/ppermute | solution.py:320
  18.4 19.3 %copy-start.16 = (bf16[192,320]{0,1:T(8,128)(2,1)S(1)}, bf16[192,320]{0,1:T(8,128)(2,1)}, u32[]{:S(2)}) copy-start(bf16[192,320]{0,1:T(8,128)(2,1)} %copy.37) | copy-start | bytes 368644
  32.2 6.6 %collective-permute-start.4 = (bf16[80,384]{1,0:T(8,128)(2,1)S(1)}, bf16[80,384]{1,0:T(8,128)(2,1)S(1)}, u32[]{:S(2)}, u32[]{:S(2)}) collective-permute-start(bf16[80,384]{1,0:T(8,128)(2,1)S(1)} %get-tuple-element.105), channel_id=1, source_target_pairs={{0,8},{8,16},{16,24},{24,0},{1,9},{9,17},{17,25},{25,1},{2,10},{10... | collective-permute-start | bytes 184328 | tf_op jit(solution)/shard_map/ppermute | solution.py:320
  33.8 7.2 %collective-permute-start.3 = (bf16[80,384]{1,0:T(8,128)(2,1)S(1)}, bf16[80,384]{1,0:T(8,128)(2,1)S(1)}, u32[]{:S(2)}, u32[]{:S(2)}) collective-permute-start(bf16[80,384]{1,0:T(8,128)(2,1)S(1)} %get-tuple-element.106), channel_id=1, source_target_pairs={{0,16},{8,24},{16,0},{24,8},{1,17},{9,25},{17,1},{25,9},{2,18},{10... | collective-permute-start | bytes 184328 | tf_op jit(solution)/shard_map/ppermute | solution.py:320
  36.4 4.6 %collective-permute-start.2 = (bf16[80,384]{1,0:T(8,128)(2,1)S(1)}, bf16[80,384]{1,0:T(8,128)(2,1)S(1)}, u32[]{:S(2)}, u32[]{:S(2)}) collective-permute-start(bf16[80,384]{1,0:T(8,128)(2,1)S(1)} %get-tuple-element.107), channel_id=1, source_target_pairs={{0,24},{8,0},{16,8},{24,16},{1,25},{9,1},{17,9},{25,17},{2,26},{10... | collective-permute-start | bytes 184328 | tf_op jit(solution)/shard_map/ppermute | solution.py:320
  44.2 4.9 %collective-permute-start.5 = (bf16[80,384]{1,0:T(8,128)(2,1)}, bf16[80,384]{1,0:T(8,128)(2,1)S(1)}, u32[]{:S(2)}, u32[]{:S(2)}) collective-permute-start(bf16[80,384]{1,0:T(8,128)(2,1)} %get-tuple-element.23), channel_id=1, source_target_pairs={{0,24},{8,0},{16,8},{24,16},{1,25},{9,1},{17,9},{25,17},{2,26},{10... | collective-permute-start | bytes 184328 | tf_op jit(solution)/shard_map/ppermute | solution.py:320
  46.9 5.3 %collective-permute-start.6 = (bf16[80,384]{1,0:T(8,128)(2,1)}, bf16[80,384]{1,0:T(8,128)(2,1)S(1)}, u32[]{:S(2)}, u32[]{:S(2)}) collective-permute-start(bf16[80,384]{1,0:T(8,128)(2,1)} %get-tuple-element.24), channel_id=1, source_target_pairs={{0,16},{8,24},{16,0},{24,8},{1,17},{9,25},{17,1},{25,9},{2,18},{10... | collective-permute-start | bytes 184328 | tf_op jit(solution)/shard_map/ppermute | solution.py:320
  46.9 6.2 %collective-permute-start.7 = (bf16[80,384]{1,0:T(8,128)(2,1)}, bf16[80,384]{1,0:T(8,128)(2,1)S(1)}, u32[]{:S(2)}, u32[]{:S(2)}) collective-permute-start(bf16[80,384]{1,0:T(8,128)(2,1)} %get-tuple-element.25), channel_id=1, source_target_pairs={{0,8},{8,16},{16,24},{24,0},{1,9},{9,17},{17,25},{25,1},{2,10},{10... | collective-permute-start | bytes 184328 | tf_op jit(solution)/shard_map/ppermute | solution.py:320
  63.9 8.8 %copy-start.3 = (bf16[2944,640]{1,0:T(8,128)(2,1)S(1)}, bf16[2944,640]{1,0:T(8,128)(2,1)}, u32[]{:S(2)}) copy-start(bf16[2944,640]{1,0:T(8,128)(2,1)} %get-tuple-element.36) | copy-start | bytes 11304964
  72.7 18.3 %collective-permute-start.10 = (bf16[1344,640]{1,0:T(8,128)(2,1)}, bf16[1344,640]{1,0:T(8,128)(2,1)}, u32[]{:S(2)}, u32[]{:S(2)}) collective-permute-start(bf16[1344,640]{1,0:T(8,128)(2,1)} %constant_dynamic-slice_fusion.1), channel_id=1, source_target_pairs={{0,1},{1,0},{2,3},{3,2},{4,5},{5,4},{6,7},{7,6},{8,9},{9,8},{10,11... | collective-permute-start | bytes 5160968 | tf_op jit(solution)/shard_map/ppermute | solution.py:253
  74.2 22.6 %collective-permute-start.35 = (bf16[1472,640]{1,0:T(8,128)(2,1)}, bf16[1472,640]{1,0:T(8,128)(2,1)}, u32[]{:S(2)}, u32[]{:S(2)}) collective-permute-start(bf16[1472,640]{1,0:T(8,128)(2,1)} %constant_dynamic-slice_fusion), channel_id=1, source_target_pairs={{0,1},{1,0},{2,3},{3,2},{4,5},{5,4},{6,7},{7,6},{8,9},{9,8},{10,11... | collective-permute-start | bytes 5652488 | tf_op jit(solution)/shard_map/ppermute | solution.py:253
  81.4 9.5 %copy-start = (bf16[2688,640]{1,0:T(8,128)(2,1)S(1)}, bf16[2688,640]{1,0:T(8,128)(2,1)}, u32[]{:S(2)}) copy-start(bf16[2688,640]{1,0:T(8,128)(2,1)} %disco.1) | copy-start | bytes 10321924
  81.4 4.6 %collective-permute-start.8 = (f32[2,4,3,641]{3,2,1,0:T(4,128)}, f32[2,4,3,641]{3,2,1,0:T(4,128)S(1)}, u32[]{:S(2)}, u32[]{:S(2)}) collective-permute-start(f32[2,4,3,641]{3,2,1,0:T(4,128)} %get-tuple-element.33), channel_id=1, source_target_pairs={{0,7},{1,0},{2,1},{3,2},{4,3},{5,4},{6,5},{7,6},{8,15},{9,8},{10,9... | collective-permute-start | bytes 184616 | tf_op jit(solution)/shard_map/ppermute | solution.py:320
  83.2 5.3 %collective-permute-start.9 = (f32[2,4,3,641]{3,2,1,0:T(4,128)}, f32[2,4,3,641]{3,2,1,0:T(4,128)}, u32[]{:S(2)}, u32[]{:S(2)}) collective-permute-start(f32[2,4,3,641]{3,2,1,0:T(4,128)} %get-tuple-element.34), channel_id=1, source_target_pairs={{0,1},{1,2},{2,3},{3,4},{4,5},{5,6},{6,7},{7,0},{8,9},{9,10},{10,1... | collective-permute-start | bytes 184616 | tf_op jit(solution)/shard_map/ppermute | solution.py:320
  92.1 9.3 %collective-permute-start.27 = (bf16[160,640]{1,0:T(8,128)(2,1)S(1)}, bf16[160,640]{1,0:T(8,128)(2,1)S(1)}, u32[]{:S(2)}, u32[]{:S(2)}) collective-permute-start(bf16[160,640]{1,0:T(8,128)(2,1)S(1)} %get-tuple-element.56), channel_id=1, source_target_pairs={{0,8},{1,9},{2,10},{3,11},{4,12},{5,13},{6,14},{7,15},{8,0},{9,1},... | collective-permute-start | bytes 614408 | tf_op jit(solution)/shard_map/ppermute | solution.py:253
  94.1 14.5 %collective-permute-start.19 = (bf16[224,640]{1,0:T(8,128)(2,1)S(1)}, bf16[224,640]{1,0:T(8,128)(2,1)S(1)}, u32[]{:S(2)}, u32[]{:S(2)}) collective-permute-start(bf16[224,640]{1,0:T(8,128)(2,1)S(1)} %get-tuple-element.58), channel_id=1, source_target_pairs={{0,4},{1,5},{2,6},{3,7},{4,0},{5,1},{6,2},{7,3},{8,12},{9,13},{10,... | collective-permute-start | bytes 860168 | tf_op jit(solution)/shard_map/ppermute | solution.py:253
  96.0 18.4 %collective-permute-start.11 = (bf16[288,640]{1,0:T(8,128)(2,1)S(1)}, bf16[288,640]{1,0:T(8,128)(2,1)S(1)}, u32[]{:S(2)}, u32[]{:S(2)}) collective-permute-start(bf16[288,640]{1,0:T(8,128)(2,1)S(1)} %get-tuple-element.60), channel_id=1, source_target_pairs={{0,2},{1,3},{2,0},{3,1},{4,6},{5,7},{6,4},{7,5},{8,10},{9,11},{10,... | collective-permute-start | bytes 1105928 | tf_op jit(solution)/shard_map/ppermute | solution.py:253
  97.9 18.2 %collective-permute-start.36 = (bf16[160,640]{1,0:T(8,128)(2,1)S(1)}, bf16[160,640]{1,0:T(8,128)(2,1)S(1)}, u32[]{:S(2)}, u32[]{:S(2)}) collective-permute-start(bf16[160,640]{1,0:T(8,128)(2,1)S(1)} %get-tuple-element.52), channel_id=1, source_target_pairs={{0,8},{1,9},{2,10},{3,11},{4,12},{5,13},{6,14},{7,15},{8,0},{9,1},... | collective-permute-start | bytes 614408 | tf_op jit(solution)/shard_map/ppermute | solution.py:253
  100.5 26.6 %collective-permute-start.52 = (bf16[256,640]{1,0:T(8,128)(2,1)S(1)}, bf16[256,640]{1,0:T(8,128)(2,1)S(1)}, u32[]{:S(2)}, u32[]{:S(2)}) collective-permute-start(bf16[256,640]{1,0:T(8,128)(2,1)S(1)} %get-tuple-element.50), channel_id=1, source_target_pairs={{0,4},{1,5},{2,6},{3,7},{4,0},{5,1},{6,2},{7,3},{8,12},{9,13},{10,... | collective-permute-start | bytes 983048 | tf_op jit(solution)/shard_map/ppermute | solution.py:253
  101.5 5.4 %collective-permute-start.28 = (bf16[80,640]{1,0:T(8,128)(2,1)S(1)}, bf16[80,640]{1,0:T(8,128)(2,1)S(1)}, u32[]{:S(2)}, u32[]{:S(2)}) collective-permute-start(bf16[80,640]{1,0:T(8,128)(2,1)S(1)} %get-tuple-element.98), channel_id=1, source_target_pairs={{0,2},{1,3},{2,0},{3,1},{4,6},{5,7},{6,4},{7,5},{8,10},{9,11},{10,... | collective-permute-start | bytes 307208 | tf_op jit(solution)/shard_map/ppermute | solution.py:253
  106.9 33.3 %collective-permute-start.44 = (bf16[320,640]{1,0:T(8,128)(2,1)S(1)}, bf16[320,640]{1,0:T(8,128)(2,1)S(1)}, u32[]{:S(2)}, u32[]{:S(2)}) collective-permute-start(bf16[320,640]{1,0:T(8,128)(2,1)S(1)} %get-tuple-element.54), channel_id=1, source_target_pairs={{0,2},{1,3},{2,0},{3,1},{4,6},{5,7},{6,4},{7,5},{8,10},{9,11},{10,... | collective-permute-start | bytes 1228808 | tf_op jit(solution)/shard_map/ppermute | solution.py:253
  108.6 4.2 %collective-permute-start.29 = (bf16[40,640]{1,0:T(8,128)(2,1)S(1)}, bf16[40,640]{1,0:T(8,128)(2,1)S(1)}, u32[]{:S(2)}, u32[]{:S(2)}) collective-permute-start(bf16[40,640]{1,0:T(8,128)(2,1)S(1)} %add_convert_fusion.47), channel_id=1, source_target_pairs={{0,4},{1,5},{2,6},{3,7},{4,0},{5,1},{6,2},{7,3},{8,12},{9,13},{10,... | collective-permute-start | bytes 153608 | tf_op jit(solution)/shard_map/ppermute | solution.py:253
  112.8 7.5 %collective-permute-start.20 = (bf16[112,640]{1,0:T(8,128)(2,1)S(1)}, bf16[112,640]{1,0:T(8,128)(2,1)S(1)}, u32[]{:S(2)}, u32[]{:S(2)}) collective-permute-start(bf16[112,640]{1,0:T(8,128)(2,1)S(1)} %get-tuple-element.86), channel_id=1, source_target_pairs={{0,8},{1,9},{2,10},{3,11},{4,12},{5,13},{6,14},{7,15},{8,0},{9,1},... | collective-permute-start | bytes 430088 | tf_op jit(solution)/shard_map/ppermute | solution.py:253
  114.4 5.6 %collective-permute-start.30 = (bf16[40,640]{1,0:T(8,128)(2,1)S(1)}, bf16[40,640]{1,0:T(8,128)(2,1)S(1)}, u32[]{:S(2)}, u32[]{:S(2)}) collective-permute-start(bf16[40,640]{1,0:T(8,128)(2,1)S(1)} %add_convert_fusion.46), channel_id=1, source_target_pairs={{0,16},{1,17},{2,18},{3,19},{4,20},{5,21},{6,22},{7,23},{8,24},{9,... | collective-permute-start | bytes 153608 | tf_op jit(solution)/shard_map/ppermute | solution.py:253
  116.2 16.1 %collective-permute-start.12 = (bf16[144,640]{1,0:T(8,128)(2,1)S(1)}, bf16[144,640]{1,0:T(8,128)(2,1)S(1)}, u32[]{:S(2)}, u32[]{:S(2)}) collective-permute-start(bf16[144,640]{1,0:T(8,128)(2,1)S(1)} %get-tuple-element.76), channel_id=1, source_target_pairs={{0,4},{1,5},{2,6},{3,7},{4,0},{5,1},{6,2},{7,3},{8,12},{9,13},{10,... | collective-permute-start | bytes 552968 | tf_op jit(solution)/shard_map/ppermute | solution.py:253
  120.0 6.7 %collective-permute-start.37 = (bf16[80,640]{1,0:T(8,128)(2,1)S(1)}, bf16[80,640]{1,0:T(8,128)(2,1)S(1)}, u32[]{:S(2)}, u32[]{:S(2)}) collective-permute-start(bf16[80,640]{1,0:T(8,128)(2,1)S(1)} %get-tuple-element.92), channel_id=1, source_target_pairs={{0,2},{1,3},{2,0},{3,1},{4,6},{5,7},{6,4},{7,5},{8,10},{9,11},{10,... | collective-permute-start | bytes 307208 | tf_op jit(solution)/shard_map/ppermute | solution.py:253
  120.3 4.6 %collective-permute-start.31 = (bf16[40,640]{1,0:T(8,128)(2,1)S(1)}, bf16[40,640]{1,0:T(8,128)(2,1)S(1)}, u32[]{:S(2)}, u32[]{:S(2)}) collective-permute-start(bf16[40,640]{1,0:T(8,128)(2,1)S(1)} %add_convert_fusion.45), channel_id=1, source_target_pairs={{0,4},{1,5},{2,6},{3,7},{4,0},{5,1},{6,2},{7,3},{8,12},{9,13},{10,... | collective-permute-start | bytes 153608 | tf_op jit(solution)/shard_map/ppermute | solution.py:253
  124.9 4.3 %collective-permute-start.21 = (bf16[56,640]{1,0:T(8,128)(2,1)S(1)}, bf16[56,640]{1,0:T(8,128)(2,1)S(1)}, u32[]{:S(2)}, u32[]{:S(2)}) collective-permute-start(bf16[56,640]{1,0:T(8,128)(2,1)S(1)} %add_convert_fusion.39), channel_id=1, source_target_pairs={{0,2},{1,3},{2,0},{3,1},{4,6},{5,7},{6,4},{7,5},{8,10},{9,11},{10,... | collective-permute-start | bytes 215048 | tf_op jit(solution)/shard_map/ppermute | solution.py:253
  126.7 7.6 %collective-permute-start.32 = (bf16[80,640]{1,0:T(8,128)(2,1)S(1)}, bf16[80,640]{1,0:T(8,128)(2,1)S(1)}, u32[]{:S(2)}, u32[]{:S(2)}) collective-permute-start(bf16[80,640]{1,0:T(8,128)(2,1)S(1)} %pad_maximum_fusion.23), channel_id=1, source_target_pairs={{0,2},{1,3},{2,0},{3,1},{4,6},{5,7},{6,4},{7,5},{8,10},{9,11},{10,... | collective-permute-start | bytes 307208 | tf_op jit(solution)/shard_map/ppermute | solution.py:253
  127.1 4.2 %collective-permute-start.38 = (bf16[40,640]{1,0:T(8,128)(2,1)S(1)}, bf16[40,640]{1,0:T(8,128)(2,1)S(1)}, u32[]{:S(2)}, u32[]{:S(2)}) collective-permute-start(bf16[40,640]{1,0:T(8,128)(2,1)S(1)} %add_convert_fusion.43), channel_id=1, source_target_pairs={{0,4},{1,5},{2,6},{3,7},{4,0},{5,1},{6,2},{7,3},{8,12},{9,13},{10,... | collective-permute-start | bytes 153608 | tf_op jit(solution)/shard_map/ppermute | solution.py:253
  129.3 17.2 %collective-permute-start.53 = (bf16[128,640]{1,0:T(8,128)(2,1)S(1)}, bf16[128,640]{1,0:T(8,128)(2,1)S(1)}, u32[]{:S(2)}, u32[]{:S(2)}) collective-permute-start(bf16[128,640]{1,0:T(8,128)(2,1)S(1)} %get-tuple-element.80), channel_id=1, source_target_pairs={{0,8},{1,9},{2,10},{3,11},{4,12},{5,13},{6,14},{7,15},{8,0},{9,1},... | collective-permute-start | bytes 491528 | tf_op jit(solution)/shard_map/ppermute | solution.py:253
  131.3 6.5 %collective-permute-start.22 = (bf16[56,640]{1,0:T(8,128)(2,1)S(1)}, bf16[56,640]{1,0:T(8,128)(2,1)S(1)}, u32[]{:S(2)}, u32[]{:S(2)}) collective-permute-start(bf16[56,640]{1,0:T(8,128)(2,1)S(1)} %add_convert_fusion.38), channel_id=1, source_target_pairs={{0,16},{1,17},{2,18},{3,19},{4,20},{5,21},{6,22},{7,23},{8,24},{9,... | collective-permute-start | bytes 215048 | tf_op jit(solution)/shard_map/ppermute | solution.py:253
  132.3 6.1 %collective-permute-start.39 = (bf16[40,640]{1,0:T(8,128)(2,1)S(1)}, bf16[40,640]{1,0:T(8,128)(2,1)S(1)}, u32[]{:S(2)}, u32[]{:S(2)}) collective-permute-start(bf16[40,640]{1,0:T(8,128)(2,1)S(1)} %add_convert_fusion.42), channel_id=1, source_target_pairs={{0,16},{1,17},{2,18},{3,19},{4,20},{5,21},{6,22},{7,23},{8,24},{9,... | collective-permute-start | bytes 153608 | tf_op jit(solution)/shard_map/ppermute | solution.py:253
  134.4 11.7 %collective-permute-start.13 = (bf16[72,640]{1,0:T(8,128)(2,1)S(1)}, bf16[72,640]{1,0:T(8,128)(2,1)S(1)}, u32[]{:S(2)}, u32[]{:S(2)}) collective-permute-start(bf16[72,640]{1,0:T(8,128)(2,1)S(1)} %add_convert_fusion.31), channel_id=1, source_target_pairs={{0,8},{1,9},{2,10},{3,11},{4,12},{5,13},{6,14},{7,15},{8,0},{9,1},... | collective-permute-start | bytes 276488 | tf_op jit(solution)/shard_map/ppermute | solution.py:253
  137.8 17.3 %collective-permute-start.33 = (bf16[160,640]{1,0:T(8,128)(2,1)S(1)}, bf16[160,640]{1,0:T(8,128)(2,1)S(1)}, u32[]{:S(2)}, u32[]{:S(2)}) collective-permute-start(bf16[160,640]{1,0:T(8,128)(2,1)S(1)} %pad_maximum_fusion.17), channel_id=1, source_target_pairs={{0,8},{1,9},{2,10},{3,11},{4,12},{5,13},{6,14},{7,15},{8,0},{9,1},... | collective-permute-start | bytes 614408 | tf_op jit(solution)/shard_map/ppermute | solution.py:253
  138.4 7.5 %collective-permute-start.23 = (bf16[56,640]{1,0:T(8,128)(2,1)S(1)}, bf16[56,640]{1,0:T(8,128)(2,1)S(1)}, u32[]{:S(2)}, u32[]{:S(2)}) collective-permute-start(bf16[56,640]{1,0:T(8,128)(2,1)S(1)} %add_convert_fusion.37), channel_id=1, source_target_pairs={{0,2},{1,3},{2,0},{3,1},{4,6},{5,7},{6,4},{7,5},{8,10},{9,11},{10,... | collective-permute-start | bytes 215048 | tf_op jit(solution)/shard_map/ppermute | solution.py:253
  140.2 4.2 %collective-permute-start.40 = (bf16[40,640]{1,0:T(8,128)(2,1)S(1)}, bf16[40,640]{1,0:T(8,128)(2,1)S(1)}, u32[]{:S(2)}, u32[]{:S(2)}) collective-permute-start(bf16[40,640]{1,0:T(8,128)(2,1)S(1)} %add_convert_fusion.41), channel_id=1, source_target_pairs={{0,4},{1,5},{2,6},{3,7},{4,0},{5,1},{6,2},{7,3},{8,12},{9,13},{10,... | collective-permute-start | bytes 153608 | tf_op jit(solution)/shard_map/ppermute | solution.py:253
  144.4 13.9 %collective-permute-start.45 = (bf16[160,640]{1,0:T(8,128)(2,1)S(1)}, bf16[160,640]{1,0:T(8,128)(2,1)S(1)}, u32[]{:S(2)}, u32[]{:S(2)}) collective-permute-start(bf16[160,640]{1,0:T(8,128)(2,1)S(1)} %get-tuple-element.72), channel_id=1, source_target_pairs={{0,4},{1,5},{2,6},{3,7},{4,0},{5,1},{6,2},{7,3},{8,12},{9,13},{10,... | collective-permute-start | bytes 614408 | tf_op jit(solution)/shard_map/ppermute | solution.py:253
  145.9 4.7 %collective-permute-start.41 = (bf16[80,640]{1,0:T(8,128)(2,1)S(1)}, bf16[80,640]{1,0:T(8,128)(2,1)S(1)}, u32[]{:S(2)}, u32[]{:S(2)}) collective-permute-start(bf16[80,640]{1,0:T(8,128)(2,1)S(1)} %pad_maximum_fusion.24), channel_id=1, source_target_pairs={{0,2},{1,3},{2,0},{3,1},{4,6},{5,7},{6,4},{7,5},{8,10},{9,11},{10,... | collective-permute-start | bytes 307208 | tf_op jit(solution)/shard_map/ppermute | solution.py:253
  146.0 12.2 %collective-permute-start.24 = (bf16[112,640]{1,0:T(8,128)(2,1)S(1)}, bf16[112,640]{1,0:T(8,128)(2,1)S(1)}, u32[]{:S(2)}, u32[]{:S(2)}) collective-permute-start(bf16[112,640]{1,0:T(8,128)(2,1)S(1)} %pad_maximum_fusion.22), channel_id=1, source_target_pairs={{0,8},{1,9},{2,10},{3,11},{4,12},{5,13},{6,14},{7,15},{8,0},{9,1},... | collective-permute-start | bytes 430088 | tf_op jit(solution)/shard_map/ppermute | solution.py:253
  146.5 5.6 %collective-permute-start.14 = (bf16[72,640]{1,0:T(8,128)(2,1)S(1)}, bf16[72,640]{1,0:T(8,128)(2,1)S(1)}, u32[]{:S(2)}, u32[]{:S(2)}) collective-permute-start(bf16[72,640]{1,0:T(8,128)(2,1)S(1)} %add_convert_fusion.30), channel_id=1, source_target_pairs={{0,16},{1,17},{2,18},{3,19},{4,20},{5,21},{6,22},{7,23},{8,24},{9,... | collective-permute-start | bytes 276488 | tf_op jit(solution)/shard_map/ppermute | solution.py:253
  150.6 4.4 %collective-permute-start.54 = (bf16[64,640]{1,0:T(8,128)(2,1)S(1)}, bf16[64,640]{1,0:T(8,128)(2,1)S(1)}, u32[]{:S(2)}, u32[]{:S(2)}) collective-permute-start(bf16[64,640]{1,0:T(8,128)(2,1)S(1)} %add_convert_fusion.35), channel_id=1, source_target_pairs={{0,2},{1,3},{2,0},{3,1},{4,6},{5,7},{6,4},{7,5},{8,10},{9,11},{10,... | collective-permute-start | bytes 245768 | tf_op jit(solution)/shard_map/ppermute | solution.py:253
  152.1 17.3 %collective-permute-start.42 = (bf16[160,640]{1,0:T(8,128)(2,1)S(1)}, bf16[160,640]{1,0:T(8,128)(2,1)S(1)}, u32[]{:S(2)}, u32[]{:S(2)}) collective-permute-start(bf16[160,640]{1,0:T(8,128)(2,1)S(1)} %pad_maximum_fusion.18), channel_id=1, source_target_pairs={{0,8},{1,9},{2,10},{3,11},{4,12},{5,13},{6,14},{7,15},{8,0},{9,1},... | collective-permute-start | bytes 614408 | tf_op jit(solution)/shard_map/ppermute | solution.py:253
  155.1 8.7 %collective-permute-start.15 = (bf16[72,640]{1,0:T(8,128)(2,1)S(1)}, bf16[72,640]{1,0:T(8,128)(2,1)S(1)}, u32[]{:S(2)}, u32[]{:S(2)}) collective-permute-start(bf16[72,640]{1,0:T(8,128)(2,1)S(1)} %add_convert_fusion.29), channel_id=1, source_target_pairs={{0,8},{1,9},{2,10},{3,11},{4,12},{5,13},{6,14},{7,15},{8,0},{9,1},... | collective-permute-start | bytes 276488 | tf_op jit(solution)/shard_map/ppermute | solution.py:253
  155.2 5.4 %collective-permute-start.55 = (bf16[64,640]{1,0:T(8,128)(2,1)S(1)}, bf16[64,640]{1,0:T(8,128)(2,1)S(1)}, u32[]{:S(2)}, u32[]{:S(2)}) collective-permute-start(bf16[64,640]{1,0:T(8,128)(2,1)S(1)} %add_convert_fusion.34), channel_id=1, source_target_pairs={{0,16},{1,17},{2,18},{3,19},{4,20},{5,21},{6,22},{7,23},{8,24},{9,... | collective-permute-start | bytes 245768 | tf_op jit(solution)/shard_map/ppermute | solution.py:253
  158.2 54.2 %collective-permute-start.34 = (bf16[320,640]{1,0:T(8,128)(2,1)}, bf16[320,640]{1,0:T(8,128)(2,1)S(1)}, u32[]{:S(2)}, u32[]{:S(2)}) collective-permute-start(bf16[320,640]{1,0:T(8,128)(2,1)} %pad_maximum_fusion.10), channel_id=1, source_target_pairs={{0,1},{1,0},{2,3},{3,2},{4,5},{5,4},{6,7},{7,6},{8,9},{9,8},{10,11... | collective-permute-start | bytes 1228808 | tf_op jit(solution)/shard_map/ppermute | solution.py:253
  158.3 7.1 %collective-permute-start.46 = (bf16[80,640]{1,0:T(8,128)(2,1)S(1)}, bf16[80,640]{1,0:T(8,128)(2,1)S(1)}, u32[]{:S(2)}, u32[]{:S(2)}) collective-permute-start(bf16[80,640]{1,0:T(8,128)(2,1)S(1)} %add_convert_fusion.23), channel_id=1, source_target_pairs={{0,8},{1,9},{2,10},{3,11},{4,12},{5,13},{6,14},{7,15},{8,0},{9,1},... | collective-permute-start | bytes 307208 | tf_op jit(solution)/shard_map/ppermute | solution.py:253
  160.6 20.0 %collective-permute-start.25 = (bf16[224,640]{1,0:T(8,128)(2,1)S(1)}, bf16[224,640]{1,0:T(8,128)(2,1)S(1)}, u32[]{:S(2)}, u32[]{:S(2)}) collective-permute-start(bf16[224,640]{1,0:T(8,128)(2,1)S(1)} %pad_maximum_fusion.16), channel_id=1, source_target_pairs={{0,4},{1,5},{2,6},{3,7},{4,0},{5,1},{6,2},{7,3},{8,12},{9,13},{10,... | collective-permute-start | bytes 860168 | tf_op jit(solution)/shard_map/ppermute | solution.py:253
  163.8 4.5 %collective-permute-start.56 = (bf16[64,640]{1,0:T(8,128)(2,1)S(1)}, bf16[64,640]{1,0:T(8,128)(2,1)S(1)}, u32[]{:S(2)}, u32[]{:S(2)}) collective-permute-start(bf16[64,640]{1,0:T(8,128)(2,1)S(1)} %add_convert_fusion.33), channel_id=1, source_target_pairs={{0,2},{1,3},{2,0},{3,1},{4,6},{5,7},{6,4},{7,5},{8,10},{9,11},{10,... | collective-permute-start | bytes 245768 | tf_op jit(solution)/shard_map/ppermute | solution.py:253
  165.4 8.8 %collective-permute-start.16 = (bf16[144,640]{1,0:T(8,128)(2,1)S(1)}, bf16[144,640]{1,0:T(8,128)(2,1)S(1)}, u32[]{:S(2)}, u32[]{:S(2)}) collective-permute-start(bf16[144,640]{1,0:T(8,128)(2,1)S(1)} %pad_maximum_fusion.20), channel_id=1, source_target_pairs={{0,4},{1,5},{2,6},{3,7},{4,0},{5,1},{6,2},{7,3},{8,12},{9,13},{10,... | collective-permute-start | bytes 552968 | tf_op jit(solution)/shard_map/ppermute | solution.py:253
  168.3 5.8 %collective-permute-start.47 = (bf16[80,640]{1,0:T(8,128)(2,1)S(1)}, bf16[80,640]{1,0:T(8,128)(2,1)S(1)}, u32[]{:S(2)}, u32[]{:S(2)}) collective-permute-start(bf16[80,640]{1,0:T(8,128)(2,1)S(1)} %add_convert_fusion.22), channel_id=1, source_target_pairs={{0,16},{1,17},{2,18},{3,19},{4,20},{5,21},{6,22},{7,23},{8,24},{9,... | collective-permute-start | bytes 307208 | tf_op jit(solution)/shard_map/ppermute | solution.py:253
  169.5 6.3 %collective-permute-start.57 = (bf16[128,640]{1,0:T(8,128)(2,1)S(1)}, bf16[128,640]{1,0:T(8,128)(2,1)S(1)}, u32[]{:S(2)}, u32[]{:S(2)}) collective-permute-start(bf16[128,640]{1,0:T(8,128)(2,1)S(1)} %pad_maximum_fusion.21), channel_id=1, source_target_pairs={{0,8},{1,9},{2,10},{3,11},{4,12},{5,13},{6,14},{7,15},{8,0},{9,1},... | collective-permute-start | bytes 491528 | tf_op jit(solution)/shard_map/ppermute | solution.py:253
  174.1 20.2 %collective-permute-start.43 = (bf16[320,640]{1,0:T(8,128)(2,1)S(1)}, bf16[320,640]{1,0:T(8,128)(2,1)S(1)}, u32[]{:S(2)}, u32[]{:S(2)}) collective-permute-start(bf16[320,640]{1,0:T(8,128)(2,1)S(1)} %pad_maximum_fusion.11), channel_id=1, source_target_pairs={{0,1},{1,0},{2,3},{3,2},{4,5},{5,4},{6,7},{7,6},{8,9},{9,8},{10,11... | collective-permute-start | bytes 1228808 | tf_op jit(solution)/shard_map/ppermute | solution.py:253
  174.2 5.4 %collective-permute-start.48 = (bf16[80,640]{1,0:T(8,128)(2,1)S(1)}, bf16[80,640]{1,0:T(8,128)(2,1)S(1)}, u32[]{:S(2)}, u32[]{:S(2)}) collective-permute-start(bf16[80,640]{1,0:T(8,128)(2,1)S(1)} %add_convert_fusion.21), channel_id=1, source_target_pairs={{0,8},{1,9},{2,10},{3,11},{4,12},{5,13},{6,14},{7,15},{8,0},{9,1},... | collective-permute-start | bytes 307208 | tf_op jit(solution)/shard_map/ppermute | solution.py:253
  175.8 30.2 %collective-permute-start.17 = (bf16[288,640]{1,0:T(8,128)(2,1)}, bf16[288,640]{1,0:T(8,128)(2,1)}, u32[]{:S(2)}, u32[]{:S(2)}) collective-permute-start(bf16[288,640]{1,0:T(8,128)(2,1)} %pad_maximum_fusion.14), channel_id=1, source_target_pairs={{0,2},{1,3},{2,0},{3,1},{4,6},{5,7},{6,4},{7,5},{8,10},{9,11},{10,... | collective-permute-start | bytes 1105928 | tf_op jit(solution)/shard_map/ppermute | solution.py:253
  179.5 25.0 %collective-permute-start.58 = (bf16[256,640]{1,0:T(8,128)(2,1)}, bf16[256,640]{1,0:T(8,128)(2,1)}, u32[]{:S(2)}, u32[]{:S(2)}) collective-permute-start(bf16[256,640]{1,0:T(8,128)(2,1)} %pad_maximum_fusion.15), channel_id=1, source_target_pairs={{0,4},{1,5},{2,6},{3,7},{4,0},{5,1},{6,2},{7,3},{8,12},{9,13},{10,... | collective-permute-start | bytes 983048 | tf_op jit(solution)/shard_map/ppermute | solution.py:253
  180.5 12.9 %collective-permute-start.49 = (bf16[160,640]{1,0:T(8,128)(2,1)S(1)}, bf16[160,640]{1,0:T(8,128)(2,1)S(1)}, u32[]{:S(2)}, u32[]{:S(2)}) collective-permute-start(bf16[160,640]{1,0:T(8,128)(2,1)S(1)} %pad_maximum_fusion.19), channel_id=1, source_target_pairs={{0,4},{1,5},{2,6},{3,7},{4,0},{5,1},{6,2},{7,3},{8,12},{9,13},{10,... | collective-permute-start | bytes 614408 | tf_op jit(solution)/shard_map/ppermute | solution.py:253
  193.5 18.8 %collective-permute-start.26 = (bf16[448,640]{1,0:T(8,128)(2,1)}, bf16[448,640]{1,0:T(8,128)(2,1)S(1)}, u32[]{:S(2)}, u32[]{:S(2)}) collective-permute-start(bf16[448,640]{1,0:T(8,128)(2,1)} %pad_maximum_fusion.8), channel_id=1, source_target_pairs={{0,1},{1,0},{2,3},{3,2},{4,5},{5,4},{6,7},{7,6},{8,9},{9,8},{10,11... | collective-permute-start | bytes 1720328 | tf_op jit(solution)/shard_map/ppermute | solution.py:253
  194.3 13.2 %collective-permute-start.50 = (bf16[320,640]{1,0:T(8,128)(2,1)}, bf16[320,640]{1,0:T(8,128)(2,1)}, u32[]{:S(2)}, u32[]{:S(2)}) collective-permute-start(bf16[320,640]{1,0:T(8,128)(2,1)} %pad_maximum_fusion.12), channel_id=1, source_target_pairs={{0,2},{1,3},{2,0},{3,1},{4,6},{5,7},{6,4},{7,5},{8,10},{9,11},{10,... | collective-permute-start | bytes 1228808 | tf_op jit(solution)/shard_map/ppermute | solution.py:253
  205.7 4.3 %collective-permute-start.59 = (bf16[512,640]{1,0:T(8,128)(2,1)S(1)}, bf16[512,640]{1,0:T(8,128)(2,1)S(1)}, u32[]{:S(2)}, u32[]{:S(2)}) collective-permute-start(bf16[512,640]{1,0:T(8,128)(2,1)S(1)} %pad_maximum_fusion.7), channel_id=1, source_target_pairs={{0,1},{1,0},{2,3},{3,2},{4,5},{5,4},{6,7},{7,6},{8,9},{9,8},{10,11... | collective-permute-start | bytes 1966088 | tf_op jit(solution)/shard_map/ppermute | solution.py:253
  207.2 4.9 %collective-permute-start.18 = (bf16[576,640]{1,0:T(8,128)(2,1)S(1)}, bf16[576,640]{1,0:T(8,128)(2,1)S(1)}, u32[]{:S(2)}, u32[]{:S(2)}) collective-permute-start(bf16[576,640]{1,0:T(8,128)(2,1)S(1)} %pad_maximum_fusion.6), channel_id=1, source_target_pairs={{0,1},{1,0},{2,3},{3,2},{4,5},{5,4},{6,7},{7,6},{8,9},{9,8},{10,11... | collective-permute-start | bytes 2211848 | tf_op jit(solution)/shard_map/ppermute | solution.py:253
  209.8 12.8 %collective-permute-start.51 = (bf16[640,640]{1,0:T(8,128)(2,1)}, bf16[640,640]{1,0:T(8,128)(2,1)}, u32[]{:S(2)}, u32[]{:S(2)}) collective-permute-start(bf16[640,640]{1,0:T(8,128)(2,1)} %pad_maximum_fusion.5), channel_id=1, source_target_pairs={{0,1},{1,0},{2,3},{3,2},{4,5},{5,4},{6,7},{7,6},{8,9},{9,8},{10,11... | collective-permute-start | bytes 2457608 | tf_op jit(solution)/shard_map/ppermute | solution.py:253
  (22 other events, 53.5 us)

commit v2 on v1

--- a/solution.py
+++ b/solution.py
@@ -40,6 +40,7 @@
         out_specs=[pl.BlockSpec(memory_space=pltpu.VMEM)] * len(outs),
         scratch_shapes=list(scratch),
         compiler_params=pltpu.CompilerParams(vmem_limit_bytes=VMEM_LIMIT),
+        cost_estimate=pl.CostEstimate(flops=0, bytes_accessed=0, transcendentals=0),
         name=name,
     )(*args)
 
@@ -105,7 +106,7 @@
     seeded_rows = jnp.concatenate(
         [wide[m, r * slot : r * slot + lon_pad, :chans] for m in range(members) for r in range(rows)], axis=0
     )
-    conv = dot(spread_out[:, : bases * chans], w_disco[...])
+    conv = dot(spread_out[:, : bases * chans], w_disco[...], 1, 1)
     hidden = (seeded_rows + conv).astype(BF16)
     hidden_out[...] = hidden
     pre = dot(hidden, w_expand[...])
@@ -116,11 +117,12 @@
     act = (pre * half).astype(BF16)
     gelu_out[...] = act
     slope_out[...] = (half + 0.5 * pre * (1.0 - th * th) * (rate * (1.0 + 3 * 0.044715 * square))).astype(BF16)
-    mixed = (hidden.astype(F32) + dot(act, w_reduce[...])).astype(BF16)
+    mixed = (hidden.astype(F32) + dot(act, w_reduce[...], 1, 1)).astype(BF16)
     mixed_out[...] = mixed
-    fields = dot(mixed, w_decode[...])
-    outs = fields.shape[1]
-    turned = jnp.swapaxes(jnp.pad(fields, ((0, 0), (0, up(outs, LANES) - outs))), 0, 1)
+    turned = dot(w_decode[...], mixed, 1, 1)
+    outs = turned.shape[0]
+    if up(outs, TILE) > outs:
+        turned = jnp.concatenate([turned, jnp.zeros((up(outs, TILE) - outs, turned.shape[1]), F32)], axis=0)
     for q in range(share):
         low, high = q * piece, min((q + 1) * piece, up(outs, TILE))
         if high > low:
@@ -145,12 +147,14 @@
         outs[i][...] = (slope(fields[i] - observed) - paired * (1.0 / (total - 1))).astype(BF16)
 
 
-def last_rows(values, col, height=TILE):
-    tail = values[:, col:]
-    extra = LANES - tail.shape[1]
-    if extra:
-        tail = jnp.concatenate([tail, jnp.zeros((tail.shape[0], extra), tail.dtype)], axis=1)
-    return jnp.swapaxes(tail.astype(F32), 0, 1)[:height].astype(BF16)
+def turn(x):
+    n, c = x.shape
+    wide = jnp.concatenate([x.astype(F32), jnp.zeros((n, up(c, LANES) - c), F32)], axis=1)
+    return jnp.swapaxes(wide, 0, 1)[: up(c, TILE)].astype(BF16)
+
+
+def misc_rows(count, width):
+    return -(-count // width), count - count // width * width
 
 
 def fold_rows(rows, width, first, into):
@@ -164,52 +168,138 @@
     return into, first + count
 
 
-def backward_body(
-    dims, scale, me, *refs,
-):
-    share, piece, outs, chans, hidden_units, width = dims
+def fold_ends(left_turned, left, right, width, at, misc):
+    count = right.shape[1]
+    last = dot(left_turned[width:], right)
+    misc, at = fold_rows(last[0:1], width, at, misc)
+    rest = count // width * width
+    lanes = dot(turn(right[:, rest:])[:TILE], left[:, :width])
+    for i in range(count - rest):
+        misc, at = fold_rows(lanes[i : i + 1], width, at, misc)
+    return misc, at
+
+
+class Halves:
+    def __init__(self, bit, keep, send):
+        self.bit, self.keep, self.send = bit, keep, send
+        self.half = keep.shape[0]
+
+    def put(self, row, value):
+        value = value.astype(BF16)
+        for side in (0, 1):
+            low, high = max(row, side * self.half), min(row + value.shape[0], (side + 1) * self.half)
+            if low >= high:
+                continue
+            part = value[low - row : high - row]
+            at = slice(low - side * self.half, high - side * self.half)
+
+            @pl.when(self.bit == side)
+            def _():
+                self.keep[at, :] = part
+
+            @pl.when(self.bit != side)
+            def _():
+                self.send[at, :] = part
+
+    def zero_from(self, row):
+        count = 2 * self.half - row
+        if count:
+            self.put(row, jnp.zeros((count, self.keep.shape[1]), F32))
+
+
+def backward_body(dims, scale, place, *refs):
+    share, piece, outs, chans, hidden_units, width, taps_count = dims
     grads = refs[:share]
-    (w_decode, w_reduce, w_expand, slopes, hidden, gelu, mixed, packed, hidden_grad_out, turned_grad) = refs[share:]
+    (
+        w_decode, w_reduce, w_expand, slopes, hidden, gelu, mixed, spread,
+        keep, send, hidden_grad_out, hidden_turned, mixed_turned, turned_grad,
+    ) = refs[share:]
     for d in range(share):
-        turned_grad[pl.ds(pl.multiple_of(lax.rem(me[0] + d, share) * piece, TILE), piece), :] = grads[d][...]
+        turned_grad[pl.ds(pl.multiple_of(lax.rem(place[0] + d, share) * piece, TILE), piece), :] = grads[d][...]
     field_t = turned_grad[: up(outs, TILE)]
+    packed = Halves(place[1], keep, send)
     field = jnp.swapaxes(field_t.astype(F32), 0, 1).astype(BF16)[:, :outs]
-    mixed_grad = dot(field, w_decode[...], 1, 1).astype(BF16)
-    gelu_grad = dot(mixed_grad, w_reduce[...], 1, 1)
+    mixed_grad = dot(field, w_decode[...]).astype(BF16)
+    gelu_grad = dot(mixed_grad, w_reduce[...])
     pre_grad = (gelu_grad * slopes[...].astype(F32)).astype(BF16)
     hidden_grad = (mixed_grad.astype(F32) + dot(pre_grad, w_expand[...], 1, 1)).astype(BF16)
     hidden_grad_out[...] = hidden_grad
+    hidden_grad_t = turn(hidden_grad)
+    hidden_turned[...] = hidden_grad_t
+    mixed_grad_t = turn(mixed_grad)
+    mixed_turned[...] = mixed_grad_t
+    hidden_t = turn(hidden[...])
     row = 0
-    misc = jnp.zeros((TILE, width), F32)
-    packed[row : row + hidden_units, :] = (dot(gelu[...], mixed_grad[:, :width], 0, 0) * scale).astype(BF16)
-    tail = dot(last_rows(mixed_grad, width), gelu[...])
-    misc, at = fold_rows(tail[0:1], width, 0, misc)
-    row += up(hidden_units, TILE)
     for part in range(hidden_units // width):
-        packed[row : row + chans, :] = (dot(hidden[...], pre_grad[:, part * width : (part + 1) * width], 0, 0) * scale).astype(BF16)
-        row += up(chans, TILE)
-    rest = hidden_units // width * width
-    tail = dot(last_rows(pre_grad, rest), hidden[...])
-    for i in range(hidden_units - rest):
-        misc, at = fold_rows(tail[i : i + 1], width, at, misc)
-    packed[row : row + outs, :] = (dot(field_t[:outs], mixed[:, :width]) * scale).astype(BF16)
+        packed.put(row, dot(hidden_t[:width], pre_grad[:, part * width : (part + 1) * width]) * scale)
+        row += width
+    decode_grad = dot(field_t[:outs], mixed[:, :width]) * scale
+    if up(outs, TILE) > outs:
+        decode_grad = jnp.concatenate([decode_grad, jnp.zeros((up(outs, TILE) - outs, width), F32)], axis=0)
+    packed.put(row, decode_grad)
     row += up(outs, TILE)
-    tail = dot(last_rows(mixed[...], width), field)
+    misc = jnp.zeros((misc_height(chans, hidden_units, outs, taps_count, width), width), F32)
+    misc, at = fold_ends(hidden_t, hidden[...], pre_grad, width, 0, misc)
+    misc, at = fold_ends(mixed_grad_t, mixed_grad, gelu[...], width, at, misc)
+    misc, at = fold_ends(hidden_grad_t, hidden_grad, spread[:, :taps_count], width, at, misc)
+    tail = dot(turn(mixed[:, width:])[:TILE], field)
     misc, at = fold_rows(tail[0:1], width, at, misc)
-    packed[row : row + TILE, :] = (misc * scale).astype(BF16)
-    if packed.shape[0] > row + TILE:
-        packed[row + TILE :, :] = jnp.zeros((packed.shape[0] - row - TILE, width), BF16)
-
-
-def disco_body(scale, width, tall, spread, hidden_grad, packed):
-    grad = hidden_grad[...]
-    value = dot(spread[...], grad[:, :width], 0, 0)
-    packed[:tall, :] = (value[:tall] * scale).astype(BF16)
-    tail = dot(last_rows(grad, width), spread[...])
-    misc, at = fold_rows(tail[0:1, :tall], width, 0, jnp.zeros((TILE, width), F32))
-    packed[tall : tall + TILE, :] = (misc * scale).astype(BF16)
-    if packed.shape[0] > tall + TILE:
-        packed[tall + TILE :, :] = jnp.zeros((packed.shape[0] - tall - TILE, width), BF16)
+    packed.put(row, misc * scale)
+    packed.zero_from(row + misc.shape[0])
+
+
+def misc_height(chans, hidden_units, outs, taps_count, width):
+    return up(2 * sum(misc_rows(hidden_units, width)) + sum(misc_rows(taps_count, width)) + 1, TILE)
+
+
+def product_body(scale, width, blocks, place, *refs):
+    packed = Halves(place[1], refs[-2], refs[-1])
+    row = 0
+    for left, right, part in blocks:
+        packed.put(row, dot(refs[left][:width, :], refs[right][:, part * width : (part + 1) * width]) * scale)
+        row += width
+    packed.zero_from(row)
+
+
+def put_matrix(out, block_of, misc, at, width):
+    count = out.shape[1]
+    for part in range(count // width):
+        out[:width, part * width : (part + 1) * width] = block_of(part)
+    wide, lanes = misc_rows(count, width)
+    rest = count // width * width
+    if lanes:
+        ends = jnp.swapaxes(misc[at + wide : at + wide + lanes], 0, 1)
+        out[:width, rest:] = ends.astype(BF16)
+    for t in range(wide):
+        size = min(width, count - t * width)
+        out[width : width + 1, t * width : t * width + size] = misc[at + t : at + t + 1, :size].astype(BF16)
+    return at + wide + lanes
+
+
+def finish_first_body(dims, summed, expand_out, decode_out, misc_out):
+    chans, hidden_units, outs, taps_count, width = dims
+    base = hidden_units // width * width
+    height = misc_out.shape[0]
+    misc_out[...] = summed[base + up(outs, TILE) : base + up(outs, TILE) + height, :]
+    misc = misc_out[...].astype(F32)
+    put_matrix(expand_out, lambda part: summed[part * width : (part + 1) * width, :], misc, 0, width)
+    decode_out[:, :width] = summed[base : base + outs, :]
+    at = 2 * sum(misc_rows(hidden_units, width)) + sum(misc_rows(taps_count, width))
+    turned = jnp.swapaxes(misc[at : at + 8], 0, 1)
+    decode_out[:, width:] = turned[:outs, : decode_out.shape[1] - width].astype(BF16)
+
+
+def finish_rest_body(dims, second, third, misc_ref, reduce_out, disco_out):
+    hidden_units, taps_count, width = dims
+    misc = misc_ref[...].astype(F32)
+    at = sum(misc_rows(hidden_units, width))
+    blocks = hidden_units // width
+    at = put_matrix(reduce_out, lambda part: second[part * width : (part + 1) * width, :], misc, at, width)
+    put_matrix(
+        disco_out,
+        lambda part: second[blocks * width : (blocks + 1) * width, :] if part == 0 else third[(part - 1) * width : part * width, :],
+        misc, at, width,
+    )
 
 
 def collect_body(dims, hidden_grad, w_disco, stencil, out, left_out, right_out):
@@ -218,7 +308,7 @@
     points = rows * lon_pad
     width = chan_pad - LANES
     full = bases * width + LANES
-    grad = dot(hidden_grad[...], w_disco[...], 1, 1).astype(BF16)
+    grad = dot(hidden_grad[...], w_disco[...]).astype(BF16)
     grad = jnp.concatenate([grad, jnp.zeros((grad.shape[0], full - grad.shape[1]), BF16)], axis=1)
     for m in range(members):
         total = None
@@ -262,57 +352,56 @@
     return (a.astype(F32) + b.astype(F32)).astype(BF16)
 
 
-def pick(state, start, count):
-    kept, offset, got, got_offset = state
-    mine = lax.dynamic_slice_in_dim(kept, offset + start, count, axis=0)
-    return add_rounded(mine, lax.dynamic_slice_in_dim(got, got_offset + start, count, axis=0))
-
-
 def streams():
     core, *lon = bits_of("lon")
     mem = bits_of("member")
-    first = [(d, d) for d in lon + mem]
-    second = [(d, d) for d in lon[1:] + mem[:1] + lon[:1] + mem[1:]]
-    third = [(d, d) for d in mem[:1] + lon + mem[1:]]
-    return (core, core), [first, second, third]
+    orders = [mem[:1] + lon + mem[1:], lon + mem, lon[1:] + mem[:1] + lon[:1] + mem[1:]]
+    return [[(d, d) for d in [core] + order] for order in orders]
 
 
 def row_unit():
-    core, orders = streams()
-    return 2 * 8 * 2 ** (len(orders[0]) - 1)
-
-
-def all_sum(x, shares=(3, 3, 2)):
-    core, orders = streams()
-    count = x.shape[0] // 2
-    bit = my_bit(core)
-    got = swap(lax.dynamic_slice_in_dim(x, (1 - bit) * count, count, axis=0), core)
-    unit = row_unit() // 2
-    units = count // unit
-    sizes = [units * s // sum(shares) * unit for s in shares[1:]]
-    sizes = [count - sum(sizes)] + sizes
-    steps = len(orders[0])
-    lanes = range(len(orders))
-    offsets = [sum(sizes[:i]) for i in lanes]
-    states = [(x, bit * count + offsets[i], got, offsets[i]) for i in lanes]
-    rows, trail = list(sizes), []
-    for s in range(steps - 1):
-        rows = [r // 2 for r in rows]
-        sides = [my_bit(orders[i][s]) for i in lanes]
-        gots = [swap(pick(states[i], (1 - sides[i]) * rows[i], rows[i]), orders[i][s]) for i in lanes]
-        states = [(pick(states[i], sides[i] * rows[i], rows[i]), 0, gots[i], 0) for i in lanes]
-        trail.append(sides)
-    mine = [pick(states[i], 0, rows[i]) for i in lanes]
-    outs = [add_rounded(mine[i], swap(mine[i], orders[i][-1])) for i in lanes]
-    for s in range(steps - 2, -1, -1):
-        gots = [swap(outs[i], orders[i][s]) for i in lanes]
-        first = [trail[s][i] == 0 for i in lanes]
-        outs = [
-            jnp.concatenate([jnp.where(f, o, g), jnp.where(f, g, o)], axis=0)
-            for f, o, g in zip(first, outs, gots)
+    return 8 * 2 ** (len(streams()[0]) - 1)
+
+
+class Stream:
+    def __init__(self, keep, send, order):
+        self.kept, self.order = keep, order
+        self.got = swap(send, order[0])
+        self.bits = [my_bit(order[0])]
+        self.steps = [self.halve] * (len(order) - 2) + [self.exchange, self.added] + [self.join] * (len(order) - 1)
+
+    def advance(self, last=None):
+        if last is not None and last is not self:
+            self.got, last.kept = lax.optimization_barrier((self.got, last.kept))
+        self.steps.pop(0)()
+        return self
+
+    def halve(self):
+        pair = self.order[len(self.bits)]
+        count, bit = self.kept.shape[0] // 2, my_bit(pair)
+        parts = [
+            add_rounded(*(lax.dynamic_slice_in_dim(x, which * count, count, axis=0) for x in (self.kept, self.got)))
+            for which in (1 - bit, bit)
         ]
-    others = [swap(o, core) for o in outs]
-    return jnp.concatenate([jnp.where(bit == side, o, q) for side in (0, 1) for o, q in zip(outs, others)], axis=0)
+        self.got, self.kept = swap(parts[0], pair), parts[1]
+        self.bits.append(bit)
+
+    def exchange(self):
+        self.kept = add_rounded(self.kept, self.got)
+        self.got = swap(self.kept, self.order[-1])
+
+    def added(self):
+        self.kept = add_rounded(self.kept, self.got)
+        self.send_back()
+
+    def join(self):
+        low = self.bits.pop() == 0
+        self.kept = jnp.concatenate([jnp.where(low, self.kept, self.got), jnp.where(low, self.got, self.kept)], axis=0)
+        self.send_back()
+
+    def send_back(self):
+        if self.bits:
+            self.got = swap(self.kept, self.order[len(self.bits) - 1])
 
 
 def shifted(x, axis, by):
@@ -342,8 +431,10 @@
     full = bases * width + LANES
     piece = TILE * -(-up(outs, TILE) // (TILE * share))
     me = lax.axis_index("member")
-    left = shifted(latent[:, :, lons - reach :], "lon", 1)
-    right = shifted(latent[:, :, :reach], "lon", -1)
+    by_lon = jnp.swapaxes(latent, 1, 2)
+    left = jnp.swapaxes(shifted(by_lon[:, lons - reach :], "lon", 1), 1, 2)
+    right = jnp.swapaxes(shifted(by_lon[:, :reach], "lon", -1), 1, 2)
+    disco_t, reduce_t, decode_t = w_disco.T, w_reduce.T, w_decode.T
     dims = (members, rows, lons, chans, lon_pad, slot, bases, piece, share)
     stencil, spread, hidden, gelu, slopes, mixed, fields = vmem_call(
         functools.partial(forward_body, dims),
@@ -358,7 +449,7 @@
         ],
         [
             member_seeds, row_bands, disco_basis.astype(F32).reshape(-1),
-            latent, left, right, member_table, w_disco, w_expand, w_reduce, w_decode,
+            latent, left, right, member_table, disco_t, w_expand, reduce_t, decode_t,
         ],
         smem=3,
         scratch=[pltpu.VMEM((members, rows * slot, up(chans, LANES)), F32)],
@@ -377,33 +468,81 @@
     back = spread_out(lambda d: grads[d], "member")
     scale = 1.0 / math.sqrt(total_members * rows * lons * lax.axis_size("lon"))
     unit = row_unit()
-    height = up(hidden_units, TILE) + hidden_units // width * up(chans, TILE) + up(outs, TILE) + TILE
-    packed, hidden_grad = vmem_call(
-        functools.partial(backward_body, (share, piece, outs, chans, hidden_units, width), scale),
-        [((up(height, unit), width), BF16), ((flat, chans), BF16)],
-        [me.astype(jnp.int32).reshape(1)] + back + [w_decode, w_reduce, w_expand, slopes, hidden, gelu, mixed],
+    taps_count = bases * chans
+    height = hidden_units // width * width + up(outs, TILE) + misc_height(chans, hidden_units, outs, taps_count, width)
+    place = jnp.stack([me, lax.axis_index("lon") % 2]).astype(jnp.int32)
+    orders = streams()
+
+    def halves(rows):
+        return [((up(rows, unit) // 2, width), BF16)] * 2
+
+    keep, send, hidden_grad, hidden_turned, mixed_turned = vmem_call(
+        functools.partial(backward_body, (share, piece, outs, chans, hidden_units, width, taps_count), scale),
+        halves(height) + [
+            ((flat, chans), BF16),
+            ((up(chans, TILE), flat), BF16),
+            ((up(chans, TILE), flat), BF16),
+        ],
+        [place] + back + [decode_t, reduce_t, w_expand, slopes, hidden, gelu, mixed, spread],
         smem=1,
         scratch=[pltpu.VMEM((share * piece, flat), BF16)],
         name="backward",
     )
-    tall = up(bases * chans, TILE)
-    (packed_disco,) = vmem_call(
-        functools.partial(disco_body, scale, width, tall),
-        [((up(tall + TILE, unit), width), BF16)],
-        [spread, hidden_grad],
-        name="disco",
-    )
-    summed = all_sum(packed)
-    summed_disco = all_sum(packed_disco)
+    first = Stream(keep, send, orders[0])
+    blocks = hidden_units // width
+    keep, send = vmem_call(
+        functools.partial(product_body, scale, width, [(0, 1, p) for p in range(blocks)] + [(2, 3, 0)]),
+        halves((blocks + 1) * width),
+        [place, mixed_turned, gelu, hidden_turned, spread],
+        smem=1,
+        name="second_products",
+    )
+    second = Stream(keep, send, orders[1])
+    first.advance()
+    hidden_turned, first.kept = lax.optimization_barrier((hidden_turned, first.kept))
+    wide_blocks = taps_count // width
+    keep, send = vmem_call(
+        functools.partial(product_body, scale, width, [(0, 1, p) for p in range(1, wide_blocks)]),
+        halves((wide_blocks - 1) * width),
+        [place, hidden_turned, spread],
+        smem=1,
+        name="third_products",
+    )
+    third = Stream(keep, send, orders[2])
+    second.advance()
+    last = third.advance(second)
+    hidden_grad, third.kept = lax.optimization_barrier((hidden_grad, third.kept))
     dims = (members, rows, lons, chans, lon_pad, slot, bases)
     latent_grad, to_left, to_right = vmem_call(
         functools.partial(collect_body, dims),
         [(latent.shape, F32), ((members, rows, reach, chans), F32), ((members, rows, reach, chans), F32)],
-        [hidden_grad, w_disco, stencil],
+        [hidden_grad, disco_t, stencil],
         name="collect",
     )
+    first.got, latent_grad = lax.optimization_barrier((first.got, latent_grad))
     from_right = shifted(to_left, "lon", -1)
     from_left = shifted(to_right, "lon", 1)
+    while third.steps:
+        for stream in (first, second, third):
+            if stream.steps:
+                last = stream.advance(last)
+    first, second, third = first.kept, second.kept, third.kept
+    grad_expand, decode_grad_t, misc = vmem_call(
+        functools.partial(finish_first_body, (chans, hidden_units, outs, taps_count, width)),
+        [
+            (w_expand.shape, BF16),
+            (decode_t.shape, BF16),
+            ((misc_height(chans, hidden_units, outs, taps_count, width), width), BF16),
+        ],
+        [first],
+        name="finish_first",
+    )
+    reduce_grad_t, disco_grad_t = vmem_call(
+        functools.partial(finish_rest_body, (hidden_units, taps_count, width)),
+        [(reduce_t.shape, BF16), (disco_t.shape, BF16)],
+        [second, third, misc],
+        name="finish_rest",
+    )
     edge = [(0, 0, 0)] * 2
     latent_grad = (
         latent_grad
@@ -411,27 +550,7 @@
         + lax.pad(from_left, jnp.float32(0), edge + [(0, lons - reach, 0), (0, 0, 0)])
     ).astype(BF16)
 
-    def column(block, first, count):
-        wide = -(-count // width)
-        return block[first : first + wide].reshape(-1)[:count]
-
-    disco_col = column(summed_disco, tall, bases * chans)
-    grad_disco = jnp.concatenate([summed_disco[: bases * chans], disco_col[:, None]], axis=1)
-    row = 0
-    misc = height - TILE
-    grad_reduce = jnp.concatenate([summed[:hidden_units], column(summed, misc, hidden_units)[:, None]], axis=1)
-    misc += -(-hidden_units // width)
-    row += up(hidden_units, TILE)
-    parts = []
-    for part in range(hidden_units // width):
-        parts.append(summed[row : row + chans])
-        row += up(chans, TILE)
-    for i in range(hidden_units - hidden_units // width * width):
-        parts.append(column(summed, misc, chans)[:, None])
-        misc += -(-chans // width)
-    grad_expand = jnp.concatenate(parts, axis=1)
-    grad_decode = jnp.concatenate([summed[row : row + outs].T, column(summed, misc, outs)[None]], axis=0)
-    return latent_grad, grad_disco, grad_expand, grad_reduce, grad_decode
+    return latent_grad, disco_grad_t.T, grad_expand, reduce_grad_t.T, decode_grad_t.T
 
 
 def solution(mesh):

time: 233 us -> 168 us (0.72)
  local copies, waits for them, and re-layouts: 44.3 us -> 8.67 us
  starting transfers between devices: 58.3 us -> 33.6 us
  Pallas kernels: 37 us -> 51.4 us
  other arithmetic: 29.4 us -> 19.2 us
  waiting for transfers between devices: 61.4 us -> 54.1 us
    ppermute x50 -> x27, starting transfers between devices: 44.4 us -> 20.4 us  [swap(): return lax.ppermute(x, ('member', 'lon'), perm)]
    unnamed x60 -> x39, local copies, waits for them, and re-layouts: 23.7 us -> 5.78 us
    pallas_call x5 -> x8, Pallas kernels: 37 us -> 51.4 us  [vmem_call(): pl.pallas_call(body, out_shape=[jax.ShapeDtypeStruct(shape, dtype) for sh...]
    select_n x21 -> x12, other arithmetic: 7.63 us -> 1.33 us  [join(): jnp.where(low, self.kept, self.got)]
    broadcast_in_dim x4 -> x0, local copies, waits for them, and re-layouts: 5.06 us -> none  [the longest x2 3.01 us: per_device(): parts.append(column(summed, misc, chans)[:, None])]
    concatenate x23 -> x12, other arithmetic: 10.1 us -> 5.36 us  [join(): jnp.concatenate([jnp.where(low, self.kept, self.got), jnp.where(low, self...]
    dynamic_slice x2 -> x0, local copies, waits for them, and re-layouts: 4.31 us -> none  [all_sum(): lax.dynamic_slice_in_dim(x, (1 - bit) * count, count, axis=0)]
    ppermute x50 -> x27, waiting for transfers between devices: 48 us -> 43.8 us  [swap(): return lax.ppermute(x, ('member', 'lon'), perm)]
  transfers between devices with their start and end apart: 60 -> 37, of which waited for: 25 -> 22; matrix products, arithmetic and copies ran while one was open for 24% -> 12% of each run, Pallas kernels for 3% -> 13%
where the time goes in v2:
time: 168 us
  waiting for transfers between devices  54.1 us (32%)
  Pallas kernels  51.4 us (31%)
  starting transfers between devices  33.6 us (20%)
  other arithmetic  19.2 us (11%)
  local copies, waits for them, and re-layouts  8.67 us (5%)
    pallas_call x8, Pallas kernels, vmem_call(): pl.pallas_call(body, out_shape=[jax.ShapeDtypeStruct(shape, dtype) for sh...  51.4 us
    ppermute x27, waiting for transfers between devices, swap(): return lax.ppermute(x, ('member', 'lon'), perm)  43.8 us
    ppermute x27, starting transfers between devices, swap(): return lax.ppermute(x, ('member', 'lon'), perm)  20.4 us
    ppermute x10, starting transfers between devices, shifted(): return lax.ppermute(x, axis, [(i, (i + by) % size) for i in range(size)])  13.1 us
    convert_element_type x15, other arithmetic, add_rounded(): return (a.astype(F32) + b.astype(F32)).astype(BF16)  11.1 us
    ppermute x10, waiting for transfers between devices, shifted(): return lax.ppermute(x, axis, [(i, (i + by) % size) for i in range(size)])  10.3 us
    unnamed x39, local copies, waits for them, and re-layouts  5.78 us
    concatenate x12, other arithmetic, join(): jnp.concatenate([jnp.where(low, self.kept, self.got), jnp.where(low, self...  5.36 us
  transfers between devices with their start and end apart: 37, of which 22 were waited for; matrix products, arithmetic and copies ran while one was open for 12% of the time, Pallas kernels for 13%

profile of v2, /device:TPU:0, one launch (start us, length us, event | category | flops | bytes accessed | tf_op | source)
XLA Modules:
  0.0 168.0 jit_solution(3189554813897749971)
XLA Ops:
  0.7 1.1 copy.27.latent
  1.9 3.4 %collective-permute-start.1 = (bf16[2,3,4,641]{3,1,2,0:T(4,128)(2,1)S(1)}, bf16[2,3,4,641]{3,1,2,0:T(4,128)(2,1)S(1)}, u32[]{:S(2)}, u32[]{:S(2)}) collective-permute-start(bf16[2,3,4,641]{3,1,2,0:T(4,128)(2,1)S(1)} %get-tuple-element.215), channel_id=1, source_target_pairs={{0,7},{1,0},{2,1},{3,2},{4,3},{5,4},{6,5},{7,6},{8,15},{9,8},{10,9... | collective-permute-start | bytes 92312 | tf_op jit(solution)/shard_map/ppermute | solution.py:409
  5.8 0.8 reshape.22.basis
  7.0 2.7 %collective-permute-done = bf16[2,3,4,641]{3,1,2,0:T(4,128)(2,1)S(1)} collective-permute-done((bf16[2,3,4,641]{3,1,2,0:T(4,128)(2,1)S(1)}, bf16[2,3,4,641]{3,1,2,0:T(4,128)(2,1)S(1)}, u32[]{:S(2)}, u32[]{:S(2)}) %collective-permute-start) | collective-permute-done | bytes 30800 | tf_op jit(solution)/shard_map/ppermute | solution.py:409
  10.3 11.2 %forward.1 = (bf16[768,256]{1,0:T(8,128)(2,1)}, bf16[384,2688]{1,0:T(8,128)(2,1)}, bf16[384,641]{1,0:T(8,128)(2,1)}, bf16[384,1282]{1,0:T(8,128)(2,1)}, bf16[384...) custom-call(s32[2]{0:T(128)} %seeds.1, s32[4]{0:T(128)} %bands.1, f32[3136]{0:T(1024)} %reshape.22.basis, ...), custom_call_target="tpu_custom_call" | custom-call | tf_op jit(solution)/shard_map/forward/pallas_call | solution.py:36
  21.5 1.6 dynamic-slice_bitcast_fusion
  23.1 1.6 collective-permute-start.4
  24.7 2.6 %collective-permute-start.3 = (bf16[80,384]{1,0:T(8,128)(2,1)S(1)}, bf16[80,384]{1,0:T(8,128)(2,1)S(1)}, u32[]{:S(2)}, u32[]{:S(2)}) collective-permute-start(bf16[80,384]{1,0:T(8,128)(2,1)S(1)} %get-tuple-element.230), channel_id=1, source_target_pairs={{0,16},{8,24},{16,0},{24,8},{1,17},{9,25},{17,1},{25,9},{2,18},{10... | collective-permute-start | bytes 184328 | tf_op jit(solution)/shard_map/ppermute | solution.py:409
  27.2 1.3 collective-permute-start.2
  28.6 0.7 fusion.refs_4_
  29.8 1.7 %collective-permute-done.2.refs_1_ = bf16[80,384]{1,0:T(8,128)(2,1)S(1)} collective-permute-done((bf16[80,384]{1,0:T(8,128)(2,1)S(1)}, bf16[80,384]{1,0:T(8,128)(2,1)S(1)}, u32[]{:S(2)}, u32[]{:S(2)}) %collective-permute-start.2) | collective-permute-done | bytes 61472 | tf_op jit(solution)/shard_map/ppermute | solution.py:409
  31.5 0.6 copy-done.9
  32.1 2.5 %crps.1 = (bf16[80,384]{1,0:T(8,128)(2,1)}, bf16[80,384]{1,0:T(8,128)(2,1)}, bf16[80,384]{1,0:T(8,128)(2,1)}, bf16[80,384]{1,0:T(8,128)(2,1)}) custom-call(bf16[80,384]{1,0:T(8,128)(2,1)} %get-tuple-element.232.refs_0_, bf16[80,384]{1,0:T(8,128)(2,1)} %copy-done.9, bf16[80,384]{1,0:T(8,128)(2,1)} %copy-done.8, bf16[80,384]{1,0:T(8,128)(2,1)} %copy-done.7, ...), custom_call_target="tpu_custom_call" | custom-call | tf_op jit(solution)/shard_map/crps/pallas_call | solution.py:36
  34.6 3.1 %collective-permute-start.5 = (bf16[80,384]{1,0:T(8,128)(2,1)}, bf16[80,384]{1,0:T(8,128)(2,1)S(1)}, u32[]{:S(2)}, u32[]{:S(2)}) collective-permute-start(bf16[80,384]{1,0:T(8,128)(2,1)} %get-tuple-element.91), channel_id=1, source_target_pairs={{0,24},{8,0},{16,8},{24,16},{1,25},{9,1},{17,9},{25,17},{2,26},{10... | collective-permute-start | bytes 184328 | tf_op jit(solution)/shard_map/ppermute | solution.py:409
  38.9 1.0 collective-permute-done.5.refs_1_
  39.9 3.1 %collective-permute-done.6.refs_2_ = bf16[80,384]{1,0:T(8,128)(2,1)S(1)} collective-permute-done((bf16[80,384]{1,0:T(8,128)(2,1)}, bf16[80,384]{1,0:T(8,128)(2,1)S(1)}, u32[]{:S(2)}, u32[]{:S(2)}) %collective-permute-start.6) | collective-permute-done | bytes 61472 | tf_op jit(solution)/shard_map/ppermute | solution.py:409
  43.1 0.9 collective-permute-done.7.refs_3_
  44.0 0.6 copy-done.12
  44.6 11.2 %backward.1 = (bf16[832,640]{1,0:T(8,128)(2,1)}, bf16[832,640]{1,0:T(8,128)(2,1)}, bf16[384,641]{1,0:T(8,128)(2,1)}, bf16[656,384]{1,0:T(8,128)(2,1)}, bf16[656,384]{1,0:T(8,128)(2,1)}) custom-call(s32[2]{0:T(128)} %pad_add_fusion.place, bf16[80,384]{1,0:T(8,128)(2,1)} %get-tuple-element.90.refs_0_, bf16[80,384]{1,0:T(8,128)(2,1)} %copy-done.10, ...), custom_call_target="tpu_custom_call" | custom-call | tf_op jit(solution)/shard_map/backward/pallas_call | solution.py:36
  55.8 6.1 %second_products.1 = (bf16[960,640]{1,0:T(8,128)(2,1)}, bf16[960,640]{1,0:T(8,128)(2,1)}) custom-call(s32[2]{0:T(128)} %pad_add_fusion.place, bf16[656,384]{1,0:T(8,128)(2,1)} %get-tuple-element.106.refs_0_, bf16[384,1282]{1,0:T(8,128)(2,1)} %get-tuple-element.96.refs_9_.refs_1_, bf16[656,384]{1,0:T(8,128)(2,1)} %get-tuple-element.103.refs_0_.refs_2_, ...), custom_call_target="tpu_custom_call" | custom-call | tf_op jit(solution)/shard_map/second_products/pallas_call | solution.py:36
  62.4 1.5 add_convert_fusion.6
  63.9 5.6 %third_products.1 = (bf16[960,640]{1,0:T(8,128)(2,1)}, bf16[960,640]{1,0:T(8,128)(2,1)}) custom-call(s32[2]{0:T(128)} %pad_add_fusion.place, bf16[656,384]{1,0:T(8,128)(2,1)} %get-tuple-element.103.refs_0_.refs_2_, bf16[384,2688]{1,0:T(8,128)(2,1)} %get-tuple-element.98.refs_11_.refs_1_.refs_3_), custom_call_target="tpu_custom_call" | custom-call | tf_op jit(solution)/shard_map/third_products/pallas_call | solution.py:36
  69.6 1.0 copy-done.2
  70.6 2.5 %add_convert_fusion = (bf16[480,640]{1,0:T(8,128)(2,1)}, bf16[480,640]{1,0:T(8,128)(2,1)S(1)}) fusion(bf16[960,640]{1,0:T(8,128)(2,1)} %copy-done.2, s32[]{:T(128)S(6)} %select_n.389, bf16[960,640]{1,0:T(8,128)(2,1)S(1)} %copy-done.1, s32[]{:T(128)S(6)} %select_n.382), kind=kLoop, calls=%fused_computation.5 | loop fusion | flops 2457600 | bytes 3686408 | tf_op jit(solution)/shard_map/convert_element_type | solution.py:352
  73.2 2.4 %add_convert_fusion.1 = (bf16[480,640]{1,0:T(8,128)(2,1)}, bf16[480,640]{1,0:T(8,128)(2,1)S(1)}) fusion(bf16[960,640]{1,0:T(8,128)(2,1)} %collective-permute-done.10, s32[]{:T(128)S(6)} %select_n.387, bf16[960,640]{1,0:T(8,128)(2,1)S(1)} %copy-done.3, s32[]{:T(128)S(6)} %select_n.379), kind=kLoop, calls=%fused_computation.6 | loop fusion | flops 2457600 | bytes 3686408 | tf_op jit(solution)/shard_map/convert_element_type | solution.py:352
  75.6 1.1 collective-permute-start.15
  76.8 6.6 %collect.1 = (f32[2,4,45,641]{3,2,1,0:T(8,128)}, f32[2,4,3,641]{3,2,1,0:T(4,128)}, f32[2,4,3,641]{3,2,1,0:T(4,128)}) custom-call(bf16[384,641]{1,0:T(8,128)(2,1)} %get-tuple-element.110.hidden_grad, bf16[641,2564]{1,0:T(8,128)(2,1)} %bitcast.24, bf16[768,256]{1,0:T(8,128)(2,1)} %get-tuple-element.111.stencil), custom_call_target="tpu_custom_call" | custom-call | tf_op jit(solution)/shard_map/collect/pallas_call | solution.py:36
  83.3 0.8 collective-permute-done.9
  84.2 1.9 %add_convert_fusion.12 = (bf16[208,640]{1,0:T(8,128)(2,1)}, bf16[208,640]{1,0:T(8,128)(2,1)S(1)}) fusion(bf16[416,640]{1,0:T(8,128)(2,1)} %collective-permute-done.9, s32[]{:T(128)S(6)} %select_n.385, bf16[416,640]{1,0:T(8,128)(2,1)S(1)} %get-tuple-element.116, s32[]{:T(128)S(6)} %select_n.390), kind=kLoop, calls=%fused_computation.31 | loop fusion | flops 1064960 | bytes 1597448 | tf_op jit(solution)/shard_map/convert_element_type | solution.py:352
  86.0 3.5 %collective-permute-done.16 = bf16[480,640]{1,0:T(8,128)(2,1)S(1)} collective-permute-done((bf16[480,640]{1,0:T(8,128)(2,1)}, bf16[480,640]{1,0:T(8,128)(2,1)S(1)}, u32[]{:S(2)}, u32[]{:S(2)}) %collective-permute-start.16) | collective-permute-done | bytes 614432 | tf_op jit(solution)/shard_map/ppermute | solution.py:343
  90.1 1.0 collective-permute-start.18
  91.1 1.0 collective-permute-done.15
  92.1 1.2 add_convert_fusion.9
  93.3 1.8 %collective-permute-start.17 = (bf16[240,640]{1,0:T(8,128)(2,1)S(1)}, bf16[240,640]{1,0:T(8,128)(2,1)S(1)}, u32[]{:S(2)}, u32[]{:S(2)}) collective-permute-start(bf16[240,640]{1,0:T(8,128)(2,1)S(1)} %get-tuple-element.200), channel_id=1, source_target_pairs={{0,8},{1,9},{2,10},{3,11},{4,12},{5,13},{6,14},{7,15},{8,0},{9,1},... | collective-permute-start | bytes 921608 | tf_op jit(solution)/shard_map/ppermute | solution.py:343
  95.6 2.4 %collective-permute-done.14 = bf16[208,640]{1,0:T(8,128)(2,1)} collective-permute-done((bf16[208,640]{1,0:T(8,128)(2,1)}, bf16[208,640]{1,0:T(8,128)(2,1)}, u32[]{:S(2)}, u32[]{:S(2)}) %collective-permute-start.14) | collective-permute-done | bytes 266272 | tf_op jit(solution)/shard_map/ppermute | solution.py:343
  98.0 1.0 add_convert_fusion.23
  99.1 0.7 collective-permute-start.21
  99.9 1.8 %collective-permute-start.20 = (bf16[120,640]{1,0:T(8,128)(2,1)S(1)}, bf16[120,640]{1,0:T(8,128)(2,1)S(1)}, u32[]{:S(2)}, u32[]{:S(2)}) collective-permute-start(bf16[120,640]{1,0:T(8,128)(2,1)S(1)} %get-tuple-element.213), channel_id=1, source_target_pairs={{0,8},{1,9},{2,10},{3,11},{4,12},{5,13},{6,14},{7,15},{8,0},{9,1},... | collective-permute-start | bytes 460808 | tf_op jit(solution)/shard_map/ppermute | solution.py:343
  101.7 1.1 collective-permute-done.17
  102.9 1.2 collective-permute-done.21
  104.2 1.2 collective-permute-start.23
  105.4 3.0 %collective-permute-start.19 = (bf16[120,640]{1,0:T(8,128)(2,1)S(1)}, bf16[120,640]{1,0:T(8,128)(2,1)S(1)}, u32[]{:S(2)}, u32[]{:S(2)}) collective-permute-start(bf16[120,640]{1,0:T(8,128)(2,1)S(1)} %get-tuple-element.212), channel_id=1, source_target_pairs={{0,2},{1,3},{2,0},{3,1},{4,6},{5,7},{6,4},{7,5},{8,10},{9,11},{10,... | collective-permute-start | bytes 460808 | tf_op jit(solution)/shard_map/ppermute | solution.py:343
  108.5 1.3 collective-permute-start.22
  109.8 1.9 %collective-permute-done.19 = bf16[120,640]{1,0:T(8,128)(2,1)S(1)} collective-permute-done((bf16[120,640]{1,0:T(8,128)(2,1)S(1)}, bf16[120,640]{1,0:T(8,128)(2,1)S(1)}, u32[]{:S(2)}, u32[]{:S(2)}) %collective-permute-start.19) | collective-permute-done | bytes 153632 | tf_op jit(solution)/shard_map/ppermute | solution.py:343
  111.7 1.3 collective-permute-start.26
  113.0 6.7 %collective-permute-done.23 = bf16[104,640]{1,0:T(8,128)(2,1)S(1)} collective-permute-done((bf16[104,640]{1,0:T(8,128)(2,1)S(1)}, bf16[104,640]{1,0:T(8,128)(2,1)S(1)}, u32[]{:S(2)}, u32[]{:S(2)}) %collective-permute-start.23) | collective-permute-done | bytes 133152 | tf_op jit(solution)/shard_map/ppermute | solution.py:343
  119.7 3.2 %collective-permute-done.22 = bf16[120,640]{1,0:T(8,128)(2,1)S(1)} collective-permute-done((bf16[120,640]{1,0:T(8,128)(2,1)S(1)}, bf16[120,640]{1,0:T(8,128)(2,1)S(1)}, u32[]{:S(2)}, u32[]{:S(2)}) %collective-permute-start.22) | collective-permute-done | bytes 153632 | tf_op jit(solution)/shard_map/ppermute | solution.py:343
  123.0 2.1 %collective-permute-done.26 = bf16[120,640]{1,0:T(8,128)(2,1)S(1)} collective-permute-done((bf16[120,640]{1,0:T(8,128)(2,1)S(1)}, bf16[120,640]{1,0:T(8,128)(2,1)S(1)}, u32[]{:S(2)}, u32[]{:S(2)}) %collective-permute-start.26) | collective-permute-done | bytes 153632 | tf_op jit(solution)/shard_map/ppermute | solution.py:343
  125.1 1.1 collective-permute-start.28
  126.3 1.1 collective-permute-start.27
  127.4 0.9 collective-permute-done.24
  128.4 0.8 collective-permute-start.31
  129.2 2.9 %collective-permute-done.28 = bf16[120,640]{1,0:T(8,128)(2,1)S(1)} collective-permute-done((bf16[120,640]{1,0:T(8,128)(2,1)S(1)}, bf16[120,640]{1,0:T(8,128)(2,1)S(1)}, u32[]{:S(2)}, u32[]{:S(2)}) %collective-permute-start.28) | collective-permute-done | bytes 153632 | tf_op jit(solution)/shard_map/ppermute | solution.py:343
  132.3 3.3 %collective-permute-done.27 = bf16[208,640]{1,0:T(8,128)(2,1)S(1)} collective-permute-done((bf16[208,640]{1,0:T(8,128)(2,1)S(1)}, bf16[208,640]{1,0:T(8,128)(2,1)S(1)}, u32[]{:S(2)}, u32[]{:S(2)}) %collective-permute-start.27) | collective-permute-done | bytes 266272 | tf_op jit(solution)/shard_map/ppermute | solution.py:343
  135.9 1.1 collective-permute-start.33
  137.0 5.1 %collective-permute-done.30 = bf16[240,640]{1,0:T(8,128)(2,1)S(1)} collective-permute-done((bf16[240,640]{1,0:T(8,128)(2,1)S(1)}, bf16[240,640]{1,0:T(8,128)(2,1)S(1)}, u32[]{:S(2)}, u32[]{:S(2)}) %collective-permute-start.30) | collective-permute-done | bytes 307232 | tf_op jit(solution)/shard_map/ppermute | solution.py:343
  142.2 0.7 collective-permute-start.32
  142.9 7.6 %collective-permute-done.29 = bf16[416,640]{1,0:T(8,128)(2,1)S(1)} collective-permute-done((bf16[416,640]{1,0:T(8,128)(2,1)S(1)}, bf16[416,640]{1,0:T(8,128)(2,1)S(1)}, u32[]{:S(2)}, u32[]{:S(2)}) %collective-permute-start.29) | collective-permute-done | bytes 532512 | tf_op jit(solution)/shard_map/ppermute | solution.py:343
  152.4 1.1 copy.24
  154.5 1.5 pad_maximum_fusion.2.summed
  156.0 3.2 %finish_first.1 = (bf16[641,1282]{1,0:T(8,128)(2,1)}, bf16[288,641]{1,0:T(8,128)(2,1)}, bf16[32,640]{1,0:T(8,128)(2,1)}) custom-call(bf16[1664,640]{1,0:T(8,128)(2,1)} %pad_maximum_fusion.2.summed), custom_call_target="tpu_custom_call" | custom-call | tf_op jit(solution)/shard_map/finish_first/pallas_call | solution.py:36
  159.4 1.6 pad_maximum_fusion.second
  161.3 1.6 pad_maximum_fusion.1.third
  162.9 5.1 %finish_rest.1 = (bf16[641,1282]{1,0:T(8,128)(2,1)}, bf16[641,2564]{1,0:T(8,128)(2,1)}) custom-call(bf16[1920,640]{1,0:T(8,128)(2,1)} %pad_maximum_fusion.second, bf16[1920,640]{1,0:T(8,128)(2,1)} %pad_maximum_fusion.1.third, bf16[32,640]{1,0:T(8,128)(2,1)} %get-tuple-element.168.misc_ref), custom_call_target="tpu_custom_call" | custom-call | tf_op jit(solution)/shard_map/finish_rest/pallas_call | solution.py:36
  (105 shorter events, 9.3 us)
Async XLA Ops:
  0.6 4.6 %copy-start.6 = (bf16[4,45,288]{2,0,1:T(4,128)(2,1)S(1)}, bf16[4,45,288]{2,0,1:T(4,128)(2,1)}, u32[]{:S(2)}) copy-start(bf16[4,45,288]{2,0,1:T(4,128)(2,1)} %param.19) | copy-start | bytes 311044
  0.6 4.8 %copy-start.13 = (bf16[16,4,7,7]{0,1,3,2:T(4,128)(2,1)S(1)}, bf16[16,4,7,7]{0,1,3,2:T(4,128)(2,1)}, u32[]{:S(2)}) copy-start(bf16[16,4,7,7]{0,1,3,2:T(4,128)(2,1)} %param.14) | copy-start | bytes 18820
  1.8 7.9 %copy-start = (bf16[2,4,45,641]{3,2,1,0:T(8,128)(2,1)}, bf16[2,4,45,641]{3,2,1,0:T(8,128)(2,1)S(1)}, u32[]{:S(2)}) copy-start(bf16[2,4,45,641]{3,2,1,0:T(8,128)(2,1)S(1)} %copy.27.latent) | copy-start | bytes 1384564
  1.9 5.1 %collective-permute-start.1 = (bf16[2,3,4,641]{3,1,2,0:T(4,128)(2,1)S(1)}, bf16[2,3,4,641]{3,1,2,0:T(4,128)(2,1)S(1)}, u32[]{:S(2)}, u32[]{:S(2)}) collective-permute-start(bf16[2,3,4,641]{3,1,2,0:T(4,128)(2,1)S(1)} %get-tuple-element.215), channel_id=1, source_target_pairs={{0,7},{1,0},{2,1},{3,2},{4,3},{5,4},{6,5},{7,6},{8,15},{9,8},{10,9... | collective-permute-start | bytes 92312 | tf_op jit(solution)/shard_map/ppermute | solution.py:409
  5.3 4.4 %collective-permute-start = (bf16[2,3,4,641]{3,1,2,0:T(4,128)(2,1)S(1)}, bf16[2,3,4,641]{3,1,2,0:T(4,128)(2,1)S(1)}, u32[]{:S(2)}, u32[]{:S(2)}) collective-permute-start(bf16[2,3,4,641]{3,1,2,0:T(4,128)(2,1)S(1)} %get-tuple-element.216), channel_id=1, source_target_pairs={{0,1},{1,2},{2,3},{3,4},{4,5},{5,6},{6,7},{7,0},{8,9},{9,10},{10,1... | collective-permute-start | bytes 92312 | tf_op jit(solution)/shard_map/ppermute | solution.py:409
  7.0 2.7 %copy-start.14 = (bf16[2,3,4,641]{3,1,2,0:T(4,128)(2,1)}, bf16[2,3,4,641]{3,1,2,0:T(4,128)(2,1)S(1)}, u32[]{:S(2)}) copy-start(bf16[2,3,4,641]{3,1,2,0:T(4,128)(2,1)S(1)} %collective-permute-done.1) | copy-start | bytes 92308
  9.7 0.6 copy-start.15
  23.1 6.2 %collective-permute-start.4 = (bf16[80,384]{1,0:T(8,128)(2,1)S(1)}, bf16[80,384]{1,0:T(8,128)(2,1)S(1)}, u32[]{:S(2)}, u32[]{:S(2)}) collective-permute-start(bf16[80,384]{1,0:T(8,128)(2,1)S(1)} %get-tuple-element.229), channel_id=1, source_target_pairs={{0,8},{8,16},{16,24},{24,0},{1,9},{9,17},{17,25},{25,1},{2,10},{10... | collective-permute-start | bytes 184328 | tf_op jit(solution)/shard_map/ppermute | solution.py:409
  24.7 5.1 %collective-permute-start.3 = (bf16[80,384]{1,0:T(8,128)(2,1)S(1)}, bf16[80,384]{1,0:T(8,128)(2,1)S(1)}, u32[]{:S(2)}, u32[]{:S(2)}) collective-permute-start(bf16[80,384]{1,0:T(8,128)(2,1)S(1)} %get-tuple-element.230), channel_id=1, source_target_pairs={{0,16},{8,24},{16,0},{24,8},{1,17},{9,25},{17,1},{25,9},{2,18},{10... | collective-permute-start | bytes 184328 | tf_op jit(solution)/shard_map/ppermute | solution.py:409
  27.2 4.2 %collective-permute-start.2 = (bf16[80,384]{1,0:T(8,128)(2,1)S(1)}, bf16[80,384]{1,0:T(8,128)(2,1)S(1)}, u32[]{:S(2)}, u32[]{:S(2)}) collective-permute-start(bf16[80,384]{1,0:T(8,128)(2,1)S(1)} %get-tuple-element.231), channel_id=1, source_target_pairs={{0,24},{8,0},{16,8},{24,16},{1,25},{9,1},{17,9},{25,17},{2,26},{10... | collective-permute-start | bytes 184328 | tf_op jit(solution)/shard_map/ppermute | solution.py:409
  29.3 2.2 %copy-start.7 = (bf16[80,384]{1,0:T(8,128)(2,1)}, bf16[80,384]{1,0:T(8,128)(2,1)S(1)}, u32[]{:S(2)}) copy-start(bf16[80,384]{1,0:T(8,128)(2,1)S(1)} %collective-permute-done.4.refs_3_) | copy-start | bytes 184324
  29.8 1.7 %copy-start.8 = (bf16[80,384]{1,0:T(8,128)(2,1)}, bf16[80,384]{1,0:T(8,128)(2,1)S(1)}, u32[]{:S(2)}) copy-start(bf16[80,384]{1,0:T(8,128)(2,1)S(1)} %collective-permute-done.3.refs_2_) | copy-start | bytes 184324
  31.5 0.6 copy-start.9
  34.6 5.3 %collective-permute-start.5 = (bf16[80,384]{1,0:T(8,128)(2,1)}, bf16[80,384]{1,0:T(8,128)(2,1)S(1)}, u32[]{:S(2)}, u32[]{:S(2)}) collective-permute-start(bf16[80,384]{1,0:T(8,128)(2,1)} %get-tuple-element.91), channel_id=1, source_target_pairs={{0,24},{8,0},{16,8},{24,16},{1,25},{9,1},{17,9},{25,17},{2,26},{10... | collective-permute-start | bytes 184328 | tf_op jit(solution)/shard_map/ppermute | solution.py:409
  37.8 5.3 %collective-permute-start.6 = (bf16[80,384]{1,0:T(8,128)(2,1)}, bf16[80,384]{1,0:T(8,128)(2,1)S(1)}, u32[]{:S(2)}, u32[]{:S(2)}) collective-permute-start(bf16[80,384]{1,0:T(8,128)(2,1)} %get-tuple-element.92), channel_id=1, source_target_pairs={{0,16},{8,24},{16,0},{24,8},{1,17},{9,25},{17,1},{25,9},{2,18},{10... | collective-permute-start | bytes 184328 | tf_op jit(solution)/shard_map/ppermute | solution.py:409
  37.8 6.2 %collective-permute-start.7 = (bf16[80,384]{1,0:T(8,128)(2,1)}, bf16[80,384]{1,0:T(8,128)(2,1)S(1)}, u32[]{:S(2)}, u32[]{:S(2)}) collective-permute-start(bf16[80,384]{1,0:T(8,128)(2,1)} %get-tuple-element.93), channel_id=1, source_target_pairs={{0,8},{8,16},{16,24},{24,0},{1,9},{9,17},{17,25},{25,1},{2,10},{10... | collective-permute-start | bytes 184328 | tf_op jit(solution)/shard_map/ppermute | solution.py:409
  39.9 4.1 %copy-start.10 = (bf16[80,384]{1,0:T(8,128)(2,1)}, bf16[80,384]{1,0:T(8,128)(2,1)S(1)}, u32[]{:S(2)}) copy-start(bf16[80,384]{1,0:T(8,128)(2,1)S(1)} %collective-permute-done.5.refs_1_) | copy-start | bytes 184324
  43.1 0.9 copy-start.11
  44.0 0.6 copy-start.12
  55.8 6.6 %collective-permute-start.8 = (bf16[832,640]{1,0:T(8,128)(2,1)}, bf16[832,640]{1,0:T(8,128)(2,1)}, u32[]{:S(2)}, u32[]{:S(2)}) collective-permute-start(bf16[832,640]{1,0:T(8,128)(2,1)} %get-tuple-element.100), channel_id=1, source_target_pairs={{0,1},{1,0},{2,3},{3,2},{4,5},{5,4},{6,7},{7,6},{8,9},{9,8},{10,11... | collective-permute-start | bytes 3194888 | tf_op jit(solution)/shard_map/ppermute | solution.py:343
  55.8 6.6 %copy-start.5 = (bf16[832,640]{1,0:T(8,128)(2,1)S(1)}, bf16[832,640]{1,0:T(8,128)(2,1)}, u32[]{:S(2)}) copy-start(bf16[832,640]{1,0:T(8,128)(2,1)} %get-tuple-element.99) | copy-start | bytes 3194884
  61.9 7.7 %collective-permute-start.11 = (bf16[960,640]{1,0:T(8,128)(2,1)}, bf16[960,640]{1,0:T(8,128)(2,1)S(1)}, u32[]{:S(2)}, u32[]{:S(2)}) collective-permute-start(bf16[960,640]{1,0:T(8,128)(2,1)} %get-tuple-element.108), channel_id=1, source_target_pairs={{0,1},{1,0},{2,3},{3,2},{4,5},{5,4},{6,7},{7,6},{8,9},{9,8},{10,11... | collective-permute-start | bytes 3686408 | tf_op jit(solution)/shard_map/ppermute | solution.py:343
  63.9 6.7 %copy-start.1 = (bf16[960,640]{1,0:T(8,128)(2,1)S(1)}, bf16[960,640]{1,0:T(8,128)(2,1)}, u32[]{:S(2)}) copy-start(bf16[960,640]{1,0:T(8,128)(2,1)} %get-tuple-element.107) | copy-start | bytes 3686404
  69.5 3.7 %collective-permute-start.10 = (bf16[960,640]{1,0:T(8,128)(2,1)}, bf16[960,640]{1,0:T(8,128)(2,1)}, u32[]{:S(2)}, u32[]{:S(2)}) collective-permute-start(bf16[960,640]{1,0:T(8,128)(2,1)} %get-tuple-element.105), channel_id=1, source_target_pairs={{0,1},{1,0},{2,3},{3,2},{4,5},{5,4},{6,7},{7,6},{8,9},{9,8},{10,11... | collective-permute-start | bytes 3686408 | tf_op jit(solution)/shard_map/ppermute | solution.py:343
  69.6 14.6 %collective-permute-start.9 = (bf16[416,640]{1,0:T(8,128)(2,1)S(1)}, bf16[416,640]{1,0:T(8,128)(2,1)}, u32[]{:S(2)}, u32[]{:S(2)}) collective-permute-start(bf16[416,640]{1,0:T(8,128)(2,1)S(1)} %get-tuple-element.193), channel_id=1, source_target_pairs={{0,8},{1,9},{2,10},{3,11},{4,12},{5,13},{6,14},{7,15},{8,0},{9,1},... | collective-permute-start | bytes 1597448 | tf_op jit(solution)/shard_map/ppermute | solution.py:343
  69.6 1.0 copy-start.2
  70.6 2.6 %copy-start.3 = (bf16[960,640]{1,0:T(8,128)(2,1)S(1)}, bf16[960,640]{1,0:T(8,128)(2,1)}, u32[]{:S(2)}) copy-start(bf16[960,640]{1,0:T(8,128)(2,1)} %get-tuple-element.104) | copy-start | bytes 3686404
  73.1 16.5 %collective-permute-start.16 = (bf16[480,640]{1,0:T(8,128)(2,1)}, bf16[480,640]{1,0:T(8,128)(2,1)S(1)}, u32[]{:S(2)}, u32[]{:S(2)}) collective-permute-start(bf16[480,640]{1,0:T(8,128)(2,1)} %get-tuple-element.187), channel_id=1, source_target_pairs={{0,2},{1,3},{2,0},{3,1},{4,6},{5,7},{6,4},{7,5},{8,10},{9,11},{10,... | collective-permute-start | bytes 1843208 | tf_op jit(solution)/shard_map/ppermute | solution.py:343
  75.6 16.5 %collective-permute-start.15 = (bf16[480,640]{1,0:T(8,128)(2,1)}, bf16[480,640]{1,0:T(8,128)(2,1)}, u32[]{:S(2)}, u32[]{:S(2)}) collective-permute-start(bf16[480,640]{1,0:T(8,128)(2,1)} %get-tuple-element.189), channel_id=1, source_target_pairs={{0,4},{1,5},{2,6},{3,7},{4,0},{5,1},{6,2},{7,3},{8,12},{9,13},{10,... | collective-permute-start | bytes 1843208 | tf_op jit(solution)/shard_map/ppermute | solution.py:343
  89.6 8.4 %collective-permute-start.14 = (bf16[208,640]{1,0:T(8,128)(2,1)}, bf16[208,640]{1,0:T(8,128)(2,1)}, u32[]{:S(2)}, u32[]{:S(2)}) collective-permute-start(bf16[208,640]{1,0:T(8,128)(2,1)} %get-tuple-element.205), channel_id=1, source_target_pairs={{0,2},{1,3},{2,0},{3,1},{4,6},{5,7},{6,4},{7,5},{8,10},{9,11},{10,... | collective-permute-start | bytes 798728 | tf_op jit(solution)/shard_map/ppermute | solution.py:343
  90.0 5.1 %copy-start.17 = (f32[2,4,3,641]{3,2,1,0:T(4,128)S(1)}, f32[2,4,3,641]{3,2,1,0:T(4,128)}, u32[]{:S(2)}) copy-start(f32[2,4,3,641]{3,2,1,0:T(4,128)} %get-tuple-element.114) | copy-start | bytes 184612
  90.0 5.2 %copy-start.16 = (f32[2,4,3,641]{3,2,1,0:T(4,128)S(1)}, f32[2,4,3,641]{3,2,1,0:T(4,128)}, u32[]{:S(2)}) copy-start(f32[2,4,3,641]{3,2,1,0:T(4,128)} %get-tuple-element.115) | copy-start | bytes 184612
  90.1 9.0 %collective-permute-start.18 = (bf16[240,640]{1,0:T(8,128)(2,1)S(1)}, bf16[240,640]{1,0:T(8,128)(2,1)S(1)}, u32[]{:S(2)}, u32[]{:S(2)}) collective-permute-start(bf16[240,640]{1,0:T(8,128)(2,1)S(1)} %get-tuple-element.201), channel_id=1, source_target_pairs={{0,4},{1,5},{2,6},{3,7},{4,0},{5,1},{6,2},{7,3},{8,12},{9,13},{10,... | collective-permute-start | bytes 921608 | tf_op jit(solution)/shard_map/ppermute | solution.py:343
  93.3 9.5 %collective-permute-start.17 = (bf16[240,640]{1,0:T(8,128)(2,1)S(1)}, bf16[240,640]{1,0:T(8,128)(2,1)S(1)}, u32[]{:S(2)}, u32[]{:S(2)}) collective-permute-start(bf16[240,640]{1,0:T(8,128)(2,1)S(1)} %get-tuple-element.200), channel_id=1, source_target_pairs={{0,8},{1,9},{2,10},{3,11},{4,12},{5,13},{6,14},{7,15},{8,0},{9,1},... | collective-permute-start | bytes 921608 | tf_op jit(solution)/shard_map/ppermute | solution.py:343
  95.1 56.5 %collective-permute-start.12 = (f32[2,4,3,641]{3,2,1,0:T(4,128)S(1)}, f32[2,4,3,641]{3,2,1,0:T(4,128)S(1)}, u32[]{:S(2)}, u32[]{:S(2)}) collective-permute-start(f32[2,4,3,641]{3,2,1,0:T(4,128)S(1)} %copy-done.17), channel_id=1, source_target_pairs={{0,7},{1,0},{2,1},{3,2},{4,3},{5,4},{6,5},{7,6},{8,15},{9,8},{10,9... | collective-permute-start | bytes 184616 | tf_op jit(solution)/shard_map/ppermute | solution.py:409
  95.2 56.5 %collective-permute-start.13 = (f32[2,4,3,641]{3,2,1,0:T(4,128)S(1)}, f32[2,4,3,641]{3,2,1,0:T(4,128)S(1)}, u32[]{:S(2)}, u32[]{:S(2)}) collective-permute-start(f32[2,4,3,641]{3,2,1,0:T(4,128)S(1)} %copy-done.16), channel_id=1, source_target_pairs={{0,1},{1,2},{2,3},{3,4},{4,5},{5,6},{6,7},{7,0},{8,9},{9,10},{10,1... | collective-permute-start | bytes 184616 | tf_op jit(solution)/shard_map/ppermute | solution.py:409
  99.1 5.1 %collective-permute-start.21 = (bf16[104,640]{1,0:T(8,128)(2,1)S(1)}, bf16[104,640]{1,0:T(8,128)(2,1)S(1)}, u32[]{:S(2)}, u32[]{:S(2)}) collective-permute-start(bf16[104,640]{1,0:T(8,128)(2,1)S(1)} %get-tuple-element.221), channel_id=1, source_target_pairs={{0,4},{1,5},{2,6},{3,7},{4,0},{5,1},{6,2},{7,3},{8,12},{9,13},{10,... | collective-permute-start | bytes 399368 | tf_op jit(solution)/shard_map/ppermute | solution.py:343
  99.9 5.5 %collective-permute-start.20 = (bf16[120,640]{1,0:T(8,128)(2,1)S(1)}, bf16[120,640]{1,0:T(8,128)(2,1)S(1)}, u32[]{:S(2)}, u32[]{:S(2)}) collective-permute-start(bf16[120,640]{1,0:T(8,128)(2,1)S(1)} %get-tuple-element.213), channel_id=1, source_target_pairs={{0,8},{1,9},{2,10},{3,11},{4,12},{5,13},{6,14},{7,15},{8,0},{9,1},... | collective-permute-start | bytes 460808 | tf_op jit(solution)/shard_map/ppermute | solution.py:343
  104.2 15.5 %collective-permute-start.23 = (bf16[104,640]{1,0:T(8,128)(2,1)S(1)}, bf16[104,640]{1,0:T(8,128)(2,1)S(1)}, u32[]{:S(2)}, u32[]{:S(2)}) collective-permute-start(bf16[104,640]{1,0:T(8,128)(2,1)S(1)} %add_convert_fusion.22), channel_id=1, source_target_pairs={{0,16},{1,17},{2,18},{3,19},{4,20},{5,21},{6,22},{7,23},{8,24},{9,... | collective-permute-start | bytes 399368 | tf_op jit(solution)/shard_map/ppermute | solution.py:343
  105.4 6.2 %collective-permute-start.19 = (bf16[120,640]{1,0:T(8,128)(2,1)S(1)}, bf16[120,640]{1,0:T(8,128)(2,1)S(1)}, u32[]{:S(2)}, u32[]{:S(2)}) collective-permute-start(bf16[120,640]{1,0:T(8,128)(2,1)S(1)} %get-tuple-element.212), channel_id=1, source_target_pairs={{0,2},{1,3},{2,0},{3,1},{4,6},{5,7},{6,4},{7,5},{8,10},{9,11},{10,... | collective-permute-start | bytes 460808 | tf_op jit(solution)/shard_map/ppermute | solution.py:343
  108.5 14.4 %collective-permute-start.22 = (bf16[120,640]{1,0:T(8,128)(2,1)S(1)}, bf16[120,640]{1,0:T(8,128)(2,1)S(1)}, u32[]{:S(2)}, u32[]{:S(2)}) collective-permute-start(bf16[120,640]{1,0:T(8,128)(2,1)S(1)} %add_convert_fusion.16), channel_id=1, source_target_pairs={{0,16},{1,17},{2,18},{3,19},{4,20},{5,21},{6,22},{7,23},{8,24},{9,... | collective-permute-start | bytes 460808 | tf_op jit(solution)/shard_map/ppermute | solution.py:343
  111.7 13.4 %collective-permute-start.26 = (bf16[120,640]{1,0:T(8,128)(2,1)S(1)}, bf16[120,640]{1,0:T(8,128)(2,1)S(1)}, u32[]{:S(2)}, u32[]{:S(2)}) collective-permute-start(bf16[120,640]{1,0:T(8,128)(2,1)S(1)} %add_convert_fusion.15), channel_id=1, source_target_pairs={{0,16},{1,17},{2,18},{3,19},{4,20},{5,21},{6,22},{7,23},{8,24},{9,... | collective-permute-start | bytes 460808 | tf_op jit(solution)/shard_map/ppermute | solution.py:343
  119.7 6.6 %collective-permute-start.25 = (bf16[104,640]{1,0:T(8,128)(2,1)S(1)}, bf16[104,640]{1,0:T(8,128)(2,1)S(1)}, u32[]{:S(2)}, u32[]{:S(2)}) collective-permute-start(bf16[104,640]{1,0:T(8,128)(2,1)S(1)} %add_convert_fusion.21), channel_id=1, source_target_pairs={{0,4},{1,5},{2,6},{3,7},{4,0},{5,1},{6,2},{7,3},{8,12},{9,13},{10,... | collective-permute-start | bytes 399368 | tf_op jit(solution)/shard_map/ppermute | solution.py:343
  123.0 5.3 %collective-permute-start.24 = (bf16[120,640]{1,0:T(8,128)(2,1)S(1)}, bf16[120,640]{1,0:T(8,128)(2,1)S(1)}, u32[]{:S(2)}, u32[]{:S(2)}) collective-permute-start(bf16[120,640]{1,0:T(8,128)(2,1)S(1)} %add_convert_fusion.14), channel_id=1, source_target_pairs={{0,8},{1,9},{2,10},{3,11},{4,12},{5,13},{6,14},{7,15},{8,0},{9,1},... | collective-permute-start | bytes 460808 | tf_op jit(solution)/shard_map/ppermute | solution.py:343
  125.1 7.0 %collective-permute-start.28 = (bf16[120,640]{1,0:T(8,128)(2,1)S(1)}, bf16[120,640]{1,0:T(8,128)(2,1)S(1)}, u32[]{:S(2)}, u32[]{:S(2)}) collective-permute-start(bf16[120,640]{1,0:T(8,128)(2,1)S(1)} %add_convert_fusion.13), channel_id=1, source_target_pairs={{0,2},{1,3},{2,0},{3,1},{4,6},{5,7},{6,4},{7,5},{8,10},{9,11},{10,... | collective-permute-start | bytes 460808 | tf_op jit(solution)/shard_map/ppermute | solution.py:343
  126.3 9.3 %collective-permute-start.27 = (bf16[208,640]{1,0:T(8,128)(2,1)S(1)}, bf16[208,640]{1,0:T(8,128)(2,1)S(1)}, u32[]{:S(2)}, u32[]{:S(2)}) collective-permute-start(bf16[208,640]{1,0:T(8,128)(2,1)S(1)} %pad_maximum_fusion.11), channel_id=1, source_target_pairs={{0,2},{1,3},{2,0},{3,1},{4,6},{5,7},{6,4},{7,5},{8,10},{9,11},{10,... | collective-permute-start | bytes 798728 | tf_op jit(solution)/shard_map/ppermute | solution.py:343
  128.4 7.4 %collective-permute-start.31 = (bf16[240,640]{1,0:T(8,128)(2,1)S(1)}, bf16[240,640]{1,0:T(8,128)(2,1)S(1)}, u32[]{:S(2)}, u32[]{:S(2)}) collective-permute-start(bf16[240,640]{1,0:T(8,128)(2,1)S(1)} %pad_maximum_fusion.9), channel_id=1, source_target_pairs={{0,4},{1,5},{2,6},{3,7},{4,0},{5,1},{6,2},{7,3},{8,12},{9,13},{10,... | collective-permute-start | bytes 921608 | tf_op jit(solution)/shard_map/ppermute | solution.py:343
  132.2 9.9 %collective-permute-start.30 = (bf16[240,640]{1,0:T(8,128)(2,1)S(1)}, bf16[240,640]{1,0:T(8,128)(2,1)S(1)}, u32[]{:S(2)}, u32[]{:S(2)}) collective-permute-start(bf16[240,640]{1,0:T(8,128)(2,1)S(1)} %pad_maximum_fusion.10), channel_id=1, source_target_pairs={{0,8},{1,9},{2,10},{3,11},{4,12},{5,13},{6,14},{7,15},{8,0},{9,1},... | collective-permute-start | bytes 921608 | tf_op jit(solution)/shard_map/ppermute | solution.py:343
  135.7 14.8 %collective-permute-start.29 = (bf16[416,640]{1,0:T(8,128)(2,1)S(1)}, bf16[416,640]{1,0:T(8,128)(2,1)S(1)}, u32[]{:S(2)}, u32[]{:S(2)}) collective-permute-start(bf16[416,640]{1,0:T(8,128)(2,1)S(1)} %pad_maximum_fusion.8), channel_id=1, source_target_pairs={{0,8},{1,9},{2,10},{3,11},{4,12},{5,13},{6,14},{7,15},{8,0},{9,1},... | collective-permute-start | bytes 1597448 | tf_op jit(solution)/shard_map/ppermute | solution.py:343
  135.9 14.9 %collective-permute-start.33 = (bf16[480,640]{1,0:T(8,128)(2,1)S(1)}, bf16[480,640]{1,0:T(8,128)(2,1)S(1)}, u32[]{:S(2)}, u32[]{:S(2)}) collective-permute-start(bf16[480,640]{1,0:T(8,128)(2,1)S(1)} %pad_maximum_fusion.6), channel_id=1, source_target_pairs={{0,2},{1,3},{2,0},{3,1},{4,6},{5,7},{6,4},{7,5},{8,10},{9,11},{10,... | collective-permute-start | bytes 1843208 | tf_op jit(solution)/shard_map/ppermute | solution.py:343
  142.2 11.2 %collective-permute-start.32 = (bf16[480,640]{1,0:T(8,128)(2,1)S(1)}, bf16[480,640]{1,0:T(8,128)(2,1)S(1)}, u32[]{:S(2)}, u32[]{:S(2)}) collective-permute-start(bf16[480,640]{1,0:T(8,128)(2,1)S(1)} %pad_maximum_fusion.7), channel_id=1, source_target_pairs={{0,4},{1,5},{2,6},{3,7},{4,0},{5,1},{6,2},{7,3},{8,12},{9,13},{10,... | collective-permute-start | bytes 1843208 | tf_op jit(solution)/shard_map/ppermute | solution.py:343
  150.8 3.5 %collective-permute-start.36 = (bf16[832,640]{1,0:T(8,128)(2,1)S(1)}, bf16[832,640]{1,0:T(8,128)(2,1)S(1)}, u32[]{:S(2)}, u32[]{:S(2)}) collective-permute-start(bf16[832,640]{1,0:T(8,128)(2,1)S(1)} %pad_maximum_fusion.5), channel_id=1, source_target_pairs={{0,1},{1,0},{2,3},{3,2},{4,5},{5,4},{6,7},{7,6},{8,9},{9,8},{10,11... | collective-permute-start | bytes 3194888 | tf_op jit(solution)/shard_map/ppermute | solution.py:343
  151.0 1.3 copy-start.4
  151.1 4.9 %collective-permute-start.35 = (bf16[960,640]{1,0:T(8,128)(2,1)S(1)}, bf16[960,640]{1,0:T(8,128)(2,1)S(1)}, u32[]{:S(2)}, u32[]{:S(2)}) collective-permute-start(bf16[960,640]{1,0:T(8,128)(2,1)S(1)} %pad_maximum_fusion.3), channel_id=1, source_target_pairs={{0,1},{1,0},{2,3},{3,2},{4,5},{5,4},{6,7},{7,6},{8,9},{9,8},{10,11... | collective-permute-start | bytes 3686408 | tf_op jit(solution)/shard_map/ppermute | solution.py:343
  153.7 7.3 %collective-permute-start.34 = (bf16[960,640]{1,0:T(8,128)(2,1)S(1)}, bf16[960,640]{1,0:T(8,128)(2,1)S(1)}, u32[]{:S(2)}, u32[]{:S(2)}) collective-permute-start(bf16[960,640]{1,0:T(8,128)(2,1)S(1)} %pad_maximum_fusion.4), channel_id=1, source_target_pairs={{0,1},{1,0},{2,3},{3,2},{4,5},{5,4},{6,7},{7,6},{8,9},{9,8},{10,11... | collective-permute-start | bytes 3686408 | tf_op jit(solution)/shard_map/ppermute | solution.py:343

commit v3 on v2

--- a/solution.py
+++ b/solution.py
@@ -13,7 +13,8 @@
 smooth = 0.5
 LANES = 128
 TILE = 16
-VMEM_LIMIT = 56 * 2**20
+VMEM_LIMIT = 24 * 2**20
+BEGIN = 48
 F32 = jnp.float32
 BF16 = jnp.bfloat16
 
@@ -30,7 +31,7 @@
     return d * lax.rsqrt(d * d + smooth * smooth)
 
 
-def vmem_call(body, outs, args, smem=0, scratch=(), name=None):
+def vmem_call(body, outs, args, smem=0, scratch=(), name=None, moved=0):
     specs = [pl.BlockSpec(memory_space=pltpu.SMEM)] * smem
     specs += [pl.BlockSpec(memory_space=pltpu.VMEM)] * (len(args) - smem)
     return pl.pallas_call(
@@ -40,17 +41,17 @@
         out_specs=[pl.BlockSpec(memory_space=pltpu.VMEM)] * len(outs),
         scratch_shapes=list(scratch),
         compiler_params=pltpu.CompilerParams(vmem_limit_bytes=VMEM_LIMIT),
-        cost_estimate=pl.CostEstimate(flops=0, bytes_accessed=0, transcendentals=0),
+        cost_estimate=pl.CostEstimate(flops=0, bytes_accessed=moved, transcendentals=0),
         name=name,
     )(*args)
 
 
-def forward_body(
-    dims, seeds, bands, basis, latent, left, right, table, w_disco, w_expand, w_reduce, w_decode,
-    stencil_out, spread_out, hidden_out, gelu_out, slope_out, mixed_out, fields_out, wide,
-):
+def begin_body(x, out):
+    out[...] = x[...]
+
+
+def prepare_body(dims, seeds, bands, basis, table, stencil_out, offsets_out):
     members, rows, lons, chans, lon_pad, slot, bases, piece, share = dims
-    chan_pad = up(chans, LANES)
     points = rows * lon_pad
     per_tile = LANES // slot
     lane = lax.broadcasted_iota(jnp.int32, (lon_pad, LANES), 1)
@@ -82,7 +83,19 @@
     onehot = jnp.zeros((TILE, seed_count), F32)
     for m in range(members):
         onehot = jnp.where((mrow == m) & (mcol == seeds[m]), 1.0, onehot)
-    offsets = dot(onehot.astype(BF16), table[...])
+    offsets_out[...] = dot(onehot.astype(BF16), table[...])
+
+
+def forward_body(
+    dims, place, latent, left, right, stencil, offsets_in, w_disco, w_expand, w_reduce, w_decode, *refs
+):
+    members, rows, lons, chans, lon_pad, slot, bases, piece, share = dims
+    spread_out, hidden_out, gelu_out, slope_out, mixed_out = refs[:5]
+    fields_out = refs[5 : 5 + share]
+    wide, turned_fields = refs[5 + share :]
+    chan_pad = up(chans, LANES)
+    points = rows * lon_pad
+    offsets = offsets_in[...]
     wide[...] = jnp.zeros_like(wide)
     for m in range(members):
         off = offsets[m : m + 1, :]
@@ -95,7 +108,7 @@
         carry = None
         for k in range(bases):
             moved = full if k == 0 else pltpu.roll(full, k, 1)
-            out = dot(stencil_out[k * points : (k + 1) * points, :], moved.astype(BF16))
+            out = dot(stencil[k * points : (k + 1) * points, :], moved.astype(BF16))
             width = chan_pad - LANES
             first = out[:, :LANES] if carry is None else out[:, :LANES] + carry
             rows_here = slice(m * points, (m + 1) * points)
@@ -119,17 +132,13 @@
     slope_out[...] = (half + 0.5 * pre * (1.0 - th * th) * (rate * (1.0 + 3 * 0.044715 * square))).astype(BF16)
     mixed = (hidden.astype(F32) + dot(act, w_reduce[...], 1, 1)).astype(BF16)
     mixed_out[...] = mixed
-    turned = dot(w_decode[...], mixed, 1, 1)
+    turned = dot(w_decode[...], mixed, 1, 1).astype(BF16)
     outs = turned.shape[0]
-    if up(outs, TILE) > outs:
-        turned = jnp.concatenate([turned, jnp.zeros((up(outs, TILE) - outs, turned.shape[1]), F32)], axis=0)
-    for q in range(share):
-        low, high = q * piece, min((q + 1) * piece, up(outs, TILE))
-        if high > low:
-            fields_out[q, : high - low, :] = turned[low:high].astype(BF16)
-        if high < (q + 1) * piece:
-            start = max(high - low, 0)
-            fields_out[q, start:, :] = jnp.zeros((piece - start, turned.shape[1]), BF16)
+    if share * piece > outs:
+        turned = jnp.concatenate([turned, jnp.zeros((share * piece - outs, turned.shape[1]), BF16)], axis=0)
+    turned_fields[...] = turned
+    for d in range(share):
+        fields_out[d][...] = turned_fields[pl.ds(pl.multiple_of(lax.rem(place[0] + d, share) * piece, TILE), piece), :]
 
 
 def crps_body(count, points, members, total, *refs):
@@ -207,42 +216,57 @@
             self.put(row, jnp.zeros((count, self.keep.shape[1]), F32))
 
 
-def backward_body(dims, scale, place, *refs):
-    share, piece, outs, chans, hidden_units, width, taps_count = dims
+def first_body(dims, scale, place, *refs):
+    share, piece, outs, hidden_units, width = dims
     grads = refs[:share]
-    (
-        w_decode, w_reduce, w_expand, slopes, hidden, gelu, mixed, spread,
-        keep, send, hidden_grad_out, hidden_turned, mixed_turned, turned_grad,
-    ) = refs[share:]
+    w_decode, gelu, mixed, keep, send, mixed_grad_out, mixed_turned, field_out, turned_grad = refs[share:]
     for d in range(share):
         turned_grad[pl.ds(pl.multiple_of(lax.rem(place[0] + d, share) * piece, TILE), piece), :] = grads[d][...]
     field_t = turned_grad[: up(outs, TILE)]
+    field_out[...] = field_t
     packed = Halves(place[1], keep, send)
     field = jnp.swapaxes(field_t.astype(F32), 0, 1).astype(BF16)[:, :outs]
     mixed_grad = dot(field, w_decode[...]).astype(BF16)
+    mixed_grad_out[...] = mixed_grad
+    mixed_grad_t = turn(mixed_grad)
+    mixed_turned[...] = mixed_grad_t
+    row = 0
+    for part in range(hidden_units // width):
+        packed.put(row, dot(mixed_grad_t[:width], gelu[:, part * width : (part + 1) * width]) * scale)
+        row += width
+    decode_grad = dot(field_t[:outs], mixed[:, :width]) * scale
+    if up(outs, TILE) > outs:
+        decode_grad = jnp.concatenate([decode_grad, jnp.zeros((up(outs, TILE) - outs, width), F32)], axis=0)
+    packed.put(row, decode_grad)
+    packed.zero_from(row + up(outs, TILE))
+
+
+def second_body(dims, scale, place, *refs):
+    outs, chans, hidden_units, width, taps_count = dims
+    (
+        mixed_grad_in, mixed_turned, field_t, w_reduce, w_expand, slopes, hidden, gelu, mixed, spread,
+        keep, send, hidden_grad_out, hidden_turned,
+    ) = refs
+    packed = Halves(place[1], keep, send)
+    mixed_grad = mixed_grad_in[...]
     gelu_grad = dot(mixed_grad, w_reduce[...])
     pre_grad = (gelu_grad * slopes[...].astype(F32)).astype(BF16)
     hidden_grad = (mixed_grad.astype(F32) + dot(pre_grad, w_expand[...], 1, 1)).astype(BF16)
     hidden_grad_out[...] = hidden_grad
     hidden_grad_t = turn(hidden_grad)
     hidden_turned[...] = hidden_grad_t
-    mixed_grad_t = turn(mixed_grad)
-    mixed_turned[...] = mixed_grad_t
     hidden_t = turn(hidden[...])
     row = 0
     for part in range(hidden_units // width):
         packed.put(row, dot(hidden_t[:width], pre_grad[:, part * width : (part + 1) * width]) * scale)
         row += width
-    decode_grad = dot(field_t[:outs], mixed[:, :width]) * scale
-    if up(outs, TILE) > outs:
-        decode_grad = jnp.concatenate([decode_grad, jnp.zeros((up(outs, TILE) - outs, width), F32)], axis=0)
-    packed.put(row, decode_grad)
-    row += up(outs, TILE)
+    packed.put(row, dot(hidden_grad_t[:width], spread[:, :width]) * scale)
+    row += width
     misc = jnp.zeros((misc_height(chans, hidden_units, outs, taps_count, width), width), F32)
     misc, at = fold_ends(hidden_t, hidden[...], pre_grad, width, 0, misc)
-    misc, at = fold_ends(mixed_grad_t, mixed_grad, gelu[...], width, at, misc)
+    misc, at = fold_ends(mixed_turned[...], mixed_grad, gelu[...], width, at, misc)
     misc, at = fold_ends(hidden_grad_t, hidden_grad, spread[:, :taps_count], width, at, misc)
-    tail = dot(turn(mixed[:, width:])[:TILE], field)
+    tail = dot(turn(mixed[:, width:])[:TILE], field_t[:outs], 1, 1)
     misc, at = fold_rows(tail[0:1], width, at, misc)
     packed.put(row, misc * scale)
     packed.zero_from(row + misc.shape[0])
@@ -252,19 +276,42 @@
     return up(2 * sum(misc_rows(hidden_units, width)) + sum(misc_rows(taps_count, width)) + 1, TILE)
 
 
-def product_body(scale, width, blocks, place, *refs):
-    packed = Halves(place[1], refs[-2], refs[-1])
+def third_body(scale, width, place, left, right, keep, send):
+    packed = Halves(place[1], keep, send)
     row = 0
-    for left, right, part in blocks:
-        packed.put(row, dot(refs[left][:width, :], refs[right][:, part * width : (part + 1) * width]) * scale)
+    while row < keep.shape[0] * 2 // width * width:
+        at = row + width
+        packed.put(row, dot(left[:width, :], right[:, at : at + width]) * scale)
         row += width
     packed.zero_from(row)
+
+
+def combine_body(index, place, kept, got, send, keep):
+    count = keep.shape[0]
+    for target, side in ((send, 1 - place[index]), (keep, place[index])):
+        rows = pl.ds(pl.multiple_of(side * count, TILE), count)
+        target[...] = add_rounded(kept[rows, :], got[rows, :])
+
+
+class Joined:
+    def __init__(self, bit, kept, got):
+        self.bit, self.halves = bit, (kept, got)
+        self.half = kept.shape[0]
+
+    def parts(self, row, count):
+        for side in (0, 1):
+            low, high = max(row, side * self.half), min(row + count, (side + 1) * self.half)
+            if low < high:
+                kept, got = (ref[low - side * self.half : high - side * self.half, :] for ref in self.halves)
+                yield low - row, jnp.where(self.bit == side, kept, got)
 
 
 def put_matrix(out, block_of, misc, at, width):
     count = out.shape[1]
     for part in range(count // width):
-        out[:width, part * width : (part + 1) * width] = block_of(part)
+        source, row = block_of(part)
+        for offset, value in source.parts(row, width):
+            out[offset : offset + value.shape[0], part * width : (part + 1) * width] = value
     wide, lanes = misc_rows(count, width)
     rest = count // width * width
     if lanes:
@@ -276,29 +323,35 @@
     return at + wide + lanes
 
 
-def finish_first_body(dims, summed, expand_out, decode_out, misc_out):
-    chans, hidden_units, outs, taps_count, width = dims
-    base = hidden_units // width * width
-    height = misc_out.shape[0]
-    misc_out[...] = summed[base + up(outs, TILE) : base + up(outs, TILE) + height, :]
-    misc = misc_out[...].astype(F32)
-    put_matrix(expand_out, lambda part: summed[part * width : (part + 1) * width, :], misc, 0, width)
-    decode_out[:, :width] = summed[base : base + outs, :]
-    at = 2 * sum(misc_rows(hidden_units, width)) + sum(misc_rows(taps_count, width))
+def finish_second_body(dims, place, kept, got, expand_out, misc_out):
+    hidden_units, width = dims
+    source = Joined(place[1], kept, got)
+    for offset, value in source.parts((hidden_units // width + 1) * width, misc_out.shape[0]):
+        misc_out[offset : offset + value.shape[0], :] = value
+    put_matrix(expand_out, lambda part: (source, part * width), misc_out[...].astype(F32), 0, width)
+
+
+def finish_first_body(dims, place, kept, got, misc_ref, reduce_out, decode_out):
+    hidden_units, outs, taps_count, width = dims
+    source = Joined(place[1], kept, got)
+    misc = misc_ref[...].astype(F32)
+    at = sum(misc_rows(hidden_units, width))
+    at = put_matrix(reduce_out, lambda part: (source, part * width), misc, at, width)
+    at += sum(misc_rows(taps_count, width))
+    for offset, value in source.parts(hidden_units // width * width, outs):
+        decode_out[offset : offset + value.shape[0], :width] = value
     turned = jnp.swapaxes(misc[at : at + 8], 0, 1)
     decode_out[:, width:] = turned[:outs, : decode_out.shape[1] - width].astype(BF16)
 
 
-def finish_rest_body(dims, second, third, misc_ref, reduce_out, disco_out):
-    hidden_units, taps_count, width = dims
-    misc = misc_ref[...].astype(F32)
-    at = sum(misc_rows(hidden_units, width))
-    blocks = hidden_units // width
-    at = put_matrix(reduce_out, lambda part: second[part * width : (part + 1) * width, :], misc, at, width)
+def finish_third_body(dims, place, kept_second, got_second, kept, got, misc_ref, disco_out):
+    hidden_units, width = dims
+    second, third = Joined(place[1], kept_second, got_second), Joined(place[1], kept, got)
+    first = hidden_units // width * width
     put_matrix(
         disco_out,
-        lambda part: second[blocks * width : (blocks + 1) * width, :] if part == 0 else third[(part - 1) * width : part * width, :],
-        misc, at, width,
+        lambda part: (third, (part - 1) * width) if part else (second, first),
+        misc_ref[...].astype(F32), 2 * sum(misc_rows(hidden_units, width)), width,
     )
 
 
@@ -343,11 +396,6 @@
     return lax.ppermute(x, ("member", "lon"), perm)
 
 
-def my_bit(pair):
-    bits = [lax.axis_index(axis) // bit % 2 for axis, bit in pair]
-    return jnp.where(lax.axis_index("lon") % 2 == 0, bits[0], bits[1])
-
-
 def add_rounded(a, b):
     return (a.astype(F32) + b.astype(F32)).astype(BF16)
 
@@ -356,19 +404,23 @@
     core, *lon = bits_of("lon")
     mem = bits_of("member")
     orders = [mem[:1] + lon + mem[1:], lon + mem, lon[1:] + mem[:1] + lon[:1] + mem[1:]]
-    return [[(d, d) for d in [core] + order] for order in orders]
+    return [[core] + order for order in orders]
 
 
 def row_unit():
     return 8 * 2 ** (len(streams()[0]) - 1)
 
 
+def all_dims():
+    return bits_of("lon") + bits_of("member")
+
+
 class Stream:
-    def __init__(self, keep, send, order):
-        self.kept, self.order = keep, order
-        self.got = swap(send, order[0])
-        self.bits = [my_bit(order[0])]
-        self.steps = [self.halve] * (len(order) - 2) + [self.exchange, self.added] + [self.join] * (len(order) - 1)
+    def __init__(self, place, keep, send, order):
+        self.place, self.kept, self.order = place, keep, order
+        self.got = swap(send, (order[0], order[0]))
+        self.done = [order[0]]
+        self.steps = [self.halve] * (len(order) - 2) + [self.exchange, self.added] + [self.join] * (len(order) - 2)
 
     def advance(self, last=None):
         if last is not None and last is not self:
@@ -377,31 +429,36 @@
         return self
 
     def halve(self):
-        pair = self.order[len(self.bits)]
-        count, bit = self.kept.shape[0] // 2, my_bit(pair)
-        parts = [
-            add_rounded(*(lax.dynamic_slice_in_dim(x, which * count, count, axis=0) for x in (self.kept, self.got)))
-            for which in (1 - bit, bit)
-        ]
-        self.got, self.kept = swap(parts[0], pair), parts[1]
-        self.bits.append(bit)
+        dim = self.order[len(self.done)]
+        count, index = self.kept.shape[0] // 2, 1 + all_dims().index(dim)
+        if count % TILE == 0 and len(self.done) < 3:
+            shape = ((count, self.kept.shape[1]), BF16)
+            args = [self.place, self.kept, self.got]
+            send, keep = vmem_call(functools.partial(combine_body, index), [shape] * 2, args, smem=1, name="combine")
+        else:
+            bit = self.place[index]
+            send, keep = (
+                add_rounded(*(lax.dynamic_slice_in_dim(x, side * count, count, axis=0) for x in (self.kept, self.got)))
+                for side in (1 - bit, bit)
+            )
+        self.got, self.kept = swap(send, (dim, dim)), keep
+        self.done.append(dim)
 
     def exchange(self):
         self.kept = add_rounded(self.kept, self.got)
-        self.got = swap(self.kept, self.order[-1])
+        self.got = swap(self.kept, (self.order[-1],) * 2)
 
     def added(self):
         self.kept = add_rounded(self.kept, self.got)
         self.send_back()
 
     def join(self):
-        low = self.bits.pop() == 0
+        low = self.place[1 + all_dims().index(self.done.pop())] == 0
         self.kept = jnp.concatenate([jnp.where(low, self.kept, self.got), jnp.where(low, self.got, self.kept)], axis=0)
         self.send_back()
 
     def send_back(self):
-        if self.bits:
-            self.got = swap(self.kept, self.order[len(self.bits) - 1])
+        self.got = swap(self.kept, (self.done[-1],) * 2)
 
 
 def shifted(x, axis, by):
@@ -431,84 +488,96 @@
     full = bases * width + LANES
     piece = TILE * -(-up(outs, TILE) // (TILE * share))
     me = lax.axis_index("member")
+    place = jnp.stack([me] + [lax.axis_index(axis) // bit % 2 for axis, bit in all_dims()]).astype(jnp.int32)
+    (row_bands,) = vmem_call(
+        begin_body, [(row_bands.shape, row_bands.dtype)], [row_bands], name="begin", moved=BEGIN * 2**20
+    )
+    row_bands, latent = lax.optimization_barrier((row_bands, latent))
     by_lon = jnp.swapaxes(latent, 1, 2)
     left = jnp.swapaxes(shifted(by_lon[:, lons - reach :], "lon", 1), 1, 2)
     right = jnp.swapaxes(shifted(by_lon[:, :reach], "lon", -1), 1, 2)
     disco_t, reduce_t, decode_t = w_disco.T, w_reduce.T, w_decode.T
     dims = (members, rows, lons, chans, lon_pad, slot, bases, piece, share)
-    stencil, spread, hidden, gelu, slopes, mixed, fields = vmem_call(
+    stencil, offsets = vmem_call(
+        functools.partial(prepare_body, dims),
+        [((bases * points, rows * slot), BF16), ((TILE, chans), F32)],
+        [member_seeds, row_bands, disco_basis.astype(F32).reshape(-1), member_table],
+        smem=3,
+        name="prepare",
+        moved=4 * 2**20,
+    )
+    weights = [disco_t, w_expand, reduce_t, decode_t]
+    spread, hidden, gelu, slopes, mixed, *here = vmem_call(
         functools.partial(forward_body, dims),
         [
-            ((bases * points, rows * slot), BF16),
             ((flat, full), BF16),
             ((flat, chans), BF16),
             ((flat, hidden_units), BF16),
             ((flat, hidden_units), BF16),
             ((flat, chans), BF16),
-            ((share, piece, flat), BF16),
+        ]
+        + [((piece, flat), BF16)] * share,
+        [place, latent, left, right, stencil, offsets] + weights,
+        smem=1,
+        scratch=[
+            pltpu.VMEM((members, rows * slot, up(chans, LANES)), F32),
+            pltpu.VMEM((share * piece, flat), BF16),
         ],
-        [
-            member_seeds, row_bands, disco_basis.astype(F32).reshape(-1),
-            latent, left, right, member_table, disco_t, w_expand, reduce_t, decode_t,
-        ],
-        smem=3,
-        scratch=[pltpu.VMEM((members, rows * slot, up(chans, LANES)), F32)],
         name="forward",
-    )
+        moved=24 * 2**20,
+    )
+    here_out = here
     observed = jnp.pad(target, ((0, 0), (0, lon_pad - lons), (0, share * piece - outs))).reshape(points, share * piece).T
     observed = jnp.concatenate([observed] * members, axis=1)
     observed = lax.dynamic_slice_in_dim(observed, me * piece, piece, axis=0)
-    here = spread_out(lambda d: lax.dynamic_index_in_dim(fields, (me + d) % share, 0, keepdims=False), "member")
+    here = spread_out(lambda d: here_out[d], "member")
     grads = vmem_call(
         functools.partial(crps_body, share, points, members, total_members),
         [((piece, flat), BF16)] * share,
         here + [observed],
         name="crps",
+        moved=3 * 2**20,
     )
     back = spread_out(lambda d: grads[d], "member")
     scale = 1.0 / math.sqrt(total_members * rows * lons * lax.axis_size("lon"))
     unit = row_unit()
     taps_count = bases * chans
-    height = hidden_units // width * width + up(outs, TILE) + misc_height(chans, hidden_units, outs, taps_count, width)
-    place = jnp.stack([me, lax.axis_index("lon") % 2]).astype(jnp.int32)
     orders = streams()
 
     def halves(rows):
         return [((up(rows, unit) // 2, width), BF16)] * 2
 
-    keep, send, hidden_grad, hidden_turned, mixed_turned = vmem_call(
-        functools.partial(backward_body, (share, piece, outs, chans, hidden_units, width, taps_count), scale),
-        halves(height) + [
-            ((flat, chans), BF16),
-            ((up(chans, TILE), flat), BF16),
-            ((up(chans, TILE), flat), BF16),
-        ],
-        [place] + back + [decode_t, reduce_t, w_expand, slopes, hidden, gelu, mixed, spread],
+    turned_shape = ((up(chans, TILE), flat), BF16)
+    blocks = hidden_units // width
+    keep, send, mixed_grad, mixed_turned, field_turned = vmem_call(
+        functools.partial(first_body, (share, piece, outs, hidden_units, width), scale),
+        halves(blocks * width + up(outs, TILE)) + [((flat, chans), BF16), turned_shape, ((up(outs, TILE), flat), BF16)],
+        [place] + back + [decode_t, gelu, mixed],
         smem=1,
         scratch=[pltpu.VMEM((share * piece, flat), BF16)],
-        name="backward",
-    )
-    first = Stream(keep, send, orders[0])
-    blocks = hidden_units // width
-    keep, send = vmem_call(
-        functools.partial(product_body, scale, width, [(0, 1, p) for p in range(blocks)] + [(2, 3, 0)]),
-        halves((blocks + 1) * width),
-        [place, mixed_turned, gelu, hidden_turned, spread],
+        name="first_products",
+        moved=9 * 2**20,
+    )
+    first = Stream(place, keep, send, orders[0])
+    misc_shape = ((misc_height(chans, hidden_units, outs, taps_count, width), width), BF16)
+    keep, send, hidden_grad, hidden_turned = vmem_call(
+        functools.partial(second_body, (outs, chans, hidden_units, width, taps_count), scale),
+        halves((blocks + 1) * width + misc_shape[0][0]) + [((flat, chans), BF16), turned_shape],
+        [place, mixed_grad, mixed_turned, field_turned, reduce_t, w_expand, slopes, hidden, gelu, mixed, spread],
         smem=1,
         name="second_products",
     )
-    second = Stream(keep, send, orders[1])
+    second = Stream(place, keep, send, orders[1])
     first.advance()
     hidden_turned, first.kept = lax.optimization_barrier((hidden_turned, first.kept))
-    wide_blocks = taps_count // width
     keep, send = vmem_call(
-        functools.partial(product_body, scale, width, [(0, 1, p) for p in range(1, wide_blocks)]),
-        halves((wide_blocks - 1) * width),
+        functools.partial(third_body, scale, width),
+        halves((taps_count // width - 1) * width),
         [place, hidden_turned, spread],
         smem=1,
         name="third_products",
     )
-    third = Stream(keep, send, orders[2])
+    third = Stream(place, keep, send, orders[2])
     second.advance()
     last = third.advance(second)
     hidden_grad, third.kept = lax.optimization_barrier((hidden_grad, third.kept))
@@ -522,27 +591,9 @@
     first.got, latent_grad = lax.optimization_barrier((first.got, latent_grad))
     from_right = shifted(to_left, "lon", -1)
     from_left = shifted(to_right, "lon", 1)
-    while third.steps:
-        for stream in (first, second, third):
-            if stream.steps:
-                last = stream.advance(last)
-    first, second, third = first.kept, second.kept, third.kept
-    grad_expand, decode_grad_t, misc = vmem_call(
-        functools.partial(finish_first_body, (chans, hidden_units, outs, taps_count, width)),
-        [
-            (w_expand.shape, BF16),
-            (decode_t.shape, BF16),
-            ((misc_height(chans, hidden_units, outs, taps_count, width), width), BF16),
-        ],
-        [first],
-        name="finish_first",
-    )
-    reduce_grad_t, disco_grad_t = vmem_call(
-        functools.partial(finish_rest_body, (hidden_units, taps_count, width)),
-        [(reduce_t.shape, BF16), (disco_t.shape, BF16)],
-        [second, third, misc],
-        name="finish_rest",
-    )
+    for stream in (first, second, third) * 4:
+        last = stream.advance(last)
+    first.got, from_right, from_left = lax.optimization_barrier((first.got, from_right, from_left))
     edge = [(0, 0, 0)] * 2
     latent_grad = (
         latent_grad
@@ -550,7 +601,36 @@
         + lax.pad(from_left, jnp.float32(0), edge + [(0, lons - reach, 0), (0, 0, 0)])
     ).astype(BF16)
 
-    return latent_grad, disco_grad_t.T, grad_expand, reduce_grad_t.T, decode_grad_t.T
+    latent_grad = jnp.swapaxes(latent_grad, 1, 2)
+    for stream in (first, second, third):
+        last = stream.advance(last)
+    first.got, latent_grad = lax.optimization_barrier((first.got, latent_grad))
+    while third.steps:
+        for stream in (first, second, third):
+            if stream.steps:
+                last = stream.advance(last)
+    grad_expand, misc = vmem_call(
+        functools.partial(finish_second_body, (hidden_units, width)),
+        [(w_expand.shape, BF16), misc_shape],
+        [place, second.kept, second.got],
+        smem=1,
+        name="finish_second",
+    )
+    reduce_grad_t, decode_grad_t = vmem_call(
+        functools.partial(finish_first_body, (hidden_units, outs, taps_count, width)),
+        [(reduce_t.shape, BF16), (decode_t.shape, BF16)],
+        [place, first.kept, first.got, misc],
+        smem=1,
+        name="finish_first",
+    )
+    (disco_grad_t,) = vmem_call(
+        functools.partial(finish_third_body, (hidden_units, width)),
+        [(disco_t.shape, BF16)],
+        [place, second.kept, second.got, third.kept, third.got, misc],
+        smem=1,
+        name="finish_third",
+    )
+    return jnp.swapaxes(latent_grad, 1, 2), disco_grad_t.T, grad_expand, reduce_grad_t.T, decode_grad_t.T
 
 
 def solution(mesh):

time: 168 us -> 147 us (0.88)
  other arithmetic: 19.2 us -> 3.92 us
  Pallas kernels: 51.4 us -> 37.3 us
  waiting for transfers between devices: 54.1 us -> 61.6 us
    pallas_call x8 -> x17, Pallas kernels: 51.4 us -> 37.3 us  [vmem_call(): pl.pallas_call(body, out_shape=[jax.ShapeDtypeStruct(shape, dtype) for sh...]
    convert_element_type x15 -> x9, other arithmetic: 11.1 us -> 2.47 us  [add_rounded(): return (a.astype(F32) + b.astype(F32)).astype(BF16)]
    ppermute x27, waiting for transfers between devices: 43.8 us -> 52.3 us  [swap(): return lax.ppermute(x, ('member', 'lon'), perm)]
    concatenate x12 -> x9, other arithmetic: 5.36 us -> 0.57 us  [join(): jnp.concatenate([jnp.where(low, self.kept, self.got), jnp.where(low, self...]
    unnamed x39 -> x30, local copies, waits for them, and re-layouts: 5.78 us -> 5.29 us
  transfers between devices with their start and end apart: 37 -> 37, of which waited for: 22 -> 22; matrix products, arithmetic and copies ran while one was open for 12% -> 4% of each run, Pallas kernels for 13% -> 16%
where the time goes in v3:
time: 147 us
  waiting for transfers between devices  61.6 us (42%)
  Pallas kernels  37.3 us (25%)
  starting transfers between devices  34 us (23%)
  local copies, waits for them, and re-layouts  8.57 us (6%)
  other arithmetic  3.92 us (3%)
    ppermute x27, waiting for transfers between devices, swap(): return lax.ppermute(x, ('member', 'lon'), perm)  52.3 us
    pallas_call x17, Pallas kernels, vmem_call(): pl.pallas_call(body, out_shape=[jax.ShapeDtypeStruct(shape, dtype) for sh...  37.3 us
    ppermute x27, starting transfers between devices, swap(): return lax.ppermute(x, ('member', 'lon'), perm)  21.1 us
    ppermute x10, starting transfers between devices, shifted(): return lax.ppermute(x, axis, [(i, (i + by) % size) for i in range(size)])  13 us
    ppermute x10, waiting for transfers between devices, shifted(): return lax.ppermute(x, axis, [(i, (i + by) % size) for i in range(size)])  9.32 us
    unnamed x30, local copies, waits for them, and re-layouts  5.29 us
  transfers between devices with their start and end apart: 37, of which 22 were waited for; matrix products, arithmetic and copies ran while one was open for 4% of the time, Pallas kernels for 16%

profile of v3, /device:TPU:0, one launch (start us, length us, event | category | flops | bytes accessed | tf_op | source)
XLA Modules:
  0.0 146.6 jit_solution(6557695199973378735)
XLA Ops:
  0.6 0.6 copy-done.10
  1.3 1.2 copy.27.latent
  2.5 0.7 fusion.2
  3.7 2.9 %collective-permute-start.1 = (bf16[2,3,4,641]{3,1,2,0:T(4,128)(2,1)}, bf16[2,3,4,641]{3,1,2,0:T(4,128)(2,1)S(1)}, u32[]{:S(2)}, u32[]{:S(2)}) collective-permute-start(bf16[2,3,4,641]{3,1,2,0:T(4,128)(2,1)} %get-tuple-element.233), channel_id=1, source_target_pairs={{0,7},{1,0},{2,1},{3,2},{4,3},{5,4},{6,5},{7,6},{8,15},{9,8},{10,9... | collective-permute-start | bytes 92312 | tf_op jit(solution)/shard_map/ppermute | solution.py:466
  7.1 0.8 copy.23
  7.9 1.6 %prepare.1 = (bf16[768,256]{1,0:T(8,128)(2,1)S(1)}, f32[16,641]{1,0:T(8,128)S(1)}) custom-call(s32[2]{0:T(128)S(1)} %copy-done.7, s32[4]{0:T(128)S(1)} %begin.1.bands, f32[3136]{0:T(1024)S(1)} %reshape.22.basis, bf16[64,641]{1,0:T(8,128)(2,1)S(1)} %copy-done.6), custom_call_target="tpu_custom_call" | custom-call | bytes 4194304 | tf_op jit(solution)/shard_map/prepare/pallas_call | solution.py:37
  9.7 2.0 %copy-done = bf16[2564,641]{0,1:T(8,128)(2,1)S(1)} copy-done((bf16[2564,641]{0,1:T(8,128)(2,1)S(1)}, bf16[2564,641]{0,1:T(8,128)(2,1)}, u32[]{:S(2)}) %copy-start) | copy-done | bytes 3287072
  11.7 1.5 %copy-done.3 = bf16[1282,641]{0,1:T(8,128)(2,1)S(1)} copy-done((bf16[1282,641]{0,1:T(8,128)(2,1)S(1)}, bf16[1282,641]{0,1:T(8,128)(2,1)}, u32[]{:S(2)}) %copy-start.3) | copy-done | bytes 1643548
  13.2 6.9 %forward.1 = (bf16[384,2688]{1,0:T(8,128)(2,1)S(1)}, bf16[384,641]{1,0:T(8,128)(2,1)S(1)}, bf16[384,1282]{1,0:T(8,128)(2,1)S(1)}, bf16[384,1282]{1,0:T(8,128)(2,...) custom-call(s32[6]{0:T(128)S(1)} %stack.27.place, ...), custom_call_target="tpu_custom_call" | custom-call | bytes 25165824 | tf_op jit(solution)/shard_map/forward/pallas_call | solution.py:37
  20.1 4.4 %collective-permute-start.2 = (bf16[80,384]{1,0:T(8,128)(2,1)S(1)}, bf16[80,384]{1,0:T(8,128)(2,1)S(1)}, u32[]{:S(2)}, u32[]{:S(2)}) collective-permute-start(bf16[80,384]{1,0:T(8,128)(2,1)S(1)} %get-tuple-element.112), channel_id=1, source_target_pairs={{0,24},{8,0},{16,8},{24,16},{1,25},{9,1},{17,9},{25,17},{2,26},{10... | collective-permute-start | bytes 184328 | tf_op jit(solution)/shard_map/ppermute | solution.py:466
  24.5 1.0 collective-permute-start.4
  25.6 1.2 collective-permute-done.2.refs_1_
  26.8 3.0 %collective-permute-done.3.refs_2_ = bf16[80,384]{1,0:T(8,128)(2,1)S(1)} collective-permute-done((bf16[80,384]{1,0:T(8,128)(2,1)S(1)}, bf16[80,384]{1,0:T(8,128)(2,1)S(1)}, u32[]{:S(2)}, u32[]{:S(2)}) %collective-permute-start.3) | collective-permute-done | bytes 61472 | tf_op jit(solution)/shard_map/ppermute | solution.py:466
  29.8 0.7 collective-permute-done.4.refs_3_
  30.5 0.9 crps.1
  31.4 1.7 %collective-permute-start.5 = (bf16[80,384]{1,0:T(8,128)(2,1)S(1)}, bf16[80,384]{1,0:T(8,128)(2,1)S(1)}, u32[]{:S(2)}, u32[]{:S(2)}) collective-permute-start(bf16[80,384]{1,0:T(8,128)(2,1)S(1)} %get-tuple-element.116), channel_id=1, source_target_pairs={{0,24},{8,0},{16,8},{24,16},{1,25},{9,1},{17,9},{25,17},{2,26},{10... | collective-permute-start | bytes 184328 | tf_op jit(solution)/shard_map/ppermute | solution.py:466
  33.2 1.9 %collective-permute-start.7 = (bf16[80,384]{1,0:T(8,128)(2,1)S(1)}, bf16[80,384]{1,0:T(8,128)(2,1)S(1)}, u32[]{:S(2)}, u32[]{:S(2)}) collective-permute-start(bf16[80,384]{1,0:T(8,128)(2,1)S(1)} %get-tuple-element.118), channel_id=1, source_target_pairs={{0,8},{8,16},{16,24},{24,0},{1,9},{9,17},{17,25},{25,1},{2,10},{10... | collective-permute-start | bytes 184328 | tf_op jit(solution)/shard_map/ppermute | solution.py:466
  35.1 0.6 collective-permute-done.5.refs_1_
  35.7 3.8 %collective-permute-done.6.refs_2_ = bf16[80,384]{1,0:T(8,128)(2,1)S(1)} collective-permute-done((bf16[80,384]{1,0:T(8,128)(2,1)S(1)}, bf16[80,384]{1,0:T(8,128)(2,1)S(1)}, u32[]{:S(2)}, u32[]{:S(2)}) %collective-permute-start.6) | collective-permute-done | bytes 61472 | tf_op jit(solution)/shard_map/ppermute | solution.py:466
  39.5 3.4 %first_products.1 = (bf16[832,640]{1,0:T(8,128)(2,1)S(1)}, bf16[832,640]{1,0:T(8,128)(2,1)S(1)}, bf16[384,641]{1,0:T(8,128)(2,1)S(1)}, bf16[656,384]{1,0:T(8,128)(2,1)S(1)}, bf16[288,384]{1,0:T(8,128)(2,1)S(1)}) custom-call(s32[6]{0:T(128)S(1)} %stack.27.place, bf16[80,384]{1,0:T(8,128)(2,1)S(1)} %get-tuple-element.115.refs_0_, ...), custom_call_target="tpu_custom_call" | custom-call | bytes 9437184 | tf_op jit(solution)/shard_map/first_products/pallas_call | solution.py:37
  43.0 5.9 %second_products.1 = (bf16[1024,640]{1,0:T(8,128)(2,1)S(1)}, bf16[1024,640]{1,0:T(8,128)(2,1)S(1)}, bf16[384,641]{1,0:T(8,128)(2,1)S(1)}, bf16[656,384]{1,0:T(8,128)(2,1)S(1)}) custom-call(s32[6]{0:T(128)S(1)} %stack.27.place, bf16[384,641]{1,0:T(8,128)(2,1)S(1)} %get-tuple-element.124.refs_0_, bf16[656,384]{1,0:T(8,128)(2,1)S(1)} %get-tuple-element.125.refs_1_, ...), custom_call_target="tpu_custom_call" | custom-call | tf_op jit(solution)/shard_map/second_products/pallas_call | solution.py:37
  49.4 0.8 combine.6
  50.2 2.9 %third_products.1 = (bf16[960,640]{1,0:T(8,128)(2,1)S(1)}, bf16[960,640]{1,0:T(8,128)(2,1)S(1)}) custom-call(s32[6]{0:T(128)S(1)} %stack.27.place, bf16[656,384]{1,0:T(8,128)(2,1)S(1)} %get-tuple-element.133.left, bf16[384,2688]{1,0:T(8,128)(2,1)S(1)} %get-tuple-element.129.refs_9_.right), custom_call_target="tpu_custom_call" | custom-call | tf_op jit(solution)/shard_map/third_products/pallas_call | solution.py:37
  53.2 0.9 combine.7
  54.1 2.6 %collective-permute-start.13 = (bf16[512,640]{1,0:T(8,128)(2,1)S(1)}, bf16[512,640]{1,0:T(8,128)(2,1)S(1)}, u32[]{:S(2)}, u32[]{:S(2)}) collective-permute-start(bf16[512,640]{1,0:T(8,128)(2,1)S(1)} %get-tuple-element.148), channel_id=1, source_target_pairs={{0,2},{1,3},{2,0},{3,1},{4,6},{5,7},{6,4},{7,5},{8,10},{9,11},{10,... | collective-permute-start | bytes 1966088 | tf_op jit(solution)/shard_map/ppermute | solution.py:396
  56.7 0.8 combine.8
  57.6 1.0 collective-permute-start.12
  58.6 3.3 %collect.1 = (f32[2,4,45,641]{3,2,1,0:T(8,128)S(1)}, f32[2,4,3,641]{3,2,1,0:T(4,128)S(1)}, f32[2,4,3,641]{3,2,1,0:T(4,128)S(1)}) custom-call(bf16[384,641]{1,0:T(8,128)(2,1)S(1)} %get-tuple-element.141.hidden_grad, bf16[641,2564]{1,0:T(8,128)(2,1)S(1)} %bitcast.23, bf16[768,256]{1,0:T(8,128)(2,1)S(1)} %get-tuple-element.109.stencil), custom_call_target="tpu_custom_call" | custom-call | tf_op jit(solution)/shard_map/collect/pallas_call | solution.py:37
  61.9 9.0 %collective-permute-done.9.got = bf16[416,640]{1,0:T(8,128)(2,1)S(1)} collective-permute-done((bf16[416,640]{1,0:T(8,128)(2,1)S(1)}, bf16[416,640]{1,0:T(8,128)(2,1)S(1)}, u32[]{:S(2)}, u32[]{:S(2)}) %collective-permute-start.9) | collective-permute-done | bytes 532512 | tf_op jit(solution)/shard_map/ppermute | solution.py:396
  70.9 0.7 combine.9
  72.1 1.4 combine.10
  73.5 0.7 collective-permute-start.15
  74.2 0.7 combine.11
  74.9 1.2 collective-permute-start.14
  76.7 2.8 %collective-permute-done.16 = bf16[208,640]{1,0:T(8,128)(2,1)} collective-permute-done((bf16[208,640]{1,0:T(8,128)(2,1)S(1)}, bf16[208,640]{1,0:T(8,128)(2,1)}, u32[]{:S(2)}, u32[]{:S(2)}) %collective-permute-start.16) | collective-permute-done | bytes 266272 | tf_op jit(solution)/shard_map/ppermute | solution.py:396
  79.5 1.0 add_convert_fusion.12
  80.5 3.8 %collective-permute-done.15 = bf16[256,640]{1,0:T(8,128)(2,1)} collective-permute-done((bf16[256,640]{1,0:T(8,128)(2,1)}, bf16[256,640]{1,0:T(8,128)(2,1)}, u32[]{:S(2)}, u32[]{:S(2)}) %collective-permute-start.15) | collective-permute-done | bytes 327712 | tf_op jit(solution)/shard_map/ppermute | solution.py:396
  84.9 1.1 add_convert_fusion.3
  86.1 3.2 %collective-permute-done.18 = bf16[104,640]{1,0:T(8,128)(2,1)S(1)} collective-permute-done((bf16[104,640]{1,0:T(8,128)(2,1)S(1)}, bf16[104,640]{1,0:T(8,128)(2,1)S(1)}, u32[]{:S(2)}, u32[]{:S(2)}) %collective-permute-start.18) | collective-permute-done | bytes 133152 | tf_op jit(solution)/shard_map/ppermute | solution.py:396
  89.4 1.7 %collective-permute-start.20 = (bf16[104,640]{1,0:T(8,128)(2,1)S(1)}, bf16[104,640]{1,0:T(8,128)(2,1)S(1)}, u32[]{:S(2)}, u32[]{:S(2)}) collective-permute-start(bf16[104,640]{1,0:T(8,128)(2,1)S(1)} %add_convert_fusion.10), channel_id=1, source_target_pairs={{0,16},{1,17},{2,18},{3,19},{4,20},{5,21},{6,22},{7,23},{8,24},{9,... | collective-permute-start | bytes 399368 | tf_op jit(solution)/shard_map/ppermute | solution.py:396
  91.1 0.7 collective-permute-done.17
  91.8 1.6 %collective-permute-start.21 = (bf16[120,640]{1,0:T(8,128)(2,1)S(1)}, bf16[120,640]{1,0:T(8,128)(2,1)S(1)}, u32[]{:S(2)}, u32[]{:S(2)}) collective-permute-start(bf16[120,640]{1,0:T(8,128)(2,1)S(1)} %get-tuple-element.231), channel_id=1, source_target_pairs={{0,2},{1,3},{2,0},{3,1},{4,6},{5,7},{6,4},{7,5},{8,10},{9,11},{10,... | collective-permute-start | bytes 460808 | tf_op jit(solution)/shard_map/ppermute | solution.py:396
  93.5 2.5 %collective-permute-start.19 = (bf16[128,640]{1,0:T(8,128)(2,1)S(1)}, bf16[128,640]{1,0:T(8,128)(2,1)S(1)}, u32[]{:S(2)}, u32[]{:S(2)}) collective-permute-start(bf16[128,640]{1,0:T(8,128)(2,1)S(1)} %add_convert_fusion.2), channel_id=1, source_target_pairs={{0,16},{1,17},{2,18},{3,19},{4,20},{5,21},{6,22},{7,23},{8,24},{9,... | collective-permute-start | bytes 491528 | tf_op jit(solution)/shard_map/ppermute | solution.py:396
  96.0 1.1 collective-permute-done.21
  97.1 2.0 %collective-permute-start.25 = (bf16[120,640]{1,0:T(8,128)(2,1)S(1)}, bf16[120,640]{1,0:T(8,128)(2,1)S(1)}, u32[]{:S(2)}, u32[]{:S(2)}) collective-permute-start(bf16[120,640]{1,0:T(8,128)(2,1)S(1)} %add_convert_fusion.6), channel_id=1, source_target_pairs={{0,16},{1,17},{2,18},{3,19},{4,20},{5,21},{6,22},{7,23},{8,24},{9,... | collective-permute-start | bytes 460808 | tf_op jit(solution)/shard_map/ppermute | solution.py:396
  99.2 5.2 %collective-permute-done.20 = bf16[104,640]{1,0:T(8,128)(2,1)S(1)} collective-permute-done((bf16[104,640]{1,0:T(8,128)(2,1)S(1)}, bf16[104,640]{1,0:T(8,128)(2,1)S(1)}, u32[]{:S(2)}, u32[]{:S(2)}) %collective-permute-start.20) | collective-permute-done | bytes 133152 | tf_op jit(solution)/shard_map/ppermute | solution.py:396
  104.4 0.6 collective-permute-start.22
  105.1 2.8 %collective-permute-done.19 = bf16[128,640]{1,0:T(8,128)(2,1)S(1)} collective-permute-done((bf16[128,640]{1,0:T(8,128)(2,1)S(1)}, bf16[128,640]{1,0:T(8,128)(2,1)S(1)}, u32[]{:S(2)}, u32[]{:S(2)}) %collective-permute-start.19) | collective-permute-done | bytes 163872 | tf_op jit(solution)/shard_map/ppermute | solution.py:396
  108.0 1.4 collective-permute-done.22
  109.9 1.4 collective-permute-start.27
  111.4 0.8 collective-permute-start.26
  112.1 1.2 collective-permute-done.28
  113.4 1.1 collective-permute-start.30
  114.5 2.4 %collective-permute-done.27 = bf16[120,640]{1,0:T(8,128)(2,1)S(1)} collective-permute-done((bf16[120,640]{1,0:T(8,128)(2,1)S(1)}, bf16[120,640]{1,0:T(8,128)(2,1)S(1)}, u32[]{:S(2)}, u32[]{:S(2)}) %collective-permute-start.27) | collective-permute-done | bytes 153632 | tf_op jit(solution)/shard_map/ppermute | solution.py:396
  117.0 3.1 %collective-permute-done.26 = bf16[208,640]{1,0:T(8,128)(2,1)S(1)} collective-permute-done((bf16[208,640]{1,0:T(8,128)(2,1)S(1)}, bf16[208,640]{1,0:T(8,128)(2,1)S(1)}, u32[]{:S(2)}, u32[]{:S(2)}) %collective-permute-start.26) | collective-permute-done | bytes 266272 | tf_op jit(solution)/shard_map/ppermute | solution.py:396
  120.3 0.9 collective-permute-done.30
  121.3 1.1 collective-permute-start.32
  122.4 4.8 %collective-permute-done.29 = bf16[240,640]{1,0:T(8,128)(2,1)S(1)} collective-permute-done((bf16[240,640]{1,0:T(8,128)(2,1)S(1)}, bf16[240,640]{1,0:T(8,128)(2,1)S(1)}, u32[]{:S(2)}, u32[]{:S(2)}) %collective-permute-start.29) | collective-permute-done | bytes 307232 | tf_op jit(solution)/shard_map/ppermute | solution.py:396
  127.4 7.8 %collective-permute-done.33 = bf16[416,640]{1,0:T(8,128)(2,1)S(1)} collective-permute-done((bf16[416,640]{1,0:T(8,128)(2,1)S(1)}, bf16[416,640]{1,0:T(8,128)(2,1)S(1)}, u32[]{:S(2)}, u32[]{:S(2)}) %collective-permute-start.33) | collective-permute-done | bytes 532512 | tf_op jit(solution)/shard_map/ppermute | solution.py:396
  135.9 1.7 %collective-permute-done.31 = bf16[480,640]{1,0:T(8,128)(2,1)S(1)} collective-permute-done((bf16[480,640]{1,0:T(8,128)(2,1)S(1)}, bf16[480,640]{1,0:T(8,128)(2,1)S(1)}, u32[]{:S(2)}, u32[]{:S(2)}) %collective-permute-start.31) | collective-permute-done | bytes 614432 | tf_op jit(solution)/shard_map/ppermute | solution.py:396
  138.4 1.1 copy.24
  139.4 2.1 %finish_second.1 = (bf16[641,1282]{1,0:T(8,128)(2,1)}, bf16[32,640]{1,0:T(8,128)(2,1)S(1)}) custom-call(s32[6]{0:T(128)S(1)} %stack.27.place, bf16[1024,640]{1,0:T(8,128)(2,1)S(1)} %pad_maximum_fusion.kept.kept_second, bf16[1024,640]{1,0:T(8,128)(2,1)S(1)} %collective-permute-done.34.got.got_second), custom_call_target="tpu_custom_call" | custom-call | tf_op jit(solution)/shard_map/finish_second/pallas_call | solution.py:37
  141.5 2.8 %finish_third.1 = bf16[641,2564]{1,0:T(8,128)(2,1)} custom-call(s32[6]{0:T(128)S(1)} %stack.27.place, bf16[1024,640]{1,0:T(8,128)(2,1)S(1)} %pad_maximum_fusion.kept.kept_second, bf16[1024,640]{1,0:T(8,128)(2,1)S(1)} %collective-permute-done.34.got.got_second, bf16[960,640]{1,0:T(8,128)(2,1)S(1)} %pad_maximum_fusion.1.kept, ...), custom_call_target="tpu_custom_call" | custom-call | tf_op jit(solution)/shard_map/finish_third/pallas_call | solution.py:37
  144.4 2.2 %finish_first.1 = (bf16[641,1282]{1,0:T(8,128)(2,1)}, bf16[288,641]{1,0:T(8,128)(2,1)}) custom-call(s32[6]{0:T(128)S(1)} %stack.27.place, bf16[832,640]{1,0:T(8,128)(2,1)S(1)} %pad_maximum_fusion.2.kept, bf16[832,640]{1,0:T(8,128)(2,1)S(1)} %collective-permute-done.36.got, bf16[32,640]{1,0:T(8,128)(2,1)S(1)} %get-tuple-element.204.misc_ref), custom_call_target="tpu_custom_call" | custom-call | tf_op jit(solution)/shard_map/finish_first/pallas_call | solution.py:37
  (93 shorter events, 6.5 us)
Async XLA Ops:
  0.6 0.7 copy-start.10
  1.3 5.3 %copy-start.13 = (bf16[16,4,7,7]{0,1,3,2:T(4,128)(2,1)S(1)}, bf16[16,4,7,7]{0,1,3,2:T(4,128)(2,1)}, u32[]{:S(2)}) copy-start(bf16[16,4,7,7]{0,1,3,2:T(4,128)(2,1)} %param.14) | copy-start | bytes 18820
  1.3 5.8 %copy-start.12 = (bf16[4,45,288]{2,0,1:T(4,128)(2,1)S(1)}, bf16[4,45,288]{2,0,1:T(4,128)(2,1)}, u32[]{:S(2)}) copy-start(bf16[4,45,288]{2,0,1:T(4,128)(2,1)} %param.19) | copy-start | bytes 311044
  1.3 6.6 %copy-start.6 = (bf16[64,641]{1,0:T(8,128)(2,1)S(1)}, bf16[64,641]{1,0:T(8,128)(2,1)}, u32[]{:S(2)}) copy-start(bf16[64,641]{1,0:T(8,128)(2,1)} %table.1) | copy-start | bytes 246148
  1.3 6.6 %copy-start.7 = (s32[2]{0:T(128)S(1)}, s32[2]{0:T(128)}, u32[]{:S(2)}) copy-start(s32[2]{0:T(128)} %seeds.1) | copy-start | bytes 28
  1.3 8.4 %copy-start.5 = (bf16[641,288]{0,1:T(8,128)(2,1)S(1)}, bf16[641,288]{0,1:T(8,128)(2,1)}, u32[]{:S(2)}) copy-start(bf16[641,288]{0,1:T(8,128)(2,1)} %param.18) | copy-start | bytes 1107652
  2.5 7.2 %copy-start.2 = (bf16[641,1282]{1,0:T(8,128)(2,1)S(1)}, bf16[641,1282]{1,0:T(8,128)(2,1)}, u32[]{:S(2)}) copy-start(bf16[641,1282]{1,0:T(8,128)(2,1)} %refs_4_.1) | copy-start | bytes 4930576
  3.2 6.5 %collective-permute-start = (bf16[2,3,4,641]{3,1,2,0:T(4,128)(2,1)}, bf16[2,3,4,641]{3,1,2,0:T(4,128)(2,1)S(1)}, u32[]{:S(2)}, u32[]{:S(2)}) collective-permute-start(bf16[2,3,4,641]{3,1,2,0:T(4,128)(2,1)} %get-tuple-element.234), channel_id=1, source_target_pairs={{0,1},{1,2},{2,3},{3,4},{4,5},{5,6},{6,7},{7,0},{8,9},{9,10},{10,1... | collective-permute-start | bytes 92312 | tf_op jit(solution)/shard_map/ppermute | solution.py:466
  3.7 6.0 %collective-permute-start.1 = (bf16[2,3,4,641]{3,1,2,0:T(4,128)(2,1)}, bf16[2,3,4,641]{3,1,2,0:T(4,128)(2,1)S(1)}, u32[]{:S(2)}, u32[]{:S(2)}) collective-permute-start(bf16[2,3,4,641]{3,1,2,0:T(4,128)(2,1)} %get-tuple-element.233), channel_id=1, source_target_pairs={{0,7},{1,0},{2,1},{3,2},{4,3},{5,4},{6,5},{7,6},{8,15},{9,8},{10,9... | collective-permute-start | bytes 92312 | tf_op jit(solution)/shard_map/ppermute | solution.py:466
  9.7 2.0 %copy-start = (bf16[2564,641]{0,1:T(8,128)(2,1)S(1)}, bf16[2564,641]{0,1:T(8,128)(2,1)}, u32[]{:S(2)}) copy-start(bf16[2564,641]{0,1:T(8,128)(2,1)} %param.15) | copy-start | bytes 9861148
  11.7 1.5 %copy-start.3 = (bf16[1282,641]{0,1:T(8,128)(2,1)S(1)}, bf16[1282,641]{0,1:T(8,128)(2,1)}, u32[]{:S(2)}) copy-start(bf16[1282,641]{0,1:T(8,128)(2,1)} %param.17) | copy-start | bytes 4930576
  13.2 12.3 %copy-start.11 = (bf16[192,320]{0,1:T(8,128)(2,1)S(1)}, bf16[192,320]{0,1:T(8,128)(2,1)}, u32[]{:S(2)}) copy-start(bf16[192,320]{0,1:T(8,128)(2,1)} %copy.23) | copy-start | bytes 368644
  20.1 6.7 %collective-permute-start.2 = (bf16[80,384]{1,0:T(8,128)(2,1)S(1)}, bf16[80,384]{1,0:T(8,128)(2,1)S(1)}, u32[]{:S(2)}, u32[]{:S(2)}) collective-permute-start(bf16[80,384]{1,0:T(8,128)(2,1)S(1)} %get-tuple-element.112), channel_id=1, source_target_pairs={{0,24},{8,0},{16,8},{24,16},{1,25},{9,1},{17,9},{25,17},{2,26},{10... | collective-permute-start | bytes 184328 | tf_op jit(solution)/shard_map/ppermute | solution.py:466
  24.5 5.3 %collective-permute-start.3 = (bf16[80,384]{1,0:T(8,128)(2,1)S(1)}, bf16[80,384]{1,0:T(8,128)(2,1)S(1)}, u32[]{:S(2)}, u32[]{:S(2)}) collective-permute-start(bf16[80,384]{1,0:T(8,128)(2,1)S(1)} %get-tuple-element.113), channel_id=1, source_target_pairs={{0,16},{8,24},{16,0},{24,8},{1,17},{9,25},{17,1},{25,9},{2,18},{10... | collective-permute-start | bytes 184328 | tf_op jit(solution)/shard_map/ppermute | solution.py:466
  24.5 6.0 %collective-permute-start.4 = (bf16[80,384]{1,0:T(8,128)(2,1)S(1)}, bf16[80,384]{1,0:T(8,128)(2,1)S(1)}, u32[]{:S(2)}, u32[]{:S(2)}) collective-permute-start(bf16[80,384]{1,0:T(8,128)(2,1)S(1)} %get-tuple-element.114), channel_id=1, source_target_pairs={{0,8},{8,16},{16,24},{24,0},{1,9},{9,17},{17,25},{25,1},{2,10},{10... | collective-permute-start | bytes 184328 | tf_op jit(solution)/shard_map/ppermute | solution.py:466
  31.4 11.6 %copy-start.4 = (bf16[1282,641]{0,1:T(8,128)(2,1)S(1)}, bf16[1282,641]{0,1:T(8,128)(2,1)}, u32[]{:S(2)}) copy-start(bf16[1282,641]{0,1:T(8,128)(2,1)} %param.17) | copy-start | bytes 4930576
  31.4 4.3 %collective-permute-start.5 = (bf16[80,384]{1,0:T(8,128)(2,1)S(1)}, bf16[80,384]{1,0:T(8,128)(2,1)S(1)}, u32[]{:S(2)}, u32[]{:S(2)}) collective-permute-start(bf16[80,384]{1,0:T(8,128)(2,1)S(1)} %get-tuple-element.116), channel_id=1, source_target_pairs={{0,24},{8,0},{16,8},{24,16},{1,25},{9,1},{17,9},{25,17},{2,26},{10... | collective-permute-start | bytes 184328 | tf_op jit(solution)/shard_map/ppermute | solution.py:466
  33.2 6.3 %collective-permute-start.6 = (bf16[80,384]{1,0:T(8,128)(2,1)S(1)}, bf16[80,384]{1,0:T(8,128)(2,1)S(1)}, u32[]{:S(2)}, u32[]{:S(2)}) collective-permute-start(bf16[80,384]{1,0:T(8,128)(2,1)S(1)} %get-tuple-element.117), channel_id=1, source_target_pairs={{0,16},{8,24},{16,0},{24,8},{1,17},{9,25},{17,1},{25,9},{2,18},{10... | collective-permute-start | bytes 184328 | tf_op jit(solution)/shard_map/ppermute | solution.py:466
  33.2 6.3 %collective-permute-start.7 = (bf16[80,384]{1,0:T(8,128)(2,1)S(1)}, bf16[80,384]{1,0:T(8,128)(2,1)S(1)}, u32[]{:S(2)}, u32[]{:S(2)}) collective-permute-start(bf16[80,384]{1,0:T(8,128)(2,1)S(1)} %get-tuple-element.118), channel_id=1, source_target_pairs={{0,8},{8,16},{16,24},{24,0},{1,9},{9,17},{17,25},{25,1},{2,10},{10... | collective-permute-start | bytes 184328 | tf_op jit(solution)/shard_map/ppermute | solution.py:466
  42.9 6.5 %collective-permute-start.8 = (bf16[832,640]{1,0:T(8,128)(2,1)S(1)}, bf16[832,640]{1,0:T(8,128)(2,1)S(1)}, u32[]{:S(2)}, u32[]{:S(2)}) collective-permute-start(bf16[832,640]{1,0:T(8,128)(2,1)S(1)} %get-tuple-element.122), channel_id=1, source_target_pairs={{0,1},{1,0},{2,3},{3,2},{4,5},{5,4},{6,7},{7,6},{8,9},{9,8},{10,11... | collective-permute-start | bytes 3194888 | tf_op jit(solution)/shard_map/ppermute | solution.py:396
  48.9 4.4 %collective-permute-start.11 = (bf16[1024,640]{1,0:T(8,128)(2,1)S(1)}, bf16[1024,640]{1,0:T(8,128)(2,1)S(1)}, u32[]{:S(2)}, u32[]{:S(2)}) collective-permute-start(bf16[1024,640]{1,0:T(8,128)(2,1)S(1)} %get-tuple-element.137), channel_id=1, source_target_pairs={{0,1},{1,0},{2,3},{3,2},{4,5},{5,4},{6,7},{7,6},{8,9},{9,8},{10,11... | collective-permute-start | bytes 3932168 | tf_op jit(solution)/shard_map/ppermute | solution.py:396
  53.1 3.6 %collective-permute-start.10 = (bf16[960,640]{1,0:T(8,128)(2,1)S(1)}, bf16[960,640]{1,0:T(8,128)(2,1)S(1)}, u32[]{:S(2)}, u32[]{:S(2)}) collective-permute-start(bf16[960,640]{1,0:T(8,128)(2,1)S(1)} %get-tuple-element.135), channel_id=1, source_target_pairs={{0,1},{1,0},{2,3},{3,2},{4,5},{5,4},{6,7},{7,6},{8,9},{9,8},{10,11... | collective-permute-start | bytes 3686408 | tf_op jit(solution)/shard_map/ppermute | solution.py:396
  53.2 5.3 %copy-start.1 = (bf16[2564,641]{0,1:T(8,128)(2,1)S(1)}, bf16[2564,641]{0,1:T(8,128)(2,1)}, u32[]{:S(2)}) copy-start(bf16[2564,641]{0,1:T(8,128)(2,1)} %param.15) | copy-start | bytes 9861148
  54.1 18.0 %collective-permute-start.13 = (bf16[512,640]{1,0:T(8,128)(2,1)S(1)}, bf16[512,640]{1,0:T(8,128)(2,1)S(1)}, u32[]{:S(2)}, u32[]{:S(2)}) collective-permute-start(bf16[512,640]{1,0:T(8,128)(2,1)S(1)} %get-tuple-element.148), channel_id=1, source_target_pairs={{0,2},{1,3},{2,0},{3,1},{4,6},{5,7},{6,4},{7,5},{8,10},{9,11},{10,... | collective-permute-start | bytes 1966088 | tf_op jit(solution)/shard_map/ppermute | solution.py:396
  56.7 14.2 %collective-permute-start.9 = (bf16[416,640]{1,0:T(8,128)(2,1)S(1)}, bf16[416,640]{1,0:T(8,128)(2,1)S(1)}, u32[]{:S(2)}, u32[]{:S(2)}) collective-permute-start(bf16[416,640]{1,0:T(8,128)(2,1)S(1)} %get-tuple-element.123), channel_id=1, source_target_pairs={{0,8},{1,9},{2,10},{3,11},{4,12},{5,13},{6,14},{7,15},{8,0},{9,1},... | collective-permute-start | bytes 1597448 | tf_op jit(solution)/shard_map/ppermute | solution.py:396
  57.6 16.6 %collective-permute-start.12 = (bf16[480,640]{1,0:T(8,128)(2,1)S(1)}, bf16[480,640]{1,0:T(8,128)(2,1)S(1)}, u32[]{:S(2)}, u32[]{:S(2)}) collective-permute-start(bf16[480,640]{1,0:T(8,128)(2,1)S(1)} %get-tuple-element.146), channel_id=1, source_target_pairs={{0,4},{1,5},{2,6},{3,7},{4,0},{5,1},{6,2},{7,3},{8,12},{9,13},{10,... | collective-permute-start | bytes 1843208 | tf_op jit(solution)/shard_map/ppermute | solution.py:396
  61.9 13.0 %copy-start.8 = (f32[2,4,3,641]{3,2,1,0:T(4,128)}, f32[2,4,3,641]{3,2,1,0:T(4,128)S(1)}, u32[]{:S(2)}) copy-start(f32[2,4,3,641]{3,2,1,0:T(4,128)S(1)} %get-tuple-element.175) | copy-start | bytes 184612
  61.9 13.0 %copy-start.9 = (f32[2,4,3,641]{3,2,1,0:T(4,128)}, f32[2,4,3,641]{3,2,1,0:T(4,128)S(1)}, u32[]{:S(2)}) copy-start(f32[2,4,3,641]{3,2,1,0:T(4,128)S(1)} %get-tuple-element.174) | copy-start | bytes 184612
  71.6 7.8 %collective-permute-start.16 = (bf16[208,640]{1,0:T(8,128)(2,1)S(1)}, bf16[208,640]{1,0:T(8,128)(2,1)}, u32[]{:S(2)}, u32[]{:S(2)}) collective-permute-start(bf16[208,640]{1,0:T(8,128)(2,1)S(1)} %get-tuple-element.159), channel_id=1, source_target_pairs={{0,2},{1,3},{2,0},{3,1},{4,6},{5,7},{6,4},{7,5},{8,10},{9,11},{10,... | collective-permute-start | bytes 798728 | tf_op jit(solution)/shard_map/ppermute | solution.py:396
  73.5 10.9 %collective-permute-start.15 = (bf16[256,640]{1,0:T(8,128)(2,1)}, bf16[256,640]{1,0:T(8,128)(2,1)}, u32[]{:S(2)}, u32[]{:S(2)}) collective-permute-start(bf16[256,640]{1,0:T(8,128)(2,1)} %get-tuple-element.157), channel_id=1, source_target_pairs={{0,4},{1,5},{2,6},{3,7},{4,0},{5,1},{6,2},{7,3},{8,12},{9,13},{10,... | collective-permute-start | bytes 983048 | tf_op jit(solution)/shard_map/ppermute | solution.py:396
  74.9 11.1 %collective-permute-start.14 = (bf16[240,640]{1,0:T(8,128)(2,1)S(1)}, bf16[240,640]{1,0:T(8,128)(2,1)S(1)}, u32[]{:S(2)}, u32[]{:S(2)}) collective-permute-start(bf16[240,640]{1,0:T(8,128)(2,1)S(1)} %get-tuple-element.155), channel_id=1, source_target_pairs={{0,8},{1,9},{2,10},{3,11},{4,12},{5,13},{6,14},{7,15},{8,0},{9,1},... | collective-permute-start | bytes 921608 | tf_op jit(solution)/shard_map/ppermute | solution.py:396
  76.1 31.9 %collective-permute-start.23 = (f32[2,4,3,641]{3,2,1,0:T(4,128)}, f32[2,4,3,641]{3,2,1,0:T(4,128)S(1)}, u32[]{:S(2)}, u32[]{:S(2)}) collective-permute-start(f32[2,4,3,641]{3,2,1,0:T(4,128)} %copy-done.9), channel_id=1, source_target_pairs={{0,7},{1,0},{2,1},{3,2},{4,3},{5,4},{6,5},{7,6},{8,15},{9,8},{10,9... | collective-permute-start | bytes 184616 | tf_op jit(solution)/shard_map/ppermute | solution.py:466
  76.6 31.4 %collective-permute-start.24 = (f32[2,4,3,641]{3,2,1,0:T(4,128)}, f32[2,4,3,641]{3,2,1,0:T(4,128)S(1)}, u32[]{:S(2)}, u32[]{:S(2)}) collective-permute-start(f32[2,4,3,641]{3,2,1,0:T(4,128)} %copy-done.8), channel_id=1, source_target_pairs={{0,1},{1,2},{2,3},{3,4},{4,5},{5,6},{6,7},{7,0},{8,9},{9,10},{10,1... | collective-permute-start | bytes 184616 | tf_op jit(solution)/shard_map/ppermute | solution.py:466
  84.3 5.0 %collective-permute-start.18 = (bf16[104,640]{1,0:T(8,128)(2,1)S(1)}, bf16[104,640]{1,0:T(8,128)(2,1)S(1)}, u32[]{:S(2)}, u32[]{:S(2)}) collective-permute-start(bf16[104,640]{1,0:T(8,128)(2,1)S(1)} %get-tuple-element.240), channel_id=1, source_target_pairs={{0,4},{1,5},{2,6},{3,7},{4,0},{5,1},{6,2},{7,3},{8,12},{9,13},{10,... | collective-permute-start | bytes 399368 | tf_op jit(solution)/shard_map/ppermute | solution.py:396
  86.0 5.9 %collective-permute-start.17 = (bf16[128,640]{1,0:T(8,128)(2,1)S(1)}, bf16[128,640]{1,0:T(8,128)(2,1)S(1)}, u32[]{:S(2)}, u32[]{:S(2)}) collective-permute-start(bf16[128,640]{1,0:T(8,128)(2,1)S(1)} %get-tuple-element.227), channel_id=1, source_target_pairs={{0,8},{1,9},{2,10},{3,11},{4,12},{5,13},{6,14},{7,15},{8,0},{9,1},... | collective-permute-start | bytes 491528 | tf_op jit(solution)/shard_map/ppermute | solution.py:396
  89.4 15.0 %collective-permute-start.20 = (bf16[104,640]{1,0:T(8,128)(2,1)S(1)}, bf16[104,640]{1,0:T(8,128)(2,1)S(1)}, u32[]{:S(2)}, u32[]{:S(2)}) collective-permute-start(bf16[104,640]{1,0:T(8,128)(2,1)S(1)} %add_convert_fusion.10), channel_id=1, source_target_pairs={{0,16},{1,17},{2,18},{3,19},{4,20},{5,21},{6,22},{7,23},{8,24},{9,... | collective-permute-start | bytes 399368 | tf_op jit(solution)/shard_map/ppermute | solution.py:396
  91.8 5.2 %collective-permute-start.21 = (bf16[120,640]{1,0:T(8,128)(2,1)S(1)}, bf16[120,640]{1,0:T(8,128)(2,1)S(1)}, u32[]{:S(2)}, u32[]{:S(2)}) collective-permute-start(bf16[120,640]{1,0:T(8,128)(2,1)S(1)} %get-tuple-element.231), channel_id=1, source_target_pairs={{0,2},{1,3},{2,0},{3,1},{4,6},{5,7},{6,4},{7,5},{8,10},{9,11},{10,... | collective-permute-start | bytes 460808 | tf_op jit(solution)/shard_map/ppermute | solution.py:396
  93.5 14.4 %collective-permute-start.19 = (bf16[128,640]{1,0:T(8,128)(2,1)S(1)}, bf16[128,640]{1,0:T(8,128)(2,1)S(1)}, u32[]{:S(2)}, u32[]{:S(2)}) collective-permute-start(bf16[128,640]{1,0:T(8,128)(2,1)S(1)} %add_convert_fusion.2), channel_id=1, source_target_pairs={{0,16},{1,17},{2,18},{3,19},{4,20},{5,21},{6,22},{7,23},{8,24},{9,... | collective-permute-start | bytes 491528 | tf_op jit(solution)/shard_map/ppermute | solution.py:396
  97.1 12.8 %collective-permute-start.25 = (bf16[120,640]{1,0:T(8,128)(2,1)S(1)}, bf16[120,640]{1,0:T(8,128)(2,1)S(1)}, u32[]{:S(2)}, u32[]{:S(2)}) collective-permute-start(bf16[120,640]{1,0:T(8,128)(2,1)S(1)} %add_convert_fusion.6), channel_id=1, source_target_pairs={{0,16},{1,17},{2,18},{3,19},{4,20},{5,21},{6,22},{7,23},{8,24},{9,... | collective-permute-start | bytes 460808 | tf_op jit(solution)/shard_map/ppermute | solution.py:396
  104.4 5.1 %collective-permute-start.22 = (bf16[104,640]{1,0:T(8,128)(2,1)S(1)}, bf16[104,640]{1,0:T(8,128)(2,1)S(1)}, u32[]{:S(2)}, u32[]{:S(2)}) collective-permute-start(bf16[104,640]{1,0:T(8,128)(2,1)S(1)} %add_convert_fusion.9), channel_id=1, source_target_pairs={{0,4},{1,5},{2,6},{3,7},{4,0},{5,1},{6,2},{7,3},{8,12},{9,13},{10,... | collective-permute-start | bytes 399368 | tf_op jit(solution)/shard_map/ppermute | solution.py:396
  107.9 5.4 %collective-permute-start.28 = (bf16[128,640]{1,0:T(8,128)(2,1)S(1)}, bf16[128,640]{1,0:T(8,128)(2,1)S(1)}, u32[]{:S(2)}, u32[]{:S(2)}) collective-permute-start(bf16[128,640]{1,0:T(8,128)(2,1)S(1)} %add_convert_fusion.1), channel_id=1, source_target_pairs={{0,8},{1,9},{2,10},{3,11},{4,12},{5,13},{6,14},{7,15},{8,0},{9,1},... | collective-permute-start | bytes 491528 | tf_op jit(solution)/shard_map/ppermute | solution.py:396
  109.9 7.0 %collective-permute-start.27 = (bf16[120,640]{1,0:T(8,128)(2,1)S(1)}, bf16[120,640]{1,0:T(8,128)(2,1)S(1)}, u32[]{:S(2)}, u32[]{:S(2)}) collective-permute-start(bf16[120,640]{1,0:T(8,128)(2,1)S(1)} %add_convert_fusion.5), channel_id=1, source_target_pairs={{0,2},{1,3},{2,0},{3,1},{4,6},{5,7},{6,4},{7,5},{8,10},{9,11},{10,... | collective-permute-start | bytes 460808 | tf_op jit(solution)/shard_map/ppermute | solution.py:396
  111.4 8.8 %collective-permute-start.26 = (bf16[208,640]{1,0:T(8,128)(2,1)S(1)}, bf16[208,640]{1,0:T(8,128)(2,1)S(1)}, u32[]{:S(2)}, u32[]{:S(2)}) collective-permute-start(bf16[208,640]{1,0:T(8,128)(2,1)S(1)} %pad_maximum_fusion.8), channel_id=1, source_target_pairs={{0,2},{1,3},{2,0},{3,1},{4,6},{5,7},{6,4},{7,5},{8,10},{9,11},{10,... | collective-permute-start | bytes 798728 | tf_op jit(solution)/shard_map/ppermute | solution.py:396
  113.4 7.8 %collective-permute-start.30 = (bf16[256,640]{1,0:T(8,128)(2,1)S(1)}, bf16[256,640]{1,0:T(8,128)(2,1)S(1)}, u32[]{:S(2)}, u32[]{:S(2)}) collective-permute-start(bf16[256,640]{1,0:T(8,128)(2,1)S(1)} %pad_maximum_fusion.6), channel_id=1, source_target_pairs={{0,4},{1,5},{2,6},{3,7},{4,0},{5,1},{6,2},{7,3},{8,12},{9,13},{10,... | collective-permute-start | bytes 983048 | tf_op jit(solution)/shard_map/ppermute | solution.py:396
  117.0 10.2 %collective-permute-start.29 = (bf16[240,640]{1,0:T(8,128)(2,1)S(1)}, bf16[240,640]{1,0:T(8,128)(2,1)S(1)}, u32[]{:S(2)}, u32[]{:S(2)}) collective-permute-start(bf16[240,640]{1,0:T(8,128)(2,1)S(1)} %pad_maximum_fusion.7), channel_id=1, source_target_pairs={{0,8},{1,9},{2,10},{3,11},{4,12},{5,13},{6,14},{7,15},{8,0},{9,1},... | collective-permute-start | bytes 921608 | tf_op jit(solution)/shard_map/ppermute | solution.py:396
  120.3 15.0 %collective-permute-start.33 = (bf16[416,640]{1,0:T(8,128)(2,1)S(1)}, bf16[416,640]{1,0:T(8,128)(2,1)S(1)}, u32[]{:S(2)}, u32[]{:S(2)}) collective-permute-start(bf16[416,640]{1,0:T(8,128)(2,1)S(1)} %pad_maximum_fusion.5), channel_id=1, source_target_pairs={{0,8},{1,9},{2,10},{3,11},{4,12},{5,13},{6,14},{7,15},{8,0},{9,1},... | collective-permute-start | bytes 1597448 | tf_op jit(solution)/shard_map/ppermute | solution.py:396
  121.3 14.2 %collective-permute-start.32 = (bf16[512,640]{1,0:T(8,128)(2,1)S(1)}, bf16[512,640]{1,0:T(8,128)(2,1)S(1)}, u32[]{:S(2)}, u32[]{:S(2)}) collective-permute-start(bf16[512,640]{1,0:T(8,128)(2,1)S(1)} %pad_maximum_fusion.3), channel_id=1, source_target_pairs={{0,2},{1,3},{2,0},{3,1},{4,6},{5,7},{6,4},{7,5},{8,10},{9,11},{10,... | collective-permute-start | bytes 1966088 | tf_op jit(solution)/shard_map/ppermute | solution.py:396
  127.3 10.2 %collective-permute-start.31 = (bf16[480,640]{1,0:T(8,128)(2,1)S(1)}, bf16[480,640]{1,0:T(8,128)(2,1)S(1)}, u32[]{:S(2)}, u32[]{:S(2)}) collective-permute-start(bf16[480,640]{1,0:T(8,128)(2,1)S(1)} %pad_maximum_fusion.4), channel_id=1, source_target_pairs={{0,4},{1,5},{2,6},{3,7},{4,0},{5,1},{6,2},{7,3},{8,12},{9,13},{10,... | collective-permute-start | bytes 1843208 | tf_op jit(solution)/shard_map/ppermute | solution.py:396
  135.8 3.7 %collective-permute-start.34 = (bf16[1024,640]{1,0:T(8,128)(2,1)S(1)}, bf16[1024,640]{1,0:T(8,128)(2,1)S(1)}, u32[]{:S(2)}, u32[]{:S(2)}) collective-permute-start(bf16[1024,640]{1,0:T(8,128)(2,1)S(1)} %pad_maximum_fusion.kept.kept_second), channel_id=1, source_target_pairs={{0,1},{1,0},{2,3},{3,2},{4,5},{5,4},{6,7},{7,6},{8,9},{9,8},{10,11... | collective-permute-start | bytes 3932168 | tf_op jit(solution)/shard_map/ppermute | solution.py:396
  137.8 3.7 %collective-permute-start.35 = (bf16[960,640]{1,0:T(8,128)(2,1)S(1)}, bf16[960,640]{1,0:T(8,128)(2,1)S(1)}, u32[]{:S(2)}, u32[]{:S(2)}) collective-permute-start(bf16[960,640]{1,0:T(8,128)(2,1)S(1)} %pad_maximum_fusion.1.kept), channel_id=1, source_target_pairs={{0,1},{1,0},{2,3},{3,2},{4,5},{5,4},{6,7},{7,6},{8,9},{9,8},{10,11... | collective-permute-start | bytes 3686408 | tf_op jit(solution)/shard_map/ppermute | solution.py:396
  137.9 6.5 %collective-permute-start.36 = (bf16[832,640]{1,0:T(8,128)(2,1)S(1)}, bf16[832,640]{1,0:T(8,128)(2,1)S(1)}, u32[]{:S(2)}, u32[]{:S(2)}) collective-permute-start(bf16[832,640]{1,0:T(8,128)(2,1)S(1)} %pad_maximum_fusion.2.kept), channel_id=1, source_target_pairs={{0,1},{1,0},{2,3},{3,2},{4,5},{5,4},{6,7},{7,6},{8,9},{9,8},{10,11... | collective-permute-start | bytes 3194888 | tf_op jit(solution)/shard_map/ppermute | solution.py:396

commit v4 on v3

--- a/solution.py
+++ b/solution.py
@@ -5,6 +5,7 @@
 import jax.numpy as jnp
 from jax import lax
 from jax.experimental import pallas as pl
+from jax.experimental.layout import Layout, with_layout_constraint
 from jax.experimental.pallas import tpu as pltpu
 from jax.sharding import PartitionSpec as P
 
@@ -14,7 +15,6 @@
 LANES = 128
 TILE = 16
 VMEM_LIMIT = 24 * 2**20
-BEGIN = 48
 F32 = jnp.float32
 BF16 = jnp.bfloat16
 
@@ -44,10 +44,6 @@
         cost_estimate=pl.CostEstimate(flops=0, bytes_accessed=moved, transcendentals=0),
         name=name,
     )(*args)
-
-
-def begin_body(x, out):
-    out[...] = x[...]
 
 
 def prepare_body(dims, seeds, bands, basis, table, stencil_out, offsets_out):
@@ -87,12 +83,10 @@
 
 
 def forward_body(
-    dims, place, latent, left, right, stencil, offsets_in, w_disco, w_expand, w_reduce, w_decode, *refs
+    dims, place, latent, left, right, stencil, offsets_in, w_disco, w_expand, *refs
 ):
     members, rows, lons, chans, lon_pad, slot, bases, piece, share = dims
-    spread_out, hidden_out, gelu_out, slope_out, mixed_out = refs[:5]
-    fields_out = refs[5 : 5 + share]
-    wide, turned_fields = refs[5 + share :]
+    spread_out, hidden_out, gelu_out, pre_out, wide = refs
     chan_pad = up(chans, LANES)
     points = rows * lon_pad
     offsets = offsets_in[...]
@@ -129,8 +123,14 @@
     half = 0.5 * (1.0 + th)
     act = (pre * half).astype(BF16)
     gelu_out[...] = act
-    slope_out[...] = (half + 0.5 * pre * (1.0 - th * th) * (rate * (1.0 + 3 * 0.044715 * square))).astype(BF16)
-    mixed = (hidden.astype(F32) + dot(act, w_reduce[...], 1, 1)).astype(BF16)
+    pre_out[...] = pre
+
+
+def fields_body(dims, place, hidden_in, act, w_reduce, w_decode, *refs):
+    members, rows, lons, chans, lon_pad, slot, bases, piece, share = dims
+    mixed_out, fields_out, turned_fields = refs[0], refs[1 : 1 + share], refs[1 + share]
+    hidden = hidden_in[...]
+    mixed = (hidden.astype(F32) + dot(act[...], w_reduce[...], 1, 1)).astype(BF16)
     mixed_out[...] = mixed
     turned = dot(w_decode[...], mixed, 1, 1).astype(BF16)
     outs = turned.shape[0]
@@ -138,7 +138,17 @@
         turned = jnp.concatenate([turned, jnp.zeros((share * piece - outs, turned.shape[1]), BF16)], axis=0)
     turned_fields[...] = turned
     for d in range(share):
-        fields_out[d][...] = turned_fields[pl.ds(pl.multiple_of(lax.rem(place[0] + d, share) * piece, TILE), piece), :]
+        fields_out[d][...] = turned_fields[pl.ds(pl.multiple_of((place[0] ^ d) * piece, TILE), piece), :]
+
+
+def slopes_body(pre_in, hidden, slope_out, hidden_turned):
+    rate = math.sqrt(2.0 / math.pi)
+    pre = pre_in[...]
+    square = pre * pre
+    th = jnp.tanh(rate * (pre + 0.044715 * (square * pre)))
+    half = 0.5 * (1.0 + th)
+    slope_out[...] = (half + 0.5 * pre * (1.0 - th * th) * (rate * (1.0 + 3 * 0.044715 * square))).astype(BF16)
+    hidden_turned[...] = turn(hidden[...])
 
 
 def crps_body(count, points, members, total, *refs):
@@ -221,7 +231,7 @@
     grads = refs[:share]
     w_decode, gelu, mixed, keep, send, mixed_grad_out, mixed_turned, field_out, turned_grad = refs[share:]
     for d in range(share):
-        turned_grad[pl.ds(pl.multiple_of(lax.rem(place[0] + d, share) * piece, TILE), piece), :] = grads[d][...]
+        turned_grad[pl.ds(pl.multiple_of((place[0] ^ d) * piece, TILE), piece), :] = grads[d][...]
     field_t = turned_grad[: up(outs, TILE)]
     field_out[...] = field_t
     packed = Halves(place[1], keep, send)
@@ -244,7 +254,7 @@
 def second_body(dims, scale, place, *refs):
     outs, chans, hidden_units, width, taps_count = dims
     (
-        mixed_grad_in, mixed_turned, field_t, w_reduce, w_expand, slopes, hidden, gelu, mixed, spread,
+        mixed_grad_in, mixed_turned, field_t, w_reduce, w_expand, slopes, hidden, hidden_turned_in, gelu, mixed, spread,
         keep, send, hidden_grad_out, hidden_turned,
     ) = refs
     packed = Halves(place[1], keep, send)
@@ -255,7 +265,7 @@
     hidden_grad_out[...] = hidden_grad
     hidden_grad_t = turn(hidden_grad)
     hidden_turned[...] = hidden_grad_t
-    hidden_t = turn(hidden[...])
+    hidden_t = hidden_turned_in[...]
     row = 0
     for part in range(hidden_units // width):
         packed.put(row, dot(hidden_t[:width], pre_grad[:, part * width : (part + 1) * width]) * scale)
@@ -286,9 +296,14 @@
     packed.zero_from(row)
 
 
-def combine_body(index, place, kept, got, send, keep):
+def bit_of(place, pair):
+    return jnp.where(place[1] == 0, place[pair[0]], place[pair[1]])
+
+
+def combine_body(pair, place, kept, got, send, keep):
     count = keep.shape[0]
-    for target, side in ((send, 1 - place[index]), (keep, place[index])):
+    bit = bit_of(place, pair)
+    for target, side in ((send, 1 - bit), (keep, bit)):
         rows = pl.ds(pl.multiple_of(side * count, TILE), count)
         target[...] = add_rounded(kept[rows, :], got[rows, :])
 
@@ -401,9 +416,10 @@
 
 
 def streams():
-    core, *lon = bits_of("lon")
+    core, *lon = [(d, d) for d in bits_of("lon")]
     mem = bits_of("member")
-    orders = [mem[:1] + lon + mem[1:], lon + mem, lon[1:] + mem[:1] + lon[:1] + mem[1:]]
+    mem = [(d, d) for d in mem]
+    orders = [[mem[0], lon[0], lon[1], mem[1]], [lon[0], lon[1], mem[0], mem[1]], [lon[1], mem[0], lon[0], mem[1]]]
     return [[core] + order for order in orders]
 
 
@@ -413,12 +429,16 @@
 
 def all_dims():
     return bits_of("lon") + bits_of("member")
+
+
+def places_of(pair):
+    return [1 + all_dims().index(dim) for dim in pair]
 
 
 class Stream:
     def __init__(self, place, keep, send, order):
         self.place, self.kept, self.order = place, keep, order
-        self.got = swap(send, (order[0], order[0]))
+        self.got = swap(send, order[0])
         self.done = [order[0]]
         self.steps = [self.halve] * (len(order) - 2) + [self.exchange, self.added] + [self.join] * (len(order) - 2)
 
@@ -429,36 +449,36 @@
         return self
 
     def halve(self):
-        dim = self.order[len(self.done)]
-        count, index = self.kept.shape[0] // 2, 1 + all_dims().index(dim)
+        pair = self.order[len(self.done)]
+        count, at = self.kept.shape[0] // 2, places_of(pair)
         if count % TILE == 0 and len(self.done) < 3:
             shape = ((count, self.kept.shape[1]), BF16)
             args = [self.place, self.kept, self.got]
-            send, keep = vmem_call(functools.partial(combine_body, index), [shape] * 2, args, smem=1, name="combine")
+            send, keep = vmem_call(functools.partial(combine_body, at), [shape] * 2, args, smem=1, name="combine")
         else:
-            bit = self.place[index]
+            bit = bit_of(self.place, at)
             send, keep = (
                 add_rounded(*(lax.dynamic_slice_in_dim(x, side * count, count, axis=0) for x in (self.kept, self.got)))
                 for side in (1 - bit, bit)
             )
-        self.got, self.kept = swap(send, (dim, dim)), keep
-        self.done.append(dim)
+        self.got, self.kept = swap(send, pair), keep
+        self.done.append(pair)
 
     def exchange(self):
         self.kept = add_rounded(self.kept, self.got)
-        self.got = swap(self.kept, (self.order[-1],) * 2)
+        self.got = swap(self.kept, self.order[-1])
 
     def added(self):
         self.kept = add_rounded(self.kept, self.got)
         self.send_back()
 
     def join(self):
-        low = self.place[1 + all_dims().index(self.done.pop())] == 0
+        low = bit_of(self.place, places_of(self.done.pop())) == 0
         self.kept = jnp.concatenate([jnp.where(low, self.kept, self.got), jnp.where(low, self.got, self.kept)], axis=0)
         self.send_back()
 
     def send_back(self):
-        self.got = swap(self.kept, (self.done[-1],) * 2)
+        self.got = swap(self.kept, self.done[-1])
 
 
 def shifted(x, axis, by):
@@ -466,9 +486,9 @@
     return lax.ppermute(x, axis, [(i, (i + by) % size) for i in range(size)])
 
 
-def spread_out(piece_of, axis):
+def exchanged(piece_of, axis):
     size = lax.axis_size(axis)
-    return [piece_of(0)] + [shifted(piece_of(size - d), axis, -d) for d in range(1, size)]
+    return [piece_of(0)] + [lax.ppermute(piece_of(d), axis, [(i, i ^ d) for i in range(size)]) for d in range(1, size)]
 
 
 def per_device(
@@ -489,10 +509,6 @@
     piece = TILE * -(-up(outs, TILE) // (TILE * share))
     me = lax.axis_index("member")
     place = jnp.stack([me] + [lax.axis_index(axis) // bit % 2 for axis, bit in all_dims()]).astype(jnp.int32)
-    (row_bands,) = vmem_call(
-        begin_body, [(row_bands.shape, row_bands.dtype)], [row_bands], name="begin", moved=BEGIN * 2**20
-    )
-    row_bands, latent = lax.optimization_barrier((row_bands, latent))
     by_lon = jnp.swapaxes(latent, 1, 2)
     left = jnp.swapaxes(shifted(by_lon[:, lons - reach :], "lon", 1), 1, 2)
     right = jnp.swapaxes(shifted(by_lon[:, :reach], "lon", -1), 1, 2)
@@ -506,31 +522,34 @@
         name="prepare",
         moved=4 * 2**20,
     )
-    weights = [disco_t, w_expand, reduce_t, decode_t]
-    spread, hidden, gelu, slopes, mixed, *here = vmem_call(
+    spread, hidden, gelu, pre = vmem_call(
         functools.partial(forward_body, dims),
-        [
-            ((flat, full), BF16),
-            ((flat, chans), BF16),
-            ((flat, hidden_units), BF16),
-            ((flat, hidden_units), BF16),
-            ((flat, chans), BF16),
-        ]
-        + [((piece, flat), BF16)] * share,
-        [place, latent, left, right, stencil, offsets] + weights,
-        smem=1,
-        scratch=[
-            pltpu.VMEM((members, rows * slot, up(chans, LANES)), F32),
-            pltpu.VMEM((share * piece, flat), BF16),
-        ],
+        [((flat, full), BF16), ((flat, chans), BF16), ((flat, hidden_units), BF16), ((flat, hidden_units), F32)],
+        [place, latent, left, right, stencil, offsets, disco_t, w_expand],
+        smem=1,
+        scratch=[pltpu.VMEM((members, rows * slot, up(chans, LANES)), F32)],
         name="forward",
         moved=24 * 2**20,
+    )
+    mixed, *here = vmem_call(
+        functools.partial(fields_body, dims),
+        [((flat, chans), BF16)] + [((piece, flat), BF16)] * share,
+        [place, hidden, gelu, reduce_t, decode_t],
+        smem=1,
+        scratch=[pltpu.VMEM((share * piece, flat), BF16)],
+        name="fields",
+        moved=6 * 2**20,
+    )
+    turned_shape = ((up(chans, TILE), flat), BF16)
+    slopes, input_turned = vmem_call(
+        slopes_body, [((flat, hidden_units), BF16), turned_shape], [pre, hidden], name="slopes"
     )
     here_out = here
     observed = jnp.pad(target, ((0, 0), (0, lon_pad - lons), (0, share * piece - outs))).reshape(points, share * piece).T
     observed = jnp.concatenate([observed] * members, axis=1)
     observed = lax.dynamic_slice_in_dim(observed, me * piece, piece, axis=0)
-    here = spread_out(lambda d: here_out[d], "member")
+    here = exchanged(lambda d: here_out[d], "member")
+    observed, slopes, input_turned = lax.optimization_barrier((observed, slopes, input_turned))
     grads = vmem_call(
         functools.partial(crps_body, share, points, members, total_members),
         [((piece, flat), BF16)] * share,
@@ -538,7 +557,7 @@
         name="crps",
         moved=3 * 2**20,
     )
-    back = spread_out(lambda d: grads[d], "member")
+    back = exchanged(lambda d: grads[d], "member")
     scale = 1.0 / math.sqrt(total_members * rows * lons * lax.axis_size("lon"))
     unit = row_unit()
     taps_count = bases * chans
@@ -547,7 +566,6 @@
     def halves(rows):
         return [((up(rows, unit) // 2, width), BF16)] * 2
 
-    turned_shape = ((up(chans, TILE), flat), BF16)
     blocks = hidden_units // width
     keep, send, mixed_grad, mixed_turned, field_turned = vmem_call(
         functools.partial(first_body, (share, piece, outs, hidden_units, width), scale),
@@ -563,7 +581,7 @@
     keep, send, hidden_grad, hidden_turned = vmem_call(
         functools.partial(second_body, (outs, chans, hidden_units, width, taps_count), scale),
         halves((blocks + 1) * width + misc_shape[0][0]) + [((flat, chans), BF16), turned_shape],
-        [place, mixed_grad, mixed_turned, field_turned, reduce_t, w_expand, slopes, hidden, gelu, mixed, spread],
+        [place, mixed_grad, mixed_turned, field_turned, reduce_t, w_expand, slopes, hidden, input_turned, gelu, mixed, spread],
         smem=1,
         name="second_products",
     )
@@ -601,7 +619,7 @@
         + lax.pad(from_left, jnp.float32(0), edge + [(0, lons - reach, 0), (0, 0, 0)])
     ).astype(BF16)
 
-    latent_grad = jnp.swapaxes(latent_grad, 1, 2)
+    latent_grad = with_layout_constraint(jnp.swapaxes(latent_grad, 1, 2), Layout(major_to_minor=(0, 1, 2, 3)))
     for stream in (first, second, third):
         last = stream.advance(last)
     first.got, latent_grad = lax.optimization_barrier((first.got, latent_grad))

time: 147 us -> 144 us (0.980)
  waiting for transfers between devices: 61.6 us -> 50.1 us
  starting transfers between devices: 34 us -> 40.5 us
  local copies, waits for them, and re-layouts: 8.57 us -> 4.08 us
  Pallas kernels: 37.3 us -> 41.4 us
  other arithmetic: 3.92 us -> 6.31 us
    ppermute x0 -> x6, starting transfers between devices: none -> 9.37 us  [exchanged(): lax.ppermute(piece_of(d), axis, [(i, i ^ d) for i in range(size)])]
    ppermute x10 -> x4, waiting for transfers between devices: 9.32 us -> 0.01 us  [shifted(): return lax.ppermute(x, axis, [(i, (i + by) % size) for i in range(size)])]
    ppermute x27, waiting for transfers between devices: 52.3 us -> 43.3 us  [swap(): return lax.ppermute(x, ('member', 'lon'), perm)]
    ppermute x10 -> x4, starting transfers between devices: 13 us -> 4.17 us  [shifted(): return lax.ppermute(x, axis, [(i, (i + by) % size) for i in range(size)])]
    ppermute x0 -> x6, waiting for transfers between devices: none -> 6.82 us  [exchanged(): lax.ppermute(piece_of(d), axis, [(i, i ^ d) for i in range(size)])]
    ppermute x27, starting transfers between devices: 21.1 us -> 27 us  [swap(): return lax.ppermute(x, ('member', 'lon'), perm)]
    pallas_call x17 -> x18, Pallas kernels: 37.3 us -> 41.4 us  [vmem_call(): pl.pallas_call(body, out_shape=[jax.ShapeDtypeStruct(shape, dtype) for sh...]
    unnamed x30 -> x22, local copies, waits for them, and re-layouts: 5.29 us -> 3.24 us
  transfers between devices with their start and end apart: 37 -> 37, of which waited for: 22 -> 21; matrix products, arithmetic and copies ran while one was open for 4% -> 5% of each run, Pallas kernels for 16% -> 19%
where the time goes in v4:
time: 144 us
  waiting for transfers between devices  50.1 us (35%)
  Pallas kernels  41.4 us (29%)
  starting transfers between devices  40.5 us (28%)
  other arithmetic  6.31 us (4%)
  local copies, waits for them, and re-layouts  4.08 us (3%)
    ppermute x27, waiting for transfers between devices, swap(): return lax.ppermute(x, ('member', 'lon'), perm)  43.3 us
    pallas_call x18, Pallas kernels, vmem_call(): pl.pallas_call(body, out_shape=[jax.ShapeDtypeStruct(shape, dtype) for sh...  41.4 us
    ppermute x27, starting transfers between devices, swap(): return lax.ppermute(x, ('member', 'lon'), perm)  27 us
    ppermute x6, starting transfers between devices, exchanged(): lax.ppermute(piece_of(d), axis, [(i, i ^ d) for i in range(size)])  9.37 us
    ppermute x6, waiting for transfers between devices, exchanged(): lax.ppermute(piece_of(d), axis, [(i, i ^ d) for i in range(size)])  6.82 us
    ppermute x4, starting transfers between devices, shifted(): return lax.ppermute(x, axis, [(i, (i + by) % size) for i in range(size)])  4.17 us
    convert_element_type x9, other arithmetic, add_rounded(): return (a.astype(F32) + b.astype(F32)).astype(BF16)  3.44 us
    unnamed x22, local copies, waits for them, and re-layouts  3.24 us
  transfers between devices with their start and end apart: 37, of which 21 were waited for; matrix products, arithmetic and copies ran while one was open for 5% of the time, Pallas kernels for 19%

profile of v4, /device:TPU:0, one launch (start us, length us, event | category | flops | bytes accessed | tf_op | source)
XLA Modules:
  0.0 143.6 jit_solution(14763577594663811920)
XLA Ops:
  0.7 1.2 copy.38.latent
  2.5 2.9 %collective-permute-start.1 = (bf16[2,3,4,641]{3,1,2,0:T(4,128)(2,1)S(1)}, bf16[2,3,4,641]{3,1,2,0:T(4,128)(2,1)S(1)}, u32[]{:S(2)}, u32[]{:S(2)}) collective-permute-start(bf16[2,3,4,641]{3,1,2,0:T(4,128)(2,1)S(1)} %get-tuple-element.229), channel_id=1, source_target_pairs={{0,7},{1,0},{2,1},{3,2},{4,3},{5,4},{6,5},{7,6},{8,15},{9,8},{10,9... | collective-permute-start | bytes 92312 | tf_op jit(solution)/shard_map/ppermute | solution.py:486
  6.2 1.6 %prepare.1 = (bf16[768,256]{1,0:T(8,128)(2,1)S(1)}, f32[16,641]{1,0:T(8,128)S(1)}) custom-call(s32[2]{0:T(128)S(1)} %copy-done.6, s32[4]{0:T(128)S(1)} %copy-done.7, f32[3136]{0:T(1024)S(1)} %reshape.22.basis, bf16[64,641]{1,0:T(8,128)(2,1)S(1)} %copy-done.5), custom_call_target="tpu_custom_call" | custom-call | bytes 4194304 | tf_op jit(solution)/shard_map/prepare/pallas_call | solution.py:37
  8.0 2.0 %copy-done = bf16[2564,641]{0,1:T(8,128)(2,1)S(1)} copy-done((bf16[2564,641]{0,1:T(8,128)(2,1)S(1)}, bf16[2564,641]{0,1:T(8,128)(2,1)}, u32[]{:S(2)}) %copy-start) | copy-done | bytes 3287072
  10.0 5.5 %forward.1 = (bf16[384,2688]{1,0:T(8,128)(2,1)S(1)}, bf16[384,641]{1,0:T(8,128)(2,1)S(1)}, bf16[384,1282]{1,0:T(8,128)(2,1)S(1)}, f32[384,1282]{1,0:T(8,128)S(1)}) custom-call(s32[6]{0:T(128)S(1)} %stack.27.place, bf16[2,4,45,641]{3,2,1,0:T(8,128)(2,1)S(1)} %copy.38.latent, bf16[2,4,3,641]{3,2,1,0:T(4,128)(2,1)S(1)} %bitcast.29, ...), custom_call_target="tpu_custom_call" | custom-call | bytes 25165824 | tf_op jit(solution)/shard_map/forward/pallas_call | solution.py:37
  15.5 2.3 %fields.1 = (bf16[384,641]{1,0:T(8,128)(2,1)S(1)}, bf16[80,384]{1,0:T(8,128)(2,1)S(1)}, bf16[80,384]{1,0:T(8,128)(2,1)S(1)}, bf16[80,384]{1,0:T(8,128)(2,1)S(1)}, bf16[80,384]{1,0:T(8,128)(2,1)S(1)}) custom-call(s32[6]{0:T(128)S(1)} %stack.27.place, bf16[384,641]{1,0:T(8,128)(2,1)S(1)} %get-tuple-element.112.hidden_in.hidden.refs_6_, ...), custom_call_target="tpu_custom_call" | custom-call | bytes 6291456 | tf_op jit(solution)/shard_map/fields/pallas_call | solution.py:37
  17.7 2.3 %collective-permute-start.2 = (bf16[80,384]{1,0:T(8,128)(2,1)S(1)}, bf16[80,384]{1,0:T(8,128)(2,1)S(1)}, u32[]{:S(2)}, u32[]{:S(2)}) collective-permute-start(bf16[80,384]{1,0:T(8,128)(2,1)S(1)} %get-tuple-element.115), channel_id=1, source_target_pairs={{0,8},{8,0},{16,24},{24,16},{1,9},{9,1},{17,25},{25,17},{2,10},{10... | collective-permute-start | bytes 184328 | tf_op jit(solution)/shard_map/ppermute | solution.py:491
  20.1 2.6 %collective-permute-start.3 = (bf16[80,384]{1,0:T(8,128)(2,1)S(1)}, bf16[80,384]{1,0:T(8,128)(2,1)S(1)}, u32[]{:S(2)}, u32[]{:S(2)}) collective-permute-start(bf16[80,384]{1,0:T(8,128)(2,1)S(1)} %get-tuple-element.116), channel_id=1, source_target_pairs={{0,16},{8,24},{16,0},{24,8},{1,17},{9,25},{17,1},{25,9},{2,18},{10... | collective-permute-start | bytes 184328 | tf_op jit(solution)/shard_map/ppermute | solution.py:491
  22.8 2.9 %slopes.1 = (bf16[384,1282]{1,0:T(8,128)(2,1)S(1)}, bf16[656,384]{1,0:T(8,128)(2,1)S(1)}) custom-call(f32[384,1282]{1,0:T(8,128)S(1)} %get-tuple-element.118.pre_in, bf16[384,641]{1,0:T(8,128)(2,1)S(1)} %get-tuple-element.112.hidden_in.hidden.refs_6_), custom_call_target="tpu_custom_call" | custom-call | tf_op jit(solution)/shard_map/slopes/pallas_call | solution.py:37
  25.7 1.5 %collective-permute-done.3.refs_2_ = bf16[80,384]{1,0:T(8,128)(2,1)S(1)} collective-permute-done((bf16[80,384]{1,0:T(8,128)(2,1)S(1)}, bf16[80,384]{1,0:T(8,128)(2,1)S(1)}, u32[]{:S(2)}, u32[]{:S(2)}) %collective-permute-start.3) | collective-permute-done | bytes 61472 | tf_op jit(solution)/shard_map/ppermute | solution.py:491
  27.2 1.5 %collective-permute-done.4.refs_3_ = bf16[80,384]{1,0:T(8,128)(2,1)S(1)} collective-permute-done((bf16[80,384]{1,0:T(8,128)(2,1)S(1)}, bf16[80,384]{1,0:T(8,128)(2,1)S(1)}, u32[]{:S(2)}, u32[]{:S(2)}) %collective-permute-start.4) | collective-permute-done | bytes 61472 | tf_op jit(solution)/shard_map/ppermute | solution.py:491
  28.7 0.9 crps.1
  29.6 2.2 %collective-permute-start.6 = (bf16[80,384]{1,0:T(8,128)(2,1)S(1)}, bf16[80,384]{1,0:T(8,128)(2,1)S(1)}, u32[]{:S(2)}, u32[]{:S(2)}) collective-permute-start(bf16[80,384]{1,0:T(8,128)(2,1)S(1)} %get-tuple-element.124), channel_id=1, source_target_pairs={{0,16},{8,24},{16,0},{24,8},{1,17},{9,25},{17,1},{25,9},{2,18},{10... | collective-permute-start | bytes 184328 | tf_op jit(solution)/shard_map/ppermute | solution.py:491
  31.8 2.2 %collective-permute-start.7 = (bf16[80,384]{1,0:T(8,128)(2,1)S(1)}, bf16[80,384]{1,0:T(8,128)(2,1)S(1)}, u32[]{:S(2)}, u32[]{:S(2)}) collective-permute-start(bf16[80,384]{1,0:T(8,128)(2,1)S(1)} %get-tuple-element.125), channel_id=1, source_target_pairs={{0,24},{8,16},{16,8},{24,0},{1,25},{9,17},{17,9},{25,1},{2,26},{10... | collective-permute-start | bytes 184328 | tf_op jit(solution)/shard_map/ppermute | solution.py:491
  34.0 1.3 collective-permute-done.6.refs_2_
  35.3 2.5 %collective-permute-done.7.refs_3_ = bf16[80,384]{1,0:T(8,128)(2,1)S(1)} collective-permute-done((bf16[80,384]{1,0:T(8,128)(2,1)S(1)}, bf16[80,384]{1,0:T(8,128)(2,1)S(1)}, u32[]{:S(2)}, u32[]{:S(2)}) %collective-permute-start.7) | collective-permute-done | bytes 61472 | tf_op jit(solution)/shard_map/ppermute | solution.py:491
  37.8 3.4 %first_products.1 = (bf16[832,640]{1,0:T(8,128)(2,1)S(1)}, bf16[832,640]{1,0:T(8,128)(2,1)S(1)}, bf16[384,641]{1,0:T(8,128)(2,1)S(1)}, bf16[656,384]{1,0:T(8,128)(2,1)S(1)}, bf16[288,384]{1,0:T(8,128)(2,1)S(1)}) custom-call(s32[6]{0:T(128)S(1)} %stack.27.place, bf16[80,384]{1,0:T(8,128)(2,1)S(1)} %get-tuple-element.122.refs_0_, ...), custom_call_target="tpu_custom_call" | custom-call | bytes 9437184 | tf_op jit(solution)/shard_map/first_products/pallas_call | solution.py:37
  41.3 5.9 %second_products.1 = (bf16[1024,640]{1,0:T(8,128)(2,1)S(1)}, bf16[1024,640]{1,0:T(8,128)(2,1)S(1)}, bf16[384,641]{1,0:T(8,128)(2,1)S(1)}, bf16[656,384]{1,0:T(8,128)(2,1)S(1)}) custom-call(s32[6]{0:T(128)S(1)} %stack.27.place, bf16[384,641]{1,0:T(8,128)(2,1)S(1)} %get-tuple-element.130.refs_0_, bf16[656,384]{1,0:T(8,128)(2,1)S(1)} %get-tuple-element.131.refs_1_, ...), custom_call_target="tpu_custom_call" | custom-call | tf_op jit(solution)/shard_map/second_products/pallas_call | solution.py:37
  47.7 0.8 combine.6
  48.5 3.1 %third_products.1 = (bf16[960,640]{1,0:T(8,128)(2,1)S(1)}, bf16[960,640]{1,0:T(8,128)(2,1)S(1)}) custom-call(s32[6]{0:T(128)S(1)} %stack.27.place, bf16[656,384]{1,0:T(8,128)(2,1)S(1)} %get-tuple-element.139.left, bf16[384,2688]{1,0:T(8,128)(2,1)S(1)} %get-tuple-element.135.refs_10_.right), custom_call_target="tpu_custom_call" | custom-call | tf_op jit(solution)/shard_map/third_products/pallas_call | solution.py:37
  51.8 0.9 combine.7
  52.7 1.9 %collective-permute-start.13 = (bf16[512,640]{1,0:T(8,128)(2,1)S(1)}, bf16[512,640]{1,0:T(8,128)(2,1)S(1)}, u32[]{:S(2)}, u32[]{:S(2)}) collective-permute-start(bf16[512,640]{1,0:T(8,128)(2,1)S(1)} %get-tuple-element.154), channel_id=1, source_target_pairs={{0,2},{1,3},{2,0},{3,1},{4,6},{5,7},{6,4},{7,5},{8,10},{9,11},{10,... | collective-permute-start | bytes 1966088 | tf_op jit(solution)/shard_map/ppermute | solution.py:411
  54.6 1.3 collective-permute-start.9
  55.9 0.8 combine.8
  56.7 0.9 collective-permute-start.12
  57.6 3.4 %collect.1 = (f32[2,4,45,641]{3,2,1,0:T(8,128)S(1)}, f32[2,4,3,641]{3,2,1,0:T(4,128)S(1)}, f32[2,4,3,641]{3,2,1,0:T(4,128)S(1)}) custom-call(bf16[384,641]{1,0:T(8,128)(2,1)S(1)} %get-tuple-element.147.hidden_grad, bf16[641,2564]{1,0:T(8,128)(2,1)S(1)} %bitcast.23, bf16[768,256]{1,0:T(8,128)(2,1)S(1)} %get-tuple-element.110.stencil), custom_call_target="tpu_custom_call" | custom-call | tf_op jit(solution)/shard_map/collect/pallas_call | solution.py:37
  61.0 7.8 %collective-permute-done.9.got = bf16[416,640]{1,0:T(8,128)(2,1)S(1)} collective-permute-done((bf16[416,640]{1,0:T(8,128)(2,1)S(1)}, bf16[416,640]{1,0:T(8,128)(2,1)S(1)}, u32[]{:S(2)}, u32[]{:S(2)}) %collective-permute-start.9) | collective-permute-done | bytes 532512 | tf_op jit(solution)/shard_map/ppermute | solution.py:411
  68.8 1.3 combine.9
  70.4 0.7 combine.10
  71.2 1.4 collective-permute-start.15
  72.6 0.7 combine.11
  73.3 0.8 collective-permute-start.14
  74.2 0.7 collective-permute-start.23
  74.9 3.1 %collective-permute-done.16 = bf16[208,640]{1,0:T(8,128)(2,1)} collective-permute-done((bf16[208,640]{1,0:T(8,128)(2,1)}, bf16[208,640]{1,0:T(8,128)(2,1)}, u32[]{:S(2)}, u32[]{:S(2)}) %collective-permute-start.16) | collective-permute-done | bytes 266272 | tf_op jit(solution)/shard_map/ppermute | solution.py:411
  78.1 1.0 add_convert_fusion.11
  79.1 1.9 %collective-permute-done.15 = bf16[256,640]{1,0:T(8,128)(2,1)} collective-permute-done((bf16[256,640]{1,0:T(8,128)(2,1)S(1)}, bf16[256,640]{1,0:T(8,128)(2,1)}, u32[]{:S(2)}, u32[]{:S(2)}) %collective-permute-start.15) | collective-permute-done | bytes 327712 | tf_op jit(solution)/shard_map/ppermute | solution.py:411
  81.0 1.4 collective-permute-start.18
  82.4 1.1 add_convert_fusion.2
  83.4 1.0 collective-permute-start.17
  84.4 1.1 add_convert_fusion.6
  86.0 2.3 %collective-permute-start.20 = (bf16[104,640]{1,0:T(8,128)(2,1)S(1)}, bf16[104,640]{1,0:T(8,128)(2,1)S(1)}, u32[]{:S(2)}, u32[]{:S(2)}) collective-permute-start(bf16[104,640]{1,0:T(8,128)(2,1)S(1)} %add_convert_fusion.9), channel_id=1, source_target_pairs={{0,16},{1,17},{2,18},{3,19},{4,20},{5,21},{6,22},{7,23},{8,24},{9,... | collective-permute-start | bytes 399368 | tf_op jit(solution)/shard_map/ppermute | solution.py:411
  88.4 1.3 collective-permute-done.17
  89.6 2.5 %collective-permute-start.21 = (bf16[120,640]{1,0:T(8,128)(2,1)S(1)}, bf16[120,640]{1,0:T(8,128)(2,1)S(1)}, u32[]{:S(2)}, u32[]{:S(2)}) collective-permute-start(bf16[120,640]{1,0:T(8,128)(2,1)S(1)} %get-tuple-element.227), channel_id=1, source_target_pairs={{0,2},{1,3},{2,0},{3,1},{4,6},{5,7},{6,4},{7,5},{8,10},{9,11},{10,... | collective-permute-start | bytes 460808 | tf_op jit(solution)/shard_map/ppermute | solution.py:411
  92.2 1.4 %collective-permute-start.19 = (bf16[128,640]{1,0:T(8,128)(2,1)S(1)}, bf16[128,640]{1,0:T(8,128)(2,1)S(1)}, u32[]{:S(2)}, u32[]{:S(2)}) collective-permute-start(bf16[128,640]{1,0:T(8,128)(2,1)S(1)} %add_convert_fusion.1), channel_id=1, source_target_pairs={{0,16},{1,17},{2,18},{3,19},{4,20},{5,21},{6,22},{7,23},{8,24},{9,... | collective-permute-start | bytes 491528 | tf_op jit(solution)/shard_map/ppermute | solution.py:411
  93.7 1.7 %collective-permute-done.21 = bf16[120,640]{1,0:T(8,128)(2,1)S(1)} collective-permute-done((bf16[120,640]{1,0:T(8,128)(2,1)S(1)}, bf16[120,640]{1,0:T(8,128)(2,1)S(1)}, u32[]{:S(2)}, u32[]{:S(2)}) %collective-permute-start.21) | collective-permute-done | bytes 153632 | tf_op jit(solution)/shard_map/ppermute | solution.py:411
  95.4 1.4 %collective-permute-start.25 = (bf16[120,640]{1,0:T(8,128)(2,1)S(1)}, bf16[120,640]{1,0:T(8,128)(2,1)S(1)}, u32[]{:S(2)}, u32[]{:S(2)}) collective-permute-start(bf16[120,640]{1,0:T(8,128)(2,1)S(1)} %add_convert_fusion.5), channel_id=1, source_target_pairs={{0,16},{1,17},{2,18},{3,19},{4,20},{5,21},{6,22},{7,23},{8,24},{9,... | collective-permute-start | bytes 460808 | tf_op jit(solution)/shard_map/ppermute | solution.py:411
  96.8 3.1 %collective-permute-done.20 = bf16[104,640]{1,0:T(8,128)(2,1)S(1)} collective-permute-done((bf16[104,640]{1,0:T(8,128)(2,1)S(1)}, bf16[104,640]{1,0:T(8,128)(2,1)S(1)}, u32[]{:S(2)}, u32[]{:S(2)}) %collective-permute-start.20) | collective-permute-done | bytes 133152 | tf_op jit(solution)/shard_map/ppermute | solution.py:411
  100.0 3.1 %collective-permute-start.22 = (bf16[104,640]{1,0:T(8,128)(2,1)S(1)}, bf16[104,640]{1,0:T(8,128)(2,1)S(1)}, u32[]{:S(2)}, u32[]{:S(2)}) collective-permute-start(bf16[104,640]{1,0:T(8,128)(2,1)S(1)} %add_convert_fusion.8), channel_id=1, source_target_pairs={{0,4},{1,5},{2,6},{3,7},{4,0},{5,1},{6,2},{7,3},{8,12},{9,13},{10,... | collective-permute-start | bytes 399368 | tf_op jit(solution)/shard_map/ppermute | solution.py:411
  103.1 2.0 %collective-permute-done.19 = bf16[128,640]{1,0:T(8,128)(2,1)S(1)} collective-permute-done((bf16[128,640]{1,0:T(8,128)(2,1)S(1)}, bf16[128,640]{1,0:T(8,128)(2,1)S(1)}, u32[]{:S(2)}, u32[]{:S(2)}) %collective-permute-start.19) | collective-permute-done | bytes 163872 | tf_op jit(solution)/shard_map/ppermute | solution.py:411
  105.2 0.8 collective-permute-done.22
  106.1 1.5 %fusion.2 = bf16[2,45,4,641]{3,2,1,0:T(4,128)(2,1)} fusion(f32[2,4,3,641]{3,1,2,0:T(4,128)S(1)} %collective-permute-done.24, f32[2,4,3,641]{3,1,2,0:T(4,128)S(1)} %collective-permute-done.23, f32[2,4,45,641]{3,2,1,0:T(8,128)S(1)} %get-tuple-element.188), kind=kLoop, calls=%fused_computation.12 | loop fusion | flops 692280 | bytes 1507632 | tf_op jit(solution)/shard_map/transpose | solution.py:622
  107.7 1.2 collective-permute-start.27
  109.0 0.9 collective-permute-start.26
  109.9 0.6 collective-permute-done.28
  110.6 1.5 %collective-permute-start.30 = (bf16[256,640]{1,0:T(8,128)(2,1)S(1)}, bf16[256,640]{1,0:T(8,128)(2,1)S(1)}, u32[]{:S(2)}, u32[]{:S(2)}) collective-permute-start(bf16[256,640]{1,0:T(8,128)(2,1)S(1)} %pad_maximum_fusion.6), channel_id=1, source_target_pairs={{0,4},{1,5},{2,6},{3,7},{4,0},{5,1},{6,2},{7,3},{8,12},{9,13},{10,... | collective-permute-start | bytes 983048 | tf_op jit(solution)/shard_map/ppermute | solution.py:411
  112.1 2.5 %collective-permute-done.27 = bf16[120,640]{1,0:T(8,128)(2,1)S(1)} collective-permute-done((bf16[120,640]{1,0:T(8,128)(2,1)S(1)}, bf16[120,640]{1,0:T(8,128)(2,1)S(1)}, u32[]{:S(2)}, u32[]{:S(2)}) %collective-permute-start.27) | collective-permute-done | bytes 153632 | tf_op jit(solution)/shard_map/ppermute | solution.py:411
  114.9 2.6 %collective-permute-done.26 = bf16[208,640]{1,0:T(8,128)(2,1)S(1)} collective-permute-done((bf16[208,640]{1,0:T(8,128)(2,1)S(1)}, bf16[208,640]{1,0:T(8,128)(2,1)S(1)}, u32[]{:S(2)}, u32[]{:S(2)}) %collective-permute-start.26) | collective-permute-done | bytes 266272 | tf_op jit(solution)/shard_map/ppermute | solution.py:411
  119.1 5.8 %collective-permute-done.29 = bf16[240,640]{1,0:T(8,128)(2,1)S(1)} collective-permute-done((bf16[240,640]{1,0:T(8,128)(2,1)S(1)}, bf16[240,640]{1,0:T(8,128)(2,1)S(1)}, u32[]{:S(2)}, u32[]{:S(2)}) %collective-permute-start.29) | collective-permute-done | bytes 307232 | tf_op jit(solution)/shard_map/ppermute | solution.py:411
  125.0 0.9 collective-permute-start.31
  126.0 6.2 %collective-permute-done.33 = bf16[416,640]{1,0:T(8,128)(2,1)S(1)} collective-permute-done((bf16[416,640]{1,0:T(8,128)(2,1)S(1)}, bf16[416,640]{1,0:T(8,128)(2,1)S(1)}, u32[]{:S(2)}, u32[]{:S(2)}) %collective-permute-start.33) | collective-permute-done | bytes 532512 | tf_op jit(solution)/shard_map/ppermute | solution.py:411
  132.8 2.5 %collective-permute-done.31 = bf16[480,640]{1,0:T(8,128)(2,1)S(1)} collective-permute-done((bf16[480,640]{1,0:T(8,128)(2,1)S(1)}, bf16[480,640]{1,0:T(8,128)(2,1)S(1)}, u32[]{:S(2)}, u32[]{:S(2)}) %collective-permute-start.31) | collective-permute-done | bytes 614432 | tf_op jit(solution)/shard_map/ppermute | solution.py:411
  136.1 2.1 %finish_second.1 = (bf16[641,1282]{1,0:T(8,128)(2,1)}, bf16[32,640]{1,0:T(8,128)(2,1)S(1)}) custom-call(s32[6]{0:T(128)S(1)} %stack.27.place, bf16[1024,640]{1,0:T(8,128)(2,1)S(1)} %pad_maximum_fusion.kept.kept_second, bf16[1024,640]{1,0:T(8,128)(2,1)S(1)} %collective-permute-done.34.got.got_second), custom_call_target="tpu_custom_call" | custom-call | tf_op jit(solution)/shard_map/finish_second/pallas_call | solution.py:37
  138.5 2.9 %finish_third.1 = bf16[641,2564]{1,0:T(8,128)(2,1)} custom-call(s32[6]{0:T(128)S(1)} %stack.27.place, bf16[1024,640]{1,0:T(8,128)(2,1)S(1)} %pad_maximum_fusion.kept.kept_second, bf16[1024,640]{1,0:T(8,128)(2,1)S(1)} %collective-permute-done.34.got.got_second, bf16[960,640]{1,0:T(8,128)(2,1)S(1)} %pad_maximum_fusion.1.kept, ...), custom_call_target="tpu_custom_call" | custom-call | tf_op jit(solution)/shard_map/finish_third/pallas_call | solution.py:37
  141.4 2.2 %finish_first.1 = (bf16[641,1282]{1,0:T(8,128)(2,1)}, bf16[288,641]{1,0:T(8,128)(2,1)}) custom-call(s32[6]{0:T(128)S(1)} %stack.27.place, bf16[832,640]{1,0:T(8,128)(2,1)S(1)} %pad_maximum_fusion.2.kept, bf16[832,640]{1,0:T(8,128)(2,1)S(1)} %collective-permute-done.36.got, bf16[32,640]{1,0:T(8,128)(2,1)S(1)} %get-tuple-element.210.misc_ref), custom_call_target="tpu_custom_call" | custom-call | tf_op jit(solution)/shard_map/finish_first/pallas_call | solution.py:37
  (87 shorter events, 7.3 us)
Async XLA Ops:
  0.6 4.8 %copy-start.9 = (bf16[16,4,7,7]{0,1,3,2:T(4,128)(2,1)S(1)}, bf16[16,4,7,7]{0,1,3,2:T(4,128)(2,1)}, u32[]{:S(2)}) copy-start(bf16[16,4,7,7]{0,1,3,2:T(4,128)(2,1)} %param.14) | copy-start | bytes 18820
  0.6 5.3 %copy-start.8 = (bf16[4,45,288]{2,0,1:T(4,128)(2,1)S(1)}, bf16[4,45,288]{2,0,1:T(4,128)(2,1)}, u32[]{:S(2)}) copy-start(bf16[4,45,288]{2,0,1:T(4,128)(2,1)} %param.19) | copy-start | bytes 311044
  0.7 5.5 %copy-start.6 = (s32[2]{0:T(128)S(1)}, s32[2]{0:T(128)}, u32[]{:S(2)}) copy-start(s32[2]{0:T(128)} %seeds.1) | copy-start | bytes 28
  0.7 5.5 %copy-start.5 = (bf16[64,641]{1,0:T(8,128)(2,1)S(1)}, bf16[64,641]{1,0:T(8,128)(2,1)}, u32[]{:S(2)}) copy-start(bf16[64,641]{1,0:T(8,128)(2,1)} %table.1) | copy-start | bytes 246148
  0.7 5.5 %copy-start.7 = (s32[4]{0:T(128)S(1)}, s32[4]{0:T(128)}, u32[]{:S(2)}) copy-start(s32[4]{0:T(128)} %bands.1) | copy-start | bytes 52
  1.9 6.1 %copy-start.2 = (bf16[641,1282]{1,0:T(8,128)(2,1)S(1)}, bf16[641,1282]{1,0:T(8,128)(2,1)}, u32[]{:S(2)}) copy-start(bf16[641,1282]{1,0:T(8,128)(2,1)} %refs_4_.1) | copy-start | bytes 4930576
  2.0 6.0 %collective-permute-start = (bf16[2,3,4,641]{3,1,2,0:T(4,128)(2,1)S(1)}, bf16[2,3,4,641]{3,1,2,0:T(4,128)(2,1)S(1)}, u32[]{:S(2)}, u32[]{:S(2)}) collective-permute-start(bf16[2,3,4,641]{3,1,2,0:T(4,128)(2,1)S(1)} %get-tuple-element.230), channel_id=1, source_target_pairs={{0,1},{1,2},{2,3},{3,4},{4,5},{5,6},{6,7},{7,0},{8,9},{9,10},{10,1... | collective-permute-start | bytes 92312 | tf_op jit(solution)/shard_map/ppermute | solution.py:486
  2.5 5.5 %collective-permute-start.1 = (bf16[2,3,4,641]{3,1,2,0:T(4,128)(2,1)S(1)}, bf16[2,3,4,641]{3,1,2,0:T(4,128)(2,1)S(1)}, u32[]{:S(2)}, u32[]{:S(2)}) collective-permute-start(bf16[2,3,4,641]{3,1,2,0:T(4,128)(2,1)S(1)} %get-tuple-element.229), channel_id=1, source_target_pairs={{0,7},{1,0},{2,1},{3,2},{4,3},{5,4},{6,5},{7,6},{8,15},{9,8},{10,9... | collective-permute-start | bytes 92312 | tf_op jit(solution)/shard_map/ppermute | solution.py:486
  8.0 2.0 %copy-start = (bf16[2564,641]{0,1:T(8,128)(2,1)S(1)}, bf16[2564,641]{0,1:T(8,128)(2,1)}, u32[]{:S(2)}) copy-start(bf16[2564,641]{0,1:T(8,128)(2,1)} %param.15) | copy-start | bytes 9861148
  10.0 5.5 %copy-start.3 = (bf16[1282,641]{0,1:T(8,128)(2,1)S(1)}, bf16[1282,641]{0,1:T(8,128)(2,1)}, u32[]{:S(2)}) copy-start(bf16[1282,641]{0,1:T(8,128)(2,1)} %param.17) | copy-start | bytes 4930576
  10.0 5.5 %copy-start.4 = (bf16[641,288]{0,1:T(8,128)(2,1)S(1)}, bf16[641,288]{0,1:T(8,128)(2,1)}, u32[]{:S(2)}) copy-start(bf16[641,288]{0,1:T(8,128)(2,1)} %param.18) | copy-start | bytes 1107652
  17.7 7.9 %collective-permute-start.2 = (bf16[80,384]{1,0:T(8,128)(2,1)S(1)}, bf16[80,384]{1,0:T(8,128)(2,1)S(1)}, u32[]{:S(2)}, u32[]{:S(2)}) collective-permute-start(bf16[80,384]{1,0:T(8,128)(2,1)S(1)} %get-tuple-element.115), channel_id=1, source_target_pairs={{0,8},{8,0},{16,24},{24,16},{1,9},{9,1},{17,25},{25,17},{2,10},{10... | collective-permute-start | bytes 184328 | tf_op jit(solution)/shard_map/ppermute | solution.py:491
  20.1 7.1 %collective-permute-start.3 = (bf16[80,384]{1,0:T(8,128)(2,1)S(1)}, bf16[80,384]{1,0:T(8,128)(2,1)S(1)}, u32[]{:S(2)}, u32[]{:S(2)}) collective-permute-start(bf16[80,384]{1,0:T(8,128)(2,1)S(1)} %get-tuple-element.116), channel_id=1, source_target_pairs={{0,16},{8,24},{16,0},{24,8},{1,17},{9,25},{17,1},{25,9},{2,18},{10... | collective-permute-start | bytes 184328 | tf_op jit(solution)/shard_map/ppermute | solution.py:491
  22.7 6.0 %collective-permute-start.4 = (bf16[80,384]{1,0:T(8,128)(2,1)S(1)}, bf16[80,384]{1,0:T(8,128)(2,1)S(1)}, u32[]{:S(2)}, u32[]{:S(2)}) collective-permute-start(bf16[80,384]{1,0:T(8,128)(2,1)S(1)} %get-tuple-element.117), channel_id=1, source_target_pairs={{0,24},{8,16},{16,8},{24,0},{1,25},{9,17},{17,9},{25,1},{2,26},{10... | collective-permute-start | bytes 184328 | tf_op jit(solution)/shard_map/ppermute | solution.py:491
  29.6 4.5 %collective-permute-start.5 = (bf16[80,384]{1,0:T(8,128)(2,1)S(1)}, bf16[80,384]{1,0:T(8,128)(2,1)S(1)}, u32[]{:S(2)}, u32[]{:S(2)}) collective-permute-start(bf16[80,384]{1,0:T(8,128)(2,1)S(1)} %get-tuple-element.123), channel_id=1, source_target_pairs={{0,8},{8,0},{16,24},{24,16},{1,9},{9,1},{17,25},{25,17},{2,10},{10... | collective-permute-start | bytes 184328 | tf_op jit(solution)/shard_map/ppermute | solution.py:491
  29.6 5.7 %collective-permute-start.6 = (bf16[80,384]{1,0:T(8,128)(2,1)S(1)}, bf16[80,384]{1,0:T(8,128)(2,1)S(1)}, u32[]{:S(2)}, u32[]{:S(2)}) collective-permute-start(bf16[80,384]{1,0:T(8,128)(2,1)S(1)} %get-tuple-element.124), channel_id=1, source_target_pairs={{0,16},{8,24},{16,0},{24,8},{1,17},{9,25},{17,1},{25,9},{2,18},{10... | collective-permute-start | bytes 184328 | tf_op jit(solution)/shard_map/ppermute | solution.py:491
  31.8 6.0 %collective-permute-start.7 = (bf16[80,384]{1,0:T(8,128)(2,1)S(1)}, bf16[80,384]{1,0:T(8,128)(2,1)S(1)}, u32[]{:S(2)}, u32[]{:S(2)}) collective-permute-start(bf16[80,384]{1,0:T(8,128)(2,1)S(1)} %get-tuple-element.125), channel_id=1, source_target_pairs={{0,24},{8,16},{16,8},{24,0},{1,25},{9,17},{17,9},{25,1},{2,26},{10... | collective-permute-start | bytes 184328 | tf_op jit(solution)/shard_map/ppermute | solution.py:491
  41.2 6.5 %collective-permute-start.8 = (bf16[832,640]{1,0:T(8,128)(2,1)S(1)}, bf16[832,640]{1,0:T(8,128)(2,1)S(1)}, u32[]{:S(2)}, u32[]{:S(2)}) collective-permute-start(bf16[832,640]{1,0:T(8,128)(2,1)S(1)} %get-tuple-element.128), channel_id=1, source_target_pairs={{0,1},{1,0},{2,3},{3,2},{4,5},{5,4},{6,7},{7,6},{8,9},{9,8},{10,11... | collective-permute-start | bytes 3194888 | tf_op jit(solution)/shard_map/ppermute | solution.py:411
  47.1 4.6 %collective-permute-start.11 = (bf16[1024,640]{1,0:T(8,128)(2,1)S(1)}, bf16[1024,640]{1,0:T(8,128)(2,1)S(1)}, u32[]{:S(2)}, u32[]{:S(2)}) collective-permute-start(bf16[1024,640]{1,0:T(8,128)(2,1)S(1)} %get-tuple-element.143), channel_id=1, source_target_pairs={{0,1},{1,0},{2,3},{3,2},{4,5},{5,4},{6,7},{7,6},{8,9},{9,8},{10,11... | collective-permute-start | bytes 3932168 | tf_op jit(solution)/shard_map/ppermute | solution.py:411
  51.6 4.2 %collective-permute-start.10 = (bf16[960,640]{1,0:T(8,128)(2,1)S(1)}, bf16[960,640]{1,0:T(8,128)(2,1)S(1)}, u32[]{:S(2)}, u32[]{:S(2)}) collective-permute-start(bf16[960,640]{1,0:T(8,128)(2,1)S(1)} %get-tuple-element.141), channel_id=1, source_target_pairs={{0,1},{1,0},{2,3},{3,2},{4,5},{5,4},{6,7},{7,6},{8,9},{9,8},{10,11... | collective-permute-start | bytes 3686408 | tf_op jit(solution)/shard_map/ppermute | solution.py:411
  51.7 5.9 %copy-start.1 = (bf16[2564,641]{0,1:T(8,128)(2,1)S(1)}, bf16[2564,641]{0,1:T(8,128)(2,1)}, u32[]{:S(2)}) copy-start(bf16[2564,641]{0,1:T(8,128)(2,1)} %param.15) | copy-start | bytes 9861148
  52.7 17.8 %collective-permute-start.13 = (bf16[512,640]{1,0:T(8,128)(2,1)S(1)}, bf16[512,640]{1,0:T(8,128)(2,1)S(1)}, u32[]{:S(2)}, u32[]{:S(2)}) collective-permute-start(bf16[512,640]{1,0:T(8,128)(2,1)S(1)} %get-tuple-element.154), channel_id=1, source_target_pairs={{0,2},{1,3},{2,0},{3,1},{4,6},{5,7},{6,4},{7,5},{8,10},{9,11},{10,... | collective-permute-start | bytes 1966088 | tf_op jit(solution)/shard_map/ppermute | solution.py:411
  54.6 14.2 %collective-permute-start.9 = (bf16[416,640]{1,0:T(8,128)(2,1)S(1)}, bf16[416,640]{1,0:T(8,128)(2,1)S(1)}, u32[]{:S(2)}, u32[]{:S(2)}) collective-permute-start(bf16[416,640]{1,0:T(8,128)(2,1)S(1)} %get-tuple-element.129), channel_id=1, source_target_pairs={{0,8},{1,9},{2,10},{3,11},{4,12},{5,13},{6,14},{7,15},{8,0},{9,1},... | collective-permute-start | bytes 1597448 | tf_op jit(solution)/shard_map/ppermute | solution.py:411
  56.7 15.9 %collective-permute-start.12 = (bf16[480,640]{1,0:T(8,128)(2,1)S(1)}, bf16[480,640]{1,0:T(8,128)(2,1)S(1)}, u32[]{:S(2)}, u32[]{:S(2)}) collective-permute-start(bf16[480,640]{1,0:T(8,128)(2,1)S(1)} %get-tuple-element.152), channel_id=1, source_target_pairs={{0,4},{1,5},{2,6},{3,7},{4,0},{5,1},{6,2},{7,3},{8,12},{9,13},{10,... | collective-permute-start | bytes 1843208 | tf_op jit(solution)/shard_map/ppermute | solution.py:411
  70.1 8.0 %collective-permute-start.16 = (bf16[208,640]{1,0:T(8,128)(2,1)}, bf16[208,640]{1,0:T(8,128)(2,1)}, u32[]{:S(2)}, u32[]{:S(2)}) collective-permute-start(bf16[208,640]{1,0:T(8,128)(2,1)} %get-tuple-element.165), channel_id=1, source_target_pairs={{0,2},{1,3},{2,0},{3,1},{4,6},{5,7},{6,4},{7,5},{8,10},{9,11},{10,... | collective-permute-start | bytes 798728 | tf_op jit(solution)/shard_map/ppermute | solution.py:411
  71.2 9.8 %collective-permute-start.15 = (bf16[256,640]{1,0:T(8,128)(2,1)S(1)}, bf16[256,640]{1,0:T(8,128)(2,1)}, u32[]{:S(2)}, u32[]{:S(2)}) collective-permute-start(bf16[256,640]{1,0:T(8,128)(2,1)S(1)} %get-tuple-element.163), channel_id=1, source_target_pairs={{0,4},{1,5},{2,6},{3,7},{4,0},{5,1},{6,2},{7,3},{8,12},{9,13},{10,... | collective-permute-start | bytes 983048 | tf_op jit(solution)/shard_map/ppermute | solution.py:411
  73.3 11.1 %collective-permute-start.14 = (bf16[240,640]{1,0:T(8,128)(2,1)S(1)}, bf16[240,640]{1,0:T(8,128)(2,1)}, u32[]{:S(2)}, u32[]{:S(2)}) collective-permute-start(bf16[240,640]{1,0:T(8,128)(2,1)S(1)} %get-tuple-element.161), channel_id=1, source_target_pairs={{0,8},{1,9},{2,10},{3,11},{4,12},{5,13},{6,14},{7,15},{8,0},{9,1},... | collective-permute-start | bytes 921608 | tf_op jit(solution)/shard_map/ppermute | solution.py:411
  74.2 31.0 %collective-permute-start.23 = (f32[2,4,3,641]{3,1,2,0:T(4,128)S(1)}, f32[2,4,3,641]{3,1,2,0:T(4,128)S(1)}, u32[]{:S(2)}, u32[]{:S(2)}) collective-permute-start(f32[2,4,3,641]{3,1,2,0:T(4,128)S(1)} %copy.26), channel_id=1, source_target_pairs={{0,7},{1,0},{2,1},{3,2},{4,3},{5,4},{6,5},{7,6},{8,15},{9,8},{10,9... | collective-permute-start | bytes 184616 | tf_op jit(solution)/shard_map/ppermute | solution.py:486
  74.9 30.4 %collective-permute-start.24 = (f32[2,4,3,641]{3,1,2,0:T(4,128)S(1)}, f32[2,4,3,641]{3,1,2,0:T(4,128)S(1)}, u32[]{:S(2)}, u32[]{:S(2)}) collective-permute-start(f32[2,4,3,641]{3,1,2,0:T(4,128)S(1)} %copy.27), channel_id=1, source_target_pairs={{0,1},{1,2},{2,3},{3,4},{4,5},{5,6},{6,7},{7,0},{8,9},{9,10},{10,1... | collective-permute-start | bytes 184616 | tf_op jit(solution)/shard_map/ppermute | solution.py:486
  81.0 5.0 %collective-permute-start.18 = (bf16[104,640]{1,0:T(8,128)(2,1)S(1)}, bf16[104,640]{1,0:T(8,128)(2,1)S(1)}, u32[]{:S(2)}, u32[]{:S(2)}) collective-permute-start(bf16[104,640]{1,0:T(8,128)(2,1)S(1)} %get-tuple-element.236), channel_id=1, source_target_pairs={{0,4},{1,5},{2,6},{3,7},{4,0},{5,1},{6,2},{7,3},{8,12},{9,13},{10,... | collective-permute-start | bytes 399368 | tf_op jit(solution)/shard_map/ppermute | solution.py:411
  83.4 6.2 %collective-permute-start.17 = (bf16[128,640]{1,0:T(8,128)(2,1)S(1)}, bf16[128,640]{1,0:T(8,128)(2,1)S(1)}, u32[]{:S(2)}, u32[]{:S(2)}) collective-permute-start(bf16[128,640]{1,0:T(8,128)(2,1)S(1)} %get-tuple-element.223), channel_id=1, source_target_pairs={{0,8},{1,9},{2,10},{3,11},{4,12},{5,13},{6,14},{7,15},{8,0},{9,1},... | collective-permute-start | bytes 491528 | tf_op jit(solution)/shard_map/ppermute | solution.py:411
  86.0 13.9 %collective-permute-start.20 = (bf16[104,640]{1,0:T(8,128)(2,1)S(1)}, bf16[104,640]{1,0:T(8,128)(2,1)S(1)}, u32[]{:S(2)}, u32[]{:S(2)}) collective-permute-start(bf16[104,640]{1,0:T(8,128)(2,1)S(1)} %add_convert_fusion.9), channel_id=1, source_target_pairs={{0,16},{1,17},{2,18},{3,19},{4,20},{5,21},{6,22},{7,23},{8,24},{9,... | collective-permute-start | bytes 399368 | tf_op jit(solution)/shard_map/ppermute | solution.py:411
  89.6 5.7 %collective-permute-start.21 = (bf16[120,640]{1,0:T(8,128)(2,1)S(1)}, bf16[120,640]{1,0:T(8,128)(2,1)S(1)}, u32[]{:S(2)}, u32[]{:S(2)}) collective-permute-start(bf16[120,640]{1,0:T(8,128)(2,1)S(1)} %get-tuple-element.227), channel_id=1, source_target_pairs={{0,2},{1,3},{2,0},{3,1},{4,6},{5,7},{6,4},{7,5},{8,10},{9,11},{10,... | collective-permute-start | bytes 460808 | tf_op jit(solution)/shard_map/ppermute | solution.py:411
  92.2 12.9 %collective-permute-start.19 = (bf16[128,640]{1,0:T(8,128)(2,1)S(1)}, bf16[128,640]{1,0:T(8,128)(2,1)S(1)}, u32[]{:S(2)}, u32[]{:S(2)}) collective-permute-start(bf16[128,640]{1,0:T(8,128)(2,1)S(1)} %add_convert_fusion.1), channel_id=1, source_target_pairs={{0,16},{1,17},{2,18},{3,19},{4,20},{5,21},{6,22},{7,23},{8,24},{9,... | collective-permute-start | bytes 491528 | tf_op jit(solution)/shard_map/ppermute | solution.py:411
  95.4 12.2 %collective-permute-start.25 = (bf16[120,640]{1,0:T(8,128)(2,1)S(1)}, bf16[120,640]{1,0:T(8,128)(2,1)S(1)}, u32[]{:S(2)}, u32[]{:S(2)}) collective-permute-start(bf16[120,640]{1,0:T(8,128)(2,1)S(1)} %add_convert_fusion.5), channel_id=1, source_target_pairs={{0,16},{1,17},{2,18},{3,19},{4,20},{5,21},{6,22},{7,23},{8,24},{9,... | collective-permute-start | bytes 460808 | tf_op jit(solution)/shard_map/ppermute | solution.py:411
  100.0 6.1 %collective-permute-start.22 = (bf16[104,640]{1,0:T(8,128)(2,1)S(1)}, bf16[104,640]{1,0:T(8,128)(2,1)S(1)}, u32[]{:S(2)}, u32[]{:S(2)}) collective-permute-start(bf16[104,640]{1,0:T(8,128)(2,1)S(1)} %add_convert_fusion.8), channel_id=1, source_target_pairs={{0,4},{1,5},{2,6},{3,7},{4,0},{5,1},{6,2},{7,3},{8,12},{9,13},{10,... | collective-permute-start | bytes 399368 | tf_op jit(solution)/shard_map/ppermute | solution.py:411
  105.1 5.4 %collective-permute-start.28 = (bf16[128,640]{1,0:T(8,128)(2,1)S(1)}, bf16[128,640]{1,0:T(8,128)(2,1)S(1)}, u32[]{:S(2)}, u32[]{:S(2)}) collective-permute-start(bf16[128,640]{1,0:T(8,128)(2,1)S(1)} %add_convert_fusion), channel_id=1, source_target_pairs={{0,8},{1,9},{2,10},{3,11},{4,12},{5,13},{6,14},{7,15},{8,0},{9,1},... | collective-permute-start | bytes 491528 | tf_op jit(solution)/shard_map/ppermute | solution.py:411
  107.7 7.0 %collective-permute-start.27 = (bf16[120,640]{1,0:T(8,128)(2,1)S(1)}, bf16[120,640]{1,0:T(8,128)(2,1)S(1)}, u32[]{:S(2)}, u32[]{:S(2)}) collective-permute-start(bf16[120,640]{1,0:T(8,128)(2,1)S(1)} %add_convert_fusion.4), channel_id=1, source_target_pairs={{0,2},{1,3},{2,0},{3,1},{4,6},{5,7},{6,4},{7,5},{8,10},{9,11},{10,... | collective-permute-start | bytes 460808 | tf_op jit(solution)/shard_map/ppermute | solution.py:411
  109.0 8.5 %collective-permute-start.26 = (bf16[208,640]{1,0:T(8,128)(2,1)S(1)}, bf16[208,640]{1,0:T(8,128)(2,1)S(1)}, u32[]{:S(2)}, u32[]{:S(2)}) collective-permute-start(bf16[208,640]{1,0:T(8,128)(2,1)S(1)} %pad_maximum_fusion.8), channel_id=1, source_target_pairs={{0,2},{1,3},{2,0},{3,1},{4,6},{5,7},{6,4},{7,5},{8,10},{9,11},{10,... | collective-permute-start | bytes 798728 | tf_op jit(solution)/shard_map/ppermute | solution.py:411
  110.6 7.7 %collective-permute-start.30 = (bf16[256,640]{1,0:T(8,128)(2,1)S(1)}, bf16[256,640]{1,0:T(8,128)(2,1)S(1)}, u32[]{:S(2)}, u32[]{:S(2)}) collective-permute-start(bf16[256,640]{1,0:T(8,128)(2,1)S(1)} %pad_maximum_fusion.6), channel_id=1, source_target_pairs={{0,4},{1,5},{2,6},{3,7},{4,0},{5,1},{6,2},{7,3},{8,12},{9,13},{10,... | collective-permute-start | bytes 983048 | tf_op jit(solution)/shard_map/ppermute | solution.py:411
  114.7 10.2 %collective-permute-start.29 = (bf16[240,640]{1,0:T(8,128)(2,1)S(1)}, bf16[240,640]{1,0:T(8,128)(2,1)S(1)}, u32[]{:S(2)}, u32[]{:S(2)}) collective-permute-start(bf16[240,640]{1,0:T(8,128)(2,1)S(1)} %pad_maximum_fusion.7), channel_id=1, source_target_pairs={{0,8},{1,9},{2,10},{3,11},{4,12},{5,13},{6,14},{7,15},{8,0},{9,1},... | collective-permute-start | bytes 921608 | tf_op jit(solution)/shard_map/ppermute | solution.py:411
  117.6 14.6 %collective-permute-start.33 = (bf16[416,640]{1,0:T(8,128)(2,1)S(1)}, bf16[416,640]{1,0:T(8,128)(2,1)S(1)}, u32[]{:S(2)}, u32[]{:S(2)}) collective-permute-start(bf16[416,640]{1,0:T(8,128)(2,1)S(1)} %pad_maximum_fusion.5), channel_id=1, source_target_pairs={{0,8},{1,9},{2,10},{3,11},{4,12},{5,13},{6,14},{7,15},{8,0},{9,1},... | collective-permute-start | bytes 1597448 | tf_op jit(solution)/shard_map/ppermute | solution.py:411
  118.5 13.9 %collective-permute-start.32 = (bf16[512,640]{1,0:T(8,128)(2,1)S(1)}, bf16[512,640]{1,0:T(8,128)(2,1)S(1)}, u32[]{:S(2)}, u32[]{:S(2)}) collective-permute-start(bf16[512,640]{1,0:T(8,128)(2,1)S(1)} %pad_maximum_fusion.3), channel_id=1, source_target_pairs={{0,2},{1,3},{2,0},{3,1},{4,6},{5,7},{6,4},{7,5},{8,10},{9,11},{10,... | collective-permute-start | bytes 1966088 | tf_op jit(solution)/shard_map/ppermute | solution.py:411
  125.0 10.2 %collective-permute-start.31 = (bf16[480,640]{1,0:T(8,128)(2,1)S(1)}, bf16[480,640]{1,0:T(8,128)(2,1)S(1)}, u32[]{:S(2)}, u32[]{:S(2)}) collective-permute-start(bf16[480,640]{1,0:T(8,128)(2,1)S(1)} %pad_maximum_fusion.4), channel_id=1, source_target_pairs={{0,4},{1,5},{2,6},{3,7},{4,0},{5,1},{6,2},{7,3},{8,12},{9,13},{10,... | collective-permute-start | bytes 1843208 | tf_op jit(solution)/shard_map/ppermute | solution.py:411
  132.7 3.3 %collective-permute-start.34 = (bf16[1024,640]{1,0:T(8,128)(2,1)S(1)}, bf16[1024,640]{1,0:T(8,128)(2,1)S(1)}, u32[]{:S(2)}, u32[]{:S(2)}) collective-permute-start(bf16[1024,640]{1,0:T(8,128)(2,1)S(1)} %pad_maximum_fusion.kept.kept_second), channel_id=1, source_target_pairs={{0,1},{1,0},{2,3},{3,2},{4,5},{5,4},{6,7},{7,6},{8,9},{9,8},{10,11... | collective-permute-start | bytes 3932168 | tf_op jit(solution)/shard_map/ppermute | solution.py:411
  135.5 3.0 %collective-permute-start.35 = (bf16[960,640]{1,0:T(8,128)(2,1)S(1)}, bf16[960,640]{1,0:T(8,128)(2,1)S(1)}, u32[]{:S(2)}, u32[]{:S(2)}) collective-permute-start(bf16[960,640]{1,0:T(8,128)(2,1)S(1)} %pad_maximum_fusion.1.kept), channel_id=1, source_target_pairs={{0,1},{1,0},{2,3},{3,2},{4,5},{5,4},{6,7},{7,6},{8,9},{9,8},{10,11... | collective-permute-start | bytes 3686408 | tf_op jit(solution)/shard_map/ppermute | solution.py:411
  135.6 5.8 %collective-permute-start.36 = (bf16[832,640]{1,0:T(8,128)(2,1)S(1)}, bf16[832,640]{1,0:T(8,128)(2,1)S(1)}, u32[]{:S(2)}, u32[]{:S(2)}) collective-permute-start(bf16[832,640]{1,0:T(8,128)(2,1)S(1)} %pad_maximum_fusion.2.kept), channel_id=1, source_target_pairs={{0,1},{1,0},{2,3},{3,2},{4,5},{5,4},{6,7},{7,6},{8,9},{9,8},{10,11... | collective-permute-start | bytes 3194888 | tf_op jit(solution)/shard_map/ppermute | solution.py:411

commit v5 on v4

--- a/solution.py
+++ b/solution.py
@@ -346,28 +346,19 @@
     put_matrix(expand_out, lambda part: (source, part * width), misc_out[...].astype(F32), 0, width)
 
 
-def finish_first_body(dims, place, kept, got, misc_ref, reduce_out, decode_out):
+def finish_rest_body(dims, place, kept, got, kept_second, got_second, kept_third, got_third, misc_ref, reduce_out, decode_out, disco_out):
     hidden_units, outs, taps_count, width = dims
-    source = Joined(place[1], kept, got)
+    first, second = Joined(place[1], kept, got), Joined(place[1], kept_second, got_second)
+    third = Joined(place[1], kept_third, got_third)
     misc = misc_ref[...].astype(F32)
+    base = hidden_units // width * width
     at = sum(misc_rows(hidden_units, width))
-    at = put_matrix(reduce_out, lambda part: (source, part * width), misc, at, width)
-    at += sum(misc_rows(taps_count, width))
-    for offset, value in source.parts(hidden_units // width * width, outs):
+    at = put_matrix(reduce_out, lambda part: (first, part * width), misc, at, width)
+    at = put_matrix(disco_out, lambda part: (third, (part - 1) * width) if part else (second, base), misc, at, width)
+    for offset, value in first.parts(base, outs):
         decode_out[offset : offset + value.shape[0], :width] = value
     turned = jnp.swapaxes(misc[at : at + 8], 0, 1)
     decode_out[:, width:] = turned[:outs, : decode_out.shape[1] - width].astype(BF16)
-
-
-def finish_third_body(dims, place, kept_second, got_second, kept, got, misc_ref, disco_out):
-    hidden_units, width = dims
-    second, third = Joined(place[1], kept_second, got_second), Joined(place[1], kept, got)
-    first = hidden_units // width * width
-    put_matrix(
-        disco_out,
-        lambda part: (third, (part - 1) * width) if part else (second, first),
-        misc_ref[...].astype(F32), 2 * sum(misc_rows(hidden_units, width)), width,
-    )
 
 
 def collect_body(dims, hidden_grad, w_disco, stencil, out, left_out, right_out):
@@ -634,19 +625,12 @@
         smem=1,
         name="finish_second",
     )
-    reduce_grad_t, decode_grad_t = vmem_call(
-        functools.partial(finish_first_body, (hidden_units, outs, taps_count, width)),
-        [(reduce_t.shape, BF16), (decode_t.shape, BF16)],
-        [place, first.kept, first.got, misc],
+    reduce_grad_t, decode_grad_t, disco_grad_t = vmem_call(
+        functools.partial(finish_rest_body, (hidden_units, outs, taps_count, width)),
+        [(reduce_t.shape, BF16), (decode_t.shape, BF16), (disco_t.shape, BF16)],
+        [place, first.kept, first.got, second.kept, second.got, third.kept, third.got, misc],
         smem=1,
-        name="finish_first",
-    )
-    (disco_grad_t,) = vmem_call(
-        functools.partial(finish_third_body, (hidden_units, width)),
-        [(disco_t.shape, BF16)],
-        [place, second.kept, second.got, third.kept, third.got, misc],
-        smem=1,
-        name="finish_third",
+        name="finish_rest",
     )
     return jnp.swapaxes(latent_grad, 1, 2), disco_grad_t.T, grad_expand, reduce_grad_t.T, decode_grad_t.T
 

time: 144 us -> 142 us (0.986)
  Pallas kernels: 41.4 us -> 39.7 us
    ppermute x4, starting transfers between devices: 4.17 us -> 6.08 us  [shifted(): return lax.ppermute(x, axis, [(i, (i + by) % size) for i in range(size)])]
    ppermute x4, waiting for transfers between devices: 0.01 us -> 1.88 us  [shifted(): return lax.ppermute(x, axis, [(i, (i + by) % size) for i in range(size)])]
    pallas_call x18 -> x17, Pallas kernels: 41.4 us -> 39.7 us  [vmem_call(): pl.pallas_call(body, out_shape=[jax.ShapeDtypeStruct(shape, dtype) for sh...]
    ppermute x27, waiting for transfers between devices: 43.3 us -> 41.7 us  [swap(): return lax.ppermute(x, ('member', 'lon'), perm)]
  transfers between devices with their start and end apart: 37 -> 37, of which waited for: 21 -> 21; matrix products, arithmetic and copies ran while one was open for 5% -> 5% of each run, Pallas kernels for 19% -> 17%
where the time goes in v5:
time: 142 us
  waiting for transfers between devices  49.6 us (35%)
  starting transfers between devices  41 us (29%)
  Pallas kernels  39.7 us (28%)
  other arithmetic  6.33 us (4%)
  local copies, waits for them, and re-layouts  4.08 us (3%)
    ppermute x27, waiting for transfers between devices, swap(): return lax.ppermute(x, ('member', 'lon'), perm)  41.7 us
    pallas_call x17, Pallas kernels, vmem_call(): pl.pallas_call(body, out_shape=[jax.ShapeDtypeStruct(shape, dtype) for sh...  39.7 us
    ppermute x27, starting transfers between devices, swap(): return lax.ppermute(x, ('member', 'lon'), perm)  26 us
    ppermute x6, starting transfers between devices, exchanged(): lax.ppermute(piece_of(d), axis, [(i, i ^ d) for i in range(size)])  8.9 us
    ppermute x4, starting transfers between devices, shifted(): return lax.ppermute(x, axis, [(i, (i + by) % size) for i in range(size)])  6.08 us
    ppermute x6, waiting for transfers between devices, exchanged(): lax.ppermute(piece_of(d), axis, [(i, i ^ d) for i in range(size)])  6.04 us
    convert_element_type x9, other arithmetic, add_rounded(): return (a.astype(F32) + b.astype(F32)).astype(BF16)  3.45 us
    unnamed x22, local copies, waits for them, and re-layouts  3.25 us
  transfers between devices with their start and end apart: 37, of which 21 were waited for; matrix products, arithmetic and copies ran while one was open for 5% of the time, Pallas kernels for 17%

profile of v5, /device:TPU:0, one launch (start us, length us, event | category | flops | bytes accessed | tf_op | source)
XLA Modules:
  0.0 141.8 jit_solution(1342544345546450507)
XLA Ops:
  0.7 1.2 copy.38.latent
  2.0 3.4 %collective-permute-start.1 = (bf16[2,3,4,641]{3,1,2,0:T(4,128)(2,1)S(1)}, bf16[2,3,4,641]{3,1,2,0:T(4,128)(2,1)S(1)}, u32[]{:S(2)}, u32[]{:S(2)}) collective-permute-start(bf16[2,3,4,641]{3,1,2,0:T(4,128)(2,1)S(1)} %get-tuple-element.231), channel_id=1, source_target_pairs={{0,7},{1,0},{2,1},{3,2},{4,3},{5,4},{6,5},{7,6},{8,15},{9,8},{10,9... | collective-permute-start | bytes 92312 | tf_op jit(solution)/shard_map/ppermute | solution.py:477
  6.1 1.6 %prepare.1 = (bf16[768,256]{1,0:T(8,128)(2,1)S(1)}, f32[16,641]{1,0:T(8,128)S(1)}) custom-call(s32[2]{0:T(128)S(1)} %copy-done.6, s32[4]{0:T(128)S(1)} %copy-done.7, f32[3136]{0:T(1024)S(1)} %reshape.22.basis, bf16[64,641]{1,0:T(8,128)(2,1)S(1)} %copy-done.5), custom_call_target="tpu_custom_call" | custom-call | bytes 4194304 | tf_op jit(solution)/shard_map/prepare/pallas_call | solution.py:37
  7.9 1.9 %collective-permute-done = bf16[2,3,4,641]{3,1,2,0:T(4,128)(2,1)S(1)} collective-permute-done((bf16[2,3,4,641]{3,1,2,0:T(4,128)(2,1)S(1)}, bf16[2,3,4,641]{3,1,2,0:T(4,128)(2,1)S(1)}, u32[]{:S(2)}, u32[]{:S(2)}) %collective-permute-start) | collective-permute-done | bytes 30800 | tf_op jit(solution)/shard_map/ppermute | solution.py:477
  9.8 2.0 %copy-done = bf16[2564,641]{0,1:T(8,128)(2,1)S(1)} copy-done((bf16[2564,641]{0,1:T(8,128)(2,1)S(1)}, bf16[2564,641]{0,1:T(8,128)(2,1)}, u32[]{:S(2)}) %copy-start) | copy-done | bytes 3287072
  11.7 5.5 %forward.1 = (bf16[384,2688]{1,0:T(8,128)(2,1)S(1)}, bf16[384,641]{1,0:T(8,128)(2,1)S(1)}, bf16[384,1282]{1,0:T(8,128)(2,1)S(1)}, f32[384,1282]{1,0:T(8,128)S(1)}) custom-call(s32[6]{0:T(128)S(1)} %stack.27.place, bf16[2,4,45,641]{3,2,1,0:T(8,128)(2,1)S(1)} %copy.38.latent, bf16[2,4,3,641]{3,2,1,0:T(4,128)(2,1)S(1)} %bitcast.30, ...), custom_call_target="tpu_custom_call" | custom-call | bytes 25165824 | tf_op jit(solution)/shard_map/forward/pallas_call | solution.py:37
  17.3 2.3 %fields.1 = (bf16[384,641]{1,0:T(8,128)(2,1)S(1)}, bf16[80,384]{1,0:T(8,128)(2,1)S(1)}, bf16[80,384]{1,0:T(8,128)(2,1)S(1)}, bf16[80,384]{1,0:T(8,128)(2,1)S(1)}, bf16[80,384]{1,0:T(8,128)(2,1)S(1)}) custom-call(s32[6]{0:T(128)S(1)} %stack.27.place, bf16[384,641]{1,0:T(8,128)(2,1)S(1)} %get-tuple-element.113.hidden_in.hidden.refs_6_, ...), custom_call_target="tpu_custom_call" | custom-call | bytes 6291456 | tf_op jit(solution)/shard_map/fields/pallas_call | solution.py:37
  19.5 1.6 %collective-permute-start.2 = (bf16[80,384]{1,0:T(8,128)(2,1)S(1)}, bf16[80,384]{1,0:T(8,128)(2,1)S(1)}, u32[]{:S(2)}, u32[]{:S(2)}) collective-permute-start(bf16[80,384]{1,0:T(8,128)(2,1)S(1)} %get-tuple-element.116), channel_id=1, source_target_pairs={{0,8},{8,0},{16,24},{24,16},{1,9},{9,1},{17,25},{25,17},{2,10},{10... | collective-permute-start | bytes 184328 | tf_op jit(solution)/shard_map/ppermute | solution.py:482
  21.2 2.6 %collective-permute-start.3 = (bf16[80,384]{1,0:T(8,128)(2,1)S(1)}, bf16[80,384]{1,0:T(8,128)(2,1)S(1)}, u32[]{:S(2)}, u32[]{:S(2)}) collective-permute-start(bf16[80,384]{1,0:T(8,128)(2,1)S(1)} %get-tuple-element.117), channel_id=1, source_target_pairs={{0,16},{8,24},{16,0},{24,8},{1,17},{9,25},{17,1},{25,9},{2,18},{10... | collective-permute-start | bytes 184328 | tf_op jit(solution)/shard_map/ppermute | solution.py:482
  24.1 2.9 %slopes.1 = (bf16[384,1282]{1,0:T(8,128)(2,1)S(1)}, bf16[656,384]{1,0:T(8,128)(2,1)S(1)}) custom-call(f32[384,1282]{1,0:T(8,128)S(1)} %get-tuple-element.119.pre_in, bf16[384,641]{1,0:T(8,128)(2,1)S(1)} %get-tuple-element.113.hidden_in.hidden.refs_6_), custom_call_target="tpu_custom_call" | custom-call | tf_op jit(solution)/shard_map/slopes/pallas_call | solution.py:37
  27.0 0.6 collective-permute-done.3.refs_2_
  27.6 2.6 %collective-permute-done.4.refs_3_ = bf16[80,384]{1,0:T(8,128)(2,1)S(1)} collective-permute-done((bf16[80,384]{1,0:T(8,128)(2,1)S(1)}, bf16[80,384]{1,0:T(8,128)(2,1)S(1)}, u32[]{:S(2)}, u32[]{:S(2)}) %collective-permute-start.4) | collective-permute-done | bytes 61472 | tf_op jit(solution)/shard_map/ppermute | solution.py:482
  30.2 0.9 crps.1
  31.1 1.0 collective-permute-start.6
  32.1 3.4 %collective-permute-start.7 = (bf16[80,384]{1,0:T(8,128)(2,1)S(1)}, bf16[80,384]{1,0:T(8,128)(2,1)S(1)}, u32[]{:S(2)}, u32[]{:S(2)}) collective-permute-start(bf16[80,384]{1,0:T(8,128)(2,1)S(1)} %get-tuple-element.126), channel_id=1, source_target_pairs={{0,24},{8,16},{16,8},{24,0},{1,25},{9,17},{17,9},{25,1},{2,26},{10... | collective-permute-start | bytes 184328 | tf_op jit(solution)/shard_map/ppermute | solution.py:482
  35.5 0.8 collective-permute-done.6.refs_2_
  36.3 2.0 %collective-permute-done.7.refs_3_ = bf16[80,384]{1,0:T(8,128)(2,1)S(1)} collective-permute-done((bf16[80,384]{1,0:T(8,128)(2,1)S(1)}, bf16[80,384]{1,0:T(8,128)(2,1)S(1)}, u32[]{:S(2)}, u32[]{:S(2)}) %collective-permute-start.7) | collective-permute-done | bytes 61472 | tf_op jit(solution)/shard_map/ppermute | solution.py:482
  38.4 3.4 %first_products.1 = (bf16[832,640]{1,0:T(8,128)(2,1)S(1)}, bf16[832,640]{1,0:T(8,128)(2,1)S(1)}, bf16[384,641]{1,0:T(8,128)(2,1)S(1)}, bf16[656,384]{1,0:T(8,128)(2,1)S(1)}, bf16[288,384]{1,0:T(8,128)(2,1)S(1)}) custom-call(s32[6]{0:T(128)S(1)} %stack.27.place, bf16[80,384]{1,0:T(8,128)(2,1)S(1)} %get-tuple-element.123.refs_0_, ...), custom_call_target="tpu_custom_call" | custom-call | bytes 9437184 | tf_op jit(solution)/shard_map/first_products/pallas_call | solution.py:37
  41.8 5.9 %second_products.1 = (bf16[1024,640]{1,0:T(8,128)(2,1)S(1)}, bf16[1024,640]{1,0:T(8,128)(2,1)S(1)}, bf16[384,641]{1,0:T(8,128)(2,1)S(1)}, bf16[656,384]{1,0:T(8,128)(2,1)S(1)}) custom-call(s32[6]{0:T(128)S(1)} %stack.27.place, bf16[384,641]{1,0:T(8,128)(2,1)S(1)} %get-tuple-element.131.refs_0_, bf16[656,384]{1,0:T(8,128)(2,1)S(1)} %get-tuple-element.132.refs_1_, ...), custom_call_target="tpu_custom_call" | custom-call | tf_op jit(solution)/shard_map/second_products/pallas_call | solution.py:37
  48.2 0.8 combine.6
  49.0 3.1 %third_products.1 = (bf16[960,640]{1,0:T(8,128)(2,1)S(1)}, bf16[960,640]{1,0:T(8,128)(2,1)S(1)}) custom-call(s32[6]{0:T(128)S(1)} %stack.27.place, bf16[656,384]{1,0:T(8,128)(2,1)S(1)} %get-tuple-element.140.left, bf16[384,2688]{1,0:T(8,128)(2,1)S(1)} %get-tuple-element.136.refs_10_.right), custom_call_target="tpu_custom_call" | custom-call | tf_op jit(solution)/shard_map/third_products/pallas_call | solution.py:37
  52.3 0.9 combine.7
  53.2 0.6 collective-permute-start.13
  53.9 1.3 collective-permute-start.9
  55.2 0.8 combine.8
  56.0 1.8 %collective-permute-start.12 = (bf16[480,640]{1,0:T(8,128)(2,1)S(1)}, bf16[480,640]{1,0:T(8,128)(2,1)S(1)}, u32[]{:S(2)}, u32[]{:S(2)}) collective-permute-start(bf16[480,640]{1,0:T(8,128)(2,1)S(1)} %get-tuple-element.153), channel_id=1, source_target_pairs={{0,4},{1,5},{2,6},{3,7},{4,0},{5,1},{6,2},{7,3},{8,12},{9,13},{10,... | collective-permute-start | bytes 1843208 | tf_op jit(solution)/shard_map/ppermute | solution.py:402
  57.8 3.4 %collect.1 = (f32[2,4,45,641]{3,2,1,0:T(8,128)S(1)}, f32[2,4,3,641]{3,2,1,0:T(4,128)S(1)}, f32[2,4,3,641]{3,2,1,0:T(4,128)S(1)}) custom-call(bf16[384,641]{1,0:T(8,128)(2,1)S(1)} %get-tuple-element.148.hidden_grad, bf16[641,2564]{1,0:T(8,128)(2,1)S(1)} %bitcast.23, bf16[768,256]{1,0:T(8,128)(2,1)S(1)} %get-tuple-element.111.stencil), custom_call_target="tpu_custom_call" | custom-call | tf_op jit(solution)/shard_map/collect/pallas_call | solution.py:37
  61.2 6.9 %collective-permute-done.9.got = bf16[416,640]{1,0:T(8,128)(2,1)S(1)} collective-permute-done((bf16[416,640]{1,0:T(8,128)(2,1)S(1)}, bf16[416,640]{1,0:T(8,128)(2,1)S(1)}, u32[]{:S(2)}, u32[]{:S(2)}) %collective-permute-start.9) | collective-permute-done | bytes 532512 | tf_op jit(solution)/shard_map/ppermute | solution.py:402
  68.1 1.3 combine.9
  69.4 1.5 %collective-permute-start.16 = (bf16[208,640]{1,0:T(8,128)(2,1)}, bf16[208,640]{1,0:T(8,128)(2,1)}, u32[]{:S(2)}, u32[]{:S(2)}) collective-permute-start(bf16[208,640]{1,0:T(8,128)(2,1)} %get-tuple-element.166), channel_id=1, source_target_pairs={{0,2},{1,3},{2,0},{3,1},{4,6},{5,7},{6,4},{7,5},{8,10},{9,11},{10,... | collective-permute-start | bytes 798728 | tf_op jit(solution)/shard_map/ppermute | solution.py:402
  70.8 0.7 combine.10
  71.6 0.7 collective-permute-start.15
  72.3 0.7 combine.11
  73.0 1.3 collective-permute-start.14
  74.4 2.6 %collective-permute-start.23 = (f32[2,4,3,641]{3,1,2,0:T(4,128)S(1)}, f32[2,4,3,641]{3,1,2,0:T(4,128)S(1)}, u32[]{:S(2)}, u32[]{:S(2)}) collective-permute-start(f32[2,4,3,641]{3,1,2,0:T(4,128)S(1)} %copy.26), channel_id=1, source_target_pairs={{0,7},{1,0},{2,1},{3,2},{4,3},{5,4},{6,5},{7,6},{8,15},{9,8},{10,9... | collective-permute-start | bytes 184616 | tf_op jit(solution)/shard_map/ppermute | solution.py:477
  77.4 1.0 add_convert_fusion.11
  78.4 2.0 %collective-permute-start.18 = (bf16[104,640]{1,0:T(8,128)(2,1)S(1)}, bf16[104,640]{1,0:T(8,128)(2,1)S(1)}, u32[]{:S(2)}, u32[]{:S(2)}) collective-permute-start(bf16[104,640]{1,0:T(8,128)(2,1)S(1)} %get-tuple-element.238), channel_id=1, source_target_pairs={{0,4},{1,5},{2,6},{3,7},{4,0},{5,1},{6,2},{7,3},{8,12},{9,13},{10,... | collective-permute-start | bytes 399368 | tf_op jit(solution)/shard_map/ppermute | solution.py:402
  80.4 2.3 %collective-permute-done.15 = bf16[256,640]{1,0:T(8,128)(2,1)} collective-permute-done((bf16[256,640]{1,0:T(8,128)(2,1)S(1)}, bf16[256,640]{1,0:T(8,128)(2,1)}, u32[]{:S(2)}, u32[]{:S(2)}) %collective-permute-start.15) | collective-permute-done | bytes 327712 | tf_op jit(solution)/shard_map/ppermute | solution.py:402
  82.7 1.1 add_convert_fusion.2
  83.9 1.1 add_convert_fusion.6
  85.0 3.7 %collective-permute-start.20 = (bf16[104,640]{1,0:T(8,128)(2,1)S(1)}, bf16[104,640]{1,0:T(8,128)(2,1)S(1)}, u32[]{:S(2)}, u32[]{:S(2)}) collective-permute-start(bf16[104,640]{1,0:T(8,128)(2,1)S(1)} %add_convert_fusion.9), channel_id=1, source_target_pairs={{0,16},{1,17},{2,18},{3,19},{4,20},{5,21},{6,22},{7,23},{8,24},{9,... | collective-permute-start | bytes 399368 | tf_op jit(solution)/shard_map/ppermute | solution.py:402
  88.7 1.9 %collective-permute-done.17 = bf16[128,640]{1,0:T(8,128)(2,1)S(1)} collective-permute-done((bf16[128,640]{1,0:T(8,128)(2,1)S(1)}, bf16[128,640]{1,0:T(8,128)(2,1)S(1)}, u32[]{:S(2)}, u32[]{:S(2)}) %collective-permute-start.17) | collective-permute-done | bytes 163872 | tf_op jit(solution)/shard_map/ppermute | solution.py:402
  90.6 2.2 %collective-permute-start.19 = (bf16[128,640]{1,0:T(8,128)(2,1)S(1)}, bf16[128,640]{1,0:T(8,128)(2,1)S(1)}, u32[]{:S(2)}, u32[]{:S(2)}) collective-permute-start(bf16[128,640]{1,0:T(8,128)(2,1)S(1)} %add_convert_fusion.1), channel_id=1, source_target_pairs={{0,16},{1,17},{2,18},{3,19},{4,20},{5,21},{6,22},{7,23},{8,24},{9,... | collective-permute-start | bytes 491528 | tf_op jit(solution)/shard_map/ppermute | solution.py:402
  92.8 1.1 collective-permute-done.21
  94.1 6.9 %collective-permute-done.20 = bf16[104,640]{1,0:T(8,128)(2,1)S(1)} collective-permute-done((bf16[104,640]{1,0:T(8,128)(2,1)S(1)}, bf16[104,640]{1,0:T(8,128)(2,1)S(1)}, u32[]{:S(2)}, u32[]{:S(2)}) %collective-permute-start.20) | collective-permute-done | bytes 133152 | tf_op jit(solution)/shard_map/ppermute | solution.py:402
  101.1 1.1 collective-permute-start.22
  102.2 2.1 %collective-permute-done.19 = bf16[128,640]{1,0:T(8,128)(2,1)S(1)} collective-permute-done((bf16[128,640]{1,0:T(8,128)(2,1)S(1)}, bf16[128,640]{1,0:T(8,128)(2,1)S(1)}, u32[]{:S(2)}, u32[]{:S(2)}) %collective-permute-start.19) | collective-permute-done | bytes 163872 | tf_op jit(solution)/shard_map/ppermute | solution.py:402
  104.4 1.7 %collective-permute-done.22 = bf16[104,640]{1,0:T(8,128)(2,1)S(1)} collective-permute-done((bf16[104,640]{1,0:T(8,128)(2,1)S(1)}, bf16[104,640]{1,0:T(8,128)(2,1)S(1)}, u32[]{:S(2)}, u32[]{:S(2)}) %collective-permute-start.22) | collective-permute-done | bytes 133152 | tf_op jit(solution)/shard_map/ppermute | solution.py:402
  106.1 1.5 %fusion.2 = bf16[2,45,4,641]{3,2,1,0:T(4,128)(2,1)} fusion(f32[2,4,3,641]{3,1,2,0:T(4,128)S(1)} %collective-permute-done.24, f32[2,4,3,641]{3,1,2,0:T(4,128)S(1)} %collective-permute-done.23, f32[2,4,45,641]{3,2,1,0:T(8,128)S(1)} %get-tuple-element.189), kind=kLoop, calls=%fused_computation.12 | loop fusion | flops 692280 | bytes 1507632 | tf_op jit(solution)/shard_map/transpose | solution.py:613
  108.3 1.7 %collective-permute-start.26 = (bf16[208,640]{1,0:T(8,128)(2,1)S(1)}, bf16[208,640]{1,0:T(8,128)(2,1)S(1)}, u32[]{:S(2)}, u32[]{:S(2)}) collective-permute-start(bf16[208,640]{1,0:T(8,128)(2,1)S(1)} %pad_maximum_fusion.8), channel_id=1, source_target_pairs={{0,2},{1,3},{2,0},{3,1},{4,6},{5,7},{6,4},{7,5},{8,10},{9,11},{10,... | collective-permute-start | bytes 798728 | tf_op jit(solution)/shard_map/ppermute | solution.py:402
  110.0 1.2 collective-permute-start.29
  111.2 1.8 %collective-permute-done.27 = bf16[120,640]{1,0:T(8,128)(2,1)S(1)} collective-permute-done((bf16[120,640]{1,0:T(8,128)(2,1)S(1)}, bf16[120,640]{1,0:T(8,128)(2,1)S(1)}, u32[]{:S(2)}, u32[]{:S(2)}) %collective-permute-start.27) | collective-permute-done | bytes 153632 | tf_op jit(solution)/shard_map/ppermute | solution.py:402
  113.1 1.0 collective-permute-start.32
  114.1 1.7 %collective-permute-done.26 = bf16[208,640]{1,0:T(8,128)(2,1)S(1)} collective-permute-done((bf16[208,640]{1,0:T(8,128)(2,1)S(1)}, bf16[208,640]{1,0:T(8,128)(2,1)S(1)}, u32[]{:S(2)}, u32[]{:S(2)}) %collective-permute-start.26) | collective-permute-done | bytes 266272 | tf_op jit(solution)/shard_map/ppermute | solution.py:402
  116.0 1.0 collective-permute-start.31
  117.3 1.1 collective-permute-start.30
  118.5 4.9 %collective-permute-done.32 = bf16[240,640]{1,0:T(8,128)(2,1)S(1)} collective-permute-done((bf16[240,640]{1,0:T(8,128)(2,1)S(1)}, bf16[240,640]{1,0:T(8,128)(2,1)S(1)}, u32[]{:S(2)}, u32[]{:S(2)}) %collective-permute-start.32) | collective-permute-done | bytes 307232 | tf_op jit(solution)/shard_map/ppermute | solution.py:402
  123.5 1.7 %collective-permute-start.34 = (bf16[480,640]{1,0:T(8,128)(2,1)S(1)}, bf16[480,640]{1,0:T(8,128)(2,1)S(1)}, u32[]{:S(2)}, u32[]{:S(2)}) collective-permute-start(bf16[480,640]{1,0:T(8,128)(2,1)S(1)} %pad_maximum_fusion.4), channel_id=1, source_target_pairs={{0,4},{1,5},{2,6},{3,7},{4,0},{5,1},{6,2},{7,3},{8,12},{9,13},{10,... | collective-permute-start | bytes 1843208 | tf_op jit(solution)/shard_map/ppermute | solution.py:402
  125.1 4.3 %collective-permute-done.31 = bf16[416,640]{1,0:T(8,128)(2,1)S(1)} collective-permute-done((bf16[416,640]{1,0:T(8,128)(2,1)S(1)}, bf16[416,640]{1,0:T(8,128)(2,1)S(1)}, u32[]{:S(2)}, u32[]{:S(2)}) %collective-permute-start.31) | collective-permute-done | bytes 532512 | tf_op jit(solution)/shard_map/ppermute | solution.py:402
  129.6 1.0 collective-permute-done.30
  131.0 2.7 %collective-permute-done.34 = bf16[480,640]{1,0:T(8,128)(2,1)S(1)} collective-permute-done((bf16[480,640]{1,0:T(8,128)(2,1)S(1)}, bf16[480,640]{1,0:T(8,128)(2,1)S(1)}, u32[]{:S(2)}, u32[]{:S(2)}) %collective-permute-start.34) | collective-permute-done | bytes 614432 | tf_op jit(solution)/shard_map/ppermute | solution.py:402
  134.5 2.1 %finish_second.1 = (bf16[641,1282]{1,0:T(8,128)(2,1)}, bf16[32,640]{1,0:T(8,128)(2,1)S(1)}) custom-call(s32[6]{0:T(128)S(1)} %stack.27.place, bf16[1024,640]{1,0:T(8,128)(2,1)S(1)} %pad_maximum_fusion.kept.kept_second, bf16[1024,640]{1,0:T(8,128)(2,1)S(1)} %collective-permute-done.35.got.got_second), custom_call_target="tpu_custom_call" | custom-call | tf_op jit(solution)/shard_map/finish_second/pallas_call | solution.py:37
  136.6 1.8 %collective-permute-done.33.got = bf16[832,640]{1,0:T(8,128)(2,1)S(1)} collective-permute-done((bf16[832,640]{1,0:T(8,128)(2,1)S(1)}, bf16[832,640]{1,0:T(8,128)(2,1)S(1)}, u32[]{:S(2)}, u32[]{:S(2)}) %collective-permute-start.33) | collective-permute-done | bytes 1064992 | tf_op jit(solution)/shard_map/ppermute | solution.py:402
  138.5 3.4 %finish_rest.1 = (bf16[641,1282]{1,0:T(8,128)(2,1)}, bf16[288,641]{1,0:T(8,128)(2,1)}, bf16[641,2564]{1,0:T(8,128)(2,1)}) custom-call(s32[6]{0:T(128)S(1)} %stack.27.place, bf16[832,640]{1,0:T(8,128)(2,1)S(1)} %pad_maximum_fusion.2.kept, bf16[832,640]{1,0:T(8,128)(2,1)S(1)} %collective-permute-done.33.got, ...), custom_call_target="tpu_custom_call" | custom-call | tf_op jit(solution)/shard_map/finish_rest/pallas_call | solution.py:37
  (86 shorter events, 5.5 us)
Async XLA Ops:
  0.6 4.7 %copy-start.8 = (bf16[4,45,288]{2,0,1:T(4,128)(2,1)S(1)}, bf16[4,45,288]{2,0,1:T(4,128)(2,1)}, u32[]{:S(2)}) copy-start(bf16[4,45,288]{2,0,1:T(4,128)(2,1)} %param.19) | copy-start | bytes 311044
  0.6 4.9 %copy-start.9 = (bf16[16,4,7,7]{0,1,3,2:T(4,128)(2,1)S(1)}, bf16[16,4,7,7]{0,1,3,2:T(4,128)(2,1)}, u32[]{:S(2)}) copy-start(bf16[16,4,7,7]{0,1,3,2:T(4,128)(2,1)} %param.14) | copy-start | bytes 18820
  0.7 5.5 %copy-start.7 = (s32[4]{0:T(128)S(1)}, s32[4]{0:T(128)}, u32[]{:S(2)}) copy-start(s32[4]{0:T(128)} %bands.1) | copy-start | bytes 52
  0.7 5.5 %copy-start.5 = (bf16[64,641]{1,0:T(8,128)(2,1)S(1)}, bf16[64,641]{1,0:T(8,128)(2,1)}, u32[]{:S(2)}) copy-start(bf16[64,641]{1,0:T(8,128)(2,1)} %table.1) | copy-start | bytes 246148
  0.7 5.5 %copy-start.6 = (s32[2]{0:T(128)S(1)}, s32[2]{0:T(128)}, u32[]{:S(2)}) copy-start(s32[2]{0:T(128)} %seeds.1) | copy-start | bytes 28
  1.9 7.9 %copy-start.2 = (bf16[641,1282]{1,0:T(8,128)(2,1)S(1)}, bf16[641,1282]{1,0:T(8,128)(2,1)}, u32[]{:S(2)}) copy-start(bf16[641,1282]{1,0:T(8,128)(2,1)} %refs_4_.1) | copy-start | bytes 4930576
  2.0 5.9 %collective-permute-start.1 = (bf16[2,3,4,641]{3,1,2,0:T(4,128)(2,1)S(1)}, bf16[2,3,4,641]{3,1,2,0:T(4,128)(2,1)S(1)}, u32[]{:S(2)}, u32[]{:S(2)}) collective-permute-start(bf16[2,3,4,641]{3,1,2,0:T(4,128)(2,1)S(1)} %get-tuple-element.231), channel_id=1, source_target_pairs={{0,7},{1,0},{2,1},{3,2},{4,3},{5,4},{6,5},{7,6},{8,15},{9,8},{10,9... | collective-permute-start | bytes 92312 | tf_op jit(solution)/shard_map/ppermute | solution.py:477
  5.3 4.4 %collective-permute-start = (bf16[2,3,4,641]{3,1,2,0:T(4,128)(2,1)S(1)}, bf16[2,3,4,641]{3,1,2,0:T(4,128)(2,1)S(1)}, u32[]{:S(2)}, u32[]{:S(2)}) collective-permute-start(bf16[2,3,4,641]{3,1,2,0:T(4,128)(2,1)S(1)} %get-tuple-element.232), channel_id=1, source_target_pairs={{0,1},{1,2},{2,3},{3,4},{4,5},{5,6},{6,7},{7,0},{8,9},{9,10},{10,1... | collective-permute-start | bytes 92312 | tf_op jit(solution)/shard_map/ppermute | solution.py:477
  9.8 2.0 %copy-start = (bf16[2564,641]{0,1:T(8,128)(2,1)S(1)}, bf16[2564,641]{0,1:T(8,128)(2,1)}, u32[]{:S(2)}) copy-start(bf16[2564,641]{0,1:T(8,128)(2,1)} %param.15) | copy-start | bytes 9861148
  11.7 5.5 %copy-start.3 = (bf16[1282,641]{0,1:T(8,128)(2,1)S(1)}, bf16[1282,641]{0,1:T(8,128)(2,1)}, u32[]{:S(2)}) copy-start(bf16[1282,641]{0,1:T(8,128)(2,1)} %param.17) | copy-start | bytes 4930576
  11.7 5.5 %copy-start.4 = (bf16[641,288]{0,1:T(8,128)(2,1)S(1)}, bf16[641,288]{0,1:T(8,128)(2,1)}, u32[]{:S(2)}) copy-start(bf16[641,288]{0,1:T(8,128)(2,1)} %param.18) | copy-start | bytes 1107652
  19.5 7.4 %collective-permute-start.2 = (bf16[80,384]{1,0:T(8,128)(2,1)S(1)}, bf16[80,384]{1,0:T(8,128)(2,1)S(1)}, u32[]{:S(2)}, u32[]{:S(2)}) collective-permute-start(bf16[80,384]{1,0:T(8,128)(2,1)S(1)} %get-tuple-element.116), channel_id=1, source_target_pairs={{0,8},{8,0},{16,24},{24,16},{1,9},{9,1},{17,25},{25,17},{2,10},{10... | collective-permute-start | bytes 184328 | tf_op jit(solution)/shard_map/ppermute | solution.py:482
  21.2 6.4 %collective-permute-start.3 = (bf16[80,384]{1,0:T(8,128)(2,1)S(1)}, bf16[80,384]{1,0:T(8,128)(2,1)S(1)}, u32[]{:S(2)}, u32[]{:S(2)}) collective-permute-start(bf16[80,384]{1,0:T(8,128)(2,1)S(1)} %get-tuple-element.117), channel_id=1, source_target_pairs={{0,16},{8,24},{16,0},{24,8},{1,17},{9,25},{17,1},{25,9},{2,18},{10... | collective-permute-start | bytes 184328 | tf_op jit(solution)/shard_map/ppermute | solution.py:482
  23.8 6.4 %collective-permute-start.4 = (bf16[80,384]{1,0:T(8,128)(2,1)S(1)}, bf16[80,384]{1,0:T(8,128)(2,1)S(1)}, u32[]{:S(2)}, u32[]{:S(2)}) collective-permute-start(bf16[80,384]{1,0:T(8,128)(2,1)S(1)} %get-tuple-element.118), channel_id=1, source_target_pairs={{0,24},{8,16},{16,8},{24,0},{1,25},{9,17},{17,9},{25,1},{2,26},{10... | collective-permute-start | bytes 184328 | tf_op jit(solution)/shard_map/ppermute | solution.py:482
  31.0 4.5 %collective-permute-start.5 = (bf16[80,384]{1,0:T(8,128)(2,1)S(1)}, bf16[80,384]{1,0:T(8,128)(2,1)S(1)}, u32[]{:S(2)}, u32[]{:S(2)}) collective-permute-start(bf16[80,384]{1,0:T(8,128)(2,1)S(1)} %get-tuple-element.124), channel_id=1, source_target_pairs={{0,8},{8,0},{16,24},{24,16},{1,9},{9,1},{17,25},{25,17},{2,10},{10... | collective-permute-start | bytes 184328 | tf_op jit(solution)/shard_map/ppermute | solution.py:482
  31.1 5.2 %collective-permute-start.6 = (bf16[80,384]{1,0:T(8,128)(2,1)S(1)}, bf16[80,384]{1,0:T(8,128)(2,1)S(1)}, u32[]{:S(2)}, u32[]{:S(2)}) collective-permute-start(bf16[80,384]{1,0:T(8,128)(2,1)S(1)} %get-tuple-element.125), channel_id=1, source_target_pairs={{0,16},{8,24},{16,0},{24,8},{1,17},{9,25},{17,1},{25,9},{2,18},{10... | collective-permute-start | bytes 184328 | tf_op jit(solution)/shard_map/ppermute | solution.py:482
  32.1 6.2 %collective-permute-start.7 = (bf16[80,384]{1,0:T(8,128)(2,1)S(1)}, bf16[80,384]{1,0:T(8,128)(2,1)S(1)}, u32[]{:S(2)}, u32[]{:S(2)}) collective-permute-start(bf16[80,384]{1,0:T(8,128)(2,1)S(1)} %get-tuple-element.126), channel_id=1, source_target_pairs={{0,24},{8,16},{16,8},{24,0},{1,25},{9,17},{17,9},{25,1},{2,26},{10... | collective-permute-start | bytes 184328 | tf_op jit(solution)/shard_map/ppermute | solution.py:482
  41.7 6.5 %collective-permute-start.8 = (bf16[832,640]{1,0:T(8,128)(2,1)S(1)}, bf16[832,640]{1,0:T(8,128)(2,1)S(1)}, u32[]{:S(2)}, u32[]{:S(2)}) collective-permute-start(bf16[832,640]{1,0:T(8,128)(2,1)S(1)} %get-tuple-element.129), channel_id=1, source_target_pairs={{0,1},{1,0},{2,3},{3,2},{4,5},{5,4},{6,7},{7,6},{8,9},{9,8},{10,11... | collective-permute-start | bytes 3194888 | tf_op jit(solution)/shard_map/ppermute | solution.py:402
  47.7 4.6 %collective-permute-start.11 = (bf16[1024,640]{1,0:T(8,128)(2,1)S(1)}, bf16[1024,640]{1,0:T(8,128)(2,1)S(1)}, u32[]{:S(2)}, u32[]{:S(2)}) collective-permute-start(bf16[1024,640]{1,0:T(8,128)(2,1)S(1)} %get-tuple-element.144), channel_id=1, source_target_pairs={{0,1},{1,0},{2,3},{3,2},{4,5},{5,4},{6,7},{7,6},{8,9},{9,8},{10,11... | collective-permute-start | bytes 3932168 | tf_op jit(solution)/shard_map/ppermute | solution.py:402
  52.2 3.0 %collective-permute-start.10 = (bf16[960,640]{1,0:T(8,128)(2,1)S(1)}, bf16[960,640]{1,0:T(8,128)(2,1)S(1)}, u32[]{:S(2)}, u32[]{:S(2)}) collective-permute-start(bf16[960,640]{1,0:T(8,128)(2,1)S(1)} %get-tuple-element.142), channel_id=1, source_target_pairs={{0,1},{1,0},{2,3},{3,2},{4,5},{5,4},{6,7},{7,6},{8,9},{9,8},{10,11... | collective-permute-start | bytes 3686408 | tf_op jit(solution)/shard_map/ppermute | solution.py:402
  52.3 5.5 %copy-start.1 = (bf16[2564,641]{0,1:T(8,128)(2,1)S(1)}, bf16[2564,641]{0,1:T(8,128)(2,1)}, u32[]{:S(2)}) copy-start(bf16[2564,641]{0,1:T(8,128)(2,1)} %param.15) | copy-start | bytes 9861148
  53.2 17.6 %collective-permute-start.13 = (bf16[512,640]{1,0:T(8,128)(2,1)S(1)}, bf16[512,640]{1,0:T(8,128)(2,1)S(1)}, u32[]{:S(2)}, u32[]{:S(2)}) collective-permute-start(bf16[512,640]{1,0:T(8,128)(2,1)S(1)} %get-tuple-element.155), channel_id=1, source_target_pairs={{0,2},{1,3},{2,0},{3,1},{4,6},{5,7},{6,4},{7,5},{8,10},{9,11},{10,... | collective-permute-start | bytes 1966088 | tf_op jit(solution)/shard_map/ppermute | solution.py:402
  53.9 14.2 %collective-permute-start.9 = (bf16[416,640]{1,0:T(8,128)(2,1)S(1)}, bf16[416,640]{1,0:T(8,128)(2,1)S(1)}, u32[]{:S(2)}, u32[]{:S(2)}) collective-permute-start(bf16[416,640]{1,0:T(8,128)(2,1)S(1)} %get-tuple-element.130), channel_id=1, source_target_pairs={{0,8},{1,9},{2,10},{3,11},{4,12},{5,13},{6,14},{7,15},{8,0},{9,1},... | collective-permute-start | bytes 1597448 | tf_op jit(solution)/shard_map/ppermute | solution.py:402
  56.0 16.3 %collective-permute-start.12 = (bf16[480,640]{1,0:T(8,128)(2,1)S(1)}, bf16[480,640]{1,0:T(8,128)(2,1)S(1)}, u32[]{:S(2)}, u32[]{:S(2)}) collective-permute-start(bf16[480,640]{1,0:T(8,128)(2,1)S(1)} %get-tuple-element.153), channel_id=1, source_target_pairs={{0,4},{1,5},{2,6},{3,7},{4,0},{5,1},{6,2},{7,3},{8,12},{9,13},{10,... | collective-permute-start | bytes 1843208 | tf_op jit(solution)/shard_map/ppermute | solution.py:402
  69.4 8.0 %collective-permute-start.16 = (bf16[208,640]{1,0:T(8,128)(2,1)}, bf16[208,640]{1,0:T(8,128)(2,1)}, u32[]{:S(2)}, u32[]{:S(2)}) collective-permute-start(bf16[208,640]{1,0:T(8,128)(2,1)} %get-tuple-element.166), channel_id=1, source_target_pairs={{0,2},{1,3},{2,0},{3,1},{4,6},{5,7},{6,4},{7,5},{8,10},{9,11},{10,... | collective-permute-start | bytes 798728 | tf_op jit(solution)/shard_map/ppermute | solution.py:402
  71.6 11.1 %collective-permute-start.15 = (bf16[256,640]{1,0:T(8,128)(2,1)S(1)}, bf16[256,640]{1,0:T(8,128)(2,1)}, u32[]{:S(2)}, u32[]{:S(2)}) collective-permute-start(bf16[256,640]{1,0:T(8,128)(2,1)S(1)} %get-tuple-element.164), channel_id=1, source_target_pairs={{0,4},{1,5},{2,6},{3,7},{4,0},{5,1},{6,2},{7,3},{8,12},{9,13},{10,... | collective-permute-start | bytes 983048 | tf_op jit(solution)/shard_map/ppermute | solution.py:402
  73.0 10.8 %collective-permute-start.14 = (bf16[240,640]{1,0:T(8,128)(2,1)S(1)}, bf16[240,640]{1,0:T(8,128)(2,1)}, u32[]{:S(2)}, u32[]{:S(2)}) collective-permute-start(bf16[240,640]{1,0:T(8,128)(2,1)S(1)} %get-tuple-element.162), channel_id=1, source_target_pairs={{0,8},{1,9},{2,10},{3,11},{4,12},{5,13},{6,14},{7,15},{8,0},{9,1},... | collective-permute-start | bytes 921608 | tf_op jit(solution)/shard_map/ppermute | solution.py:402
  74.4 30.1 %collective-permute-start.24 = (f32[2,4,3,641]{3,1,2,0:T(4,128)S(1)}, f32[2,4,3,641]{3,1,2,0:T(4,128)S(1)}, u32[]{:S(2)}, u32[]{:S(2)}) collective-permute-start(f32[2,4,3,641]{3,1,2,0:T(4,128)S(1)} %copy.27), channel_id=1, source_target_pairs={{0,1},{1,2},{2,3},{3,4},{4,5},{5,6},{6,7},{7,0},{8,9},{9,10},{10,1... | collective-permute-start | bytes 184616 | tf_op jit(solution)/shard_map/ppermute | solution.py:477
  74.4 30.0 %collective-permute-start.23 = (f32[2,4,3,641]{3,1,2,0:T(4,128)S(1)}, f32[2,4,3,641]{3,1,2,0:T(4,128)S(1)}, u32[]{:S(2)}, u32[]{:S(2)}) collective-permute-start(f32[2,4,3,641]{3,1,2,0:T(4,128)S(1)} %copy.26), channel_id=1, source_target_pairs={{0,7},{1,0},{2,1},{3,2},{4,3},{5,4},{6,5},{7,6},{8,15},{9,8},{10,9... | collective-permute-start | bytes 184616 | tf_op jit(solution)/shard_map/ppermute | solution.py:477
  78.4 6.5 %collective-permute-start.18 = (bf16[104,640]{1,0:T(8,128)(2,1)S(1)}, bf16[104,640]{1,0:T(8,128)(2,1)S(1)}, u32[]{:S(2)}, u32[]{:S(2)}) collective-permute-start(bf16[104,640]{1,0:T(8,128)(2,1)S(1)} %get-tuple-element.238), channel_id=1, source_target_pairs={{0,4},{1,5},{2,6},{3,7},{4,0},{5,1},{6,2},{7,3},{8,12},{9,13},{10,... | collective-permute-start | bytes 399368 | tf_op jit(solution)/shard_map/ppermute | solution.py:402
  83.8 6.8 %collective-permute-start.17 = (bf16[128,640]{1,0:T(8,128)(2,1)S(1)}, bf16[128,640]{1,0:T(8,128)(2,1)S(1)}, u32[]{:S(2)}, u32[]{:S(2)}) collective-permute-start(bf16[128,640]{1,0:T(8,128)(2,1)S(1)} %get-tuple-element.225), channel_id=1, source_target_pairs={{0,8},{1,9},{2,10},{3,11},{4,12},{5,13},{6,14},{7,15},{8,0},{9,1},... | collective-permute-start | bytes 491528 | tf_op jit(solution)/shard_map/ppermute | solution.py:402
  85.0 16.0 %collective-permute-start.20 = (bf16[104,640]{1,0:T(8,128)(2,1)S(1)}, bf16[104,640]{1,0:T(8,128)(2,1)S(1)}, u32[]{:S(2)}, u32[]{:S(2)}) collective-permute-start(bf16[104,640]{1,0:T(8,128)(2,1)S(1)} %add_convert_fusion.9), channel_id=1, source_target_pairs={{0,16},{1,17},{2,18},{3,19},{4,20},{5,21},{6,22},{7,23},{8,24},{9,... | collective-permute-start | bytes 399368 | tf_op jit(solution)/shard_map/ppermute | solution.py:402
  88.7 5.2 %collective-permute-start.21 = (bf16[120,640]{1,0:T(8,128)(2,1)S(1)}, bf16[120,640]{1,0:T(8,128)(2,1)S(1)}, u32[]{:S(2)}, u32[]{:S(2)}) collective-permute-start(bf16[120,640]{1,0:T(8,128)(2,1)S(1)} %get-tuple-element.229), channel_id=1, source_target_pairs={{0,2},{1,3},{2,0},{3,1},{4,6},{5,7},{6,4},{7,5},{8,10},{9,11},{10,... | collective-permute-start | bytes 460808 | tf_op jit(solution)/shard_map/ppermute | solution.py:402
  90.6 13.7 %collective-permute-start.19 = (bf16[128,640]{1,0:T(8,128)(2,1)S(1)}, bf16[128,640]{1,0:T(8,128)(2,1)S(1)}, u32[]{:S(2)}, u32[]{:S(2)}) collective-permute-start(bf16[128,640]{1,0:T(8,128)(2,1)S(1)} %add_convert_fusion.1), channel_id=1, source_target_pairs={{0,16},{1,17},{2,18},{3,19},{4,20},{5,21},{6,22},{7,23},{8,24},{9,... | collective-permute-start | bytes 491528 | tf_op jit(solution)/shard_map/ppermute | solution.py:402
  93.9 13.7 %collective-permute-start.25 = (bf16[120,640]{1,0:T(8,128)(2,1)S(1)}, bf16[120,640]{1,0:T(8,128)(2,1)S(1)}, u32[]{:S(2)}, u32[]{:S(2)}) collective-permute-start(bf16[120,640]{1,0:T(8,128)(2,1)S(1)} %add_convert_fusion.5), channel_id=1, source_target_pairs={{0,16},{1,17},{2,18},{3,19},{4,20},{5,21},{6,22},{7,23},{8,24},{9,... | collective-permute-start | bytes 460808 | tf_op jit(solution)/shard_map/ppermute | solution.py:402
  101.1 5.1 %collective-permute-start.22 = (bf16[104,640]{1,0:T(8,128)(2,1)S(1)}, bf16[104,640]{1,0:T(8,128)(2,1)S(1)}, u32[]{:S(2)}, u32[]{:S(2)}) collective-permute-start(bf16[104,640]{1,0:T(8,128)(2,1)S(1)} %add_convert_fusion.8), channel_id=1, source_target_pairs={{0,4},{1,5},{2,6},{3,7},{4,0},{5,1},{6,2},{7,3},{8,12},{9,13},{10,... | collective-permute-start | bytes 399368 | tf_op jit(solution)/shard_map/ppermute | solution.py:402
  104.3 5.6 %collective-permute-start.28 = (bf16[128,640]{1,0:T(8,128)(2,1)S(1)}, bf16[128,640]{1,0:T(8,128)(2,1)S(1)}, u32[]{:S(2)}, u32[]{:S(2)}) collective-permute-start(bf16[128,640]{1,0:T(8,128)(2,1)S(1)} %add_convert_fusion), channel_id=1, source_target_pairs={{0,8},{1,9},{2,10},{3,11},{4,12},{5,13},{6,14},{7,15},{8,0},{9,1},... | collective-permute-start | bytes 491528 | tf_op jit(solution)/shard_map/ppermute | solution.py:402
  107.7 5.3 %collective-permute-start.27 = (bf16[120,640]{1,0:T(8,128)(2,1)S(1)}, bf16[120,640]{1,0:T(8,128)(2,1)S(1)}, u32[]{:S(2)}, u32[]{:S(2)}) collective-permute-start(bf16[120,640]{1,0:T(8,128)(2,1)S(1)} %add_convert_fusion.4), channel_id=1, source_target_pairs={{0,2},{1,3},{2,0},{3,1},{4,6},{5,7},{6,4},{7,5},{8,10},{9,11},{10,... | collective-permute-start | bytes 460808 | tf_op jit(solution)/shard_map/ppermute | solution.py:402
  108.3 7.6 %collective-permute-start.26 = (bf16[208,640]{1,0:T(8,128)(2,1)S(1)}, bf16[208,640]{1,0:T(8,128)(2,1)S(1)}, u32[]{:S(2)}, u32[]{:S(2)}) collective-permute-start(bf16[208,640]{1,0:T(8,128)(2,1)S(1)} %pad_maximum_fusion.8), channel_id=1, source_target_pairs={{0,2},{1,3},{2,0},{3,1},{4,6},{5,7},{6,4},{7,5},{8,10},{9,11},{10,... | collective-permute-start | bytes 798728 | tf_op jit(solution)/shard_map/ppermute | solution.py:402
  110.0 7.2 %collective-permute-start.29 = (bf16[256,640]{1,0:T(8,128)(2,1)S(1)}, bf16[256,640]{1,0:T(8,128)(2,1)S(1)}, u32[]{:S(2)}, u32[]{:S(2)}) collective-permute-start(bf16[256,640]{1,0:T(8,128)(2,1)S(1)} %pad_maximum_fusion.6), channel_id=1, source_target_pairs={{0,4},{1,5},{2,6},{3,7},{4,0},{5,1},{6,2},{7,3},{8,12},{9,13},{10,... | collective-permute-start | bytes 983048 | tf_op jit(solution)/shard_map/ppermute | solution.py:402
  113.1 10.3 %collective-permute-start.32 = (bf16[240,640]{1,0:T(8,128)(2,1)S(1)}, bf16[240,640]{1,0:T(8,128)(2,1)S(1)}, u32[]{:S(2)}, u32[]{:S(2)}) collective-permute-start(bf16[240,640]{1,0:T(8,128)(2,1)S(1)} %pad_maximum_fusion.7), channel_id=1, source_target_pairs={{0,8},{1,9},{2,10},{3,11},{4,12},{5,13},{6,14},{7,15},{8,0},{9,1},... | collective-permute-start | bytes 921608 | tf_op jit(solution)/shard_map/ppermute | solution.py:402
  116.0 13.5 %collective-permute-start.31 = (bf16[416,640]{1,0:T(8,128)(2,1)S(1)}, bf16[416,640]{1,0:T(8,128)(2,1)S(1)}, u32[]{:S(2)}, u32[]{:S(2)}) collective-permute-start(bf16[416,640]{1,0:T(8,128)(2,1)S(1)} %pad_maximum_fusion.5), channel_id=1, source_target_pairs={{0,8},{1,9},{2,10},{3,11},{4,12},{5,13},{6,14},{7,15},{8,0},{9,1},... | collective-permute-start | bytes 1597448 | tf_op jit(solution)/shard_map/ppermute | solution.py:402
  117.3 13.3 %collective-permute-start.30 = (bf16[512,640]{1,0:T(8,128)(2,1)S(1)}, bf16[512,640]{1,0:T(8,128)(2,1)S(1)}, u32[]{:S(2)}, u32[]{:S(2)}) collective-permute-start(bf16[512,640]{1,0:T(8,128)(2,1)S(1)} %pad_maximum_fusion.3), channel_id=1, source_target_pairs={{0,2},{1,3},{2,0},{3,1},{4,6},{5,7},{6,4},{7,5},{8,10},{9,11},{10,... | collective-permute-start | bytes 1966088 | tf_op jit(solution)/shard_map/ppermute | solution.py:402
  123.5 10.2 %collective-permute-start.34 = (bf16[480,640]{1,0:T(8,128)(2,1)S(1)}, bf16[480,640]{1,0:T(8,128)(2,1)S(1)}, u32[]{:S(2)}, u32[]{:S(2)}) collective-permute-start(bf16[480,640]{1,0:T(8,128)(2,1)S(1)} %pad_maximum_fusion.4), channel_id=1, source_target_pairs={{0,4},{1,5},{2,6},{3,7},{4,0},{5,1},{6,2},{7,3},{8,12},{9,13},{10,... | collective-permute-start | bytes 1843208 | tf_op jit(solution)/shard_map/ppermute | solution.py:402
  130.9 3.6 %collective-permute-start.35 = (bf16[1024,640]{1,0:T(8,128)(2,1)S(1)}, bf16[1024,640]{1,0:T(8,128)(2,1)S(1)}, u32[]{:S(2)}, u32[]{:S(2)}) collective-permute-start(bf16[1024,640]{1,0:T(8,128)(2,1)S(1)} %pad_maximum_fusion.kept.kept_second), channel_id=1, source_target_pairs={{0,1},{1,0},{2,3},{3,2},{4,5},{5,4},{6,7},{7,6},{8,9},{9,8},{10,11... | collective-permute-start | bytes 3932168 | tf_op jit(solution)/shard_map/ppermute | solution.py:402
  133.9 4.5 %collective-permute-start.36 = (bf16[960,640]{1,0:T(8,128)(2,1)S(1)}, bf16[960,640]{1,0:T(8,128)(2,1)S(1)}, u32[]{:S(2)}, u32[]{:S(2)}) collective-permute-start(bf16[960,640]{1,0:T(8,128)(2,1)S(1)} %pad_maximum_fusion.1.kept_third), channel_id=1, source_target_pairs={{0,1},{1,0},{2,3},{3,2},{4,5},{5,4},{6,7},{7,6},{8,9},{9,8},{10,11... | collective-permute-start | bytes 3686408 | tf_op jit(solution)/shard_map/ppermute | solution.py:402
  134.0 4.4 %collective-permute-start.33 = (bf16[832,640]{1,0:T(8,128)(2,1)S(1)}, bf16[832,640]{1,0:T(8,128)(2,1)S(1)}, u32[]{:S(2)}, u32[]{:S(2)}) collective-permute-start(bf16[832,640]{1,0:T(8,128)(2,1)S(1)} %pad_maximum_fusion.2.kept), channel_id=1, source_target_pairs={{0,1},{1,0},{2,3},{3,2},{4,5},{5,4},{6,7},{7,6},{8,9},{9,8},{10,11... | collective-permute-start | bytes 3194888 | tf_op jit(solution)/shard_map/ppermute | solution.py:402

commit v6 on v5

--- a/solution.py
+++ b/solution.py
@@ -615,7 +615,7 @@
         last = stream.advance(last)
     first.got, latent_grad = lax.optimization_barrier((first.got, latent_grad))
     while third.steps:
-        for stream in (first, second, third):
+        for stream in (second, first, third):
             if stream.steps:
                 last = stream.advance(last)
     grad_expand, misc = vmem_call(

time: 142 us -> 141 us (level)
  transfers between devices with their start and end apart: 37 -> 37, of which waited for: 21 -> 22; matrix products, arithmetic and copies ran while one was open for 5% -> 5% of each run, Pallas kernels for 17% -> 17%
where the time goes in v6:
time: 141 us
  waiting for transfers between devices  49 us (35%)
  starting transfers between devices  40.4 us (29%)
  Pallas kernels  39.7 us (28%)
  other arithmetic  6.28 us (4%)
  local copies, waits for them, and re-layouts  4.08 us (3%)
    ppermute x27, waiting for transfers between devices, swap(): return lax.ppermute(x, ('member', 'lon'), perm)  41 us
    pallas_call x17, Pallas kernels, vmem_call(): pl.pallas_call(body, out_shape=[jax.ShapeDtypeStruct(shape, dtype) for sh...  39.7 us
    ppermute x27, starting transfers between devices, swap(): return lax.ppermute(x, ('member', 'lon'), perm)  25.5 us
    ppermute x6, starting transfers between devices, exchanged(): lax.ppermute(piece_of(d), axis, [(i, i ^ d) for i in range(size)])  8.9 us
    ppermute x4, starting transfers between devices, shifted(): return lax.ppermute(x, axis, [(i, (i + by) % size) for i in range(size)])  6.08 us
    ppermute x6, waiting for transfers between devices, exchanged(): lax.ppermute(piece_of(d), axis, [(i, i ^ d) for i in range(size)])  6.04 us
    convert_element_type x9, other arithmetic, add_rounded(): return (a.astype(F32) + b.astype(F32)).astype(BF16)  3.45 us
    unnamed x22, local copies, waits for them, and re-layouts  3.25 us
  transfers between devices with their start and end apart: 37, of which 22 were waited for; matrix products, arithmetic and copies ran while one was open for 5% of the time, Pallas kernels for 17%

profile of v6, /device:TPU:0, one launch (start us, length us, event | category | flops | bytes accessed | tf_op | source)
XLA Modules:
  0.0 140.6 jit_solution(16649413323371157566)
XLA Ops:
  0.7 1.2 copy.38.latent
  2.0 3.4 %collective-permute-start.1 = (bf16[2,3,4,641]{3,1,2,0:T(4,128)(2,1)S(1)}, bf16[2,3,4,641]{3,1,2,0:T(4,128)(2,1)S(1)}, u32[]{:S(2)}, u32[]{:S(2)}) collective-permute-start(bf16[2,3,4,641]{3,1,2,0:T(4,128)(2,1)S(1)} %get-tuple-element.231), channel_id=1, source_target_pairs={{0,7},{1,0},{2,1},{3,2},{4,3},{5,4},{6,5},{7,6},{8,15},{9,8},{10,9... | collective-permute-start | bytes 92312 | tf_op jit(solution)/shard_map/ppermute | solution.py:477
  6.1 1.6 %prepare.1 = (bf16[768,256]{1,0:T(8,128)(2,1)S(1)}, f32[16,641]{1,0:T(8,128)S(1)}) custom-call(s32[2]{0:T(128)S(1)} %copy-done.6, s32[4]{0:T(128)S(1)} %copy-done.7, f32[3136]{0:T(1024)S(1)} %reshape.22.basis, bf16[64,641]{1,0:T(8,128)(2,1)S(1)} %copy-done.5), custom_call_target="tpu_custom_call" | custom-call | bytes 4194304 | tf_op jit(solution)/shard_map/prepare/pallas_call | solution.py:37
  7.9 1.9 %collective-permute-done = bf16[2,3,4,641]{3,1,2,0:T(4,128)(2,1)S(1)} collective-permute-done((bf16[2,3,4,641]{3,1,2,0:T(4,128)(2,1)S(1)}, bf16[2,3,4,641]{3,1,2,0:T(4,128)(2,1)S(1)}, u32[]{:S(2)}, u32[]{:S(2)}) %collective-permute-start) | collective-permute-done | bytes 30800 | tf_op jit(solution)/shard_map/ppermute | solution.py:477
  9.8 2.0 %copy-done = bf16[2564,641]{0,1:T(8,128)(2,1)S(1)} copy-done((bf16[2564,641]{0,1:T(8,128)(2,1)S(1)}, bf16[2564,641]{0,1:T(8,128)(2,1)}, u32[]{:S(2)}) %copy-start) | copy-done | bytes 3287072
  11.7 5.5 %forward.1 = (bf16[384,2688]{1,0:T(8,128)(2,1)S(1)}, bf16[384,641]{1,0:T(8,128)(2,1)S(1)}, bf16[384,1282]{1,0:T(8,128)(2,1)S(1)}, f32[384,1282]{1,0:T(8,128)S(1)}) custom-call(s32[6]{0:T(128)S(1)} %stack.27.place, bf16[2,4,45,641]{3,2,1,0:T(8,128)(2,1)S(1)} %copy.38.latent, bf16[2,4,3,641]{3,2,1,0:T(4,128)(2,1)S(1)} %bitcast.30, ...), custom_call_target="tpu_custom_call" | custom-call | bytes 25165824 | tf_op jit(solution)/shard_map/forward/pallas_call | solution.py:37
  17.3 2.3 %fields.1 = (bf16[384,641]{1,0:T(8,128)(2,1)S(1)}, bf16[80,384]{1,0:T(8,128)(2,1)S(1)}, bf16[80,384]{1,0:T(8,128)(2,1)S(1)}, bf16[80,384]{1,0:T(8,128)(2,1)S(1)}, bf16[80,384]{1,0:T(8,128)(2,1)S(1)}) custom-call(s32[6]{0:T(128)S(1)} %stack.27.place, bf16[384,641]{1,0:T(8,128)(2,1)S(1)} %get-tuple-element.113.hidden_in.hidden.refs_6_, ...), custom_call_target="tpu_custom_call" | custom-call | bytes 6291456 | tf_op jit(solution)/shard_map/fields/pallas_call | solution.py:37
  19.5 1.6 %collective-permute-start.2 = (bf16[80,384]{1,0:T(8,128)(2,1)S(1)}, bf16[80,384]{1,0:T(8,128)(2,1)S(1)}, u32[]{:S(2)}, u32[]{:S(2)}) collective-permute-start(bf16[80,384]{1,0:T(8,128)(2,1)S(1)} %get-tuple-element.116), channel_id=1, source_target_pairs={{0,8},{8,0},{16,24},{24,16},{1,9},{9,1},{17,25},{25,17},{2,10},{10... | collective-permute-start | bytes 184328 | tf_op jit(solution)/shard_map/ppermute | solution.py:482
  21.2 2.6 %collective-permute-start.3 = (bf16[80,384]{1,0:T(8,128)(2,1)S(1)}, bf16[80,384]{1,0:T(8,128)(2,1)S(1)}, u32[]{:S(2)}, u32[]{:S(2)}) collective-permute-start(bf16[80,384]{1,0:T(8,128)(2,1)S(1)} %get-tuple-element.117), channel_id=1, source_target_pairs={{0,16},{8,24},{16,0},{24,8},{1,17},{9,25},{17,1},{25,9},{2,18},{10... | collective-permute-start | bytes 184328 | tf_op jit(solution)/shard_map/ppermute | solution.py:482
  24.1 2.9 %slopes.1 = (bf16[384,1282]{1,0:T(8,128)(2,1)S(1)}, bf16[656,384]{1,0:T(8,128)(2,1)S(1)}) custom-call(f32[384,1282]{1,0:T(8,128)S(1)} %get-tuple-element.119.pre_in, bf16[384,641]{1,0:T(8,128)(2,1)S(1)} %get-tuple-element.113.hidden_in.hidden.refs_6_), custom_call_target="tpu_custom_call" | custom-call | tf_op jit(solution)/shard_map/slopes/pallas_call | solution.py:37
  27.0 0.6 collective-permute-done.3.refs_2_
  27.6 2.6 %collective-permute-done.4.refs_3_ = bf16[80,384]{1,0:T(8,128)(2,1)S(1)} collective-permute-done((bf16[80,384]{1,0:T(8,128)(2,1)S(1)}, bf16[80,384]{1,0:T(8,128)(2,1)S(1)}, u32[]{:S(2)}, u32[]{:S(2)}) %collective-permute-start.4) | collective-permute-done | bytes 61472 | tf_op jit(solution)/shard_map/ppermute | solution.py:482
  30.2 0.9 crps.1
  31.1 1.0 collective-permute-start.6
  32.1 3.4 %collective-permute-start.7 = (bf16[80,384]{1,0:T(8,128)(2,1)S(1)}, bf16[80,384]{1,0:T(8,128)(2,1)S(1)}, u32[]{:S(2)}, u32[]{:S(2)}) collective-permute-start(bf16[80,384]{1,0:T(8,128)(2,1)S(1)} %get-tuple-element.126), channel_id=1, source_target_pairs={{0,24},{8,16},{16,8},{24,0},{1,25},{9,17},{17,9},{25,1},{2,26},{10... | collective-permute-start | bytes 184328 | tf_op jit(solution)/shard_map/ppermute | solution.py:482
  35.5 0.8 collective-permute-done.6.refs_2_
  36.3 2.0 %collective-permute-done.7.refs_3_ = bf16[80,384]{1,0:T(8,128)(2,1)S(1)} collective-permute-done((bf16[80,384]{1,0:T(8,128)(2,1)S(1)}, bf16[80,384]{1,0:T(8,128)(2,1)S(1)}, u32[]{:S(2)}, u32[]{:S(2)}) %collective-permute-start.7) | collective-permute-done | bytes 61472 | tf_op jit(solution)/shard_map/ppermute | solution.py:482
  38.4 3.4 %first_products.1 = (bf16[832,640]{1,0:T(8,128)(2,1)S(1)}, bf16[832,640]{1,0:T(8,128)(2,1)S(1)}, bf16[384,641]{1,0:T(8,128)(2,1)S(1)}, bf16[656,384]{1,0:T(8,128)(2,1)S(1)}, bf16[288,384]{1,0:T(8,128)(2,1)S(1)}) custom-call(s32[6]{0:T(128)S(1)} %stack.27.place, bf16[80,384]{1,0:T(8,128)(2,1)S(1)} %get-tuple-element.123.refs_0_, ...), custom_call_target="tpu_custom_call" | custom-call | bytes 9437184 | tf_op jit(solution)/shard_map/first_products/pallas_call | solution.py:37
  41.8 5.9 %second_products.1 = (bf16[1024,640]{1,0:T(8,128)(2,1)S(1)}, bf16[1024,640]{1,0:T(8,128)(2,1)S(1)}, bf16[384,641]{1,0:T(8,128)(2,1)S(1)}, bf16[656,384]{1,0:T(8,128)(2,1)S(1)}) custom-call(s32[6]{0:T(128)S(1)} %stack.27.place, bf16[384,641]{1,0:T(8,128)(2,1)S(1)} %get-tuple-element.131.refs_0_, bf16[656,384]{1,0:T(8,128)(2,1)S(1)} %get-tuple-element.132.refs_1_, ...), custom_call_target="tpu_custom_call" | custom-call | tf_op jit(solution)/shard_map/second_products/pallas_call | solution.py:37
  47.7 0.6 collective-permute-start.11
  48.2 0.8 combine.6
  49.0 3.1 %third_products.1 = (bf16[960,640]{1,0:T(8,128)(2,1)S(1)}, bf16[960,640]{1,0:T(8,128)(2,1)S(1)}) custom-call(s32[6]{0:T(128)S(1)} %stack.27.place, bf16[656,384]{1,0:T(8,128)(2,1)S(1)} %get-tuple-element.140.left, bf16[384,2688]{1,0:T(8,128)(2,1)S(1)} %get-tuple-element.136.refs_10_.right), custom_call_target="tpu_custom_call" | custom-call | tf_op jit(solution)/shard_map/third_products/pallas_call | solution.py:37
  52.3 0.9 combine.7
  53.2 0.6 collective-permute-start.13
  53.9 1.3 collective-permute-start.9
  55.2 0.8 combine.8
  56.0 1.8 %collective-permute-start.12 = (bf16[480,640]{1,0:T(8,128)(2,1)S(1)}, bf16[480,640]{1,0:T(8,128)(2,1)S(1)}, u32[]{:S(2)}, u32[]{:S(2)}) collective-permute-start(bf16[480,640]{1,0:T(8,128)(2,1)S(1)} %get-tuple-element.153), channel_id=1, source_target_pairs={{0,4},{1,5},{2,6},{3,7},{4,0},{5,1},{6,2},{7,3},{8,12},{9,13},{10,... | collective-permute-start | bytes 1843208 | tf_op jit(solution)/shard_map/ppermute | solution.py:402
  57.8 3.4 %collect.1 = (f32[2,4,45,641]{3,2,1,0:T(8,128)S(1)}, f32[2,4,3,641]{3,2,1,0:T(4,128)S(1)}, f32[2,4,3,641]{3,2,1,0:T(4,128)S(1)}) custom-call(bf16[384,641]{1,0:T(8,128)(2,1)S(1)} %get-tuple-element.148.hidden_grad, bf16[641,2564]{1,0:T(8,128)(2,1)S(1)} %bitcast.23, bf16[768,256]{1,0:T(8,128)(2,1)S(1)} %get-tuple-element.111.stencil), custom_call_target="tpu_custom_call" | custom-call | tf_op jit(solution)/shard_map/collect/pallas_call | solution.py:37
  61.2 6.9 %collective-permute-done.9.got = bf16[416,640]{1,0:T(8,128)(2,1)S(1)} collective-permute-done((bf16[416,640]{1,0:T(8,128)(2,1)S(1)}, bf16[416,640]{1,0:T(8,128)(2,1)S(1)}, u32[]{:S(2)}, u32[]{:S(2)}) %collective-permute-start.9) | collective-permute-done | bytes 532512 | tf_op jit(solution)/shard_map/ppermute | solution.py:402
  68.1 1.3 combine.9
  69.4 1.5 %collective-permute-start.16 = (bf16[208,640]{1,0:T(8,128)(2,1)}, bf16[208,640]{1,0:T(8,128)(2,1)}, u32[]{:S(2)}, u32[]{:S(2)}) collective-permute-start(bf16[208,640]{1,0:T(8,128)(2,1)} %get-tuple-element.166), channel_id=1, source_target_pairs={{0,2},{1,3},{2,0},{3,1},{4,6},{5,7},{6,4},{7,5},{8,10},{9,11},{10,... | collective-permute-start | bytes 798728 | tf_op jit(solution)/shard_map/ppermute | solution.py:402
  70.8 0.7 combine.10
  71.6 0.7 collective-permute-start.15
  72.3 0.7 combine.11
  73.0 1.3 collective-permute-start.14
  74.4 2.6 %collective-permute-start.23 = (f32[2,4,3,641]{3,1,2,0:T(4,128)S(1)}, f32[2,4,3,641]{3,1,2,0:T(4,128)S(1)}, u32[]{:S(2)}, u32[]{:S(2)}) collective-permute-start(f32[2,4,3,641]{3,1,2,0:T(4,128)S(1)} %copy.26), channel_id=1, source_target_pairs={{0,7},{1,0},{2,1},{3,2},{4,3},{5,4},{6,5},{7,6},{8,15},{9,8},{10,9... | collective-permute-start | bytes 184616 | tf_op jit(solution)/shard_map/ppermute | solution.py:477
  77.4 1.0 add_convert_fusion.11
  78.4 2.0 %collective-permute-start.18 = (bf16[104,640]{1,0:T(8,128)(2,1)S(1)}, bf16[104,640]{1,0:T(8,128)(2,1)S(1)}, u32[]{:S(2)}, u32[]{:S(2)}) collective-permute-start(bf16[104,640]{1,0:T(8,128)(2,1)S(1)} %get-tuple-element.238), channel_id=1, source_target_pairs={{0,4},{1,5},{2,6},{3,7},{4,0},{5,1},{6,2},{7,3},{8,12},{9,13},{10,... | collective-permute-start | bytes 399368 | tf_op jit(solution)/shard_map/ppermute | solution.py:402
  80.4 2.3 %collective-permute-done.15 = bf16[256,640]{1,0:T(8,128)(2,1)} collective-permute-done((bf16[256,640]{1,0:T(8,128)(2,1)S(1)}, bf16[256,640]{1,0:T(8,128)(2,1)}, u32[]{:S(2)}, u32[]{:S(2)}) %collective-permute-start.15) | collective-permute-done | bytes 327712 | tf_op jit(solution)/shard_map/ppermute | solution.py:402
  82.7 1.1 add_convert_fusion.2
  83.9 1.1 add_convert_fusion.6
  85.0 3.7 %collective-permute-start.20 = (bf16[104,640]{1,0:T(8,128)(2,1)S(1)}, bf16[104,640]{1,0:T(8,128)(2,1)S(1)}, u32[]{:S(2)}, u32[]{:S(2)}) collective-permute-start(bf16[104,640]{1,0:T(8,128)(2,1)S(1)} %add_convert_fusion.9), channel_id=1, source_target_pairs={{0,16},{1,17},{2,18},{3,19},{4,20},{5,21},{6,22},{7,23},{8,24},{9,... | collective-permute-start | bytes 399368 | tf_op jit(solution)/shard_map/ppermute | solution.py:402
  88.7 1.9 %collective-permute-done.17 = bf16[128,640]{1,0:T(8,128)(2,1)S(1)} collective-permute-done((bf16[128,640]{1,0:T(8,128)(2,1)S(1)}, bf16[128,640]{1,0:T(8,128)(2,1)S(1)}, u32[]{:S(2)}, u32[]{:S(2)}) %collective-permute-start.17) | collective-permute-done | bytes 163872 | tf_op jit(solution)/shard_map/ppermute | solution.py:402
  90.6 2.2 %collective-permute-start.19 = (bf16[128,640]{1,0:T(8,128)(2,1)S(1)}, bf16[128,640]{1,0:T(8,128)(2,1)S(1)}, u32[]{:S(2)}, u32[]{:S(2)}) collective-permute-start(bf16[128,640]{1,0:T(8,128)(2,1)S(1)} %add_convert_fusion.1), channel_id=1, source_target_pairs={{0,16},{1,17},{2,18},{3,19},{4,20},{5,21},{6,22},{7,23},{8,24},{9,... | collective-permute-start | bytes 491528 | tf_op jit(solution)/shard_map/ppermute | solution.py:402
  92.8 1.1 collective-permute-done.21
  94.1 6.9 %collective-permute-done.20 = bf16[104,640]{1,0:T(8,128)(2,1)S(1)} collective-permute-done((bf16[104,640]{1,0:T(8,128)(2,1)S(1)}, bf16[104,640]{1,0:T(8,128)(2,1)S(1)}, u32[]{:S(2)}, u32[]{:S(2)}) %collective-permute-start.20) | collective-permute-done | bytes 133152 | tf_op jit(solution)/shard_map/ppermute | solution.py:402
  101.1 1.1 collective-permute-start.22
  102.2 2.1 %collective-permute-done.19 = bf16[128,640]{1,0:T(8,128)(2,1)S(1)} collective-permute-done((bf16[128,640]{1,0:T(8,128)(2,1)S(1)}, bf16[128,640]{1,0:T(8,128)(2,1)S(1)}, u32[]{:S(2)}, u32[]{:S(2)}) %collective-permute-start.19) | collective-permute-done | bytes 163872 | tf_op jit(solution)/shard_map/ppermute | solution.py:402
  104.4 1.7 %collective-permute-done.22 = bf16[104,640]{1,0:T(8,128)(2,1)S(1)} collective-permute-done((bf16[104,640]{1,0:T(8,128)(2,1)S(1)}, bf16[104,640]{1,0:T(8,128)(2,1)S(1)}, u32[]{:S(2)}, u32[]{:S(2)}) %collective-permute-start.22) | collective-permute-done | bytes 133152 | tf_op jit(solution)/shard_map/ppermute | solution.py:402
  106.1 1.5 %fusion.2 = bf16[2,45,4,641]{3,2,1,0:T(4,128)(2,1)} fusion(f32[2,4,3,641]{3,1,2,0:T(4,128)S(1)} %collective-permute-done.24, f32[2,4,3,641]{3,1,2,0:T(4,128)S(1)} %collective-permute-done.23, f32[2,4,45,641]{3,2,1,0:T(8,128)S(1)} %get-tuple-element.189), kind=kLoop, calls=%fused_computation.12 | loop fusion | flops 692280 | bytes 1507632 | tf_op jit(solution)/shard_map/transpose | solution.py:613
  108.3 1.7 %collective-permute-start.26 = (bf16[208,640]{1,0:T(8,128)(2,1)S(1)}, bf16[208,640]{1,0:T(8,128)(2,1)S(1)}, u32[]{:S(2)}, u32[]{:S(2)}) collective-permute-start(bf16[208,640]{1,0:T(8,128)(2,1)S(1)} %pad_maximum_fusion.8), channel_id=1, source_target_pairs={{0,2},{1,3},{2,0},{3,1},{4,6},{5,7},{6,4},{7,5},{8,10},{9,11},{10,... | collective-permute-start | bytes 798728 | tf_op jit(solution)/shard_map/ppermute | solution.py:402
  110.0 1.2 collective-permute-start.28
  111.2 1.8 %collective-permute-done.29 = bf16[120,640]{1,0:T(8,128)(2,1)S(1)} collective-permute-done((bf16[120,640]{1,0:T(8,128)(2,1)S(1)}, bf16[120,640]{1,0:T(8,128)(2,1)S(1)}, u32[]{:S(2)}, u32[]{:S(2)}) %collective-permute-start.29) | collective-permute-done | bytes 153632 | tf_op jit(solution)/shard_map/ppermute | solution.py:402
  113.1 1.0 collective-permute-start.30
  114.1 1.7 %collective-permute-done.26 = bf16[208,640]{1,0:T(8,128)(2,1)S(1)} collective-permute-done((bf16[208,640]{1,0:T(8,128)(2,1)S(1)}, bf16[208,640]{1,0:T(8,128)(2,1)S(1)}, u32[]{:S(2)}, u32[]{:S(2)}) %collective-permute-start.26) | collective-permute-done | bytes 266272 | tf_op jit(solution)/shard_map/ppermute | solution.py:402
  115.8 1.3 collective-permute-done.28
  117.3 1.1 collective-permute-start.33
  118.7 3.1 %collective-permute-done.30 = bf16[240,640]{1,0:T(8,128)(2,1)S(1)} collective-permute-done((bf16[240,640]{1,0:T(8,128)(2,1)S(1)}, bf16[240,640]{1,0:T(8,128)(2,1)S(1)}, u32[]{:S(2)}, u32[]{:S(2)}) %collective-permute-start.30) | collective-permute-done | bytes 307232 | tf_op jit(solution)/shard_map/ppermute | solution.py:402
  121.9 2.1 %collective-permute-start.31 = (bf16[480,640]{1,0:T(8,128)(2,1)S(1)}, bf16[480,640]{1,0:T(8,128)(2,1)S(1)}, u32[]{:S(2)}, u32[]{:S(2)}) collective-permute-start(bf16[480,640]{1,0:T(8,128)(2,1)S(1)} %pad_maximum_fusion.4), channel_id=1, source_target_pairs={{0,4},{1,5},{2,6},{3,7},{4,0},{5,1},{6,2},{7,3},{8,12},{9,13},{10,... | collective-permute-start | bytes 1843208 | tf_op jit(solution)/shard_map/ppermute | solution.py:402
  124.0 6.6 %collective-permute-done.33 = bf16[512,640]{1,0:T(8,128)(2,1)S(1)} collective-permute-done((bf16[512,640]{1,0:T(8,128)(2,1)S(1)}, bf16[512,640]{1,0:T(8,128)(2,1)S(1)}, u32[]{:S(2)}, u32[]{:S(2)}) %collective-permute-start.33) | collective-permute-done | bytes 655392 | tf_op jit(solution)/shard_map/ppermute | solution.py:402
  133.0 1.0 collective-permute-done.35.got.got_second
  134.0 2.1 %finish_second.1 = (bf16[641,1282]{1,0:T(8,128)(2,1)}, bf16[32,640]{1,0:T(8,128)(2,1)S(1)}) custom-call(s32[6]{0:T(128)S(1)} %stack.27.place, bf16[1024,640]{1,0:T(8,128)(2,1)S(1)} %pad_maximum_fusion.kept.kept_second, bf16[1024,640]{1,0:T(8,128)(2,1)S(1)} %collective-permute-done.35.got.got_second), custom_call_target="tpu_custom_call" | custom-call | tf_op jit(solution)/shard_map/finish_second/pallas_call | solution.py:37
  136.1 1.2 collective-permute-done.34.got
  137.3 3.4 %finish_rest.1 = (bf16[641,1282]{1,0:T(8,128)(2,1)}, bf16[288,641]{1,0:T(8,128)(2,1)}, bf16[641,2564]{1,0:T(8,128)(2,1)}) custom-call(s32[6]{0:T(128)S(1)} %stack.27.place, bf16[832,640]{1,0:T(8,128)(2,1)S(1)} %pad_maximum_fusion.2.kept, bf16[832,640]{1,0:T(8,128)(2,1)S(1)} %collective-permute-done.34.got, ...), custom_call_target="tpu_custom_call" | custom-call | tf_op jit(solution)/shard_map/finish_rest/pallas_call | solution.py:37
  (86 shorter events, 5.8 us)
Async XLA Ops:
  0.6 4.7 %copy-start.8 = (bf16[4,45,288]{2,0,1:T(4,128)(2,1)S(1)}, bf16[4,45,288]{2,0,1:T(4,128)(2,1)}, u32[]{:S(2)}) copy-start(bf16[4,45,288]{2,0,1:T(4,128)(2,1)} %param.19) | copy-start | bytes 311044
  0.6 4.9 %copy-start.9 = (bf16[16,4,7,7]{0,1,3,2:T(4,128)(2,1)S(1)}, bf16[16,4,7,7]{0,1,3,2:T(4,128)(2,1)}, u32[]{:S(2)}) copy-start(bf16[16,4,7,7]{0,1,3,2:T(4,128)(2,1)} %param.14) | copy-start | bytes 18820
  0.7 5.5 %copy-start.7 = (s32[4]{0:T(128)S(1)}, s32[4]{0:T(128)}, u32[]{:S(2)}) copy-start(s32[4]{0:T(128)} %bands.1) | copy-start | bytes 52
  0.7 5.5 %copy-start.5 = (bf16[64,641]{1,0:T(8,128)(2,1)S(1)}, bf16[64,641]{1,0:T(8,128)(2,1)}, u32[]{:S(2)}) copy-start(bf16[64,641]{1,0:T(8,128)(2,1)} %table.1) | copy-start | bytes 246148
  0.7 5.5 %copy-start.6 = (s32[2]{0:T(128)S(1)}, s32[2]{0:T(128)}, u32[]{:S(2)}) copy-start(s32[2]{0:T(128)} %seeds.1) | copy-start | bytes 28
  1.9 7.9 %copy-start.2 = (bf16[641,1282]{1,0:T(8,128)(2,1)S(1)}, bf16[641,1282]{1,0:T(8,128)(2,1)}, u32[]{:S(2)}) copy-start(bf16[641,1282]{1,0:T(8,128)(2,1)} %refs_4_.1) | copy-start | bytes 4930576
  2.0 5.9 %collective-permute-start.1 = (bf16[2,3,4,641]{3,1,2,0:T(4,128)(2,1)S(1)}, bf16[2,3,4,641]{3,1,2,0:T(4,128)(2,1)S(1)}, u32[]{:S(2)}, u32[]{:S(2)}) collective-permute-start(bf16[2,3,4,641]{3,1,2,0:T(4,128)(2,1)S(1)} %get-tuple-element.231), channel_id=1, source_target_pairs={{0,7},{1,0},{2,1},{3,2},{4,3},{5,4},{6,5},{7,6},{8,15},{9,8},{10,9... | collective-permute-start | bytes 92312 | tf_op jit(solution)/shard_map/ppermute | solution.py:477
  5.3 4.4 %collective-permute-start = (bf16[2,3,4,641]{3,1,2,0:T(4,128)(2,1)S(1)}, bf16[2,3,4,641]{3,1,2,0:T(4,128)(2,1)S(1)}, u32[]{:S(2)}, u32[]{:S(2)}) collective-permute-start(bf16[2,3,4,641]{3,1,2,0:T(4,128)(2,1)S(1)} %get-tuple-element.232), channel_id=1, source_target_pairs={{0,1},{1,2},{2,3},{3,4},{4,5},{5,6},{6,7},{7,0},{8,9},{9,10},{10,1... | collective-permute-start | bytes 92312 | tf_op jit(solution)/shard_map/ppermute | solution.py:477
  9.8 2.0 %copy-start = (bf16[2564,641]{0,1:T(8,128)(2,1)S(1)}, bf16[2564,641]{0,1:T(8,128)(2,1)}, u32[]{:S(2)}) copy-start(bf16[2564,641]{0,1:T(8,128)(2,1)} %param.15) | copy-start | bytes 9861148
  11.7 5.5 %copy-start.3 = (bf16[1282,641]{0,1:T(8,128)(2,1)S(1)}, bf16[1282,641]{0,1:T(8,128)(2,1)}, u32[]{:S(2)}) copy-start(bf16[1282,641]{0,1:T(8,128)(2,1)} %param.17) | copy-start | bytes 4930576
  11.7 5.5 %copy-start.4 = (bf16[641,288]{0,1:T(8,128)(2,1)S(1)}, bf16[641,288]{0,1:T(8,128)(2,1)}, u32[]{:S(2)}) copy-start(bf16[641,288]{0,1:T(8,128)(2,1)} %param.18) | copy-start | bytes 1107652
  19.5 7.4 %collective-permute-start.2 = (bf16[80,384]{1,0:T(8,128)(2,1)S(1)}, bf16[80,384]{1,0:T(8,128)(2,1)S(1)}, u32[]{:S(2)}, u32[]{:S(2)}) collective-permute-start(bf16[80,384]{1,0:T(8,128)(2,1)S(1)} %get-tuple-element.116), channel_id=1, source_target_pairs={{0,8},{8,0},{16,24},{24,16},{1,9},{9,1},{17,25},{25,17},{2,10},{10... | collective-permute-start | bytes 184328 | tf_op jit(solution)/shard_map/ppermute | solution.py:482
  21.2 6.4 %collective-permute-start.3 = (bf16[80,384]{1,0:T(8,128)(2,1)S(1)}, bf16[80,384]{1,0:T(8,128)(2,1)S(1)}, u32[]{:S(2)}, u32[]{:S(2)}) collective-permute-start(bf16[80,384]{1,0:T(8,128)(2,1)S(1)} %get-tuple-element.117), channel_id=1, source_target_pairs={{0,16},{8,24},{16,0},{24,8},{1,17},{9,25},{17,1},{25,9},{2,18},{10... | collective-permute-start | bytes 184328 | tf_op jit(solution)/shard_map/ppermute | solution.py:482
  23.8 6.4 %collective-permute-start.4 = (bf16[80,384]{1,0:T(8,128)(2,1)S(1)}, bf16[80,384]{1,0:T(8,128)(2,1)S(1)}, u32[]{:S(2)}, u32[]{:S(2)}) collective-permute-start(bf16[80,384]{1,0:T(8,128)(2,1)S(1)} %get-tuple-element.118), channel_id=1, source_target_pairs={{0,24},{8,16},{16,8},{24,0},{1,25},{9,17},{17,9},{25,1},{2,26},{10... | collective-permute-start | bytes 184328 | tf_op jit(solution)/shard_map/ppermute | solution.py:482
  31.0 4.5 %collective-permute-start.5 = (bf16[80,384]{1,0:T(8,128)(2,1)S(1)}, bf16[80,384]{1,0:T(8,128)(2,1)S(1)}, u32[]{:S(2)}, u32[]{:S(2)}) collective-permute-start(bf16[80,384]{1,0:T(8,128)(2,1)S(1)} %get-tuple-element.124), channel_id=1, source_target_pairs={{0,8},{8,0},{16,24},{24,16},{1,9},{9,1},{17,25},{25,17},{2,10},{10... | collective-permute-start | bytes 184328 | tf_op jit(solution)/shard_map/ppermute | solution.py:482
  31.1 5.2 %collective-permute-start.6 = (bf16[80,384]{1,0:T(8,128)(2,1)S(1)}, bf16[80,384]{1,0:T(8,128)(2,1)S(1)}, u32[]{:S(2)}, u32[]{:S(2)}) collective-permute-start(bf16[80,384]{1,0:T(8,128)(2,1)S(1)} %get-tuple-element.125), channel_id=1, source_target_pairs={{0,16},{8,24},{16,0},{24,8},{1,17},{9,25},{17,1},{25,9},{2,18},{10... | collective-permute-start | bytes 184328 | tf_op jit(solution)/shard_map/ppermute | solution.py:482
  32.1 6.2 %collective-permute-start.7 = (bf16[80,384]{1,0:T(8,128)(2,1)S(1)}, bf16[80,384]{1,0:T(8,128)(2,1)S(1)}, u32[]{:S(2)}, u32[]{:S(2)}) collective-permute-start(bf16[80,384]{1,0:T(8,128)(2,1)S(1)} %get-tuple-element.126), channel_id=1, source_target_pairs={{0,24},{8,16},{16,8},{24,0},{1,25},{9,17},{17,9},{25,1},{2,26},{10... | collective-permute-start | bytes 184328 | tf_op jit(solution)/shard_map/ppermute | solution.py:482
  41.7 6.5 %collective-permute-start.8 = (bf16[832,640]{1,0:T(8,128)(2,1)S(1)}, bf16[832,640]{1,0:T(8,128)(2,1)S(1)}, u32[]{:S(2)}, u32[]{:S(2)}) collective-permute-start(bf16[832,640]{1,0:T(8,128)(2,1)S(1)} %get-tuple-element.129), channel_id=1, source_target_pairs={{0,1},{1,0},{2,3},{3,2},{4,5},{5,4},{6,7},{7,6},{8,9},{9,8},{10,11... | collective-permute-start | bytes 3194888 | tf_op jit(solution)/shard_map/ppermute | solution.py:402
  47.7 4.6 %collective-permute-start.11 = (bf16[1024,640]{1,0:T(8,128)(2,1)S(1)}, bf16[1024,640]{1,0:T(8,128)(2,1)S(1)}, u32[]{:S(2)}, u32[]{:S(2)}) collective-permute-start(bf16[1024,640]{1,0:T(8,128)(2,1)S(1)} %get-tuple-element.144), channel_id=1, source_target_pairs={{0,1},{1,0},{2,3},{3,2},{4,5},{5,4},{6,7},{7,6},{8,9},{9,8},{10,11... | collective-permute-start | bytes 3932168 | tf_op jit(solution)/shard_map/ppermute | solution.py:402
  52.2 3.0 %collective-permute-start.10 = (bf16[960,640]{1,0:T(8,128)(2,1)S(1)}, bf16[960,640]{1,0:T(8,128)(2,1)S(1)}, u32[]{:S(2)}, u32[]{:S(2)}) collective-permute-start(bf16[960,640]{1,0:T(8,128)(2,1)S(1)} %get-tuple-element.142), channel_id=1, source_target_pairs={{0,1},{1,0},{2,3},{3,2},{4,5},{5,4},{6,7},{7,6},{8,9},{9,8},{10,11... | collective-permute-start | bytes 3686408 | tf_op jit(solution)/shard_map/ppermute | solution.py:402
  52.3 5.5 %copy-start.1 = (bf16[2564,641]{0,1:T(8,128)(2,1)S(1)}, bf16[2564,641]{0,1:T(8,128)(2,1)}, u32[]{:S(2)}) copy-start(bf16[2564,641]{0,1:T(8,128)(2,1)} %param.15) | copy-start | bytes 9861148
  53.2 17.6 %collective-permute-start.13 = (bf16[512,640]{1,0:T(8,128)(2,1)S(1)}, bf16[512,640]{1,0:T(8,128)(2,1)S(1)}, u32[]{:S(2)}, u32[]{:S(2)}) collective-permute-start(bf16[512,640]{1,0:T(8,128)(2,1)S(1)} %get-tuple-element.155), channel_id=1, source_target_pairs={{0,2},{1,3},{2,0},{3,1},{4,6},{5,7},{6,4},{7,5},{8,10},{9,11},{10,... | collective-permute-start | bytes 1966088 | tf_op jit(solution)/shard_map/ppermute | solution.py:402
  53.9 14.2 %collective-permute-start.9 = (bf16[416,640]{1,0:T(8,128)(2,1)S(1)}, bf16[416,640]{1,0:T(8,128)(2,1)S(1)}, u32[]{:S(2)}, u32[]{:S(2)}) collective-permute-start(bf16[416,640]{1,0:T(8,128)(2,1)S(1)} %get-tuple-element.130), channel_id=1, source_target_pairs={{0,8},{1,9},{2,10},{3,11},{4,12},{5,13},{6,14},{7,15},{8,0},{9,1},... | collective-permute-start | bytes 1597448 | tf_op jit(solution)/shard_map/ppermute | solution.py:402
  56.0 16.3 %collective-permute-start.12 = (bf16[480,640]{1,0:T(8,128)(2,1)S(1)}, bf16[480,640]{1,0:T(8,128)(2,1)S(1)}, u32[]{:S(2)}, u32[]{:S(2)}) collective-permute-start(bf16[480,640]{1,0:T(8,128)(2,1)S(1)} %get-tuple-element.153), channel_id=1, source_target_pairs={{0,4},{1,5},{2,6},{3,7},{4,0},{5,1},{6,2},{7,3},{8,12},{9,13},{10,... | collective-permute-start | bytes 1843208 | tf_op jit(solution)/shard_map/ppermute | solution.py:402
  69.4 8.0 %collective-permute-start.16 = (bf16[208,640]{1,0:T(8,128)(2,1)}, bf16[208,640]{1,0:T(8,128)(2,1)}, u32[]{:S(2)}, u32[]{:S(2)}) collective-permute-start(bf16[208,640]{1,0:T(8,128)(2,1)} %get-tuple-element.166), channel_id=1, source_target_pairs={{0,2},{1,3},{2,0},{3,1},{4,6},{5,7},{6,4},{7,5},{8,10},{9,11},{10,... | collective-permute-start | bytes 798728 | tf_op jit(solution)/shard_map/ppermute | solution.py:402
  71.6 11.1 %collective-permute-start.15 = (bf16[256,640]{1,0:T(8,128)(2,1)S(1)}, bf16[256,640]{1,0:T(8,128)(2,1)}, u32[]{:S(2)}, u32[]{:S(2)}) collective-permute-start(bf16[256,640]{1,0:T(8,128)(2,1)S(1)} %get-tuple-element.164), channel_id=1, source_target_pairs={{0,4},{1,5},{2,6},{3,7},{4,0},{5,1},{6,2},{7,3},{8,12},{9,13},{10,... | collective-permute-start | bytes 983048 | tf_op jit(solution)/shard_map/ppermute | solution.py:402
  73.0 10.8 %collective-permute-start.14 = (bf16[240,640]{1,0:T(8,128)(2,1)S(1)}, bf16[240,640]{1,0:T(8,128)(2,1)}, u32[]{:S(2)}, u32[]{:S(2)}) collective-permute-start(bf16[240,640]{1,0:T(8,128)(2,1)S(1)} %get-tuple-element.162), channel_id=1, source_target_pairs={{0,8},{1,9},{2,10},{3,11},{4,12},{5,13},{6,14},{7,15},{8,0},{9,1},... | collective-permute-start | bytes 921608 | tf_op jit(solution)/shard_map/ppermute | solution.py:402
  74.4 30.1 %collective-permute-start.24 = (f32[2,4,3,641]{3,1,2,0:T(4,128)S(1)}, f32[2,4,3,641]{3,1,2,0:T(4,128)S(1)}, u32[]{:S(2)}, u32[]{:S(2)}) collective-permute-start(f32[2,4,3,641]{3,1,2,0:T(4,128)S(1)} %copy.27), channel_id=1, source_target_pairs={{0,1},{1,2},{2,3},{3,4},{4,5},{5,6},{6,7},{7,0},{8,9},{9,10},{10,1... | collective-permute-start | bytes 184616 | tf_op jit(solution)/shard_map/ppermute | solution.py:477
  74.4 30.0 %collective-permute-start.23 = (f32[2,4,3,641]{3,1,2,0:T(4,128)S(1)}, f32[2,4,3,641]{3,1,2,0:T(4,128)S(1)}, u32[]{:S(2)}, u32[]{:S(2)}) collective-permute-start(f32[2,4,3,641]{3,1,2,0:T(4,128)S(1)} %copy.26), channel_id=1, source_target_pairs={{0,7},{1,0},{2,1},{3,2},{4,3},{5,4},{6,5},{7,6},{8,15},{9,8},{10,9... | collective-permute-start | bytes 184616 | tf_op jit(solution)/shard_map/ppermute | solution.py:477
  78.4 6.5 %collective-permute-start.18 = (bf16[104,640]{1,0:T(8,128)(2,1)S(1)}, bf16[104,640]{1,0:T(8,128)(2,1)S(1)}, u32[]{:S(2)}, u32[]{:S(2)}) collective-permute-start(bf16[104,640]{1,0:T(8,128)(2,1)S(1)} %get-tuple-element.238), channel_id=1, source_target_pairs={{0,4},{1,5},{2,6},{3,7},{4,0},{5,1},{6,2},{7,3},{8,12},{9,13},{10,... | collective-permute-start | bytes 399368 | tf_op jit(solution)/shard_map/ppermute | solution.py:402
  83.8 6.8 %collective-permute-start.17 = (bf16[128,640]{1,0:T(8,128)(2,1)S(1)}, bf16[128,640]{1,0:T(8,128)(2,1)S(1)}, u32[]{:S(2)}, u32[]{:S(2)}) collective-permute-start(bf16[128,640]{1,0:T(8,128)(2,1)S(1)} %get-tuple-element.225), channel_id=1, source_target_pairs={{0,8},{1,9},{2,10},{3,11},{4,12},{5,13},{6,14},{7,15},{8,0},{9,1},... | collective-permute-start | bytes 491528 | tf_op jit(solution)/shard_map/ppermute | solution.py:402
  85.0 16.0 %collective-permute-start.20 = (bf16[104,640]{1,0:T(8,128)(2,1)S(1)}, bf16[104,640]{1,0:T(8,128)(2,1)S(1)}, u32[]{:S(2)}, u32[]{:S(2)}) collective-permute-start(bf16[104,640]{1,0:T(8,128)(2,1)S(1)} %add_convert_fusion.9), channel_id=1, source_target_pairs={{0,16},{1,17},{2,18},{3,19},{4,20},{5,21},{6,22},{7,23},{8,24},{9,... | collective-permute-start | bytes 399368 | tf_op jit(solution)/shard_map/ppermute | solution.py:402
  88.7 5.2 %collective-permute-start.21 = (bf16[120,640]{1,0:T(8,128)(2,1)S(1)}, bf16[120,640]{1,0:T(8,128)(2,1)S(1)}, u32[]{:S(2)}, u32[]{:S(2)}) collective-permute-start(bf16[120,640]{1,0:T(8,128)(2,1)S(1)} %get-tuple-element.229), channel_id=1, source_target_pairs={{0,2},{1,3},{2,0},{3,1},{4,6},{5,7},{6,4},{7,5},{8,10},{9,11},{10,... | collective-permute-start | bytes 460808 | tf_op jit(solution)/shard_map/ppermute | solution.py:402
  90.6 13.7 %collective-permute-start.19 = (bf16[128,640]{1,0:T(8,128)(2,1)S(1)}, bf16[128,640]{1,0:T(8,128)(2,1)S(1)}, u32[]{:S(2)}, u32[]{:S(2)}) collective-permute-start(bf16[128,640]{1,0:T(8,128)(2,1)S(1)} %add_convert_fusion.1), channel_id=1, source_target_pairs={{0,16},{1,17},{2,18},{3,19},{4,20},{5,21},{6,22},{7,23},{8,24},{9,... | collective-permute-start | bytes 491528 | tf_op jit(solution)/shard_map/ppermute | solution.py:402
  93.9 13.7 %collective-permute-start.25 = (bf16[120,640]{1,0:T(8,128)(2,1)S(1)}, bf16[120,640]{1,0:T(8,128)(2,1)S(1)}, u32[]{:S(2)}, u32[]{:S(2)}) collective-permute-start(bf16[120,640]{1,0:T(8,128)(2,1)S(1)} %add_convert_fusion.5), channel_id=1, source_target_pairs={{0,16},{1,17},{2,18},{3,19},{4,20},{5,21},{6,22},{7,23},{8,24},{9,... | collective-permute-start | bytes 460808 | tf_op jit(solution)/shard_map/ppermute | solution.py:402
  101.1 5.1 %collective-permute-start.22 = (bf16[104,640]{1,0:T(8,128)(2,1)S(1)}, bf16[104,640]{1,0:T(8,128)(2,1)S(1)}, u32[]{:S(2)}, u32[]{:S(2)}) collective-permute-start(bf16[104,640]{1,0:T(8,128)(2,1)S(1)} %add_convert_fusion.8), channel_id=1, source_target_pairs={{0,4},{1,5},{2,6},{3,7},{4,0},{5,1},{6,2},{7,3},{8,12},{9,13},{10,... | collective-permute-start | bytes 399368 | tf_op jit(solution)/shard_map/ppermute | solution.py:402
  104.3 5.6 %collective-permute-start.27 = (bf16[128,640]{1,0:T(8,128)(2,1)S(1)}, bf16[128,640]{1,0:T(8,128)(2,1)S(1)}, u32[]{:S(2)}, u32[]{:S(2)}) collective-permute-start(bf16[128,640]{1,0:T(8,128)(2,1)S(1)} %add_convert_fusion), channel_id=1, source_target_pairs={{0,8},{1,9},{2,10},{3,11},{4,12},{5,13},{6,14},{7,15},{8,0},{9,1},... | collective-permute-start | bytes 491528 | tf_op jit(solution)/shard_map/ppermute | solution.py:402
  107.7 5.3 %collective-permute-start.29 = (bf16[120,640]{1,0:T(8,128)(2,1)S(1)}, bf16[120,640]{1,0:T(8,128)(2,1)S(1)}, u32[]{:S(2)}, u32[]{:S(2)}) collective-permute-start(bf16[120,640]{1,0:T(8,128)(2,1)S(1)} %add_convert_fusion.4), channel_id=1, source_target_pairs={{0,2},{1,3},{2,0},{3,1},{4,6},{5,7},{6,4},{7,5},{8,10},{9,11},{10,... | collective-permute-start | bytes 460808 | tf_op jit(solution)/shard_map/ppermute | solution.py:402
  108.3 7.6 %collective-permute-start.26 = (bf16[208,640]{1,0:T(8,128)(2,1)S(1)}, bf16[208,640]{1,0:T(8,128)(2,1)S(1)}, u32[]{:S(2)}, u32[]{:S(2)}) collective-permute-start(bf16[208,640]{1,0:T(8,128)(2,1)S(1)} %pad_maximum_fusion.8), channel_id=1, source_target_pairs={{0,2},{1,3},{2,0},{3,1},{4,6},{5,7},{6,4},{7,5},{8,10},{9,11},{10,... | collective-permute-start | bytes 798728 | tf_op jit(solution)/shard_map/ppermute | solution.py:402
  110.0 7.2 %collective-permute-start.28 = (bf16[256,640]{1,0:T(8,128)(2,1)S(1)}, bf16[256,640]{1,0:T(8,128)(2,1)S(1)}, u32[]{:S(2)}, u32[]{:S(2)}) collective-permute-start(bf16[256,640]{1,0:T(8,128)(2,1)S(1)} %pad_maximum_fusion.6), channel_id=1, source_target_pairs={{0,4},{1,5},{2,6},{3,7},{4,0},{5,1},{6,2},{7,3},{8,12},{9,13},{10,... | collective-permute-start | bytes 983048 | tf_op jit(solution)/shard_map/ppermute | solution.py:402
  113.1 8.7 %collective-permute-start.30 = (bf16[240,640]{1,0:T(8,128)(2,1)S(1)}, bf16[240,640]{1,0:T(8,128)(2,1)S(1)}, u32[]{:S(2)}, u32[]{:S(2)}) collective-permute-start(bf16[240,640]{1,0:T(8,128)(2,1)S(1)} %pad_maximum_fusion.7), channel_id=1, source_target_pairs={{0,8},{1,9},{2,10},{3,11},{4,12},{5,13},{6,14},{7,15},{8,0},{9,1},... | collective-permute-start | bytes 921608 | tf_op jit(solution)/shard_map/ppermute | solution.py:402
  117.3 13.3 %collective-permute-start.33 = (bf16[512,640]{1,0:T(8,128)(2,1)S(1)}, bf16[512,640]{1,0:T(8,128)(2,1)S(1)}, u32[]{:S(2)}, u32[]{:S(2)}) collective-permute-start(bf16[512,640]{1,0:T(8,128)(2,1)S(1)} %pad_maximum_fusion.3), channel_id=1, source_target_pairs={{0,2},{1,3},{2,0},{3,1},{4,6},{5,7},{6,4},{7,5},{8,10},{9,11},{10,... | collective-permute-start | bytes 1966088 | tf_op jit(solution)/shard_map/ppermute | solution.py:402
  118.6 12.8 %collective-permute-start.32 = (bf16[416,640]{1,0:T(8,128)(2,1)S(1)}, bf16[416,640]{1,0:T(8,128)(2,1)S(1)}, u32[]{:S(2)}, u32[]{:S(2)}) collective-permute-start(bf16[416,640]{1,0:T(8,128)(2,1)S(1)} %pad_maximum_fusion.5), channel_id=1, source_target_pairs={{0,8},{1,9},{2,10},{3,11},{4,12},{5,13},{6,14},{7,15},{8,0},{9,1},... | collective-permute-start | bytes 1597448 | tf_op jit(solution)/shard_map/ppermute | solution.py:402
  121.9 10.2 %collective-permute-start.31 = (bf16[480,640]{1,0:T(8,128)(2,1)S(1)}, bf16[480,640]{1,0:T(8,128)(2,1)S(1)}, u32[]{:S(2)}, u32[]{:S(2)}) collective-permute-start(bf16[480,640]{1,0:T(8,128)(2,1)S(1)} %pad_maximum_fusion.4), channel_id=1, source_target_pairs={{0,4},{1,5},{2,6},{3,7},{4,0},{5,1},{6,2},{7,3},{8,12},{9,13},{10,... | collective-permute-start | bytes 1843208 | tf_op jit(solution)/shard_map/ppermute | solution.py:402
  130.9 3.1 %collective-permute-start.35 = (bf16[1024,640]{1,0:T(8,128)(2,1)S(1)}, bf16[1024,640]{1,0:T(8,128)(2,1)S(1)}, u32[]{:S(2)}, u32[]{:S(2)}) collective-permute-start(bf16[1024,640]{1,0:T(8,128)(2,1)S(1)} %pad_maximum_fusion.kept.kept_second), channel_id=1, source_target_pairs={{0,1},{1,0},{2,3},{3,2},{4,5},{5,4},{6,7},{7,6},{8,9},{9,8},{10,11... | collective-permute-start | bytes 3932168 | tf_op jit(solution)/shard_map/ppermute | solution.py:402
  132.4 4.9 %collective-permute-start.36 = (bf16[960,640]{1,0:T(8,128)(2,1)S(1)}, bf16[960,640]{1,0:T(8,128)(2,1)S(1)}, u32[]{:S(2)}, u32[]{:S(2)}) collective-permute-start(bf16[960,640]{1,0:T(8,128)(2,1)S(1)} %pad_maximum_fusion.1.kept_third), channel_id=1, source_target_pairs={{0,1},{1,0},{2,3},{3,2},{4,5},{5,4},{6,7},{7,6},{8,9},{9,8},{10,11... | collective-permute-start | bytes 3686408 | tf_op jit(solution)/shard_map/ppermute | solution.py:402
  132.5 4.8 %collective-permute-start.34 = (bf16[832,640]{1,0:T(8,128)(2,1)S(1)}, bf16[832,640]{1,0:T(8,128)(2,1)S(1)}, u32[]{:S(2)}, u32[]{:S(2)}) collective-permute-start(bf16[832,640]{1,0:T(8,128)(2,1)S(1)} %pad_maximum_fusion.2.kept), channel_id=1, source_target_pairs={{0,1},{1,0},{2,3},{3,2},{4,5},{5,4},{6,7},{7,6},{8,9},{9,8},{10,11... | collective-permute-start | bytes 3194888 | tf_op jit(solution)/shard_map/ppermute | solution.py:402
